TPU v7x, 256 devices: a whole 4x4x8 slice. The times are simulated.
256 devices in a mesh: zone: 16 (over y_hi, x, core), sector: 16 (over z, y_lo).
Axes of the slice: x: 4, y: 4 (y_hi: 2, y_lo: 2; y = y_hi * 2 + y_lo), z: 8, core: 2. Of those that a mesh axis runs over, the one named last changes fastest.
Arguments:
- kernel: bfloat16 [32, 1024, 6144], P(None, 'zone', 'sector'), may hold values from -16 to 16
- lon_halo: int32 [1024], replicated, may hold values from 12 to 48, as said below
- lat_reach: int32 [1024], P('zone'), may hold values from 8 to 32, as said below
- polar_rows: int32 [96], replicated, may hold values from 0 to 1023, as said below
- polar_shift: int32 [96], replicated, may hold values from 0 to 6143
- blend: bfloat16 [32, 32], replicated, may hold values from -1 to 1
Outputs:
- smoothed: bfloat16 [32, 1024, 6144], P(None, 'zone', 'sector')
Inputs may be any that keep to these rules, and one draw needn't show every extreme that they name: `lon_halo`: some row has the half-width 48. `lat_reach`: some row has the half-width 32. `polar_rows`: the first 48 entries are distinct rows among the first 64 rows, ascending, starting with row 0; the last 48 are distinct rows among the last 64 rows, ascending, ending with row 1023.
All inputs are finite; a program needn't handle non-finite values.
Results may differ from a plain program's by a relative error of at most 0.0071.
Values may be sent and summed in bfloat16 or wider, within the bound.
No kernel may reach another device: no remote copies, remote signals or barrier semaphores. Data moves between devices by JAX's collectives and lax.ppermute only.
A program may use at most 256 MiB of HBM per device.

v0:
```python
import jax
import jax.numpy as jnp
from jax import lax
from jax.sharding import PartitionSpec as P

HMAX = 48
LMAX = 32


def padded_2(x, sides, width, wrap):
    for axis, dim in sides:
        size, length = (lax.axis_size(axis), x.shape[dim])
        up = [(i, (i + 1) % size) for i in range(size if wrap else size - 1)]
        down = [(j, i) for i, j in up]
        last = lax.slice_in_dim(x, length - width, length, axis=dim)
        leading = lax.slice_in_dim(x, 0, width, axis=dim)
        before = lax.ppermute(last, axis, up)
        after = lax.ppermute(leading, axis, down)
        x = jnp.concatenate([before, x, after], axis=dim)
    return x


def band_matrix(half, window, width):
    half_f = half.astype(jnp.float32)
    rate = 4.5 / (half_f * half_f)
    taps = jnp.arange(-HMAX, HMAX + 1, dtype=jnp.int32).astype(jnp.float32)
    kept = jnp.abs(taps)[None, :] <= half_f[:, None]
    total = jnp.sum(
        jnp.where(kept, jnp.exp(-rate[:, None] * (taps * taps)[None, :]), jnp.float32(0.0)), axis=1
    )
    offset = (
        jnp.arange(window, dtype=jnp.int32)[:, None]
        - HMAX
        - jnp.arange(width, dtype=jnp.int32)[None, :]
    ).astype(jnp.float32)
    inside = jnp.abs(offset)[None, :, :] <= half_f[:, None, None]
    weights = jnp.where(
        inside, jnp.exp(-rate[:, None, None] * (offset * offset)[None, :, :]), jnp.float32(0.0)
    )
    return (weights / total[:, None, None]).astype(jnp.bfloat16)


def lat_matrix(reach, first_row, row_total, margin):
    count = reach.shape[0]
    reach_f = reach.astype(jnp.float32)
    rate = 4.5 / (reach_f * reach_f)
    column = jnp.arange(count + 2 * margin, dtype=jnp.int32)
    line = jnp.arange(count, dtype=jnp.int32)
    offset = column[None, :] - margin - line[:, None]
    source = first_row - margin + column
    valid = (
        (jnp.abs(offset) <= reach[:, None]) & (source >= 0)[None, :] & (source < row_total)[None, :]
    )
    offset_f = offset.astype(jnp.float32)
    weights = jnp.where(valid, jnp.exp(-rate[:, None] * (offset_f * offset_f)), jnp.float32(0.0))
    total = jnp.sum(weights, axis=1)
    return (weights / total[:, None]).astype(jnp.bfloat16)


def cut_windows(source, starts, window):

    def one_window(values, start):
        return lax.dynamic_slice_in_dim(values, start, window, 1)

    return jax.vmap(one_window)(source, starts)


def polar_apply(windows, halves, window, width):

    def one_row(packed):
        values, half = packed
        matrix = band_matrix(half[None], window, width)[0]
        return jnp.dot(values, matrix, preferred_element_type=jnp.float32).astype(jnp.bfloat16)

    return lax.map(one_row, (windows, halves))


def per_device(kernel, lon_halo, lat_reach, polar_rows, polar_shift, blend):
    shells, row_count, col_count = kernel.shape
    sectors = lax.axis_size("sector")
    zones = lax.axis_size("zone")
    full_lon = col_count * sectors
    full_lat = row_count * zones
    zone_id = lax.axis_index("zone")
    sector_id = lax.axis_index("sector")
    own_halo = lax.dynamic_slice_in_dim(lon_halo, zone_id * row_count, row_count, 0)
    padded = padded_2(kernel, (("sector", 2),), HMAX, True)
    window = col_count + 2 * HMAX

    def lon_block(block_id, result):
        first = block_id * 8
        values = lax.dynamic_slice_in_dim(padded, first, 8, 1)
        halves = lax.dynamic_slice_in_dim(own_halo, first, 8, 0)
        matrix = band_matrix(halves, window, col_count)
        smooth_rows = jnp.einsum("sik,ikj->sij", values, matrix, preferred_element_type=jnp.float32)
        return lax.dynamic_update_slice_in_dim(result, smooth_rows.astype(jnp.bfloat16), first, 1)

    lon_smooth = lax.fori_loop(
        0, row_count // 8, lon_block, jnp.zeros((shells, row_count, col_count), jnp.bfloat16)
    )
    polar_count = polar_rows.shape[0] // 2
    north_rows = polar_rows[:polar_count]
    south_rows = polar_rows[polar_count:]
    cap_index = jnp.where(zone_id == 0, north_rows, south_rows)
    shifts = jnp.where(zone_id == 0, polar_shift[:polar_count], polar_shift[polar_count:])
    halves = lon_halo[cap_index]
    chosen = jnp.clip(cap_index - zone_id * row_count, 0, row_count - 1)
    at_pole = (zone_id == 0) | (zone_id == zones - 1)
    polar_in = jnp.transpose(kernel[:, chosen, :], (1, 0, 2))
    circles = lax.all_gather(polar_in, "sector", axis=2, tiled=True)
    looped = jnp.concatenate([circles, circles[:, :, :window]], axis=2)
    starts = (sector_id * col_count - shifts - HMAX) % full_lon
    windows = cut_windows(looped, starts, window)
    polar_res = polar_apply(windows, halves, window, col_count)
    current_rows = lon_smooth[:, chosen, :]
    replaced = jnp.where(at_pole, jnp.transpose(polar_res, (1, 0, 2)), current_rows)
    lon_smooth = lon_smooth.at[:, chosen, :].set(replaced)
    framed = padded_2(lon_smooth, (("zone", 1),), LMAX, False)
    lat_weight = lat_matrix(lat_reach, zone_id * row_count, full_lat, LMAX)
    lat_smooth = jnp.einsum(
        "ir,srj->sij", lat_weight, framed, preferred_element_type=jnp.float32
    ).astype(jnp.bfloat16)
    mixed = jnp.einsum("st,tij->sij", blend, lat_smooth, preferred_element_type=jnp.float32)
    return mixed.astype(jnp.bfloat16)


def solution(mesh):
    in_specs = (P(None, "zone", "sector"), P(), P("zone"), P(), P(), P())
    out_specs = P(None, "zone", "sector")
    return jax.shard_map(
        per_device, mesh=mesh, in_specs=in_specs, out_specs=out_specs, check_vma=False
    )
```

profile of v0, /device:TPU:1, one launch (start us, length us, event | category | flops | bytes accessed | tf_op | source)
XLA Modules:
  0.0 829.5 jit_solution(16144821002494569237)
XLA Ops:
  7.4 9.2 %gather_fusion = bf16[48,32,384]{2,0,1:T(8,128)(2,1)} fusion(bf16[32,64,384]{2,1,0:T(8,128)(2,1)} %param.10, s32[1024]{0:T(1024)S(1)} %pad_clamp_fusion.1), kind=kCustom, calls=%fused_computation | custom fusion | bytes 2359488 | tf_op jit(solution)/shard_map/gather | solution.py:109
  20.9 5.3 collective-permute-start.1
  27.1 42.6 %collective-permute-done = bf16[32,64,48]{2,0,1:T(8,128)(2,1)S(1)} collective-permute-done((bf16[32,64,48]{2,0,1:T(8,128)(2,1)}, bf16[32,64,48]{2,0,1:T(8,128)(2,1)S(1)}, u32[]{:S(2)}, u32[]{:S(2)}) %collective-permute-start) | collective-permute-done | bytes 196640 | tf_op jit(solution)/shard_map/ppermute | solution.py:17
  71.2 2.6 pad_maximum_fusion.1
  74.0 24.2 %while.27 = (s32[]{:T(128)}, bf16[32,64,384]{2,0,1:T(8,128)(2,1)S(1)}, s32[64]{0:T(128)S(1)}, bf16[32,64,480]{2,0,1:T(8,128)(2,1)}, s32[]{:T(128)}, /*index=5*/s32[]{:T(128)}, s32[]{:T(128)}, s32[]{:T(128)}) while((s32[]{:T(128)}, bf16[32,64,384]{2,0,1:T(8,128)(2,1)S(1)}, s32[64]{0:T(128)S(1)}, bf16[32,64,480]{2,0,1:T(8,128)(2,1)}, s32[]{:T(128)}, ...), condition=%wide.region_2.3_spmd, body=%wide.region_0.2_spmd.sunk | while | flops 102584224 | bytes 3416151 | solution.py:98
  74.7 2.5 fusion.68
  77.7 2.5 fusion.68
  80.7 2.5 fusion.68
  83.7 2.5 fusion.68
  86.7 2.5 fusion.68
  89.7 2.5 fusion.68
  92.7 2.5 fusion.68
  95.7 2.5 fusion.68
  99.0 326.2 %all-gather.2.cloned.1.call-done = bf16[48,32,6144]{2,0,1:T(8,128)(2,1)} async-done(((bf16[48,32,384]{2,0,1:T(8,128)(2,1)}), bf16[48,32,6144]{2,0,1:T(8,128)(2,1)}) %all-gather.2.cloned.1.call-update) | async-done | bytes 18874384 | tf_op jit(solution)/shard_map/all_gather | solution.py:110
  426.6 17.8 %pad_maximum_fusion = bf16[48,32,6624]{2,0,1:T(8,128)(2,1)} fusion(bf16[48,32,480]{2,0,1:T(8,128)(2,1)S(1)} %slice-done, bf16[48,32,6144]{2,0,1:T(8,128)(2,1)} %all-gather.2.cloned.1.call-done), kind=kLoop, calls=%fused_computation.41 | loop fusion | flops 40697856 | bytes 40697856 | tf_op jit(solution)/shard_map/concatenate | solution.py:111
  444.4 109.3 %copy.21 = bf16[48,32,6624]{1,0,2:T(8,128)(2,1)} copy(bf16[48,32,6624]{2,0,1:T(8,128)(2,1)} %pad_maximum_fusion) | data formatting | bytes 40697856 | tf_op jit(solution)/shard_map/concatenate | solution.py:111
  553.7 25.5 %gather_fusion.3 = bf16[48,32,480]{1,0,2:T(8,128)(2,1)} fusion(bf16[48,32,6624]{1,0,2:T(8,128)(2,1)} %copy.21, s32[48]{0:T(128)S(1)} %fusion.54), kind=kCustom, calls=%fused_computation.3 | custom fusion | bytes 2949696 | tf_op jit(solution)/shard_map/vmap()/gather | solution.py:63
  579.1 7.1 copy.22
  586.2 206.2 %while.28 = (s32[]{:T(128)}, bf16[48,32,384]{2,1,0:T(8,128)(2,1)}, bf16[48,32,480]{2,1,0:T(8,128)(2,1)}, s32[48]{0:T(128)S(1)}, s32[]{:T(128)}, /*index=5*/f32[1]{0:T(128)}) while((s32[]{:T(128)}, bf16[48,32,384]{2,1,0:T(8,128)(2,1)}, bf16[48,32,480]{2,1,0:T(8,128)(2,1)}, s32[48]{0:T(128)S(1)}, s32[]{:T(128)}, /*index=5*/f32[1]{0:T(128)}) %tuple.76), condition=%wide.region_5.6_spmd, body=%wide.region_3.5_spmd.sunk | while | flops 13468909 | bytes 63877 | solution.py:75
  588.0 2.4 fusion.72
  600.9 2.5 fusion.72
  613.8 2.5 fusion.72
  622.4 2.5 fusion.72
  635.2 2.5 fusion.72
  639.5 2.5 fusion.72
  652.4 2.5 fusion.72
  656.7 2.5 fusion.72
  669.6 2.5 fusion.72
  673.9 2.5 fusion.72
  686.8 2.5 fusion.72
  691.1 2.5 fusion.72
  695.4 2.5 fusion.72
  699.7 2.4 fusion.72
  704.0 2.5 fusion.72
  721.2 2.5 fusion.72
  725.5 2.5 fusion.72
  738.4 2.5 fusion.72
  755.6 2.5 fusion.72
  759.9 2.5 fusion.72
  764.2 2.5 fusion.72
  772.7 2.5 fusion.72
  777.0 2.5 fusion.72
  785.6 2.5 fusion.72
  789.9 2.5 fusion.72
  793.6 5.3 scatter_fusion
  799.6 4.7 collective-permute-start.2
  806.5 6.7 collective-permute-done.2
  813.2 4.5 collective-permute-done.3
  (246 shorter events, 138.0 us)
Async XLA Ops:
  6.5 813.2 %copy-start = (bf16[32,32]{1,0:T(8,128)(2,1)S(1)}, bf16[32,32]{1,0:T(8,128)(2,1)}, u32[]{:S(2)}) copy-start(bf16[32,32]{1,0:T(8,128)(2,1)} %param.15) | copy-start | bytes 6148
  6.5 418.6 %all-gather.2.cloned.1.call-start = ((), (), s32[]{:S(2)}) async-start(), calls=%async_computation | async-start | bytes 20054016 | tf_op jit(solution)/shard_map/all_gather | solution.py:110
  7.4 9.2 %copy-start.1 = (bf16[32,64,384]{2,1,0:T(8,128)(2,1)S(1)}, bf16[32,64,384]{2,1,0:T(8,128)(2,1)}, u32[]{:S(2)}) copy-start(bf16[32,64,384]{2,1,0:T(8,128)(2,1)} %param.10) | copy-start | bytes 4718596
  17.5 8.7 %copy-start.2 = (s32[1024]{0:T(1024)S(1)}, s32[1024]{0:T(1024)}, u32[]{:S(2)}) copy-start(s32[1024]{0:T(1024)} %param.11) | copy-start | bytes 12292
  17.5 9.5 %copy-start.3 = (s32[96]{0:T(128)S(1)}, s32[96]{0:T(128)}, u32[]{:S(2)}) copy-start(s32[96]{0:T(128)} %param.14) | copy-start | bytes 1156
  18.8 50.9 %collective-permute-start = (bf16[32,64,48]{2,0,1:T(8,128)(2,1)}, bf16[32,64,48]{2,0,1:T(8,128)(2,1)S(1)}, u32[]{:S(2)}, u32[]{:S(2)}) collective-permute-start(bf16[32,64,48]{2,0,1:T(8,128)(2,1)} %get-tuple-element.208), channel_id=1, source_target_pairs={{0,1},{1,2},{2,3},{3,4},{4,5},{5,6},{6,7},{7,8},{8,9},{9,10},{10,1... | collective-permute-start | bytes 589832 | tf_op jit(solution)/shard_map/ppermute | solution.py:17
  20.9 50.3 %collective-permute-start.1 = (bf16[32,64,48]{2,0,1:T(8,128)(2,1)}, bf16[32,64,48]{2,0,1:T(8,128)(2,1)S(1)}, u32[]{:S(2)}, u32[]{:S(2)}) collective-permute-start(bf16[32,64,48]{2,0,1:T(8,128)(2,1)} %get-tuple-element.209), channel_id=1, source_target_pairs={{1,0},{2,1},{3,2},{4,3},{5,4},{6,5},{7,6},{8,7},{9,8},{10,9},{11,1... | collective-permute-start | bytes 589832 | tf_op jit(solution)/shard_map/ppermute | solution.py:18
  425.2 1.4 slice-start
  799.4 6.8 copy-start.4
  799.6 13.6 %collective-permute-start.2 = (bf16[32,32,384]{2,1,0:T(8,128)(2,1)S(1)}, bf16[32,32,384]{2,1,0:T(8,128)(2,1)}, u32[]{:S(2)}, u32[]{:S(2)}) collective-permute-start(bf16[32,32,384]{2,1,0:T(8,128)(2,1)S(1)} %get-tuple-element.206), channel_id=1, source_target_pairs={{0,16},{16,32},{32,48},{48,64},{64,80},{80,96},{96,112},{112,128},... | collective-permute-start | bytes 2359304 | tf_op jit(solution)/shard_map/ppermute | solution.py:17
  804.3 13.4 %collective-permute-start.3 = (bf16[32,32,384]{2,1,0:T(8,128)(2,1)S(1)}, bf16[32,32,384]{2,1,0:T(8,128)(2,1)}, u32[]{:S(2)}, u32[]{:S(2)}) collective-permute-start(bf16[32,32,384]{2,1,0:T(8,128)(2,1)S(1)} %get-tuple-element.207), channel_id=1, source_target_pairs={{16,0},{32,16},{48,32},{64,48},{80,64},{96,80},{112,96},{128,112},... | collective-permute-start | bytes 2359304 | tf_op jit(solution)/shard_map/ppermute | solution.py:18
Sparse Core Ops, SparseCore 0:
  16.7 408.4 all-gather.1
where the time goes:
time: 844 us; the launch traced here: 830 us
  waiting for transfers between devices  382 us (45%)
  local copies, waits for them, and re-layouts  192 us (23%)
  matrix products  141 us (17%)
  other arithmetic  57.5 us (7%)
  loops' own time  29.9 us (4%)
  starting transfers between devices  14 us (2%)
  between operations  13.6 us (2%)
    all_gather x1, waiting for transfers between devices, per_device(): circles = lax.all_gather(polar_in, 'sector', axis=2, tiled=True)  326 us
    dot_general x48, matrix products, one_row(): jnp.dot(values, matrix, preferred_element_type=jnp.float32)  118 us
    concatenate x1, local copies, waits for them, and re-layouts, per_device(): looped = jnp.concatenate([circles, circles[:, :, :window]], axis=2)  109 us
    ppermute x2, waiting for transfers between devices, padded_2(): before = lax.ppermute(last, axis, up)  49.3 us
    reduce_sum x56, other arithmetic, band_matrix(): jnp.sum(jnp.where(kept, jnp.exp(-rate[:, None] * (taps * taps)[None, :]),...  32.5 us
    another operation x1, loops' own time, polar_apply(): return lax.map(one_row, (windows, halves))  29.4 us
    dynamic_slice x48, local copies, waits for them, and re-layouts, polar_apply(): return lax.map(one_row, (windows, halves))  28.1 us
    gather x1, local copies, waits for them, and re-layouts, one_window(): return lax.dynamic_slice_in_dim(values, start, window, 1)  25.5 us
  transfers between devices with their start and end apart: 5, of which 5 were waited for; matrix products, arithmetic and copies ran while one was open for 4% of the time, Pallas kernels for 0%

commit v1 on v0

v1 whole, which is shorter than its diff:
```python
import functools

import jax
import jax.numpy as jnp
from jax import lax
from jax.experimental import pallas as pl
from jax.experimental.pallas import tpu as pltpu
from jax.sharding import PartitionSpec as P

HMAX = 48
LMAX = 32
LANES = 128
F32 = jnp.float32
BF16 = jnp.bfloat16
VMEM_LIMIT = 40 * 1024 * 1024


def pack_kernel(zone_ref, rows_ref, x_ref, send_ref, low_ref, high_ref, wide_ref):
    shells, row_count, col_count = x_ref.shape
    total = shells * row_count
    half = total // 2
    zone = zone_ref[0]
    tiles = col_count // LANES
    for t in range(tiles):
        wide_ref[t] = x_ref[:, :, t * LANES : (t + 1) * LANES].reshape(total, LANES).astype(F32)
    holders, held = send_ref.shape[1], send_ref.shape[2]
    cap = jnp.where(zone < 8, 0, holders * held)

    def one_holder(k, carry):
        for r in range(held):
            row = jnp.clip(rows_ref[cap + k * held + r] - zone * row_count, 0, row_count - 1)
            for t in range(tiles):
                values = wide_ref[t, pl.ds(row, shells, stride=row_count), :].astype(BF16)
                for part in range(2):
                    send_ref[part, k, r, t * 16 : (t + 1) * 16, :] = values[part * 16 : (part + 1) * 16]
        return carry

    lax.fori_loop(0, holders, one_holder, 0)
    gap = jnp.zeros((half, LANES - 2 * HMAX), F32)
    for out_ref, t, first in ((low_ref, 0, 0), (high_ref, tiles - 1, LANES - HMAX)):
        edge = wide_ref[t, :, first : first + HMAX]
        out_ref[...] = jnp.concatenate([edge[:half], edge[half:], gap], axis=1).astype(BF16)


def band_rate(half_width):
    half_f = jnp.full((1, LANES), half_width, jnp.int32).astype(F32)
    rate = 4.5 / (half_f * half_f)
    tap = (lax.broadcasted_iota(jnp.int32, (1, LANES), 1) - HMAX).astype(F32)
    terms = jnp.where(jnp.abs(tap) <= half_f, jnp.exp(-rate * (tap * tap)), 0.0)
    total = jnp.sum(terms, axis=1, keepdims=True)
    return half_f, rate, total


def lon_kernel(zone_ref, halo_ref, x_ref, before_ref, after_ref, reach_ref, blend_ref,
               out_ref, weight_ref, mix_ref, wide_ref, done_ref):
    shells, row_count, col_count = x_ref.shape
    total = shells * row_count
    half = total // 2
    zone = zone_ref[0]

    def edge(ref):
        packed = ref[...].astype(F32)
        return jnp.concatenate([packed[:, :HMAX], packed[:, HMAX : 2 * HMAX]], axis=0)

    tiles = col_count // LANES
    wide = jnp.concatenate(
        [
            edge(before_ref),
            x_ref[...].reshape(total, col_count).astype(F32),
            edge(after_ref),
            jnp.zeros((total, LANES - 2 * HMAX), F32),
        ],
        axis=1,
    )
    for t in range(tiles + 1):
        wide_ref[t] = wide[:, t * LANES : (t + 1) * LANES]
    depth = 2 * LANES
    offset = (
        lax.broadcasted_iota(jnp.int32, (depth, LANES), 1)
        - lax.broadcasted_iota(jnp.int32, (depth, LANES), 0)
        + HMAX
    ).astype(F32)
    square = offset * offset
    distance = jnp.abs(offset)

    def one_row(i, carry):
        half_f, rate, terms = band_rate(halo_ref[zone * row_count + i])
        band = jnp.where(distance <= half_f, jnp.exp(-rate * square), 0.0) / terms
        values = [wide_ref[t, pl.ds(i, shells, stride=row_count), :].astype(BF16) for t in range(tiles + 1)]
        stacked = jnp.concatenate(
            [jnp.concatenate(values[:tiles], axis=0), jnp.concatenate(values[1:], axis=0)], axis=1
        )
        result = jnp.dot(stacked, band.astype(BF16), preferred_element_type=F32)
        for t in range(tiles):
            done_ref[t, pl.ds(i, shells, stride=row_count), :] = result[t * shells : (t + 1) * shells]
        return carry

    lax.fori_loop(0, row_count, one_row, 0)
    for t in range(tiles):
        out_ref[:, :, t * LANES : (t + 1) * LANES] = done_ref[t].astype(BF16).reshape(shells, row_count, LANES)
    frame_rows = weight_ref.shape[1]
    reach = reach_ref[...]
    column = lax.broadcasted_iota(jnp.int32, (row_count, frame_rows), 1)
    line = lax.broadcasted_iota(jnp.int32, (row_count, frame_rows), 0)
    away = column - LMAX - line
    source = zone * row_count - LMAX + column
    valid = (jnp.abs(away) <= reach) & (source >= 0) & (source < halo_ref.shape[0])
    reach_f = reach.astype(F32)
    away_f = away.astype(F32)
    weights = jnp.where(valid, jnp.exp(-(4.5 / (reach_f * reach_f)) * (away_f * away_f)), 0.0)
    weight_ref[...] = (weights / jnp.sum(weights, axis=1, keepdims=True)).astype(BF16)
    size = mix_ref.shape[0]
    group = size // shells
    spread = (
        lax.broadcasted_iota(jnp.int32, (size, shells), 0) // group
        == lax.broadcasted_iota(jnp.int32, (size, shells), 1)
    ).astype(F32).astype(BF16)
    tall = jnp.dot(spread, blend_ref[...], preferred_element_type=F32).astype(BF16)
    full = lax.dot_general(tall, spread, (((1,), (1,)), ((), ())), preferred_element_type=F32)
    same = (
        lax.broadcasted_iota(jnp.int32, (size, size), 0) % group
        == lax.broadcasted_iota(jnp.int32, (size, size), 1) % group
    )
    mix_ref[...] = jnp.where(same, full, 0.0).astype(BF16)


def hold_kernel(place_ref, rows_ref, shift_ref, halo_ref, x_ref, out_ref, circle_ref):
    sectors, held, block, _ = x_ref.shape
    zone, sector = place_ref[0], place_ref[1]
    cap = jnp.where(zone < 8, 0, sectors * held)
    part = 16
    length = sectors * block
    full_lon = length // part * LANES
    for r in range(held):
        for copy in range(2):
            circle_ref[r, copy * length : (copy + 1) * length, :] = x_ref[:, r].reshape(length, LANES)
        circle_ref[r, 2 * length : 2 * length + 2 * part, :] = circle_ref[r, 0 : 2 * part, :]
    for r in range(held):
        entry = cap + sector * held + r
        half_f, rate, terms = band_rate(halo_ref[rows_ref[entry]])
        start = lax.rem(2 * full_lon - shift_ref[entry] - HMAX, full_lon)
        first = start // LANES
        rest = start - first * LANES
        depth = 3 * LANES
        offset = (
            lax.broadcasted_iota(jnp.int32, (depth, LANES), 1)
            - lax.broadcasted_iota(jnp.int32, (depth, LANES), 0)
            + (rest + HMAX)
        ).astype(F32)
        band = jnp.where(jnp.abs(offset) <= half_f, jnp.exp(-rate * (offset * offset)), 0.0) / terms
        values = jnp.concatenate(
            [circle_ref[r, pl.ds(pl.multiple_of((first + u) * part, part), length), :] for u in range(3)], axis=1
        )
        result = jnp.dot(values, band.astype(BF16), preferred_element_type=F32)
        out_ref[:, r] = result.astype(BF16).reshape(sectors, block, LANES)


def lat_kernel(zone_ref, rows_ref, above_ref, own_ref, below_ref, mine_ref, other_ref, weight_ref, mix_ref,
               out_ref, frame_ref, lat_ref):
    shells, row_count, col_count = own_ref.shape
    frame_rows = row_count + 2 * LMAX
    zone = zone_ref[0]
    zones = 16
    tiles = col_count // LANES

    def one_frame(s, carry):
        base = pl.multiple_of(s * frame_rows, frame_rows)
        for t in range(tiles):
            columns = slice(t * LANES, (t + 1) * LANES)
            frame_ref[t, pl.ds(base, LMAX), :] = above_ref[s, :, columns].astype(F32)
            frame_ref[t, pl.ds(base + LMAX, row_count), :] = own_ref[s, :, columns].astype(F32)
            frame_ref[t, pl.ds(base + LMAX + row_count, LMAX), :] = below_ref[s, :, columns].astype(F32)
        return carry

    lax.fori_loop(0, shells, one_frame, 0)

    @pl.when((zone <= 1) | (zone >= zones - 2))
    def _():
        holders, held, block, _ = mine_ref.shape
        cap = jnp.where(zone < 8, 0, holders * held)
        outer = (zone == 0) | (zone == zones - 1)
        mine_part = jnp.where(outer, 0, 1)

        def one_holder(k, carry):
            for r in range(held):
                place = rows_ref[cap + k * held + r] - zone * row_count + LMAX

                @pl.when((place >= 0) & (place < frame_rows))
                def _():
                    for ref, part in ((mine_ref, mine_part), (other_ref, 1 - mine_part)):
                        for t in range(tiles):
                            frame_ref[
                                t, pl.ds(part * (16 * frame_rows) + place, 16, stride=frame_rows), :
                            ] = ref[k, r, t * 16 : (t + 1) * 16, :].astype(F32)

            return carry

        lax.fori_loop(0, holders, one_holder, 0)

    weight = weight_ref[...]

    def one_shell(s, carry):
        base = pl.multiple_of(s * frame_rows, frame_rows)
        values = jnp.concatenate(
            [frame_ref[t, pl.ds(base, frame_rows), :].astype(BF16) for t in range(tiles)], axis=1
        )
        lat_ref[s] = jnp.dot(weight, values, preferred_element_type=F32).astype(BF16)
        return carry

    lax.fori_loop(0, shells, one_shell, 0)
    group = mix_ref.shape[0] // shells
    for g in range(row_count // group):
        values = lat_ref[:, g * group : (g + 1) * group, :].reshape(shells * group, col_count)
        mixed = jnp.dot(mix_ref[...], values, preferred_element_type=F32)
        out_ref[:, g * group : (g + 1) * group, :] = mixed.astype(BF16).reshape(shells, group, col_count)


def call(kernel, name, out_shape, scalars, arrays, scratch, flops=0, moved=0):
    smem = pl.BlockSpec(memory_space=pltpu.SMEM)
    vmem = pl.BlockSpec(memory_space=pltpu.VMEM)
    many = isinstance(out_shape, tuple)
    return pl.pallas_call(
        kernel,
        out_shape=out_shape,
        in_specs=[smem] * len(scalars) + [vmem] * len(arrays),
        out_specs=(vmem,) * len(out_shape) if many else vmem,
        scratch_shapes=scratch,
        compiler_params=pltpu.CompilerParams(vmem_limit_bytes=VMEM_LIMIT),
        cost_estimate=pl.CostEstimate(flops=flops, bytes_accessed=moved, transcendentals=0),
        name=name,
    )(*scalars, *arrays)


def per_device(kernel, lon_halo, lat_reach, polar_rows, polar_shift, blend):
    shells, row_count, col_count = kernel.shape
    sectors = lax.axis_size("sector")
    zones = lax.axis_size("zone")
    zone_id = lax.axis_index("zone").astype(jnp.int32)
    sector_id = lax.axis_index("sector").astype(jnp.int32)
    place = jnp.stack([zone_id, sector_id])
    held = polar_rows.shape[0] // 2 // sectors
    tiles = col_count // LANES
    block = tiles * 16
    half = shells * row_count // 2
    struct = jax.ShapeDtypeStruct

    send, low, high = call(
        pack_kernel,
        "pack_polar_rows_and_edges",
        (
            struct((2, sectors, held, block, LANES), BF16),
            struct((half, LANES), BF16),
            struct((half, LANES), BF16),
        ),
        [place, polar_rows],
        [kernel],
        [pltpu.VMEM((tiles, shells * row_count, LANES), F32)],
        moved=4 << 20,
    )
    last = zones - 1
    given = lax.ppermute(send[1], "zone", [(0, 1), (last, last - 1)])
    up = [(i, (i + 1) % sectors) for i in range(sectors)]
    down = [(j, i) for i, j in up]
    before = lax.ppermute(high, "sector", up)
    after = lax.ppermute(low, "sector", down)
    inner = (zone_id == 1) | (zone_id == last - 1)
    parts = jnp.where(inner, given, send[0])
    circles = lax.all_to_all(parts, "sector", 0, 0, tiled=True)
    lon_smooth, lat_weight, mix = call(
        lon_kernel,
        "smooth_along_longitude",
        (
            struct((shells, row_count, col_count), BF16),
            struct((row_count, row_count + 2 * LMAX), BF16),
            struct((shells * 16, shells * 16), BF16),
        ),
        [place, lon_halo],
        [kernel, before, after, lat_reach[:, None], blend],
        [
            pltpu.VMEM((tiles + 1, shells * row_count, LANES), F32),
            pltpu.VMEM((tiles, shells * row_count, LANES), F32),
        ],
        flops=1 << 32,
        moved=16 << 20,
    )
    north = [(i, i + 1) for i in range(zones - 1)]
    south = [(j, i) for i, j in north]
    above = lax.ppermute(lon_smooth[:, row_count - LMAX :], "zone", north)
    below = lax.ppermute(lon_smooth[:, :LMAX], "zone", south)
    turned = call(
        hold_kernel,
        "smooth_and_turn_polar_circles",
        struct((sectors, held, block, LANES), BF16),
        [place, polar_rows, polar_shift, lon_halo],
        [circles],
        [pltpu.VMEM((held, 2 * sectors * block + 32, LANES), BF16)],
        flops=1 << 30,
        moved=4 << 20,
    )
    mine = lax.all_to_all(turned, "sector", 0, 0, tiled=True)
    other = lax.ppermute(mine, "zone", [(0, 1), (1, 0), (last, last - 1), (last - 1, last)])
    return call(
        lat_kernel,
        "smooth_along_latitude_and_blend",
        struct((shells, row_count, col_count), BF16),
        [place, polar_rows],
        [above, lon_smooth, below, mine, other, lat_weight, mix],
        [
            pltpu.VMEM((tiles, shells * (row_count + 2 * LMAX), LANES), F32),
            pltpu.VMEM((shells, row_count, col_count), BF16),
        ],
        flops=1 << 31,
        moved=8 << 20,
    )


def solution(mesh):
    in_specs = (P(None, "zone", "sector"), P(), P("zone"), P(), P(), P())
    out_specs = P(None, "zone", "sector")
    return jax.shard_map(
        per_device, mesh=mesh, in_specs=in_specs, out_specs=out_specs, check_vma=False
    )
```

time: 844 us -> 100 us (0.12); the launches traced: 830 us -> 98.2 us
  waiting for transfers between devices: 382 us -> 25.2 us
  local copies, waits for them, and re-layouts: 192 us -> 7.92 us
  matrix products: 141 us -> 0 us
  other arithmetic: 57.5 us -> 0.95 us
  Pallas kernels: 0 us -> 37.4 us
  loops' own time: 29.9 us -> 0 us
  between operations: 13.6 us -> 0.16 us
  starting transfers between devices: 14 us -> 26.6 us
    all_gather x1 -> x0, waiting for transfers between devices: 326 us -> none  [per_device(): circles = lax.all_gather(polar_in, 'sector', axis=2, tiled=True)]
    dot_general x58 -> x0, matrix products: 141 us -> none  [the longest x48 118 us: one_row(): jnp.dot(values, matrix, preferred_element_type=jnp.float32)]
    concatenate x1 -> x0, local copies, waits for them, and re-layouts: 109 us -> none  [per_device(): looped = jnp.concatenate([circles, circles[:, :, :window]], axis=2)]
    ppermute x4 -> x6, waiting for transfers between devices: 55.4 us -> 11.5 us  [the longest x1 5.15 us: per_device(): below = lax.ppermute(lon_smooth[:, :LMAX], 'zone', south)]
    pallas_call x0 -> x4, Pallas kernels: none -> 37.4 us  [call(): pl.pallas_call(kernel, out_shape=out_shape, in_specs=[smem] * len(scalars...]
    gather x4 -> x0, local copies, waits for them, and re-layouts: 36.2 us -> none  [the longest x1 25.5 us: one_window(): return lax.dynamic_slice_in_dim(values, start, window, 1)]
    reduce_sum x57 -> x0, other arithmetic: 32.7 us -> none  [the longest x56 32.5 us: band_matrix(): jnp.sum(jnp.where(kept, jnp.exp(-rate[:, None] * (taps * taps)[None, :]),...]
    another operation x2 -> x0, loops' own time: 29.9 us -> none  [the longest x1 29.4 us: polar_apply(): return lax.map(one_row, (windows, halves))]
  transfers between devices with their start and end apart: 5 -> 8, of which waited for: 5 -> 4; matrix products, arithmetic and copies ran while one was open for 4% -> 1% of each run, Pallas kernels for 0% -> 24%
where the time goes in v1:
time: 100 us; the launch traced here: 98.2 us
  Pallas kernels  37.4 us (37%)
  starting transfers between devices  26.6 us (27%)
  waiting for transfers between devices  25.2 us (25%)
  local copies, waits for them, and re-layouts  7.92 us (8%)
    pallas_call x4, Pallas kernels, call(): pl.pallas_call(kernel, out_shape=out_shape, in_specs=[smem] * len(scalars...  37.4 us
    all_to_all x1, waiting for transfers between devices, per_device(): circles = lax.all_to_all(parts, 'sector', 0, 0, tiled=True)  13.7 us
    all_to_all x1, starting transfers between devices, per_device(): circles = lax.all_to_all(parts, 'sector', 0, 0, tiled=True)  8.01 us
    unnamed x28, local copies, waits for them, and re-layouts  6.44 us
    all_to_all x1, starting transfers between devices, per_device(): mine = lax.all_to_all(turned, 'sector', 0, 0, tiled=True)  5.17 us
    ppermute x1, waiting for transfers between devices, per_device(): below = lax.ppermute(lon_smooth[:, :LMAX], 'zone', south)  5.15 us
    ppermute x1, waiting for transfers between devices, per_device(): given = lax.ppermute(send[1], 'zone', [(0, 1), (last, last - 1)])  4.71 us
    ppermute x1, starting transfers between devices, per_device(): below = lax.ppermute(lon_smooth[:, :LMAX], 'zone', south)  3.95 us
  transfers between devices with their start and end apart: 8, of which 4 were waited for; matrix products, arithmetic and copies ran while one was open for 1% of the time, Pallas kernels for 24%

profile of v1, /device:TPU:1, one launch (start us, length us, event | category | flops | bytes accessed | tf_op | source)
XLA Modules:
  0.0 98.2 jit_solution(3943419012177796878)
XLA Ops:
  0.0 0.1 pad_add_fusion.zone_ref.place_ref
  0.1 0.0 copy-start
  0.1 1.4 %copy-done = bf16[32,64,384]{2,1,0:T(8,128)(2,1)S(1)} copy-done((bf16[32,64,384]{2,1,0:T(8,128)(2,1)S(1)}, bf16[32,64,384]{2,1,0:T(8,128)(2,1)}, u32[]{:S(2)}) %copy-start) | copy-done | bytes 1572888
  1.5 0.7 copy-done.2
  2.1 3.6 %pack_polar_rows_and_edges.1 = (bf16[2,16,3,48,128]{4,3,2,1,0:T(8,128)(2,1)S(1)}, bf16[1024,128]{1,0:T(8,128)(2,1)S(1)}, bf16[1024,128]{1,0:T(8,128)(2,1)S(1)}) custom-call(s32[2]{0:T(128)S(1)} %pad_add_fusion.zone_ref.place_ref, s32[96]{0:T(128)S(1)} %copy-done.2, bf16[32,64,384]{2,1,0:T(8,128)(2,1)S(1)} %copy-done), custom_call_target="tpu_custom_call" | custom-call | bytes 4194304 | tf_op jit(solution)/shard_map/pack_polar_rows_and_edges/pallas_call | solution.py:222
  5.8 0.0 copy-start.3
  5.8 0.0 copy-start.9
  5.8 0.0 copy-start.10
  5.9 1.4 %collective-permute-start.4 = (bf16[16,3,48,128]{3,2,1,0:T(8,128)(2,1)S(1)}, bf16[16,3,48,128]{3,2,1,0:T(8,128)(2,1)S(1)}, u32[]{:S(2)}, u32[]{:S(2)}) collective-permute-start(bf16[16,3,48,128]{3,2,1,0:T(8,128)(2,1)S(1)} %slice_bitcast_fusion), channel_id=1, source_target_pairs={{0,16},{240,224},{1,17},{241,225},{2,18},{242,226},{3,19},{243,227... | collective-permute-start | bytes 1769480 | tf_op jit(solution)/shard_map/ppermute | solution.py:261
  7.3 4.7 %collective-permute-done.4 = bf16[16,3,48,128]{3,2,1,0:T(8,128)(2,1)S(1)} collective-permute-done((bf16[16,3,48,128]{3,2,1,0:T(8,128)(2,1)S(1)}, bf16[16,3,48,128]{3,2,1,0:T(8,128)(2,1)S(1)}, u32[]{:S(2)}, u32[]{:S(2)}) %collective-permute-start.4) | collective-permute-done | bytes 589856 | tf_op jit(solution)/shard_map/ppermute | solution.py:261
  12.0 0.9 bitcast_select_fusion
  12.9 8.0 %all-to-all-start = ((bf16[16,3,48,128]{3,2,1,0:T(8,128)(2,1)}), bf16[16,3,48,128]{3,2,1,0:T(8,128)(2,1)S(1)}, u32[]{:S(2)}, u32[]{:S(2)}) async-start(bf16[16,3,48,128]{3,2,1,0:T(8,128)(2,1)} %bitcast_select_fusion), calls=%async_computation | async-start | bytes 1179648 | tf_op jit(solution)/shard_map/all_to_all | solution.py:268
  20.9 1.4 %collective-permute-start = (bf16[1024,128]{1,0:T(8,128)(2,1)S(1)}, bf16[1024,128]{1,0:T(8,128)(2,1)S(1)}, u32[]{:S(2)}, u32[]{:S(2)}) collective-permute-start(bf16[1024,128]{1,0:T(8,128)(2,1)S(1)} %get-tuple-element.11), channel_id=1, source_target_pairs={{0,1},{1,2},{2,3},{3,4},{4,5},{5,6},{6,7},{7,8},{8,9},{9,10},{10,1... | collective-permute-start | bytes 786440 | tf_op jit(solution)/shard_map/ppermute | solution.py:264
  22.3 0.0 copy-start.13
  22.3 0.0 copy-start.1
  22.3 0.0 copy-start.8
  22.3 2.3 %collective-permute-start.1 = (bf16[1024,128]{1,0:T(8,128)(2,1)S(1)}, bf16[1024,128]{1,0:T(8,128)(2,1)S(1)}, u32[]{:S(2)}, u32[]{:S(2)}) collective-permute-start(bf16[1024,128]{1,0:T(8,128)(2,1)S(1)} %get-tuple-element.12), channel_id=1, source_target_pairs={{1,0},{2,1},{3,2},{4,3},{5,4},{6,5},{7,6},{8,7},{9,8},{10,9},{11,1... | collective-permute-start | bytes 786440 | tf_op jit(solution)/shard_map/ppermute | solution.py:265
  24.6 13.7 %all-to-all-done.x_ref = bf16[16,3,48,128]{3,2,1,0:T(8,128)(2,1)S(1)} async-done(((bf16[16,3,48,128]{3,2,1,0:T(8,128)(2,1)}), bf16[16,3,48,128]{3,2,1,0:T(8,128)(2,1)S(1)}, u32[]{:S(2)}, u32[]{:S(2)}) %all-to-all-start) | async-done | bytes 589856 | tf_op jit(solution)/shard_map/all_to_all | solution.py:268
  38.3 0.0 copy-done.3
  38.3 0.0 copy-done.9
  38.3 0.0 copy-done.10
  38.3 2.3 %smooth_and_turn_polar_circles.1 = bf16[16,3,48,128]{3,2,1,0:T(8,128)(2,1)} custom-call(s32[2]{0:T(128)S(1)} %pad_add_fusion.zone_ref.place_ref, s32[96]{0:T(128)S(1)} %copy-done.3, s32[96]{0:T(128)S(1)} %copy-done.10, s32[1024]{0:T(1024)S(1)} %copy-done.9, bf16[16,3,48,128]{3,2,1,0:T(8,128)(2,1)S(1)} %all-to-all-done.x_ref), custom_call_target="tpu_custom_call" | custom-call | flops 1073741824 | bytes 4194304 | tf_op jit(solution)/shard_map/smooth_and_turn_polar_circles/pallas_call | solution.py:222
  40.6 5.2 %all-to-all-start.1 = ((bf16[16,3,48,128]{3,2,1,0:T(8,128)(2,1)}), bf16[16,3,48,128]{3,2,1,0:T(8,128)(2,1)}, u32[]{:S(2)}, u32[]{:S(2)}) async-start(bf16[16,3,48,128]{3,2,1,0:T(8,128)(2,1)} %smooth_and_turn_polar_circles.1), calls=%async_computation.1 | async-start | bytes 1179648 | tf_op jit(solution)/shard_map/all_to_all | solution.py:300
  45.8 0.0 copy-done.13
  45.8 0.1 copy.7.reach_ref
  45.9 0.0 collective-permute-done.before_ref
  45.9 0.0 copy-start.4
  45.9 0.7 copy-done.4
  46.6 0.0 collective-permute-done.1.after_ref
  46.6 0.0 copy-start.6
  46.6 0.7 copy-done.6
  47.3 0.0 copy-done.1
  47.3 0.0 copy-done.8
  47.3 0.9 copy-done.5
  48.3 0.9 copy-done.7
  49.2 21.2 %smooth_along_longitude.1 = (bf16[32,64,384]{2,1,0:T(8,128)(2,1)S(1)}, bf16[64,128]{1,0:T(8,128)(2,1)S(1)}, bf16[512,512]{1,0:T(8,128)(2,1)S(1)}) custom-call(s32[2]{0:T(128)S(1)} %pad_add_fusion.zone_ref.place_ref, s32[1024]{0:T(1024)S(1)} %copy-done.9, bf16[32,64,384]{2,1,0:T(8,128)(2,1)S(1)} %copy-done.1, bf16[1024,128]{1,0:T(8,128)(2,1)S(1)} %copy-done.5, ...), custom_call_target="tpu_custom_call" | custom-call | flops 4294967296 | bytes 16777216 | tf_op jit(solution)/shard_map/smooth_along_longitude/pallas_call | solution.py:222
  70.4 0.0 copy-start.11
  70.4 1.3 %fusion = (bf16[32,32,384]{2,1,0:T(8,128)(2,1)}, bf16[32,32,384]{2,1,0:T(8,128)(2,1)}) fusion(bf16[32,64,384]{2,1,0:T(8,128)(2,1)S(1)} %get-tuple-element.13.own_ref), kind=kLoop, calls=%fused_computation.3 | loop fusion | bytes 3145728 | tf_op jit(solution)/shard_map/slice | solution.py:289
  71.7 0.0 copy-done.11
  71.7 4.0 %collective-permute-start.3 = (bf16[32,32,384]{2,1,0:T(8,128)(2,1)}, bf16[32,32,384]{2,1,0:T(8,128)(2,1)S(1)}, u32[]{:S(2)}, u32[]{:S(2)}) collective-permute-start(bf16[32,32,384]{2,1,0:T(8,128)(2,1)} %get-tuple-element.17), channel_id=1, source_target_pairs={{16,0},{32,16},{48,32},{64,48},{80,64},{96,80},{112,96},{128,112},... | collective-permute-start | bytes 2359304 | tf_op jit(solution)/shard_map/ppermute | solution.py:289
  75.7 1.9 %collective-permute-start.2 = (bf16[32,32,384]{2,1,0:T(8,128)(2,1)}, bf16[32,32,384]{2,1,0:T(8,128)(2,1)S(1)}, u32[]{:S(2)}, u32[]{:S(2)}) collective-permute-start(bf16[32,32,384]{2,1,0:T(8,128)(2,1)} %get-tuple-element.18), channel_id=1, source_target_pairs={{0,16},{16,32},{32,48},{48,64},{64,80},{80,96},{96,112},{112,128},... | collective-permute-start | bytes 2359304 | tf_op jit(solution)/shard_map/ppermute | solution.py:288
  77.6 0.0 all-to-all-done.1.mine_ref
  77.6 2.5 %collective-permute-start.5 = (bf16[16,3,48,128]{3,2,1,0:T(8,128)(2,1)}, bf16[16,3,48,128]{3,2,1,0:T(8,128)(2,1)S(1)}, u32[]{:S(2)}, u32[]{:S(2)}) collective-permute-start(bf16[16,3,48,128]{3,2,1,0:T(8,128)(2,1)} %all-to-all-done.1.mine_ref), channel_id=1, source_target_pairs={{0,16},{16,0},{240,224},{224,240},{1,17},{17,1},{241,225},{225,241... | collective-permute-start | bytes 1769480 | tf_op jit(solution)/shard_map/ppermute | solution.py:301
  80.1 5.2 %collective-permute-done.3.below_ref = bf16[32,32,384]{2,1,0:T(8,128)(2,1)S(1)} collective-permute-done((bf16[32,32,384]{2,1,0:T(8,128)(2,1)}, bf16[32,32,384]{2,1,0:T(8,128)(2,1)S(1)}, u32[]{:S(2)}, u32[]{:S(2)}) %collective-permute-start.3) | collective-permute-done | bytes 786464 | tf_op jit(solution)/shard_map/ppermute | solution.py:289
  85.2 1.6 %collective-permute-done.2.above_ref = bf16[32,32,384]{2,1,0:T(8,128)(2,1)S(1)} collective-permute-done((bf16[32,32,384]{2,1,0:T(8,128)(2,1)}, bf16[32,32,384]{2,1,0:T(8,128)(2,1)S(1)}, u32[]{:S(2)}, u32[]{:S(2)}) %collective-permute-start.2) | collective-permute-done | bytes 786464 | tf_op jit(solution)/shard_map/ppermute | solution.py:288
  86.9 0.0 collective-permute-done.5.other_ref
  86.9 1.0 %copy-done.12 = bf16[512,512]{1,0:T(8,128)(2,1)S(1)} copy-done((bf16[512,512]{1,0:T(8,128)(2,1)S(1)}, bf16[512,512]{1,0:T(8,128)(2,1)}, u32[]{:S(2)}) %copy-start.12) | copy-done | bytes 524312
  87.9 10.3 %smooth_along_latitude_and_blend.1 = bf16[32,64,384]{2,1,0:T(8,128)(2,1)} custom-call(s32[2]{0:T(128)S(1)} %pad_add_fusion.zone_ref.place_ref, s32[96]{0:T(128)S(1)} %copy-done.3, bf16[32,32,384]{2,1,0:T(8,128)(2,1)S(1)} %collective-permute-done.2.above_ref, bf16[32,64,384]{2,1,0:T(8,128)(2,1)S(1)} %get-tuple-element.13.own_ref, ...), custom_call_target="tpu_custom_call" | custom-call | flops 2147483648 | bytes 8388608 | tf_op jit(solution)/shard_map/smooth_along_latitude_and_blend/pallas_call | solution.py:222
  (5 shorter events, 0.0 us)
Async XLA Ops:
  0.1 1.4 %copy-start = (bf16[32,64,384]{2,1,0:T(8,128)(2,1)S(1)}, bf16[32,64,384]{2,1,0:T(8,128)(2,1)}, u32[]{:S(2)}) copy-start(bf16[32,64,384]{2,1,0:T(8,128)(2,1)} %x_ref.3) | copy-start | bytes 4718596
  1.5 0.7 copy-start.2
  5.8 32.5 %copy-start.3 = (s32[96]{0:T(128)S(1)}, s32[96]{0:T(128)}, u32[]{:S(2)}) copy-start(s32[96]{0:T(128)} %rows_ref.5) | copy-start | bytes 1156
  5.8 32.4 %copy-start.9 = (s32[1024]{0:T(1024)S(1)}, s32[1024]{0:T(1024)}, u32[]{:S(2)}) copy-start(s32[1024]{0:T(1024)} %halo_ref.3) | copy-start | bytes 12292
  5.8 32.4 %copy-start.10 = (s32[96]{0:T(128)S(1)}, s32[96]{0:T(128)}, u32[]{:S(2)}) copy-start(s32[96]{0:T(128)} %shift_ref.1) | copy-start | bytes 1156
  5.9 6.2 %collective-permute-start.4 = (bf16[16,3,48,128]{3,2,1,0:T(8,128)(2,1)S(1)}, bf16[16,3,48,128]{3,2,1,0:T(8,128)(2,1)S(1)}, u32[]{:S(2)}, u32[]{:S(2)}) collective-permute-start(bf16[16,3,48,128]{3,2,1,0:T(8,128)(2,1)S(1)} %slice_bitcast_fusion), channel_id=1, source_target_pairs={{0,16},{240,224},{1,17},{241,225},{2,18},{242,226},{3,19},{243,227... | collective-permute-start | bytes 1769480 | tf_op jit(solution)/shard_map/ppermute | solution.py:261
  12.9 25.4 %all-to-all-start = ((bf16[16,3,48,128]{3,2,1,0:T(8,128)(2,1)}), bf16[16,3,48,128]{3,2,1,0:T(8,128)(2,1)S(1)}, u32[]{:S(2)}, u32[]{:S(2)}) async-start(bf16[16,3,48,128]{3,2,1,0:T(8,128)(2,1)} %bitcast_select_fusion), calls=%async_computation | async-start | bytes 1179648 | tf_op jit(solution)/shard_map/all_to_all | solution.py:268
  20.9 25.0 %collective-permute-start = (bf16[1024,128]{1,0:T(8,128)(2,1)S(1)}, bf16[1024,128]{1,0:T(8,128)(2,1)S(1)}, u32[]{:S(2)}, u32[]{:S(2)}) collective-permute-start(bf16[1024,128]{1,0:T(8,128)(2,1)S(1)} %get-tuple-element.11), channel_id=1, source_target_pairs={{0,1},{1,2},{2,3},{3,4},{4,5},{5,6},{6,7},{7,8},{8,9},{9,10},{10,1... | collective-permute-start | bytes 786440 | tf_op jit(solution)/shard_map/ppermute | solution.py:264
  22.3 23.5 %copy-start.13 = (s32[64]{0:T(128)S(1)}, s32[64]{0:T(128)}, u32[]{:S(2)}) copy-start(s32[64]{0:T(128)} %param.8) | copy-start | bytes 772
  22.3 25.0 %copy-start.1 = (bf16[32,64,384]{2,1,0:T(8,128)(2,1)S(1)}, bf16[32,64,384]{2,1,0:T(8,128)(2,1)}, u32[]{:S(2)}) copy-start(bf16[32,64,384]{2,1,0:T(8,128)(2,1)} %x_ref.3) | copy-start | bytes 4718596
  22.3 25.0 %copy-start.8 = (bf16[32,32]{1,0:T(8,128)(2,1)S(1)}, bf16[32,32]{1,0:T(8,128)(2,1)}, u32[]{:S(2)}) copy-start(bf16[32,32]{1,0:T(8,128)(2,1)} %blend_ref.1) | copy-start | bytes 6148
  22.3 24.3 %collective-permute-start.1 = (bf16[1024,128]{1,0:T(8,128)(2,1)S(1)}, bf16[1024,128]{1,0:T(8,128)(2,1)S(1)}, u32[]{:S(2)}, u32[]{:S(2)}) collective-permute-start(bf16[1024,128]{1,0:T(8,128)(2,1)S(1)} %get-tuple-element.12), channel_id=1, source_target_pairs={{1,0},{2,1},{3,2},{4,3},{5,4},{6,5},{7,6},{8,7},{9,8},{10,9},{11,1... | collective-permute-start | bytes 786440 | tf_op jit(solution)/shard_map/ppermute | solution.py:265
  40.6 37.0 %all-to-all-start.1 = ((bf16[16,3,48,128]{3,2,1,0:T(8,128)(2,1)}), bf16[16,3,48,128]{3,2,1,0:T(8,128)(2,1)}, u32[]{:S(2)}, u32[]{:S(2)}) async-start(bf16[16,3,48,128]{3,2,1,0:T(8,128)(2,1)} %smooth_and_turn_polar_circles.1), calls=%async_computation.1 | async-start | bytes 1179648 | tf_op jit(solution)/shard_map/all_to_all | solution.py:300
  45.9 0.7 copy-start.4
  46.6 0.7 copy-start.6
  47.3 1.0 copy-start.5
  48.2 0.9 copy-start.7
  70.4 1.4 %copy-start.11 = (bf16[512,512]{1,0:T(8,128)(2,1)}, bf16[512,512]{1,0:T(8,128)(2,1)S(1)}, u32[]{:S(2)}) copy-start(bf16[512,512]{1,0:T(8,128)(2,1)S(1)} %get-tuple-element.16.mix_ref) | copy-start | bytes 1572868
  71.7 13.5 %collective-permute-start.3 = (bf16[32,32,384]{2,1,0:T(8,128)(2,1)}, bf16[32,32,384]{2,1,0:T(8,128)(2,1)S(1)}, u32[]{:S(2)}, u32[]{:S(2)}) collective-permute-start(bf16[32,32,384]{2,1,0:T(8,128)(2,1)} %get-tuple-element.17), channel_id=1, source_target_pairs={{16,0},{32,16},{48,32},{64,48},{80,64},{96,80},{112,96},{128,112},... | collective-permute-start | bytes 2359304 | tf_op jit(solution)/shard_map/ppermute | solution.py:289
  75.7 11.2 %collective-permute-start.2 = (bf16[32,32,384]{2,1,0:T(8,128)(2,1)}, bf16[32,32,384]{2,1,0:T(8,128)(2,1)S(1)}, u32[]{:S(2)}, u32[]{:S(2)}) collective-permute-start(bf16[32,32,384]{2,1,0:T(8,128)(2,1)} %get-tuple-element.18), channel_id=1, source_target_pairs={{0,16},{16,32},{32,48},{48,64},{64,80},{80,96},{96,112},{112,128},... | collective-permute-start | bytes 2359304 | tf_op jit(solution)/shard_map/ppermute | solution.py:288
  77.6 9.2 %collective-permute-start.5 = (bf16[16,3,48,128]{3,2,1,0:T(8,128)(2,1)}, bf16[16,3,48,128]{3,2,1,0:T(8,128)(2,1)S(1)}, u32[]{:S(2)}, u32[]{:S(2)}) collective-permute-start(bf16[16,3,48,128]{3,2,1,0:T(8,128)(2,1)} %all-to-all-done.1.mine_ref), channel_id=1, source_target_pairs={{0,16},{16,0},{240,224},{224,240},{1,17},{17,1},{241,225},{225,241... | collective-permute-start | bytes 1769480 | tf_op jit(solution)/shard_map/ppermute | solution.py:301
  86.9 1.0 %copy-start.12 = (bf16[512,512]{1,0:T(8,128)(2,1)S(1)}, bf16[512,512]{1,0:T(8,128)(2,1)}, u32[]{:S(2)}) copy-start(bf16[512,512]{1,0:T(8,128)(2,1)} %copy-done.11) | copy-start | bytes 1572868

commit v2 on v0

v2 whole, which is shorter than its diff:
```python
import jax
import jax.numpy as jnp
from jax import lax
from jax.experimental import pallas as pl
from jax.experimental.pallas import tpu as pltpu
from jax.sharding import PartitionSpec as P

HMAX = 48
LMAX = 32
LANES = 128
PART = 16
UNROLL = 8
F32 = jnp.float32
BF16 = jnp.bfloat16
VMEM_LIMIT = 32 * 1024 * 1024


def lanes_of(rows):
    return lax.broadcasted_iota(jnp.int32, (rows, LANES), 1)


def write_edges(x_ref, low_ref, high_ref):
    shells, row_count, col_count = x_ref.shape
    half = shells // 2
    size = half * row_count
    lane = lanes_of(size)

    def part(first, column):
        return x_ref[first : first + half, :, column : column + LANES].reshape(size, LANES).astype(F32)

    last = col_count - LANES
    low_ref[...] = jnp.where(lane < HMAX, part(0, 0), pltpu.roll(part(half, 0), HMAX, 1)).astype(BF16)
    high_ref[...] = jnp.where(
        lane < HMAX, pltpu.roll(part(0, last), HMAX, 1), pltpu.roll(part(half, last), 2 * HMAX, 1)
    ).astype(BF16)


def write_polar(half, place_ref, rows_ref, x_ref, send_ref, wide_ref):
    _, row_count, col_count = x_ref.shape
    tiles = col_count // LANES
    zone = place_ref[0]
    for t in range(tiles):
        wide_ref[t] = (
            x_ref[half * PART : (half + 1) * PART, :, t * LANES : (t + 1) * LANES]
            .reshape(PART * row_count, LANES)
            .astype(F32)
        )
    holders, held = send_ref.shape[0], send_ref.shape[1]
    cap = jnp.where(zone < 8, 0, holders * held)
    for k in range(holders):
        for r in range(held):
            row = jnp.clip(rows_ref[cap + k * held + r] - zone * row_count, 0, row_count - 1)
            for t in range(tiles):
                values = wide_ref[t, pl.ds(row, PART, stride=row_count), :]
                send_ref[k, r, t * PART : (t + 1) * PART, :] = values.astype(BF16)


def first_kernel(place_ref, rows_ref, x_ref, send_ref, low_ref, high_ref, wide_ref):
    write_polar(1, place_ref, rows_ref, x_ref, send_ref, wide_ref)
    write_edges(x_ref, low_ref, high_ref)


def second_kernel(place_ref, rows_ref, x_ref, low_ref, send_ref, wide_ref):
    write_polar(0, place_ref, rows_ref, x_ref, send_ref, wide_ref)


def band_terms(half_f):
    rate = 4.5 / (half_f * half_f)
    tap = (lanes_of(half_f.shape[0]) - HMAX).astype(F32)
    terms = jnp.where(jnp.abs(tap) <= half_f, jnp.exp(-rate * (tap * tap)), 0.0)
    return rate, jnp.broadcast_to(1.0 / jnp.sum(terms, axis=1, keepdims=True), half_f.shape)


def lon_kernel(place_ref, halo_ref, x_ref, before_ref, after_ref, reach_ref, blend_ref,
               out_ref, weight_ref, mix_ref, wide_ref, done_ref, half_ref, rate_ref, scale_ref):
    shells, row_count, col_count = x_ref.shape
    total = shells * row_count
    size = total // 2
    tiles = col_count // LANES
    zone = place_ref[0]
    for i in range(row_count):
        half_ref[i : i + 1, :] = jnp.full((1, LANES), halo_ref[zone * row_count + i], jnp.int32).astype(F32)
    rate_ref[...], scale_ref[...] = band_terms(half_ref[...])
    lane = lanes_of(size)
    for part in range(2):
        rows = pl.ds(part * size, size)
        shell = slice(part * (shells // 2), (part + 1) * (shells // 2))
        edge = before_ref[...].astype(F32)
        previous = edge if part == 0 else pltpu.roll(edge, LANES - HMAX, 1)
        for t in range(tiles):
            turned = pltpu.roll(
                x_ref[shell, :, t * LANES : (t + 1) * LANES].reshape(size, LANES).astype(F32), HMAX, 1
            )
            wide_ref[t, rows, :] = jnp.where(lane < HMAX, previous, turned)
            previous = turned
        edge = after_ref[...].astype(F32)
        edge = pltpu.roll(edge, HMAX, 1) if part == 0 else edge
        wide_ref[tiles, rows, :] = jnp.where(lane < HMAX, previous, jnp.where(lane < 2 * HMAX, edge, 0.0))
    depth = 2 * LANES
    offset = (lanes_of(depth) - lax.broadcasted_iota(jnp.int32, (depth, LANES), 0) + HMAX).astype(F32)
    square = offset * offset
    distance = jnp.abs(offset)

    def some_rows(block, carry):
        for u in range(UNROLL):
            i = block * UNROLL + u
            line = pl.ds(i, 1)
            band = jnp.where(distance <= half_ref[line, :], jnp.exp(-rate_ref[line, :] * square), 0.0)
            band = (band * scale_ref[line, :]).astype(BF16)
            values = [wide_ref[t, pl.ds(i, shells, stride=row_count), :].astype(BF16) for t in range(tiles + 1)]
            stacked = jnp.concatenate(
                [jnp.concatenate(values[:tiles], axis=0), jnp.concatenate(values[1:], axis=0)], axis=1
            )
            result = jnp.dot(stacked, band, preferred_element_type=F32)
            for t in range(tiles):
                done_ref[t, pl.ds(i, shells, stride=row_count), :] = result[t * shells : (t + 1) * shells]
        return carry

    lax.fori_loop(0, row_count // UNROLL, some_rows, 0)
    for t in range(tiles):
        out_ref[:, :, t * LANES : (t + 1) * LANES] = done_ref[t].astype(BF16).reshape(shells, row_count, LANES)
    frame_rows = weight_ref.shape[1]
    reach = reach_ref[...]
    column = lax.broadcasted_iota(jnp.int32, (row_count, frame_rows), 1)
    away = column - LMAX - lax.broadcasted_iota(jnp.int32, (row_count, frame_rows), 0)
    source = zone * row_count - LMAX + column
    valid = (jnp.abs(away) <= reach) & (source >= 0) & (source < halo_ref.shape[0])
    reach_f = reach.astype(F32)
    away_f = away.astype(F32)
    weights = jnp.where(valid, jnp.exp(-(4.5 / (reach_f * reach_f)) * (away_f * away_f)), 0.0)
    weight_ref[...] = (weights / jnp.sum(weights, axis=1, keepdims=True)).astype(BF16)
    length = mix_ref.shape[0]
    group = length // shells
    spread = (
        lax.broadcasted_iota(jnp.int32, (length, shells), 0) // group
        == lax.broadcasted_iota(jnp.int32, (length, shells), 1)
    ).astype(F32).astype(BF16)
    tall = jnp.dot(spread, blend_ref[...], preferred_element_type=F32).astype(BF16)
    full = lax.dot_general(tall, spread, (((1,), (1,)), ((), ())), preferred_element_type=F32)
    same = (
        lax.broadcasted_iota(jnp.int32, (length, length), 0) % group
        == lax.broadcasted_iota(jnp.int32, (length, length), 1) % group
    )
    mix_ref[...] = jnp.where(same, full, 0.0).astype(BF16)


def hold_kernel(place_ref, rows_ref, shift_ref, halo_ref, x_ref, after_ref, out_ref, circle_ref):
    sectors, held, block, _ = x_ref.shape
    zone, sector = place_ref[0], place_ref[1]
    cap = jnp.where(zone < 8, 0, sectors * held)
    length = sectors * block
    full_lon = length // PART * LANES
    depth = 3 * LANES
    for r in range(held):
        for copy in range(2):
            circle_ref[r, copy * length : (copy + 1) * length, :] = x_ref[:, r].reshape(length, LANES)
        circle_ref[r, 2 * length : 2 * length + 2 * PART, :] = circle_ref[r, 0 : 2 * PART, :]
    for r in range(held):
        entry = cap + sector * held + r
        half_f = jnp.full((1, LANES), halo_ref[rows_ref[entry]], jnp.int32).astype(F32)
        rate, scale = band_terms(half_f)
        start = lax.rem(2 * full_lon - shift_ref[entry] - HMAX, full_lon)
        first = start // LANES
        rest = start - first * LANES
        offset = (
            lanes_of(depth) - lax.broadcasted_iota(jnp.int32, (depth, LANES), 0) + (rest + HMAX)
        ).astype(F32)
        band = jnp.where(jnp.abs(offset) <= half_f, jnp.exp(-rate * (offset * offset)), 0.0) * scale
        values = jnp.concatenate(
            [circle_ref[r, pl.ds(pl.multiple_of((first + u) * PART, PART), length), :] for u in range(3)], axis=1
        )
        result = jnp.dot(values, band.astype(BF16), preferred_element_type=F32)
        out_ref[:, r] = result.astype(BF16).reshape(sectors, block, LANES)


def lat_kernel(place_ref, rows_ref, above_ref, own_ref, below_ref, weight_ref,
               out_ref, polar_weight_ref, pick_ref):
    shells, row_count, col_count = own_ref.shape
    frame_rows = weight_ref.shape[1]
    polar = pick_ref.shape[0]
    zone = place_ref[0]
    cap = jnp.where(zone < 8, 0, polar)
    lane = lanes_of(1)
    for p in range(polar):
        pick_ref[p : p + 1, :] = (lane == rows_ref[cap + p] - zone * row_count + LMAX).astype(F32)
    pick = pick_ref[...]
    weight = weight_ref[...]
    polar_weight_ref[...] = lax.dot_general(
        weight, pick.astype(BF16), (((1,), (1,)), ((), ())), preferred_element_type=F32
    ).astype(BF16)
    rest = (weight.astype(F32) * (1.0 - jnp.sum(pick, axis=0, keepdims=True))).astype(BF16)

    def some_shells(block, carry):
        for u in range(4):
            s = block * 4 + u
            values = jnp.concatenate([above_ref[s], own_ref[s], below_ref[s]], axis=0)
            out_ref[s] = jnp.dot(rest, values, preferred_element_type=F32)
        return carry

    lax.fori_loop(0, shells // 4, some_shells, 0)


def final_kernel(place_ref, lat_ref, mine_ref, other_ref, polar_weight_ref, mix_ref, out_ref, polar_ref, sum_ref):
    shells, row_count, col_count = lat_ref.shape
    holders, held, block, _ = mine_ref.shape
    tiles = col_count // LANES
    polar = holders * held
    zone = place_ref[0]
    outer = (zone == 0) | (zone == 15)
    mine_first = jnp.where(outer, 0, PART * polar)
    for ref, first in ((mine_ref, mine_first), (other_ref, PART * polar - mine_first)):
        for k in range(holders):
            for r in range(held):
                for t in range(tiles):
                    polar_ref[t, pl.ds(first + k * held + r, PART, stride=polar), :] = ref[
                        k, r, t * PART : (t + 1) * PART, :
                    ].astype(F32)
    weight = polar_weight_ref[...]

    def some_shells(index, carry):
        for u in range(4):
            s = index * 4 + u
            base = pl.multiple_of(s * polar, PART)
            values = jnp.concatenate(
                [polar_ref[t, pl.ds(base, polar), :].astype(BF16) for t in range(tiles)], axis=1
            )
            sum_ref[s] = lat_ref[s] + jnp.dot(weight, values, preferred_element_type=F32)
        return carry

    lax.fori_loop(0, shells // 4, some_shells, 0)
    group = mix_ref.shape[0] // shells
    mix = mix_ref[...]
    for g in range(row_count // (2 * group)):
        mixed = []
        for e in range(2):
            first = (2 * g + e) * group
            values = sum_ref[:, first : first + group, :].reshape(shells * group, col_count).astype(BF16)
            mixed.append(jnp.dot(mix, values, preferred_element_type=F32).reshape(shells, group, col_count))
        out_ref[:, 2 * g * group : 2 * (g + 1) * group, :] = jnp.concatenate(mixed, axis=1).astype(BF16)


def call(kernel, name, out_shape, scalars, arrays, scratch, flops=0, moved=0, unread=()):
    smem = pl.BlockSpec(memory_space=pltpu.SMEM)
    vmem = pl.BlockSpec(memory_space=pltpu.VMEM)
    anywhere = pl.BlockSpec(memory_space=pl.ANY)
    many = isinstance(out_shape, tuple)
    return pl.pallas_call(
        kernel,
        out_shape=out_shape,
        in_specs=[smem] * len(scalars) + [vmem] * len(arrays) + [anywhere] * len(unread),
        out_specs=(vmem,) * len(out_shape) if many else vmem,
        scratch_shapes=scratch,
        compiler_params=pltpu.CompilerParams(vmem_limit_bytes=VMEM_LIMIT),
        cost_estimate=pl.CostEstimate(flops=flops, bytes_accessed=moved, transcendentals=0),
        name=name,
    )(*scalars, *arrays, *unread)


struct = jax.ShapeDtypeStruct


def pack(place, polar_rows, kernel, sectors):
    shells, row_count, col_count = kernel.shape
    tiles = col_count // LANES
    held = polar_rows.shape[0] // 2 // sectors
    send = struct((sectors, held, tiles * PART, LANES), BF16)
    edge = struct((shells * row_count // 2, LANES), BF16)
    wide = pltpu.VMEM((tiles, PART * row_count, LANES), F32)
    given, low, high = call(
        first_kernel, "pack_half_of_shells_and_edges", (send, edge, edge), [place, polar_rows], [kernel], [wide],
        moved=4 << 20,
    )
    kept = call(
        second_kernel, "pack_other_half_of_shells", send, [place, polar_rows], [kernel], [wide],
        moved=4 << 20, unread=[low],
    )
    return given, kept, low, high


def smooth_lon(place, lon_halo, kernel, before, after, reach, blend):
    shells, row_count, col_count = kernel.shape
    tiles = col_count // LANES
    rows = pltpu.VMEM((row_count, LANES), F32)
    return call(
        lon_kernel,
        "smooth_along_longitude",
        (
            struct((shells, row_count, col_count), BF16),
            struct((row_count, row_count + 2 * LMAX), BF16),
            struct((shells * 8, shells * 8), BF16),
        ),
        [place, lon_halo],
        [kernel, before, after, reach, blend],
        [
            pltpu.VMEM((tiles + 1, shells * row_count, LANES), F32),
            pltpu.VMEM((tiles, shells * row_count, LANES), F32),
            rows,
            rows,
            rows,
        ],
        flops=1 << 32,
        moved=16 << 20,
    )


def hold(place, polar_rows, polar_shift, lon_halo, circles, after):
    sectors, held, block, _ = circles.shape
    return call(
        hold_kernel,
        "smooth_and_turn_polar_circles",
        struct(circles.shape, BF16),
        [place, polar_rows, polar_shift, lon_halo],
        [circles],
        [pltpu.VMEM((held, 2 * sectors * block + 2 * PART, LANES), BF16)],
        flops=1 << 30,
        moved=4 << 20,
        unread=[after],
    )


def smooth_lat(place, polar_rows, above, own, below, weight):
    row_count, frame_rows = weight.shape
    polar = polar_rows.shape[0] // 2
    return call(
        lat_kernel,
        "smooth_along_latitude",
        (struct(own.shape, F32), struct((row_count, polar), BF16)),
        [place, polar_rows],
        [above, own, below, weight],
        [pltpu.VMEM((polar, frame_rows), F32)],
        flops=1 << 30,
        moved=8 << 20,
    )


def finish(place, lat, mine, other, polar_weight, mix):
    shells, _, col_count = lat.shape
    polar = polar_weight.shape[1]
    return call(
        final_kernel,
        "add_polar_rows_and_blend",
        struct(lat.shape, BF16),
        [place],
        [lat, mine, other, polar_weight, mix],
        [pltpu.VMEM((col_count // LANES, shells * polar, LANES), F32), pltpu.VMEM(lat.shape, F32)],
        flops=1 << 31,
        moved=8 << 20,
    )


def per_device(kernel, lon_halo, lat_reach, polar_rows, polar_shift, blend):
    shells, row_count, col_count = kernel.shape
    sectors = lax.axis_size("sector")
    zones = lax.axis_size("zone")
    zone_id = lax.axis_index("zone").astype(jnp.int32)
    sector_id = lax.axis_index("sector").astype(jnp.int32)
    place = jnp.stack([zone_id, sector_id])
    last = zones - 1
    up = [(i, (i + 1) % sectors) for i in range(sectors)]
    down = [(j, i) for i, j in up]
    packed, kept, low, high = pack(place, polar_rows, kernel, sectors)
    given = lax.ppermute(packed, "zone", [(0, 1), (last, last - 1)])
    before = lax.ppermute(high, "sector", up)
    after = lax.ppermute(low, "sector", down)
    inner = (zone_id == 1) | (zone_id == last - 1)
    circles = lax.all_to_all(jnp.where(inner, given, kept), "sector", 0, 0, tiled=True)
    lon_smooth, lat_weight, mix = smooth_lon(place, lon_halo, kernel, before, after, lat_reach[:, None], blend)
    north = [(i, i + 1) for i in range(zones - 1)]
    south = [(j, i) for i, j in north]
    above = lax.ppermute(lon_smooth[:, row_count - LMAX :], "zone", north)
    below = lax.ppermute(lon_smooth[:, :LMAX], "zone", south)
    turned = hold(place, polar_rows, polar_shift, lon_halo, circles, lat_weight)
    mine = lax.all_to_all(turned, "sector", 0, 0, tiled=True)
    lat, polar_weight = smooth_lat(place, polar_rows, above, lon_smooth, below, lat_weight)
    mine, lat = lax.optimization_barrier((mine, lat))
    other = lax.ppermute(mine, "zone", [(0, 1), (1, 0), (last, last - 1), (last - 1, last)])
    return finish(place, lat, mine, other, polar_weight, mix)


def solution(mesh):
    in_specs = (P(None, "zone", "sector"), P(), P("zone"), P(), P(), P())
    out_specs = P(None, "zone", "sector")
    return jax.shard_map(
        per_device, mesh=mesh, in_specs=in_specs, out_specs=out_specs, check_vma=False
    )
```

time: 844 us -> 96.5 us (0.11)
  the two profiles are of different devices: /device:TPU:1 before, /device:TPU:24 now
where the time goes in v2:
time: 96.5 us; the launch traced here: 95.9 us
  waiting for transfers between devices  36.7 us (38%)
  starting transfers between devices  27.1 us (28%)
  Pallas kernels  21.8 us (23%)
  local copies, waits for them, and re-layouts  9.19 us (10%)
    pallas_call x6, Pallas kernels, call(): pl.pallas_call(kernel, out_shape=out_shape, in_specs=[smem] * len(scalars...  21.8 us
    ppermute x1, waiting for transfers between devices, per_device(): before = lax.ppermute(high, 'sector', up)  16.4 us
    all_to_all x1, starting transfers between devices, per_device(): lax.all_to_all(jnp.where(inner, given, kept), 'sector', 0, 0, tiled=True)  9.94 us
    ppermute x1, waiting for transfers between devices, per_device(): below = lax.ppermute(lon_smooth[:, :LMAX], 'zone', south)  9.86 us
    unnamed x28, local copies, waits for them, and re-layouts  8.93 us
    ppermute x1, waiting for transfers between devices, per_device(): above = lax.ppermute(lon_smooth[:, row_count - LMAX:], 'zone', north)  8.72 us
    all_to_all x1, starting transfers between devices, per_device(): mine = lax.all_to_all(turned, 'sector', 0, 0, tiled=True)  7.13 us
    ppermute x1, starting transfers between devices, per_device(): below = lax.ppermute(lon_smooth[:, :LMAX], 'zone', south)  3.86 us
  transfers between devices with their start and end apart: 8, of which 4 were waited for; matrix products, arithmetic and copies ran while one was open for 0% of the time, Pallas kernels for 13%

profile of v2, /device:TPU:24, one launch (start us, length us, event | category | flops | bytes accessed | tf_op | source)
XLA Modules:
  0.0 95.9 jit_solution(8422190899813464407)
XLA Ops:
  0.0 0.0 copy-start.3
  0.0 0.1 pad_add_fusion.place_ref
  0.1 0.0 copy-start
  0.1 1.4 %copy-done = bf16[32,64,384]{2,1,0:T(8,128)(2,1)S(1)} copy-done((bf16[32,64,384]{2,1,0:T(8,128)(2,1)S(1)}, bf16[32,64,384]{2,1,0:T(8,128)(2,1)}, u32[]{:S(2)}) %copy-start) | copy-done | bytes 1572888
  1.5 0.0 copy-start.2
  1.5 0.7 copy-done.2
  2.1 2.1 %pack_half_of_shells_and_edges.1 = (bf16[16,3,48,128]{3,2,1,0:T(8,128)(2,1)S(1)}, bf16[1024,128]{1,0:T(8,128)(2,1)S(1)}, bf16[1024,128]{1,0:T(8,128)(2,1)S(1)}) custom-call(s32[2]{0:T(128)S(1)} %pad_add_fusion.place_ref, s32[96]{0:T(128)S(1)} %copy-done.2, bf16[32,64,384]{2,1,0:T(8,128)(2,1)S(1)} %copy-done), custom_call_target="tpu_custom_call" | custom-call | bytes 4194304 | tf_op jit(solution)/shard_map/pack_half_of_shells_and_edges/pallas_call | solution.py:247
  4.3 1.5 %collective-permute-start = (bf16[16,3,48,128]{3,2,1,0:T(8,128)(2,1)S(1)}, bf16[16,3,48,128]{3,2,1,0:T(8,128)(2,1)}, u32[]{:S(2)}, u32[]{:S(2)}) collective-permute-start(bf16[16,3,48,128]{3,2,1,0:T(8,128)(2,1)S(1)} %get-tuple-element.15), channel_id=1, source_target_pairs={{0,16},{240,224},{1,17},{241,225},{2,18},{242,226},{3,19},{243,227... | collective-permute-start | bytes 1769480 | tf_op jit(solution)/shard_map/ppermute | solution.py:362
  5.8 0.0 copy-done.3
  5.8 0.0 copy-done.1
  5.8 1.9 %pack_other_half_of_shells.1 = bf16[16,3,48,128]{3,2,1,0:T(8,128)(2,1)S(1)} custom-call(s32[2]{0:T(128)S(1)} %pad_add_fusion.place_ref, s32[96]{0:T(128)S(1)} %copy-done.3, bf16[32,64,384]{2,1,0:T(8,128)(2,1)S(1)} %copy-done.1, bf16[1024,128]{1,0:T(8,128)(2,1)S(1)} %get-tuple-element.16.low_ref), custom_call_target="tpu_custom_call" | custom-call | bytes 4194304 | tf_op jit(solution)/shard_map/pack_other_half_of_shells/pallas_call | solution.py:247
  7.7 0.0 copy-start.13
  7.7 0.0 copy-start.8
  7.7 0.0 copy-start.9
  7.7 0.0 collective-permute-done
  7.7 0.9 broadcast_select_fusion
  8.6 9.9 %all-to-all-start = ((bf16[16,3,48,128]{3,2,1,0:T(8,128)(2,1)}), bf16[16,3,48,128]{3,2,1,0:T(8,128)(2,1)}, u32[]{:S(2)}, u32[]{:S(2)}) async-start(bf16[16,3,48,128]{3,2,1,0:T(8,128)(2,1)} %broadcast_select_fusion), calls=%async_computation | async-start | bytes 1179648 | tf_op jit(solution)/shard_map/all_to_all | solution.py:366
  18.5 1.5 %collective-permute-start.1 = (bf16[1024,128]{1,0:T(8,128)(2,1)S(1)}, bf16[1024,128]{1,0:T(8,128)(2,1)S(1)}, u32[]{:S(2)}, u32[]{:S(2)}) collective-permute-start(bf16[1024,128]{1,0:T(8,128)(2,1)S(1)} %get-tuple-element.17), channel_id=1, source_target_pairs={{0,1},{1,2},{2,3},{3,4},{4,5},{5,6},{6,7},{7,8},{8,9},{9,10},{10,1... | collective-permute-start | bytes 786440 | tf_op jit(solution)/shard_map/ppermute | solution.py:363
  20.0 0.6 collective-permute-start.2
  20.6 0.0 copy-done.13
  20.6 0.1 copy.7.reach_ref
  20.7 16.4 %collective-permute-done.1.before_ref = bf16[1024,128]{1,0:T(8,128)(2,1)S(1)} collective-permute-done((bf16[1024,128]{1,0:T(8,128)(2,1)S(1)}, bf16[1024,128]{1,0:T(8,128)(2,1)S(1)}, u32[]{:S(2)}, u32[]{:S(2)}) %collective-permute-start.1) | collective-permute-done | bytes 262176 | tf_op jit(solution)/shard_map/ppermute | solution.py:363
  37.1 0.7 copy-done.4
  37.8 1.7 %collective-permute-done.2.after_ref = bf16[1024,128]{1,0:T(8,128)(2,1)S(1)} collective-permute-done((bf16[1024,128]{1,0:T(8,128)(2,1)S(1)}, bf16[1024,128]{1,0:T(8,128)(2,1)S(1)}, u32[]{:S(2)}, u32[]{:S(2)}) %collective-permute-start.2) | collective-permute-done | bytes 262176 | tf_op jit(solution)/shard_map/ppermute | solution.py:364
  39.5 0.7 copy-done.6
  40.2 0.0 copy-done.8
  40.2 0.0 copy-done.9
  40.2 0.9 copy-done.5
  41.1 0.9 copy-done.7
  42.1 7.7 %smooth_along_longitude.1 = (bf16[32,64,384]{2,1,0:T(8,128)(2,1)S(1)}, bf16[64,128]{1,0:T(8,128)(2,1)S(1)}, bf16[256,256]{1,0:T(8,128)(2,1)S(1)}) custom-call(s32[2]{0:T(128)S(1)} %pad_add_fusion.place_ref, s32[1024]{0:T(1024)S(1)} %copy-done.9, bf16[32,64,384]{2,1,0:T(8,128)(2,1)S(1)} %copy-done.1, bf16[1024,128]{1,0:T(8,128)(2,1)S(1)} %copy-done.5, ...), custom_call_target="tpu_custom_call" | custom-call | flops 4294967296 | bytes 16777216 | tf_op jit(solution)/shard_map/smooth_along_longitude/pallas_call | solution.py:247
  49.8 0.0 all-to-all-done.x_ref
  49.8 0.0 copy-done.10
  49.9 2.7 %smooth_and_turn_polar_circles.1 = bf16[16,3,48,128]{3,2,1,0:T(8,128)(2,1)} custom-call(s32[2]{0:T(128)S(1)} %pad_add_fusion.place_ref, s32[96]{0:T(128)S(1)} %copy-done.3, s32[96]{0:T(128)S(1)} %copy-done.10, s32[1024]{0:T(1024)S(1)} %copy-done.9, bf16[16,3,48,128]{3,2,1,0:T(8,128)(2,1)} %all-to-all-done.x_ref, ...), custom_call_target="tpu_custom_call" | custom-call | flops 1073741824 | bytes 4194304 | tf_op jit(solution)/shard_map/smooth_and_turn_polar_circles/pallas_call | solution.py:247
  52.6 7.1 %all-to-all-start.1 = ((bf16[16,3,48,128]{3,2,1,0:T(8,128)(2,1)}), bf16[16,3,48,128]{3,2,1,0:T(8,128)(2,1)S(1)}, u32[]{:S(2)}, u32[]{:S(2)}) async-start(bf16[16,3,48,128]{3,2,1,0:T(8,128)(2,1)} %smooth_and_turn_polar_circles.1), calls=%async_computation.1 | async-start | bytes 1179648 | tf_op jit(solution)/shard_map/all_to_all | solution.py:373
  59.7 0.2 fusion
  59.9 3.9 %collective-permute-start.4 = (bf16[32,32,384]{2,1,0:T(8,128)(2,1)S(1)}, bf16[32,32,384]{2,1,0:T(8,128)(2,1)S(1)}, u32[]{:S(2)}, u32[]{:S(2)}) collective-permute-start(bf16[32,32,384]{2,1,0:T(8,128)(2,1)S(1)} %get-tuple-element.25), channel_id=1, source_target_pairs={{16,0},{32,16},{48,32},{64,48},{80,64},{96,80},{112,96},{128,112},... | collective-permute-start | bytes 2359304 | tf_op jit(solution)/shard_map/ppermute | solution.py:371
  63.7 1.9 %collective-permute-start.3 = (bf16[32,32,384]{2,1,0:T(8,128)(2,1)S(1)}, bf16[32,32,384]{2,1,0:T(8,128)(2,1)S(1)}, u32[]{:S(2)}, u32[]{:S(2)}) collective-permute-start(bf16[32,32,384]{2,1,0:T(8,128)(2,1)S(1)} %get-tuple-element.26), channel_id=1, source_target_pairs={{0,16},{16,32},{32,48},{48,64},{64,80},{80,96},{96,112},{112,128},... | collective-permute-start | bytes 2359304 | tf_op jit(solution)/shard_map/ppermute | solution.py:370
  65.7 9.9 %collective-permute-done.4.below_ref = bf16[32,32,384]{2,1,0:T(8,128)(2,1)S(1)} collective-permute-done((bf16[32,32,384]{2,1,0:T(8,128)(2,1)S(1)}, bf16[32,32,384]{2,1,0:T(8,128)(2,1)S(1)}, u32[]{:S(2)}, u32[]{:S(2)}) %collective-permute-start.4) | collective-permute-done | bytes 786464 | tf_op jit(solution)/shard_map/ppermute | solution.py:371
  75.5 8.7 %collective-permute-done.3.above_ref = bf16[32,32,384]{2,1,0:T(8,128)(2,1)S(1)} collective-permute-done((bf16[32,32,384]{2,1,0:T(8,128)(2,1)S(1)}, bf16[32,32,384]{2,1,0:T(8,128)(2,1)S(1)}, u32[]{:S(2)}, u32[]{:S(2)}) %collective-permute-start.3) | collective-permute-done | bytes 786464 | tf_op jit(solution)/shard_map/ppermute | solution.py:370
  84.2 2.4 %smooth_along_latitude.1 = (f32[32,64,384]{2,1,0:T(8,128)S(1)}, bf16[64,48]{1,0:T(8,128)(2,1)S(1)}) custom-call(s32[2]{0:T(128)S(1)} %pad_add_fusion.place_ref, s32[96]{0:T(128)S(1)} %copy-done.3, bf16[32,32,384]{2,1,0:T(8,128)(2,1)S(1)} %collective-permute-done.3.above_ref, bf16[32,64,384]{2,1,0:T(8,128)(2,1)S(1)} %get-tuple-element.19.own_ref, ...), custom_call_target="tpu_custom_call" | custom-call | flops 1073741824 | bytes 8388608 | tf_op jit(solution)/shard_map/smooth_along_latitude/pallas_call | solution.py:247
  86.7 0.0 copy-start.11
  86.7 1.6 %copy-done.11 = f32[32,64,384]{2,1,0:T(8,128)} copy-done((f32[32,64,384]{2,1,0:T(8,128)}, f32[32,64,384]{2,1,0:T(8,128)S(1)}, u32[]{:S(2)}) %copy-start.11) | copy-done | bytes 3145752
  88.3 0.0 all-to-all-done.1.mine_ref
  88.3 0.7 collective-permute-start.5
  89.0 0.0 collective-permute-done.5.other_ref
  89.0 0.0 copy-start.12
  89.1 1.9 %copy-done.12 = f32[32,64,384]{2,1,0:T(8,128)S(1)} copy-done((f32[32,64,384]{2,1,0:T(8,128)S(1)}, f32[32,64,384]{2,1,0:T(8,128)}, u32[]{:S(2)}) %copy-start.12) | copy-done | bytes 3145752
  90.9 5.0 %add_polar_rows_and_blend.1 = bf16[32,64,384]{2,1,0:T(8,128)(2,1)} custom-call(s32[2]{0:T(128)S(1)} %pad_add_fusion.place_ref, f32[32,64,384]{2,1,0:T(8,128)S(1)} %copy-done.12, bf16[16,3,48,128]{3,2,1,0:T(8,128)(2,1)S(1)} %all-to-all-done.1.mine_ref, bf16[16,3,48,128]{3,2,1,0:T(8,128)(2,1)S(1)} %collective-permute-done.5.other_ref, ...), custom_call_target="tpu_custom_call" | custom-call | flops 2147483648 | bytes 8388608 | tf_op jit(solution)/shard_map/add_polar_rows_and_blend/pallas_call | solution.py:247
  (6 shorter events, 0.0 us)
Async XLA Ops:
  0.0 5.8 %copy-start.3 = (s32[96]{0:T(128)S(1)}, s32[96]{0:T(128)}, u32[]{:S(2)}) copy-start(s32[96]{0:T(128)} %rows_ref.7) | copy-start | bytes 1156
  0.1 1.4 %copy-start = (bf16[32,64,384]{2,1,0:T(8,128)(2,1)S(1)}, bf16[32,64,384]{2,1,0:T(8,128)(2,1)}, u32[]{:S(2)}) copy-start(bf16[32,64,384]{2,1,0:T(8,128)(2,1)} %x_ref.5) | copy-start | bytes 4718596
  1.5 0.7 copy-start.2
  2.1 3.6 %copy-start.1 = (bf16[32,64,384]{2,1,0:T(8,128)(2,1)S(1)}, bf16[32,64,384]{2,1,0:T(8,128)(2,1)}, u32[]{:S(2)}) copy-start(bf16[32,64,384]{2,1,0:T(8,128)(2,1)} %x_ref.5) | copy-start | bytes 4718596
  4.3 3.4 %collective-permute-start = (bf16[16,3,48,128]{3,2,1,0:T(8,128)(2,1)S(1)}, bf16[16,3,48,128]{3,2,1,0:T(8,128)(2,1)}, u32[]{:S(2)}, u32[]{:S(2)}) collective-permute-start(bf16[16,3,48,128]{3,2,1,0:T(8,128)(2,1)S(1)} %get-tuple-element.15), channel_id=1, source_target_pairs={{0,16},{240,224},{1,17},{241,225},{2,18},{242,226},{3,19},{243,227... | collective-permute-start | bytes 1769480 | tf_op jit(solution)/shard_map/ppermute | solution.py:362
  7.7 12.9 %copy-start.13 = (s32[64]{0:T(128)S(1)}, s32[64]{0:T(128)}, u32[]{:S(2)}) copy-start(s32[64]{0:T(128)} %param.8) | copy-start | bytes 772
  7.7 32.5 %copy-start.8 = (bf16[32,32]{1,0:T(8,128)(2,1)S(1)}, bf16[32,32]{1,0:T(8,128)(2,1)}, u32[]{:S(2)}) copy-start(bf16[32,32]{1,0:T(8,128)(2,1)} %blend_ref.1) | copy-start | bytes 6148
  7.7 32.5 %copy-start.9 = (s32[1024]{0:T(1024)S(1)}, s32[1024]{0:T(1024)}, u32[]{:S(2)}) copy-start(s32[1024]{0:T(1024)} %halo_ref.3) | copy-start | bytes 12292
  8.6 41.2 %all-to-all-start = ((bf16[16,3,48,128]{3,2,1,0:T(8,128)(2,1)}), bf16[16,3,48,128]{3,2,1,0:T(8,128)(2,1)}, u32[]{:S(2)}, u32[]{:S(2)}) async-start(bf16[16,3,48,128]{3,2,1,0:T(8,128)(2,1)} %broadcast_select_fusion), calls=%async_computation | async-start | bytes 1179648 | tf_op jit(solution)/shard_map/all_to_all | solution.py:366
  18.5 18.5 %collective-permute-start.1 = (bf16[1024,128]{1,0:T(8,128)(2,1)S(1)}, bf16[1024,128]{1,0:T(8,128)(2,1)S(1)}, u32[]{:S(2)}, u32[]{:S(2)}) collective-permute-start(bf16[1024,128]{1,0:T(8,128)(2,1)S(1)} %get-tuple-element.17), channel_id=1, source_target_pairs={{0,1},{1,2},{2,3},{3,4},{4,5},{5,6},{6,7},{7,8},{8,9},{9,10},{10,1... | collective-permute-start | bytes 786440 | tf_op jit(solution)/shard_map/ppermute | solution.py:363
  20.0 19.5 %collective-permute-start.2 = (bf16[1024,128]{1,0:T(8,128)(2,1)S(1)}, bf16[1024,128]{1,0:T(8,128)(2,1)S(1)}, u32[]{:S(2)}, u32[]{:S(2)}) collective-permute-start(bf16[1024,128]{1,0:T(8,128)(2,1)S(1)} %get-tuple-element.16.low_ref), channel_id=1, source_target_pairs={{1,0},{2,1},{3,2},{4,3},{5,4},{6,5},{7,6},{8,7},{9,8},{10,9},{11,1... | collective-permute-start | bytes 786440 | tf_op jit(solution)/shard_map/ppermute | solution.py:364
  20.6 29.3 %copy-start.10 = (s32[96]{0:T(128)S(1)}, s32[96]{0:T(128)}, u32[]{:S(2)}) copy-start(s32[96]{0:T(128)} %shift_ref.1) | copy-start | bytes 1156
  37.1 0.7 copy-start.4
  39.5 0.7 copy-start.6
  40.2 1.0 copy-start.5
  41.1 0.9 copy-start.7
  52.6 35.8 %all-to-all-start.1 = ((bf16[16,3,48,128]{3,2,1,0:T(8,128)(2,1)}), bf16[16,3,48,128]{3,2,1,0:T(8,128)(2,1)S(1)}, u32[]{:S(2)}, u32[]{:S(2)}) async-start(bf16[16,3,48,128]{3,2,1,0:T(8,128)(2,1)} %smooth_and_turn_polar_circles.1), calls=%async_computation.1 | async-start | bytes 1179648 | tf_op jit(solution)/shard_map/all_to_all | solution.py:373
  59.9 15.7 %collective-permute-start.4 = (bf16[32,32,384]{2,1,0:T(8,128)(2,1)S(1)}, bf16[32,32,384]{2,1,0:T(8,128)(2,1)S(1)}, u32[]{:S(2)}, u32[]{:S(2)}) collective-permute-start(bf16[32,32,384]{2,1,0:T(8,128)(2,1)S(1)} %get-tuple-element.25), channel_id=1, source_target_pairs={{16,0},{32,16},{48,32},{64,48},{80,64},{96,80},{112,96},{128,112},... | collective-permute-start | bytes 2359304 | tf_op jit(solution)/shard_map/ppermute | solution.py:371
  63.7 20.5 %collective-permute-start.3 = (bf16[32,32,384]{2,1,0:T(8,128)(2,1)S(1)}, bf16[32,32,384]{2,1,0:T(8,128)(2,1)S(1)}, u32[]{:S(2)}, u32[]{:S(2)}) collective-permute-start(bf16[32,32,384]{2,1,0:T(8,128)(2,1)S(1)} %get-tuple-element.26), channel_id=1, source_target_pairs={{0,16},{16,32},{32,48},{48,64},{64,80},{80,96},{96,112},{112,128},... | collective-permute-start | bytes 2359304 | tf_op jit(solution)/shard_map/ppermute | solution.py:370
  86.7 1.6 %copy-start.11 = (f32[32,64,384]{2,1,0:T(8,128)}, f32[32,64,384]{2,1,0:T(8,128)S(1)}, u32[]{:S(2)}) copy-start(f32[32,64,384]{2,1,0:T(8,128)S(1)} %get-tuple-element.21.lat_ref) | copy-start | bytes 9437188
  88.3 0.7 collective-permute-start.5
  89.0 1.9 %copy-start.12 = (f32[32,64,384]{2,1,0:T(8,128)S(1)}, f32[32,64,384]{2,1,0:T(8,128)}, u32[]{:S(2)}) copy-start(f32[32,64,384]{2,1,0:T(8,128)} %copy-done.11) | copy-start | bytes 9437188

commit v3 on v2

--- a/solution.py
+++ b/solution.py
@@ -12,26 +12,32 @@
 UNROLL = 8
 F32 = jnp.float32
 BF16 = jnp.bfloat16
-VMEM_LIMIT = 32 * 1024 * 1024
 
 
 def lanes_of(rows):
     return lax.broadcasted_iota(jnp.int32, (rows, LANES), 1)
 
 
-def write_edges(x_ref, low_ref, high_ref):
+def edge_kernel(x_ref, low_ref, high_ref, tile_ref, sems):
     shells, row_count, col_count = x_ref.shape
     half = shells // 2
     size = half * row_count
     lane = lanes_of(size)
-
-    def part(first, column):
-        return x_ref[first : first + half, :, column : column + LANES].reshape(size, LANES).astype(F32)
-
-    last = col_count - LANES
-    low_ref[...] = jnp.where(lane < HMAX, part(0, 0), pltpu.roll(part(half, 0), HMAX, 1)).astype(BF16)
+    first = (0, col_count - LANES)
+    copies = [
+        pltpu.make_async_copy(x_ref.at[:, :, pl.ds(first[e], LANES)], tile_ref.at[e], sems.at[e]) for e in range(2)
+    ]
+    for copy in copies:
+        copy.start()
+
+    def part(e, shell):
+        return tile_ref[e, shell : shell + half].reshape(size, LANES).astype(F32)
+
+    copies[0].wait()
+    low_ref[...] = jnp.where(lane < HMAX, part(0, 0), pltpu.roll(part(0, half), HMAX, 1)).astype(BF16)
+    copies[1].wait()
     high_ref[...] = jnp.where(
-        lane < HMAX, pltpu.roll(part(0, last), HMAX, 1), pltpu.roll(part(half, last), 2 * HMAX, 1)
+        lane < HMAX, pltpu.roll(part(1, 0), HMAX, 1), pltpu.roll(part(1, half), 2 * HMAX, 1)
     ).astype(BF16)
 
 
@@ -55,12 +61,11 @@
                 send_ref[k, r, t * PART : (t + 1) * PART, :] = values.astype(BF16)
 
 
-def first_kernel(place_ref, rows_ref, x_ref, send_ref, low_ref, high_ref, wide_ref):
+def first_kernel(place_ref, rows_ref, x_ref, low_ref, send_ref, wide_ref):
     write_polar(1, place_ref, rows_ref, x_ref, send_ref, wide_ref)
-    write_edges(x_ref, low_ref, high_ref)
-
-
-def second_kernel(place_ref, rows_ref, x_ref, low_ref, send_ref, wide_ref):
+
+
+def second_kernel(place_ref, rows_ref, x_ref, given_ref, send_ref, wide_ref):
     write_polar(0, place_ref, rows_ref, x_ref, send_ref, wide_ref)
 
 
@@ -200,11 +205,14 @@
     lax.fori_loop(0, shells // 4, some_shells, 0)
 
 
-def final_kernel(place_ref, lat_ref, mine_ref, other_ref, polar_weight_ref, mix_ref, out_ref, polar_ref, sum_ref):
+def final_kernel(place_ref, mine_ref, other_ref, polar_weight_ref, mix_ref, lat_ref,
+                 out_ref, polar_ref, sum_ref, sem):
     shells, row_count, col_count = lat_ref.shape
-    holders, held, block, _ = mine_ref.shape
+    holders, held = mine_ref.shape[:2]
     tiles = col_count // LANES
     polar = holders * held
+    fetch = pltpu.make_async_copy(lat_ref, sum_ref, sem)
+    fetch.start()
     zone = place_ref[0]
     outer = (zone == 0) | (zone == 15)
     mine_first = jnp.where(outer, 0, PART * polar)
@@ -216,6 +224,7 @@
                         k, r, t * PART : (t + 1) * PART, :
                     ].astype(F32)
     weight = polar_weight_ref[...]
+    fetch.wait()
 
     def some_shells(index, carry):
         for u in range(4):
@@ -224,7 +233,7 @@
             values = jnp.concatenate(
                 [polar_ref[t, pl.ds(base, polar), :].astype(BF16) for t in range(tiles)], axis=1
             )
-            sum_ref[s] = lat_ref[s] + jnp.dot(weight, values, preferred_element_type=F32)
+            sum_ref[s] += jnp.dot(weight, values, preferred_element_type=F32)
         return carry
 
     lax.fori_loop(0, shells // 4, some_shells, 0)
@@ -239,7 +248,7 @@
         out_ref[:, 2 * g * group : 2 * (g + 1) * group, :] = jnp.concatenate(mixed, axis=1).astype(BF16)
 
 
-def call(kernel, name, out_shape, scalars, arrays, scratch, flops=0, moved=0, unread=()):
+def call(kernel, name, out_shape, scalars, arrays, scratch, flops=0, moved=0, direct=(), mib=16):
     smem = pl.BlockSpec(memory_space=pltpu.SMEM)
     vmem = pl.BlockSpec(memory_space=pltpu.VMEM)
     anywhere = pl.BlockSpec(memory_space=pl.ANY)
@@ -247,13 +256,13 @@
     return pl.pallas_call(
         kernel,
         out_shape=out_shape,
-        in_specs=[smem] * len(scalars) + [vmem] * len(arrays) + [anywhere] * len(unread),
+        in_specs=[smem] * len(scalars) + [vmem] * len(arrays) + [anywhere] * len(direct),
         out_specs=(vmem,) * len(out_shape) if many else vmem,
         scratch_shapes=scratch,
-        compiler_params=pltpu.CompilerParams(vmem_limit_bytes=VMEM_LIMIT),
+        compiler_params=pltpu.CompilerParams(vmem_limit_bytes=mib << 20),
         cost_estimate=pl.CostEstimate(flops=flops, bytes_accessed=moved, transcendentals=0),
         name=name,
-    )(*scalars, *arrays, *unread)
+    )(*scalars, *arrays, *direct)
 
 
 struct = jax.ShapeDtypeStruct
@@ -266,13 +275,18 @@
     send = struct((sectors, held, tiles * PART, LANES), BF16)
     edge = struct((shells * row_count // 2, LANES), BF16)
     wide = pltpu.VMEM((tiles, PART * row_count, LANES), F32)
-    given, low, high = call(
-        first_kernel, "pack_half_of_shells_and_edges", (send, edge, edge), [place, polar_rows], [kernel], [wide],
-        moved=4 << 20,
+    tile = pltpu.VMEM((2, shells, row_count, LANES), BF16)
+    low, high = call(
+        edge_kernel, "cut_edges", (edge, edge), [], [], [tile, pltpu.SemaphoreType.DMA((2,))],
+        moved=4 << 20, direct=[kernel],
+    )
+    given = call(
+        first_kernel, "pack_half_of_shells", send, [place, polar_rows], [kernel], [wide],
+        moved=4 << 20, direct=[low],
     )
     kept = call(
         second_kernel, "pack_other_half_of_shells", send, [place, polar_rows], [kernel], [wide],
-        moved=4 << 20, unread=[low],
+        moved=4 << 20, direct=[given],
     )
     return given, kept, low, high
 
@@ -300,6 +314,7 @@
         ],
         flops=1 << 32,
         moved=16 << 20,
+        mib=20,
     )
 
 
@@ -314,7 +329,7 @@
         [pltpu.VMEM((held, 2 * sectors * block + 2 * PART, LANES), BF16)],
         flops=1 << 30,
         moved=4 << 20,
-        unread=[after],
+        direct=[after],
     )
 
 
@@ -341,10 +356,16 @@
         "add_polar_rows_and_blend",
         struct(lat.shape, BF16),
         [place],
-        [lat, mine, other, polar_weight, mix],
-        [pltpu.VMEM((col_count // LANES, shells * polar, LANES), F32), pltpu.VMEM(lat.shape, F32)],
+        [mine, other, polar_weight, mix],
+        [
+            pltpu.VMEM((col_count // LANES, shells * polar, LANES), F32),
+            pltpu.VMEM(lat.shape, F32),
+            pltpu.SemaphoreType.DMA,
+        ],
         flops=1 << 31,
         moved=8 << 20,
+        direct=[lat],
+        mib=50,
     )
 
 
@@ -363,7 +384,8 @@
     before = lax.ppermute(high, "sector", up)
     after = lax.ppermute(low, "sector", down)
     inner = (zone_id == 1) | (zone_id == last - 1)
-    circles = lax.all_to_all(jnp.where(inner, given, kept), "sector", 0, 0, tiled=True)
+    parts, before, after = lax.optimization_barrier((jnp.where(inner, given, kept), before, after))
+    circles = lax.all_to_all(parts, "sector", 0, 0, tiled=True)
     lon_smooth, lat_weight, mix = smooth_lon(place, lon_halo, kernel, before, after, lat_reach[:, None], blend)
     north = [(i, i + 1) for i in range(zones - 1)]
     south = [(j, i) for i, j in north]

time: 96.5 us -> 89.7 us (0.930)
  local copies, waits for them, and re-layouts: 9.19 us -> 3.98 us
  Pallas kernels: 21.8 us -> 24.1 us
  starting transfers between devices: 27.1 us -> 25.1 us
  waiting for transfers between devices: 36.7 us -> 34.8 us
    all_to_all x1, waiting for transfers between devices: 0.01 us -> 8.34 us  [per_device(): circles = lax.all_to_all(parts, 'sector', 0, 0, tiled=True)]
    ppermute x1, waiting for transfers between devices: 16.4 us -> 8.91 us  [per_device(): before = lax.ppermute(high, 'sector', up)]
    unnamed x28 -> x20, local copies, waits for them, and re-layouts: 8.93 us -> 3.73 us
    pallas_call x6 -> x7, Pallas kernels: 21.8 us -> 24.1 us  [call(): pl.pallas_call(kernel, out_shape=out_shape, in_specs=[smem] * len(scalars...]
    all_to_all x1, starting transfers between devices: 7.13 us -> 4.95 us  [per_device(): mine = lax.all_to_all(turned, 'sector', 0, 0, tiled=True)]
    ppermute x1, waiting for transfers between devices: 1.68 us -> 0.01 us  [per_device(): after = lax.ppermute(low, 'sector', down)]
  transfers between devices with their start and end apart: 8 -> 8, of which waited for: 4 -> 4; matrix products, arithmetic and copies ran while one was open for 0% -> 1% of each run, Pallas kernels for 13% -> 14%
where the time goes in v3:
time: 89.7 us; the launch traced here: 89.1 us
  waiting for transfers between devices  34.8 us (39%)
  starting transfers between devices  25.1 us (28%)
  Pallas kernels  24.1 us (27%)
  local copies, waits for them, and re-layouts  3.98 us (4%)
  other arithmetic  0.97 us (1%)
    pallas_call x7, Pallas kernels, call(): pl.pallas_call(kernel, out_shape=out_shape, in_specs=[smem] * len(scalars...  24.1 us
    all_to_all x1, starting transfers between devices, per_device(): circles = lax.all_to_all(parts, 'sector', 0, 0, tiled=True)  9.72 us
    ppermute x1, waiting for transfers between devices, per_device(): below = lax.ppermute(lon_smooth[:, :LMAX], 'zone', south)  9.67 us
    ppermute x1, waiting for transfers between devices, per_device(): before = lax.ppermute(high, 'sector', up)  8.91 us
    all_to_all x1, waiting for transfers between devices, per_device(): circles = lax.all_to_all(parts, 'sector', 0, 0, tiled=True)  8.34 us
    ppermute x1, waiting for transfers between devices, per_device(): above = lax.ppermute(lon_smooth[:, row_count - LMAX:], 'zone', north)  7.89 us
    all_to_all x1, starting transfers between devices, per_device(): mine = lax.all_to_all(turned, 'sector', 0, 0, tiled=True)  4.95 us
    unnamed x20, local copies, waits for them, and re-layouts  3.73 us
  transfers between devices with their start and end apart: 8, of which 4 were waited for; matrix products, arithmetic and copies ran while one was open for 1% of the time, Pallas kernels for 14%

profile of v3, /device:TPU:24, one launch (start us, length us, event | category | flops | bytes accessed | tf_op | source)
XLA Modules:
  0.0 89.1 jit_solution(2438271699864821749)
XLA Ops:
  0.0 0.0 copy-start.2
  0.0 0.0 copy-start
  0.0 1.4 %copy-done = bf16[32,64,384]{2,1,0:T(8,128)(2,1)S(1)} copy-done((bf16[32,64,384]{2,1,0:T(8,128)(2,1)S(1)}, bf16[32,64,384]{2,1,0:T(8,128)(2,1)}, u32[]{:S(2)}) %copy-start) | copy-done | bytes 1572888
  1.4 1.2 %cut_edges.1 = (bf16[1024,128]{1,0:T(8,128)(2,1)S(1)}, bf16[1024,128]{1,0:T(8,128)(2,1)}) custom-call(bf16[32,64,384]{2,1,0:T(8,128)(2,1)S(1)} %copy-done), custom_call_target="tpu_custom_call" | custom-call | bytes 4194304 | tf_op jit(solution)/shard_map/cut_edges/pallas_call | solution.py:256
  2.7 0.1 pad_add_fusion.place_ref
  2.8 0.0 copy-done.2
  2.8 1.9 %pack_half_of_shells.1.given_ref = bf16[16,3,48,128]{3,2,1,0:T(8,128)(2,1)S(1)} custom-call(s32[2]{0:T(128)S(1)} %pad_add_fusion.place_ref, s32[96]{0:T(128)S(1)} %copy-done.2, bf16[32,64,384]{2,1,0:T(8,128)(2,1)S(1)} %copy-done, bf16[1024,128]{1,0:T(8,128)(2,1)S(1)} %get-tuple-element.17.low_ref), custom_call_target="tpu_custom_call" | custom-call | bytes 4194304 | tf_op jit(solution)/shard_map/pack_half_of_shells/pallas_call | solution.py:256
  4.6 1.5 %collective-permute-start = (bf16[16,3,48,128]{3,2,1,0:T(8,128)(2,1)S(1)}, bf16[16,3,48,128]{3,2,1,0:T(8,128)(2,1)}, u32[]{:S(2)}, u32[]{:S(2)}) collective-permute-start(bf16[16,3,48,128]{3,2,1,0:T(8,128)(2,1)S(1)} %pack_half_of_shells.1.given_ref), channel_id=1, source_target_pairs={{0,16},{240,224},{1,17},{241,225},{2,18},{242,226},{3,19},{243,227... | collective-permute-start | bytes 1769480 | tf_op jit(solution)/shard_map/ppermute | solution.py:383
  6.1 0.7 collective-permute-start.2
  6.9 2.2 %collective-permute-start.1 = (bf16[1024,128]{1,0:T(8,128)(2,1)}, bf16[1024,128]{1,0:T(8,128)(2,1)}, u32[]{:S(2)}, u32[]{:S(2)}) collective-permute-start(bf16[1024,128]{1,0:T(8,128)(2,1)} %get-tuple-element.18), channel_id=1, source_target_pairs={{0,1},{1,2},{2,3},{3,4},{4,5},{5,6},{6,7},{7,8},{8,9},{9,10},{10,1... | collective-permute-start | bytes 786440 | tf_op jit(solution)/shard_map/ppermute | solution.py:384
  9.1 1.9 %pack_other_half_of_shells.1 = bf16[16,3,48,128]{3,2,1,0:T(8,128)(2,1)S(1)} custom-call(s32[2]{0:T(128)S(1)} %pad_add_fusion.place_ref, s32[96]{0:T(128)S(1)} %copy-done.2, bf16[32,64,384]{2,1,0:T(8,128)(2,1)S(1)} %copy-done, bf16[16,3,48,128]{3,2,1,0:T(8,128)(2,1)S(1)} %pack_half_of_shells.1.given_ref), custom_call_target="tpu_custom_call" | custom-call | bytes 4194304 | tf_op jit(solution)/shard_map/pack_other_half_of_shells/pallas_call | solution.py:256
  10.9 0.0 copy-start.9
  10.9 0.0 copy-start.1
  11.0 0.0 copy-start.3
  11.0 0.0 copy-start.4
  11.0 0.0 collective-permute-done
  11.0 0.9 broadcast_select_fusion
  11.9 8.9 %collective-permute-done.1.before_ref = bf16[1024,128]{1,0:T(8,128)(2,1)} collective-permute-done((bf16[1024,128]{1,0:T(8,128)(2,1)}, bf16[1024,128]{1,0:T(8,128)(2,1)}, u32[]{:S(2)}, u32[]{:S(2)}) %collective-permute-start.1) | collective-permute-done | bytes 262176 | tf_op jit(solution)/shard_map/ppermute | solution.py:384
  20.8 0.0 collective-permute-done.2.after_ref
  20.8 9.7 %all-to-all-start = ((bf16[16,3,48,128]{3,2,1,0:T(8,128)(2,1)}), bf16[16,3,48,128]{3,2,1,0:T(8,128)(2,1)}, u32[]{:S(2)}, u32[]{:S(2)}) async-start(bf16[16,3,48,128]{3,2,1,0:T(8,128)(2,1)} %broadcast_select_fusion), calls=%async_computation | async-start | bytes 1179648 | tf_op jit(solution)/shard_map/all_to_all | solution.py:388
  30.5 0.0 copy-done.9
  30.5 0.1 copy.7.reach_ref
  30.6 0.0 copy-done.1
  30.6 0.0 copy-done.3
  30.6 0.0 copy-done.4
  30.6 0.0 copy-start.5
  30.7 8.1 %smooth_along_longitude.1 = (bf16[32,64,384]{2,1,0:T(8,128)(2,1)S(1)}, bf16[64,128]{1,0:T(8,128)(2,1)S(1)}, bf16[256,256]{1,0:T(8,128)(2,1)S(1)}) custom-call(s32[2]{0:T(128)S(1)} %pad_add_fusion.place_ref, s32[1024]{0:T(1024)S(1)} %copy-done.4, bf16[32,64,384]{2,1,0:T(8,128)(2,1)S(1)} %copy-done.1, bf16[1024,128]{1,0:T(8,128)(2,1)} %collective-permute-done.1.before_ref, ...), custom_call_target="tpu_custom_call" | custom-call | flops 4294967296 | bytes 16777216 | tf_op jit(solution)/shard_map/smooth_along_longitude/pallas_call | solution.py:256
  38.8 0.0 copy-start.7
  38.8 0.6 copy-done.7
  39.4 8.3 %all-to-all-done.x_ref = bf16[16,3,48,128]{3,2,1,0:T(8,128)(2,1)} async-done(((bf16[16,3,48,128]{3,2,1,0:T(8,128)(2,1)}), bf16[16,3,48,128]{3,2,1,0:T(8,128)(2,1)}, u32[]{:S(2)}, u32[]{:S(2)}) %all-to-all-start) | async-done | bytes 589856 | tf_op jit(solution)/shard_map/all_to_all | solution.py:388
  47.8 0.0 copy-done.5
  47.8 2.7 %smooth_and_turn_polar_circles.1 = bf16[16,3,48,128]{3,2,1,0:T(8,128)(2,1)} custom-call(s32[2]{0:T(128)S(1)} %pad_add_fusion.place_ref, s32[96]{0:T(128)S(1)} %copy-done.2, s32[96]{0:T(128)S(1)} %copy-done.5, s32[1024]{0:T(1024)S(1)} %copy-done.4, bf16[16,3,48,128]{3,2,1,0:T(8,128)(2,1)} %all-to-all-done.x_ref, ...), custom_call_target="tpu_custom_call" | custom-call | flops 1073741824 | bytes 4194304 | tf_op jit(solution)/shard_map/smooth_and_turn_polar_circles/pallas_call | solution.py:256
  50.5 4.9 %all-to-all-start.1 = ((bf16[16,3,48,128]{3,2,1,0:T(8,128)(2,1)}), bf16[16,3,48,128]{3,2,1,0:T(8,128)(2,1)S(1)}, u32[]{:S(2)}, u32[]{:S(2)}) async-start(bf16[16,3,48,128]{3,2,1,0:T(8,128)(2,1)} %smooth_and_turn_polar_circles.1), calls=%async_computation.1 | async-start | bytes 1179648 | tf_op jit(solution)/shard_map/all_to_all | solution.py:395
  55.5 0.2 fusion
  55.6 3.3 %collective-permute-start.4 = (bf16[32,32,384]{2,1,0:T(8,128)(2,1)S(1)}, bf16[32,32,384]{2,1,0:T(8,128)(2,1)S(1)}, u32[]{:S(2)}, u32[]{:S(2)}) collective-permute-start(bf16[32,32,384]{2,1,0:T(8,128)(2,1)S(1)} %get-tuple-element.29), channel_id=1, source_target_pairs={{16,0},{32,16},{48,32},{64,48},{80,64},{96,80},{112,96},{128,112},... | collective-permute-start | bytes 2359304 | tf_op jit(solution)/shard_map/ppermute | solution.py:393
  58.9 0.0 copy-start.8
  58.9 2.1 %collective-permute-start.3 = (bf16[32,32,384]{2,1,0:T(8,128)(2,1)S(1)}, bf16[32,32,384]{2,1,0:T(8,128)(2,1)S(1)}, u32[]{:S(2)}, u32[]{:S(2)}) collective-permute-start(bf16[32,32,384]{2,1,0:T(8,128)(2,1)S(1)} %get-tuple-element.30), channel_id=1, source_target_pairs={{0,16},{16,32},{32,48},{48,64},{64,80},{80,96},{96,112},{112,128},... | collective-permute-start | bytes 2359304 | tf_op jit(solution)/shard_map/ppermute | solution.py:392
  61.0 9.7 %collective-permute-done.4.below_ref = bf16[32,32,384]{2,1,0:T(8,128)(2,1)S(1)} collective-permute-done((bf16[32,32,384]{2,1,0:T(8,128)(2,1)S(1)}, bf16[32,32,384]{2,1,0:T(8,128)(2,1)S(1)}, u32[]{:S(2)}, u32[]{:S(2)}) %collective-permute-start.4) | collective-permute-done | bytes 786464 | tf_op jit(solution)/shard_map/ppermute | solution.py:393
  70.7 7.9 %collective-permute-done.3.above_ref = bf16[32,32,384]{2,1,0:T(8,128)(2,1)S(1)} collective-permute-done((bf16[32,32,384]{2,1,0:T(8,128)(2,1)S(1)}, bf16[32,32,384]{2,1,0:T(8,128)(2,1)S(1)}, u32[]{:S(2)}, u32[]{:S(2)}) %collective-permute-start.3) | collective-permute-done | bytes 786464 | tf_op jit(solution)/shard_map/ppermute | solution.py:392
  78.5 2.4 %smooth_along_latitude.1 = (f32[32,64,384]{2,1,0:T(8,128)S(1)}, bf16[64,48]{1,0:T(8,128)(2,1)S(1)}) custom-call(s32[2]{0:T(128)S(1)} %pad_add_fusion.place_ref, s32[96]{0:T(128)S(1)} %copy-done.2, bf16[32,32,384]{2,1,0:T(8,128)(2,1)S(1)} %collective-permute-done.3.above_ref, bf16[32,64,384]{2,1,0:T(8,128)(2,1)S(1)} %get-tuple-element.23.own_ref, ...), custom_call_target="tpu_custom_call" | custom-call | flops 1073741824 | bytes 8388608 | tf_op jit(solution)/shard_map/smooth_along_latitude/pallas_call | solution.py:256
  81.0 0.0 copy-start.6
  81.0 1.6 %copy-done.6 = f32[32,64,384]{2,1,0:T(8,128)} copy-done((f32[32,64,384]{2,1,0:T(8,128)}, f32[32,64,384]{2,1,0:T(8,128)S(1)}, u32[]{:S(2)}) %copy-start.6) | copy-done | bytes 3145752
  82.6 0.0 all-to-all-done.1.mine_ref
  82.6 0.7 collective-permute-start.5
  83.3 0.0 collective-permute-done.5.other_ref
  83.3 0.0 copy-done.8
  83.4 5.8 %add_polar_rows_and_blend.1 = bf16[32,64,384]{2,1,0:T(8,128)(2,1)} custom-call(s32[2]{0:T(128)S(1)} %pad_add_fusion.place_ref, bf16[16,3,48,128]{3,2,1,0:T(8,128)(2,1)S(1)} %all-to-all-done.1.mine_ref, bf16[16,3,48,128]{3,2,1,0:T(8,128)(2,1)S(1)} %collective-permute-done.5.other_ref, bf16[64,48]{1,0:T(8,128)(2,1)S(1)} %get-tuple-element.26.polar_weight_ref, ...), custom_call_target="tpu_custom_call" | custom-call | flops 2147483648 | bytes 8388608 | tf_op jit(solution)/shard_map/add_polar_rows_and_blend/pallas_call | solution.py:256
Async XLA Ops:
  0.0 2.8 %copy-start.2 = (s32[96]{0:T(128)S(1)}, s32[96]{0:T(128)}, u32[]{:S(2)}) copy-start(s32[96]{0:T(128)} %rows_ref.7) | copy-start | bytes 1156
  0.0 1.4 %copy-start = (bf16[32,64,384]{2,1,0:T(8,128)(2,1)S(1)}, bf16[32,64,384]{2,1,0:T(8,128)(2,1)}, u32[]{:S(2)}) copy-start(bf16[32,64,384]{2,1,0:T(8,128)(2,1)} %x_ref.7) | copy-start | bytes 4718596
  4.6 6.4 %collective-permute-start = (bf16[16,3,48,128]{3,2,1,0:T(8,128)(2,1)S(1)}, bf16[16,3,48,128]{3,2,1,0:T(8,128)(2,1)}, u32[]{:S(2)}, u32[]{:S(2)}) collective-permute-start(bf16[16,3,48,128]{3,2,1,0:T(8,128)(2,1)S(1)} %pack_half_of_shells.1.given_ref), channel_id=1, source_target_pairs={{0,16},{240,224},{1,17},{241,225},{2,18},{242,226},{3,19},{243,227... | collective-permute-start | bytes 1769480 | tf_op jit(solution)/shard_map/ppermute | solution.py:383
  6.1 14.7 %collective-permute-start.2 = (bf16[1024,128]{1,0:T(8,128)(2,1)S(1)}, bf16[1024,128]{1,0:T(8,128)(2,1)S(1)}, u32[]{:S(2)}, u32[]{:S(2)}) collective-permute-start(bf16[1024,128]{1,0:T(8,128)(2,1)S(1)} %get-tuple-element.17.low_ref), channel_id=1, source_target_pairs={{1,0},{2,1},{3,2},{4,3},{5,4},{6,5},{7,6},{8,7},{9,8},{10,9},{11,1... | collective-permute-start | bytes 786440 | tf_op jit(solution)/shard_map/ppermute | solution.py:385
  6.9 13.9 %collective-permute-start.1 = (bf16[1024,128]{1,0:T(8,128)(2,1)}, bf16[1024,128]{1,0:T(8,128)(2,1)}, u32[]{:S(2)}, u32[]{:S(2)}) collective-permute-start(bf16[1024,128]{1,0:T(8,128)(2,1)} %get-tuple-element.18), channel_id=1, source_target_pairs={{0,1},{1,2},{2,3},{3,4},{4,5},{5,6},{6,7},{7,8},{8,9},{9,10},{10,1... | collective-permute-start | bytes 786440 | tf_op jit(solution)/shard_map/ppermute | solution.py:384
  10.9 19.6 %copy-start.9 = (s32[64]{0:T(128)S(1)}, s32[64]{0:T(128)}, u32[]{:S(2)}) copy-start(s32[64]{0:T(128)} %param.8) | copy-start | bytes 772
  10.9 19.7 %copy-start.1 = (bf16[32,64,384]{2,1,0:T(8,128)(2,1)S(1)}, bf16[32,64,384]{2,1,0:T(8,128)(2,1)}, u32[]{:S(2)}) copy-start(bf16[32,64,384]{2,1,0:T(8,128)(2,1)} %x_ref.7) | copy-start | bytes 4718596
  11.0 19.7 %copy-start.3 = (bf16[32,32]{1,0:T(8,128)(2,1)S(1)}, bf16[32,32]{1,0:T(8,128)(2,1)}, u32[]{:S(2)}) copy-start(bf16[32,32]{1,0:T(8,128)(2,1)} %blend_ref.1) | copy-start | bytes 6148
  11.0 19.7 %copy-start.4 = (s32[1024]{0:T(1024)S(1)}, s32[1024]{0:T(1024)}, u32[]{:S(2)}) copy-start(s32[1024]{0:T(1024)} %halo_ref.3) | copy-start | bytes 12292
  20.8 27.0 %all-to-all-start = ((bf16[16,3,48,128]{3,2,1,0:T(8,128)(2,1)}), bf16[16,3,48,128]{3,2,1,0:T(8,128)(2,1)}, u32[]{:S(2)}, u32[]{:S(2)}) async-start(bf16[16,3,48,128]{3,2,1,0:T(8,128)(2,1)} %broadcast_select_fusion), calls=%async_computation | async-start | bytes 1179648 | tf_op jit(solution)/shard_map/all_to_all | solution.py:388
  30.6 17.1 %copy-start.5 = (s32[96]{0:T(128)S(1)}, s32[96]{0:T(128)}, u32[]{:S(2)}) copy-start(s32[96]{0:T(128)} %shift_ref.1) | copy-start | bytes 1156
  38.8 0.6 copy-start.7
  50.5 32.1 %all-to-all-start.1 = ((bf16[16,3,48,128]{3,2,1,0:T(8,128)(2,1)}), bf16[16,3,48,128]{3,2,1,0:T(8,128)(2,1)S(1)}, u32[]{:S(2)}, u32[]{:S(2)}) async-start(bf16[16,3,48,128]{3,2,1,0:T(8,128)(2,1)} %smooth_and_turn_polar_circles.1), calls=%async_computation.1 | async-start | bytes 1179648 | tf_op jit(solution)/shard_map/all_to_all | solution.py:395
  55.6 15.0 %collective-permute-start.4 = (bf16[32,32,384]{2,1,0:T(8,128)(2,1)S(1)}, bf16[32,32,384]{2,1,0:T(8,128)(2,1)S(1)}, u32[]{:S(2)}, u32[]{:S(2)}) collective-permute-start(bf16[32,32,384]{2,1,0:T(8,128)(2,1)S(1)} %get-tuple-element.29), channel_id=1, source_target_pairs={{16,0},{32,16},{48,32},{64,48},{80,64},{96,80},{112,96},{128,112},... | collective-permute-start | bytes 2359304 | tf_op jit(solution)/shard_map/ppermute | solution.py:393
  58.9 24.4 %copy-start.8 = (bf16[256,256]{1,0:T(8,128)(2,1)S(1)}, bf16[256,256]{1,0:T(8,128)(2,1)}, u32[]{:S(2)}) copy-start(bf16[256,256]{1,0:T(8,128)(2,1)} %copy-done.7) | copy-start | bytes 393220
  58.9 19.6 %collective-permute-start.3 = (bf16[32,32,384]{2,1,0:T(8,128)(2,1)S(1)}, bf16[32,32,384]{2,1,0:T(8,128)(2,1)S(1)}, u32[]{:S(2)}, u32[]{:S(2)}) collective-permute-start(bf16[32,32,384]{2,1,0:T(8,128)(2,1)S(1)} %get-tuple-element.30), channel_id=1, source_target_pairs={{0,16},{16,32},{32,48},{48,64},{64,80},{80,96},{96,112},{112,128},... | collective-permute-start | bytes 2359304 | tf_op jit(solution)/shard_map/ppermute | solution.py:392
  81.0 1.6 %copy-start.6 = (f32[32,64,384]{2,1,0:T(8,128)}, f32[32,64,384]{2,1,0:T(8,128)S(1)}, u32[]{:S(2)}) copy-start(f32[32,64,384]{2,1,0:T(8,128)S(1)} %get-tuple-element.28.lat_ref) | copy-start | bytes 9437188
  82.6 0.7 collective-permute-start.5

commit v4 on v3

--- a/solution.py
+++ b/solution.py
@@ -18,7 +18,7 @@
     return lax.broadcasted_iota(jnp.int32, (rows, LANES), 1)
 
 
-def edge_kernel(x_ref, low_ref, high_ref, tile_ref, sems):
+def edge_kernel(place_ref, x_ref, near_ref, far_ref, tile_ref, sems):
     shells, row_count, col_count = x_ref.shape
     half = shells // 2
     size = half * row_count
@@ -33,12 +33,13 @@
     def part(e, shell):
         return tile_ref[e, shell : shell + half].reshape(size, LANES).astype(F32)
 
+    even = lax.rem(place_ref[1], 2) == 0
     copies[0].wait()
-    low_ref[...] = jnp.where(lane < HMAX, part(0, 0), pltpu.roll(part(0, half), HMAX, 1)).astype(BF16)
+    low = jnp.where(lane < HMAX, part(0, 0), pltpu.roll(part(0, half), HMAX, 1))
     copies[1].wait()
-    high_ref[...] = jnp.where(
-        lane < HMAX, pltpu.roll(part(1, 0), HMAX, 1), pltpu.roll(part(1, half), 2 * HMAX, 1)
-    ).astype(BF16)
+    high = jnp.where(lane < HMAX, pltpu.roll(part(1, 0), HMAX, 1), pltpu.roll(part(1, half), 2 * HMAX, 1))
+    near_ref[...] = jnp.where(even, high, low).astype(BF16)
+    far_ref[...] = jnp.where(even, low, high).astype(BF16)
 
 
 def write_polar(half, place_ref, rows_ref, x_ref, send_ref, wide_ref):
@@ -61,7 +62,7 @@
                 send_ref[k, r, t * PART : (t + 1) * PART, :] = values.astype(BF16)
 
 
-def first_kernel(place_ref, rows_ref, x_ref, low_ref, send_ref, wide_ref):
+def first_kernel(place_ref, rows_ref, x_ref, far_ref, send_ref, wide_ref):
     write_polar(1, place_ref, rows_ref, x_ref, send_ref, wide_ref)
 
 
@@ -76,8 +77,8 @@
     return rate, jnp.broadcast_to(1.0 / jnp.sum(terms, axis=1, keepdims=True), half_f.shape)
 
 
-def lon_kernel(place_ref, halo_ref, x_ref, before_ref, after_ref, reach_ref, blend_ref,
-               out_ref, weight_ref, mix_ref, wide_ref, done_ref, half_ref, rate_ref, scale_ref):
+def lon_kernel(place_ref, halo_ref, x_ref, near_ref, far_ref, reach_ref, blend_ref,
+               out_ref, near_rows_ref, far_rows_ref, weight_ref, mix_ref, wide_ref, done_ref, half_ref, rate_ref, scale_ref):
     shells, row_count, col_count = x_ref.shape
     total = shells * row_count
     size = total // 2
@@ -87,19 +88,22 @@
         half_ref[i : i + 1, :] = jnp.full((1, LANES), halo_ref[zone * row_count + i], jnp.int32).astype(F32)
     rate_ref[...], scale_ref[...] = band_terms(half_ref[...])
     lane = lanes_of(size)
+    even = lax.rem(place_ref[1], 2) == 0
+    near = near_ref[...].astype(F32)
+    far = far_ref[...].astype(F32)
+    before = jnp.where(even, far, near)
+    after = jnp.where(even, near, far)
     for part in range(2):
         rows = pl.ds(part * size, size)
         shell = slice(part * (shells // 2), (part + 1) * (shells // 2))
-        edge = before_ref[...].astype(F32)
-        previous = edge if part == 0 else pltpu.roll(edge, LANES - HMAX, 1)
+        previous = before if part == 0 else pltpu.roll(before, LANES - HMAX, 1)
         for t in range(tiles):
             turned = pltpu.roll(
                 x_ref[shell, :, t * LANES : (t + 1) * LANES].reshape(size, LANES).astype(F32), HMAX, 1
             )
             wide_ref[t, rows, :] = jnp.where(lane < HMAX, previous, turned)
             previous = turned
-        edge = after_ref[...].astype(F32)
-        edge = pltpu.roll(edge, HMAX, 1) if part == 0 else edge
+        edge = pltpu.roll(after, HMAX, 1) if part == 0 else after
         wide_ref[tiles, rows, :] = jnp.where(lane < HMAX, previous, jnp.where(lane < 2 * HMAX, edge, 0.0))
     depth = 2 * LANES
     offset = (lanes_of(depth) - lax.broadcasted_iota(jnp.int32, (depth, LANES), 0) + HMAX).astype(F32)
@@ -124,6 +128,10 @@
     lax.fori_loop(0, row_count // UNROLL, some_rows, 0)
     for t in range(tiles):
         out_ref[:, :, t * LANES : (t + 1) * LANES] = done_ref[t].astype(BF16).reshape(shells, row_count, LANES)
+    odd = lax.rem(zone, 2)
+    last = row_count - LMAX
+    near_rows_ref[...] = out_ref[:, pl.ds(pl.multiple_of((1 - odd) * last, LMAX), LMAX), :]
+    far_rows_ref[...] = out_ref[:, pl.ds(pl.multiple_of(odd * last, LMAX), LMAX), :]
     frame_rows = weight_ref.shape[1]
     reach = reach_ref[...]
     column = lax.broadcasted_iota(jnp.int32, (row_count, frame_rows), 1)
@@ -178,7 +186,7 @@
         out_ref[:, r] = result.astype(BF16).reshape(sectors, block, LANES)
 
 
-def lat_kernel(place_ref, rows_ref, above_ref, own_ref, below_ref, weight_ref,
+def lat_kernel(place_ref, rows_ref, near_ref, own_ref, far_ref, weight_ref,
                out_ref, polar_weight_ref, pick_ref):
     shells, row_count, col_count = own_ref.shape
     frame_rows = weight_ref.shape[1]
@@ -193,12 +201,19 @@
     polar_weight_ref[...] = lax.dot_general(
         weight, pick.astype(BF16), (((1,), (1,)), ((), ())), preferred_element_type=F32
     ).astype(BF16)
-    rest = (weight.astype(F32) * (1.0 - jnp.sum(pick, axis=0, keepdims=True))).astype(BF16)
+    rest = weight.astype(F32) * (1.0 - jnp.sum(pick, axis=0, keepdims=True))
+    wide = lanes_of(row_count)
+    turned = jnp.where(
+        wide < LMAX,
+        pltpu.roll(rest, LMAX, 1),
+        jnp.where(wide < frame_rows - LMAX, rest, pltpu.roll(rest, frame_rows - LMAX, 1)),
+    )
+    rest = jnp.where(lax.rem(zone, 2) == 0, turned, rest).astype(BF16)
 
     def some_shells(block, carry):
         for u in range(4):
             s = block * 4 + u
-            values = jnp.concatenate([above_ref[s], own_ref[s], below_ref[s]], axis=0)
+            values = jnp.concatenate([near_ref[s], own_ref[s], far_ref[s]], axis=0)
             out_ref[s] = jnp.dot(rest, values, preferred_element_type=F32)
         return carry
 
@@ -206,7 +221,7 @@
 
 
 def final_kernel(place_ref, mine_ref, other_ref, polar_weight_ref, mix_ref, lat_ref,
-                 out_ref, polar_ref, sum_ref, sem):
+                 out_ref, polar_ref, sum_ref, stage_ref, sem, sems):
     shells, row_count, col_count = lat_ref.shape
     holders, held = mine_ref.shape[:2]
     tiles = col_count // LANES
@@ -239,16 +254,22 @@
     lax.fori_loop(0, shells // 4, some_shells, 0)
     group = mix_ref.shape[0] // shells
     mix = mix_ref[...]
+    stores = []
     for g in range(row_count // (2 * group)):
         mixed = []
         for e in range(2):
             first = (2 * g + e) * group
             values = sum_ref[:, first : first + group, :].reshape(shells * group, col_count).astype(BF16)
             mixed.append(jnp.dot(mix, values, preferred_element_type=F32).reshape(shells, group, col_count))
-        out_ref[:, 2 * g * group : 2 * (g + 1) * group, :] = jnp.concatenate(mixed, axis=1).astype(BF16)
-
-
-def call(kernel, name, out_shape, scalars, arrays, scratch, flops=0, moved=0, direct=(), mib=16):
+        rows = pl.ds(2 * g * group, 2 * group)
+        stage_ref[:, rows, :] = jnp.concatenate(mixed, axis=1).astype(BF16)
+        stores.append(pltpu.make_async_copy(stage_ref.at[:, rows], out_ref.at[:, rows], sems.at[g]))
+        stores[-1].start()
+    for store in stores:
+        store.wait()
+
+
+def call(kernel, name, out_shape, scalars, arrays, scratch, flops=0, moved=0, direct=(), far=False, mib=16):
     smem = pl.BlockSpec(memory_space=pltpu.SMEM)
     vmem = pl.BlockSpec(memory_space=pltpu.VMEM)
     anywhere = pl.BlockSpec(memory_space=pl.ANY)
@@ -257,7 +278,7 @@
         kernel,
         out_shape=out_shape,
         in_specs=[smem] * len(scalars) + [vmem] * len(arrays) + [anywhere] * len(direct),
-        out_specs=(vmem,) * len(out_shape) if many else vmem,
+        out_specs=(vmem,) * len(out_shape) if many else anywhere if far else vmem,
         scratch_shapes=scratch,
         compiler_params=pltpu.CompilerParams(vmem_limit_bytes=mib << 20),
         cost_estimate=pl.CostEstimate(flops=flops, bytes_accessed=moved, transcendentals=0),
@@ -276,22 +297,22 @@
     edge = struct((shells * row_count // 2, LANES), BF16)
     wide = pltpu.VMEM((tiles, PART * row_count, LANES), F32)
     tile = pltpu.VMEM((2, shells, row_count, LANES), BF16)
-    low, high = call(
-        edge_kernel, "cut_edges", (edge, edge), [], [], [tile, pltpu.SemaphoreType.DMA((2,))],
+    near, far = call(
+        edge_kernel, "cut_edges", (edge, edge), [place], [], [tile, pltpu.SemaphoreType.DMA((2,))],
         moved=4 << 20, direct=[kernel],
     )
     given = call(
         first_kernel, "pack_half_of_shells", send, [place, polar_rows], [kernel], [wide],
-        moved=4 << 20, direct=[low],
+        moved=4 << 20, direct=[far],
     )
     kept = call(
         second_kernel, "pack_other_half_of_shells", send, [place, polar_rows], [kernel], [wide],
         moved=4 << 20, direct=[given],
     )
-    return given, kept, low, high
-
-
-def smooth_lon(place, lon_halo, kernel, before, after, reach, blend):
+    return given, kept, near, far
+
+
+def smooth_lon(place, lon_halo, kernel, near, far, reach, blend):
     shells, row_count, col_count = kernel.shape
     tiles = col_count // LANES
     rows = pltpu.VMEM((row_count, LANES), F32)
@@ -300,11 +321,13 @@
         "smooth_along_longitude",
         (
             struct((shells, row_count, col_count), BF16),
+            struct((shells, LMAX, col_count), BF16),
+            struct((shells, LMAX, col_count), BF16),
             struct((row_count, row_count + 2 * LMAX), BF16),
             struct((shells * 8, shells * 8), BF16),
         ),
         [place, lon_halo],
-        [kernel, before, after, reach, blend],
+        [kernel, near, far, reach, blend],
         [
             pltpu.VMEM((tiles + 1, shells * row_count, LANES), F32),
             pltpu.VMEM((tiles, shells * row_count, LANES), F32),
@@ -333,7 +356,7 @@
     )
 
 
-def smooth_lat(place, polar_rows, above, own, below, weight):
+def smooth_lat(place, polar_rows, near, own, far, weight):
     row_count, frame_rows = weight.shape
     polar = polar_rows.shape[0] // 2
     return call(
@@ -341,7 +364,7 @@
         "smooth_along_latitude",
         (struct(own.shape, F32), struct((row_count, polar), BF16)),
         [place, polar_rows],
-        [above, own, below, weight],
+        [near, own, far, weight],
         [pltpu.VMEM((polar, frame_rows), F32)],
         flops=1 << 30,
         moved=8 << 20,
@@ -360,10 +383,13 @@
         [
             pltpu.VMEM((col_count // LANES, shells * polar, LANES), F32),
             pltpu.VMEM(lat.shape, F32),
+            pltpu.VMEM(lat.shape, BF16),
             pltpu.SemaphoreType.DMA,
+            pltpu.SemaphoreType.DMA((4,)),
         ],
         flops=1 << 31,
         moved=8 << 20,
+        far=True,
         direct=[lat],
         mib=50,
     )
@@ -377,23 +403,24 @@
     sector_id = lax.axis_index("sector").astype(jnp.int32)
     place = jnp.stack([zone_id, sector_id])
     last = zones - 1
-    up = [(i, (i + 1) % sectors) for i in range(sectors)]
-    down = [(j, i) for i, j in up]
-    packed, kept, low, high = pack(place, polar_rows, kernel, sectors)
+    packed, kept, near, far = pack(place, polar_rows, kernel, sectors)
     given = lax.ppermute(packed, "zone", [(0, 1), (last, last - 1)])
-    before = lax.ppermute(high, "sector", up)
-    after = lax.ppermute(low, "sector", down)
+    far = lax.ppermute(far, "sector", [(i, (i + 1 if i % 2 else i - 1) % sectors) for i in range(sectors)])
+    near = lax.ppermute(near, "sector", [(i, i ^ 1) for i in range(sectors)])
     inner = (zone_id == 1) | (zone_id == last - 1)
-    parts, before, after = lax.optimization_barrier((jnp.where(inner, given, kept), before, after))
+    parts, near, far = lax.optimization_barrier((jnp.where(inner, given, kept), near, far))
     circles = lax.all_to_all(parts, "sector", 0, 0, tiled=True)
-    lon_smooth, lat_weight, mix = smooth_lon(place, lon_halo, kernel, before, after, lat_reach[:, None], blend)
-    north = [(i, i + 1) for i in range(zones - 1)]
-    south = [(j, i) for i, j in north]
-    above = lax.ppermute(lon_smooth[:, row_count - LMAX :], "zone", north)
-    below = lax.ppermute(lon_smooth[:, :LMAX], "zone", south)
+    lon_smooth, near_rows, far_rows, lat_weight, mix = smooth_lon(
+        place, lon_halo, kernel, near, far, lat_reach[:, None], blend
+    )
+    far_rows = lax.ppermute(
+        far_rows, "zone", [(i, i + 1 if i % 2 else i - 1) for i in range(1, zones - 1)]
+    )
+    near_rows = lax.ppermute(near_rows, "zone", [(i, i ^ 1) for i in range(zones)])
     turned = hold(place, polar_rows, polar_shift, lon_halo, circles, lat_weight)
+    turned, near_rows, far_rows = lax.optimization_barrier((turned, near_rows, far_rows))
     mine = lax.all_to_all(turned, "sector", 0, 0, tiled=True)
-    lat, polar_weight = smooth_lat(place, polar_rows, above, lon_smooth, below, lat_weight)
+    lat, polar_weight = smooth_lat(place, polar_rows, near_rows, lon_smooth, far_rows, lat_weight)
     mine, lat = lax.optimization_barrier((mine, lat))
     other = lax.ppermute(mine, "zone", [(0, 1), (1, 0), (last, last - 1), (last - 1, last)])
     return finish(place, lat, mine, other, polar_weight, mix)

time: 89.7 us -> 91.6 us (1.021)
  the two profiles are of different devices: /device:TPU:24 before, /device:TPU:7 now
where the time goes in v4:
time: 91.6 us; the launch traced here: 91.1 us
  waiting for transfers between devices  30.9 us (34%)
  starting transfers between devices  26.7 us (29%)
  Pallas kernels  24.7 us (27%)
  local copies, waits for them, and re-layouts  7.68 us (8%)
  other arithmetic  0.95 us (1%)
    pallas_call x7, Pallas kernels, call(): pl.pallas_call(kernel, out_shape=out_shape, in_specs=[smem] * len(scalars...  24.7 us
    all_to_all x1, waiting for transfers between devices, per_device(): mine = lax.all_to_all(turned, 'sector', 0, 0, tiled=True)  10.7 us
    ppermute x1, waiting for transfers between devices, per_device(): lax.ppermute(far_rows, 'zone', [(i, i + 1 if i % 2 else i - 1) for i in r...  10.6 us
    ppermute x1, waiting for transfers between devices, per_device(): near = lax.ppermute(near, 'sector', [(i, i ^ 1) for i in range(sectors)])  9.58 us
    all_to_all x1, starting transfers between devices, per_device(): mine = lax.all_to_all(turned, 'sector', 0, 0, tiled=True)  7.76 us
    unnamed x24, local copies, waits for them, and re-layouts  6.94 us
    ppermute x1, starting transfers between devices, per_device(): lax.ppermute(far, 'sector', [(i, (i + 1 if i % 2 else i - 1) % sectors) f...  6.59 us
    all_to_all x1, starting transfers between devices, per_device(): circles = lax.all_to_all(parts, 'sector', 0, 0, tiled=True)  4.95 us
  transfers between devices with their start and end apart: 8, of which 3 were waited for; matrix products, arithmetic and copies ran while one was open for 2% of the time, Pallas kernels for 17%

profile of v4, /device:TPU:7, one launch (start us, length us, event | category | flops | bytes accessed | tf_op | source)
XLA Modules:
  0.0 91.1 jit_solution(108247939890405739)
XLA Ops:
  0.0 0.0 copy-start.2
  0.0 0.1 pad_add_fusion.place_ref
  0.1 0.0 copy-start
  0.1 1.4 %copy-done = bf16[32,64,384]{2,1,0:T(8,128)(2,1)S(1)} copy-done((bf16[32,64,384]{2,1,0:T(8,128)(2,1)S(1)}, bf16[32,64,384]{2,1,0:T(8,128)(2,1)}, u32[]{:S(2)}) %copy-start) | copy-done | bytes 1572888
  1.5 1.8 %cut_edges.1 = (bf16[1024,128]{1,0:T(8,128)(2,1)}, bf16[1024,128]{1,0:T(8,128)(2,1)S(1)}) custom-call(s32[2]{0:T(128)S(1)} %pad_add_fusion.place_ref, bf16[32,64,384]{2,1,0:T(8,128)(2,1)S(1)} %copy-done), custom_call_target="tpu_custom_call" | custom-call | bytes 4194304 | tf_op jit(solution)/shard_map/cut_edges/pallas_call | solution.py:277
  3.3 0.0 copy-done.2
  3.3 1.9 %pack_half_of_shells.1.given_ref = bf16[16,3,48,128]{3,2,1,0:T(8,128)(2,1)S(1)} custom-call(s32[2]{0:T(128)S(1)} %pad_add_fusion.place_ref, s32[96]{0:T(128)S(1)} %copy-done.2, bf16[32,64,384]{2,1,0:T(8,128)(2,1)S(1)} %copy-done, bf16[1024,128]{1,0:T(8,128)(2,1)S(1)} %get-tuple-element.22.far_ref), custom_call_target="tpu_custom_call" | custom-call | bytes 4194304 | tf_op jit(solution)/shard_map/pack_half_of_shells/pallas_call | solution.py:277
  5.2 1.5 %collective-permute-start = (bf16[16,3,48,128]{3,2,1,0:T(8,128)(2,1)S(1)}, bf16[16,3,48,128]{3,2,1,0:T(8,128)(2,1)}, u32[]{:S(2)}, u32[]{:S(2)}) collective-permute-start(bf16[16,3,48,128]{3,2,1,0:T(8,128)(2,1)S(1)} %pack_half_of_shells.1.given_ref), channel_id=1, source_target_pairs={{0,16},{240,224},{1,17},{241,225},{2,18},{242,226},{3,19},{243,227... | collective-permute-start | bytes 1769480 | tf_op jit(solution)/shard_map/ppermute | solution.py:407
  6.7 6.6 %collective-permute-start.2 = (bf16[1024,128]{1,0:T(8,128)(2,1)S(1)}, bf16[1024,128]{1,0:T(8,128)(2,1)S(1)}, u32[]{:S(2)}, u32[]{:S(2)}) collective-permute-start(bf16[1024,128]{1,0:T(8,128)(2,1)S(1)} %get-tuple-element.22.far_ref), channel_id=1, source_target_pairs={{0,15},{1,2},{2,1},{3,4},{4,3},{5,6},{6,5},{7,8},{8,7},{9,10},{10,... | collective-permute-start | bytes 786440 | tf_op jit(solution)/shard_map/ppermute | solution.py:408
  13.3 0.0 collective-permute-start.1
  13.3 1.9 %pack_other_half_of_shells.1 = bf16[16,3,48,128]{3,2,1,0:T(8,128)(2,1)S(1)} custom-call(s32[2]{0:T(128)S(1)} %pad_add_fusion.place_ref, s32[96]{0:T(128)S(1)} %copy-done.2, bf16[32,64,384]{2,1,0:T(8,128)(2,1)S(1)} %copy-done, bf16[16,3,48,128]{3,2,1,0:T(8,128)(2,1)S(1)} %pack_half_of_shells.1.given_ref), custom_call_target="tpu_custom_call" | custom-call | bytes 4194304 | tf_op jit(solution)/shard_map/pack_other_half_of_shells/pallas_call | solution.py:277
  15.2 0.0 copy-start.1
  15.2 0.0 copy-start.3
  15.2 0.0 collective-permute-done
  15.2 0.9 broadcast_select_fusion
  16.1 9.6 %collective-permute-done.1.near_ref = bf16[1024,128]{1,0:T(8,128)(2,1)S(1)} collective-permute-done((bf16[1024,128]{1,0:T(8,128)(2,1)}, bf16[1024,128]{1,0:T(8,128)(2,1)S(1)}, u32[]{:S(2)}, u32[]{:S(2)}) %collective-permute-start.1) | collective-permute-done | bytes 262176 | tf_op jit(solution)/shard_map/ppermute | solution.py:409
  25.7 0.0 collective-permute-done.2.far_ref
  25.7 4.9 %all-to-all-start = ((bf16[16,3,48,128]{3,2,1,0:T(8,128)(2,1)}), bf16[16,3,48,128]{3,2,1,0:T(8,128)(2,1)S(1)}, u32[]{:S(2)}, u32[]{:S(2)}) async-start(bf16[16,3,48,128]{3,2,1,0:T(8,128)(2,1)} %broadcast_select_fusion), calls=%async_computation | async-start | bytes 1179648 | tf_op jit(solution)/shard_map/all_to_all | solution.py:412
  30.6 0.7 copy.7.reach_ref
  31.4 0.0 copy-done.1
  31.4 0.0 copy-done.3
  31.4 0.0 copy-start.4
  31.4 0.7 copy-done.4
  32.1 0.0 copy-start.5
  32.1 0.0 copy-start.6
  32.1 8.9 %smooth_along_longitude.1 = (bf16[32,64,384]{2,1,0:T(8,128)(2,1)S(1)}, bf16[32,32,384]{2,1,0:T(8,128)(2,1)}, bf16[32,32,384]{2,1,0:T(8,128)(2,1)}, bf16[64,128]{1,0:T(8,128)(2,1)S(1)}, bf16[256,256]{1,0:T(8,128)(2,1)S(1)}) custom-call(s32[2]{0:T(128)S(1)} %pad_add_fusion.place_ref, s32[1024]{0:T(1024)S(1)} %copy-done.4, bf16[32,64,384]{2,1,0:T(8,128)(2,1)S(1)} %copy-done.1, ...), custom_call_target="tpu_custom_call" | custom-call | flops 4294967296 | bytes 16777216 | tf_op jit(solution)/shard_map/smooth_along_longitude/pallas_call | solution.py:277
  41.0 0.0 copy-start.8
  41.0 1.1 %copy-done.8 = bf16[32,64,384]{2,1,0:T(8,128)(2,1)} copy-done((bf16[32,64,384]{2,1,0:T(8,128)(2,1)}, bf16[32,64,384]{2,1,0:T(8,128)(2,1)S(1)}, u32[]{:S(2)}) %copy-start.8) | copy-done | bytes 1572888
  42.2 0.6 copy-done.10
  42.8 0.8 collective-permute-start.3
  43.6 4.4 %collective-permute-start.4 = (bf16[32,32,384]{2,1,0:T(8,128)(2,1)}, bf16[32,32,384]{2,1,0:T(8,128)(2,1)S(1)}, u32[]{:S(2)}, u32[]{:S(2)}) collective-permute-start(bf16[32,32,384]{2,1,0:T(8,128)(2,1)} %get-tuple-element.29), channel_id=1, source_target_pairs={{16,32},{32,16},{48,64},{64,48},{80,96},{96,80},{112,128},{128,112... | collective-permute-start | bytes 2359304 | tf_op jit(solution)/shard_map/ppermute | solution.py:416
  48.0 0.0 all-to-all-done.x_ref
  48.0 0.0 copy-done.5
  48.1 0.0 copy-done.6
  48.1 2.3 %smooth_and_turn_polar_circles.1 = bf16[16,3,48,128]{3,2,1,0:T(8,128)(2,1)} custom-call(s32[2]{0:T(128)S(1)} %pad_add_fusion.place_ref, s32[96]{0:T(128)S(1)} %copy-done.2, s32[96]{0:T(128)S(1)} %copy-done.6, s32[1024]{0:T(1024)S(1)} %copy-done.5, bf16[16,3,48,128]{3,2,1,0:T(8,128)(2,1)S(1)} %all-to-all-done.x_ref, ...), custom_call_target="tpu_custom_call" | custom-call | flops 1073741824 | bytes 4194304 | tf_op jit(solution)/shard_map/smooth_and_turn_polar_circles/pallas_call | solution.py:277
  50.4 0.0 collective-permute-done.3.near_ref
  50.4 10.6 %collective-permute-done.4.far_ref = bf16[32,32,384]{2,1,0:T(8,128)(2,1)S(1)} collective-permute-done((bf16[32,32,384]{2,1,0:T(8,128)(2,1)}, bf16[32,32,384]{2,1,0:T(8,128)(2,1)S(1)}, u32[]{:S(2)}, u32[]{:S(2)}) %collective-permute-start.4) | collective-permute-done | bytes 786464 | tf_op jit(solution)/shard_map/ppermute | solution.py:416
  60.9 7.8 %all-to-all-start.1 = ((bf16[16,3,48,128]{3,2,1,0:T(8,128)(2,1)}), bf16[16,3,48,128]{3,2,1,0:T(8,128)(2,1)S(1)}, u32[]{:S(2)}, u32[]{:S(2)}) async-start(bf16[16,3,48,128]{3,2,1,0:T(8,128)(2,1)} %smooth_and_turn_polar_circles.1), calls=%async_computation.1 | async-start | bytes 1179648 | tf_op jit(solution)/shard_map/all_to_all | solution.py:422
  68.7 0.0 copy-start.9
  68.7 1.4 %copy-done.9 = bf16[32,64,384]{2,1,0:T(8,128)(2,1)S(1)} copy-done((bf16[32,64,384]{2,1,0:T(8,128)(2,1)S(1)}, bf16[32,64,384]{2,1,0:T(8,128)(2,1)}, u32[]{:S(2)}) %copy-start.9) | copy-done | bytes 1572888
  70.1 2.4 %smooth_along_latitude.1 = (f32[32,64,384]{2,1,0:T(8,128)S(1)}, bf16[64,48]{1,0:T(8,128)(2,1)S(1)}) custom-call(s32[2]{0:T(128)S(1)} %pad_add_fusion.place_ref, s32[96]{0:T(128)S(1)} %copy-done.2, bf16[32,32,384]{2,1,0:T(8,128)(2,1)S(1)} %collective-permute-done.3.near_ref, bf16[32,64,384]{2,1,0:T(8,128)(2,1)S(1)} %copy-done.9, ...), custom_call_target="tpu_custom_call" | custom-call | flops 1073741824 | bytes 8388608 | tf_op jit(solution)/shard_map/smooth_along_latitude/pallas_call | solution.py:277
  72.6 0.0 copy-start.7
  72.6 1.6 %copy-done.7 = f32[32,64,384]{2,1,0:T(8,128)} copy-done((f32[32,64,384]{2,1,0:T(8,128)}, f32[32,64,384]{2,1,0:T(8,128)S(1)}, u32[]{:S(2)}) %copy-start.7) | copy-done | bytes 3145752
  74.2 10.7 %all-to-all-done.1.mine_ref = bf16[16,3,48,128]{3,2,1,0:T(8,128)(2,1)S(1)} async-done(((bf16[16,3,48,128]{3,2,1,0:T(8,128)(2,1)}), bf16[16,3,48,128]{3,2,1,0:T(8,128)(2,1)S(1)}, u32[]{:S(2)}, u32[]{:S(2)}) %all-to-all-start.1) | async-done | bytes 589856 | tf_op jit(solution)/shard_map/all_to_all | solution.py:422
  85.0 0.7 collective-permute-start.5
  85.7 0.0 collective-permute-done.5.other_ref
  85.7 0.0 copy-done.11
  85.7 5.4 %add_polar_rows_and_blend.1 = bf16[32,64,384]{2,1,0:T(8,128)(2,1)} custom-call(s32[2]{0:T(128)S(1)} %pad_add_fusion.place_ref, bf16[16,3,48,128]{3,2,1,0:T(8,128)(2,1)S(1)} %all-to-all-done.1.mine_ref, bf16[16,3,48,128]{3,2,1,0:T(8,128)(2,1)S(1)} %collective-permute-done.5.other_ref, bf16[64,48]{1,0:T(8,128)(2,1)S(1)} %get-tuple-element.36.polar_weight_ref, ...), custom_call_target="tpu_custom_call" | custom-call | flops 2147483648 | bytes 8388608 | tf_op jit(solution)/shard_map/add_polar_rows_and_blend/pallas_call | solution.py:277
  (2 shorter events, 0.0 us)
Async XLA Ops:
  0.0 3.3 %copy-start.2 = (s32[96]{0:T(128)S(1)}, s32[96]{0:T(128)}, u32[]{:S(2)}) copy-start(s32[96]{0:T(128)} %rows_ref.7) | copy-start | bytes 1156
  0.1 1.4 %copy-start = (bf16[32,64,384]{2,1,0:T(8,128)(2,1)S(1)}, bf16[32,64,384]{2,1,0:T(8,128)(2,1)}, u32[]{:S(2)}) copy-start(bf16[32,64,384]{2,1,0:T(8,128)(2,1)} %x_ref.7) | copy-start | bytes 4718596
  5.2 10.0 %collective-permute-start = (bf16[16,3,48,128]{3,2,1,0:T(8,128)(2,1)S(1)}, bf16[16,3,48,128]{3,2,1,0:T(8,128)(2,1)}, u32[]{:S(2)}, u32[]{:S(2)}) collective-permute-start(bf16[16,3,48,128]{3,2,1,0:T(8,128)(2,1)S(1)} %pack_half_of_shells.1.given_ref), channel_id=1, source_target_pairs={{0,16},{240,224},{1,17},{241,225},{2,18},{242,226},{3,19},{243,227... | collective-permute-start | bytes 1769480 | tf_op jit(solution)/shard_map/ppermute | solution.py:407
  6.7 19.0 %collective-permute-start.2 = (bf16[1024,128]{1,0:T(8,128)(2,1)S(1)}, bf16[1024,128]{1,0:T(8,128)(2,1)S(1)}, u32[]{:S(2)}, u32[]{:S(2)}) collective-permute-start(bf16[1024,128]{1,0:T(8,128)(2,1)S(1)} %get-tuple-element.22.far_ref), channel_id=1, source_target_pairs={{0,15},{1,2},{2,1},{3,4},{4,3},{5,6},{6,5},{7,8},{8,7},{9,10},{10,... | collective-permute-start | bytes 786440 | tf_op jit(solution)/shard_map/ppermute | solution.py:408
  13.3 12.4 %collective-permute-start.1 = (bf16[1024,128]{1,0:T(8,128)(2,1)}, bf16[1024,128]{1,0:T(8,128)(2,1)S(1)}, u32[]{:S(2)}, u32[]{:S(2)}) collective-permute-start(bf16[1024,128]{1,0:T(8,128)(2,1)} %get-tuple-element.23), channel_id=1, source_target_pairs={{0,1},{1,0},{2,3},{3,2},{4,5},{5,4},{6,7},{7,6},{8,9},{9,8},{10,11... | collective-permute-start | bytes 786440 | tf_op jit(solution)/shard_map/ppermute | solution.py:409
  15.2 16.2 %copy-start.1 = (bf16[32,64,384]{2,1,0:T(8,128)(2,1)S(1)}, bf16[32,64,384]{2,1,0:T(8,128)(2,1)}, u32[]{:S(2)}) copy-start(bf16[32,64,384]{2,1,0:T(8,128)(2,1)} %x_ref.7) | copy-start | bytes 4718596
  15.2 16.2 %copy-start.3 = (bf16[32,32]{1,0:T(8,128)(2,1)S(1)}, bf16[32,32]{1,0:T(8,128)(2,1)}, u32[]{:S(2)}) copy-start(bf16[32,32]{1,0:T(8,128)(2,1)} %blend_ref.1) | copy-start | bytes 6148
  25.7 22.4 %all-to-all-start = ((bf16[16,3,48,128]{3,2,1,0:T(8,128)(2,1)}), bf16[16,3,48,128]{3,2,1,0:T(8,128)(2,1)S(1)}, u32[]{:S(2)}, u32[]{:S(2)}) async-start(bf16[16,3,48,128]{3,2,1,0:T(8,128)(2,1)} %broadcast_select_fusion), calls=%async_computation | async-start | bytes 1179648 | tf_op jit(solution)/shard_map/all_to_all | solution.py:412
  31.4 0.7 copy-start.4
  32.1 16.0 %copy-start.5 = (s32[1024]{0:T(1024)S(1)}, s32[1024]{0:T(1024)}, u32[]{:S(2)}) copy-start(s32[1024]{0:T(1024)} %halo_ref.3) | copy-start | bytes 12292
  32.1 16.0 %copy-start.6 = (s32[96]{0:T(128)S(1)}, s32[96]{0:T(128)}, u32[]{:S(2)}) copy-start(s32[96]{0:T(128)} %shift_ref.1) | copy-start | bytes 1156
  41.0 1.1 %copy-start.8 = (bf16[32,64,384]{2,1,0:T(8,128)(2,1)}, bf16[32,64,384]{2,1,0:T(8,128)(2,1)S(1)}, u32[]{:S(2)}) copy-start(bf16[32,64,384]{2,1,0:T(8,128)(2,1)S(1)} %get-tuple-element.32.own_ref) | copy-start | bytes 4718596
  42.2 0.6 copy-start.10
  42.8 7.6 %collective-permute-start.3 = (bf16[32,32,384]{2,1,0:T(8,128)(2,1)}, bf16[32,32,384]{2,1,0:T(8,128)(2,1)S(1)}, u32[]{:S(2)}, u32[]{:S(2)}) collective-permute-start(bf16[32,32,384]{2,1,0:T(8,128)(2,1)} %get-tuple-element.28), channel_id=1, source_target_pairs={{0,16},{16,0},{32,48},{48,32},{64,80},{80,64},{96,112},{112,96},{1... | collective-permute-start | bytes 2359304 | tf_op jit(solution)/shard_map/ppermute | solution.py:419
  43.6 17.3 %collective-permute-start.4 = (bf16[32,32,384]{2,1,0:T(8,128)(2,1)}, bf16[32,32,384]{2,1,0:T(8,128)(2,1)S(1)}, u32[]{:S(2)}, u32[]{:S(2)}) collective-permute-start(bf16[32,32,384]{2,1,0:T(8,128)(2,1)} %get-tuple-element.29), channel_id=1, source_target_pairs={{16,32},{32,16},{48,64},{64,48},{80,96},{96,80},{112,128},{128,112... | collective-permute-start | bytes 2359304 | tf_op jit(solution)/shard_map/ppermute | solution.py:416
  60.9 24.0 %all-to-all-start.1 = ((bf16[16,3,48,128]{3,2,1,0:T(8,128)(2,1)}), bf16[16,3,48,128]{3,2,1,0:T(8,128)(2,1)S(1)}, u32[]{:S(2)}, u32[]{:S(2)}) async-start(bf16[16,3,48,128]{3,2,1,0:T(8,128)(2,1)} %smooth_and_turn_polar_circles.1), calls=%async_computation.1 | async-start | bytes 1179648 | tf_op jit(solution)/shard_map/all_to_all | solution.py:422
  68.7 1.4 %copy-start.9 = (bf16[32,64,384]{2,1,0:T(8,128)(2,1)S(1)}, bf16[32,64,384]{2,1,0:T(8,128)(2,1)}, u32[]{:S(2)}) copy-start(bf16[32,64,384]{2,1,0:T(8,128)(2,1)} %copy-done.8) | copy-start | bytes 4718596
  70.1 15.5 %copy-start.11 = (bf16[256,256]{1,0:T(8,128)(2,1)S(1)}, bf16[256,256]{1,0:T(8,128)(2,1)}, u32[]{:S(2)}) copy-start(bf16[256,256]{1,0:T(8,128)(2,1)} %copy-done.10) | copy-start | bytes 393220
  72.6 1.6 %copy-start.7 = (f32[32,64,384]{2,1,0:T(8,128)}, f32[32,64,384]{2,1,0:T(8,128)S(1)}, u32[]{:S(2)}) copy-start(f32[32,64,384]{2,1,0:T(8,128)S(1)} %get-tuple-element.38.lat_ref) | copy-start | bytes 9437188
  85.0 0.7 collective-permute-start.5

commit v5 on v4

--- a/solution.py
+++ b/solution.py
@@ -335,7 +335,7 @@
             rows,
             rows,
         ],
-        flops=1 << 32,
+        flops=1 << 36,
         moved=16 << 20,
         mib=20,
     )
@@ -366,7 +366,7 @@
         [place, polar_rows],
         [near, own, far, weight],
         [pltpu.VMEM((polar, frame_rows), F32)],
-        flops=1 << 30,
+        flops=1 << 36,
         moved=8 << 20,
     )
 
@@ -408,7 +408,7 @@
     far = lax.ppermute(far, "sector", [(i, (i + 1 if i % 2 else i - 1) % sectors) for i in range(sectors)])
     near = lax.ppermute(near, "sector", [(i, i ^ 1) for i in range(sectors)])
     inner = (zone_id == 1) | (zone_id == last - 1)
-    parts, near, far = lax.optimization_barrier((jnp.where(inner, given, kept), near, far))
+    parts = jnp.where(inner, given, kept)
     circles = lax.all_to_all(parts, "sector", 0, 0, tiled=True)
     lon_smooth, near_rows, far_rows, lat_weight, mix = smooth_lon(
         place, lon_halo, kernel, near, far, lat_reach[:, None], blend
@@ -418,7 +418,6 @@
     )
     near_rows = lax.ppermute(near_rows, "zone", [(i, i ^ 1) for i in range(zones)])
     turned = hold(place, polar_rows, polar_shift, lon_halo, circles, lat_weight)
-    turned, near_rows, far_rows = lax.optimization_barrier((turned, near_rows, far_rows))
     mine = lax.all_to_all(turned, "sector", 0, 0, tiled=True)
     lat, polar_weight = smooth_lat(place, polar_rows, near_rows, lon_smooth, far_rows, lat_weight)
     mine, lat = lax.optimization_barrier((mine, lat))

time: 91.6 us -> 77.4 us (0.84)
  the two profiles are of different devices: /device:TPU:7 before, /device:TPU:1 now
where the time goes in v5:
time: 77.4 us; the launch traced here: 76.9 us
  starting transfers between devices  25.6 us (33%)
  Pallas kernels  25.4 us (33%)
  waiting for transfers between devices  17.8 us (23%)
  local copies, waits for them, and re-layouts  5.73 us (7%)
  other arithmetic  2.11 us (3%)
    pallas_call x7, Pallas kernels, call(): pl.pallas_call(kernel, out_shape=out_shape, in_specs=[smem] * len(scalars...  25.4 us
    all_to_all x1, waiting for transfers between devices, per_device(): mine = lax.all_to_all(turned, 'sector', 0, 0, tiled=True)  8.87 us
    ppermute x1, starting transfers between devices, per_device(): lax.ppermute(far, 'sector', [(i, (i + 1 if i % 2 else i - 1) % sectors) f...  7.5 us
    unnamed x20, local copies, waits for them, and re-layouts  5.63 us
    all_to_all x1, starting transfers between devices, per_device(): mine = lax.all_to_all(turned, 'sector', 0, 0, tiled=True)  5.08 us
    ppermute x1, waiting for transfers between devices, per_device(): near = lax.ppermute(near, 'sector', [(i, i ^ 1) for i in range(sectors)])  4.22 us
    all_to_all x1, starting transfers between devices, per_device(): circles = lax.all_to_all(parts, 'sector', 0, 0, tiled=True)  4.17 us
    ppermute x1, starting transfers between devices, per_device(): lax.ppermute(mine, 'zone', [(0, 1), (1, 0), (last, last - 1), (last - 1,...  3.89 us
  transfers between devices with their start and end apart: 8, of which 4 were waited for; matrix products, arithmetic and copies ran while one was open for 3% of the time, Pallas kernels for 21%

profile of v5, /device:TPU:1, one launch (start us, length us, event | category | flops | bytes accessed | tf_op | source)
XLA Modules:
  0.0 76.9 jit_solution(12934523380114783146)
XLA Ops:
  0.0 0.0 copy-start.2
  0.0 0.1 pad_add_fusion.place_ref
  0.1 0.0 copy-start
  0.1 1.4 %copy-done = bf16[32,64,384]{2,1,0:T(8,128)(2,1)S(1)} copy-done((bf16[32,64,384]{2,1,0:T(8,128)(2,1)S(1)}, bf16[32,64,384]{2,1,0:T(8,128)(2,1)}, u32[]{:S(2)}) %copy-start) | copy-done | bytes 1572888
  1.5 1.8 %cut_edges.1 = (bf16[1024,128]{1,0:T(8,128)(2,1)}, bf16[1024,128]{1,0:T(8,128)(2,1)S(1)}) custom-call(s32[2]{0:T(128)S(1)} %pad_add_fusion.place_ref, bf16[32,64,384]{2,1,0:T(8,128)(2,1)S(1)} %copy-done), custom_call_target="tpu_custom_call" | custom-call | bytes 4194304 | tf_op jit(solution)/shard_map/cut_edges/pallas_call | solution.py:277
  3.3 0.0 copy-done.2
  3.3 1.9 %pack_half_of_shells.1.given_ref = bf16[16,3,48,128]{3,2,1,0:T(8,128)(2,1)S(1)} custom-call(s32[2]{0:T(128)S(1)} %pad_add_fusion.place_ref, s32[96]{0:T(128)S(1)} %copy-done.2, bf16[32,64,384]{2,1,0:T(8,128)(2,1)S(1)} %copy-done, bf16[1024,128]{1,0:T(8,128)(2,1)S(1)} %get-tuple-element.16.far_ref), custom_call_target="tpu_custom_call" | custom-call | bytes 4194304 | tf_op jit(solution)/shard_map/pack_half_of_shells/pallas_call | solution.py:277
  5.2 0.0 copy-start.9
  5.2 1.3 %collective-permute-start = (bf16[16,3,48,128]{3,2,1,0:T(8,128)(2,1)S(1)}, bf16[16,3,48,128]{3,2,1,0:T(8,128)(2,1)}, u32[]{:S(2)}, u32[]{:S(2)}) collective-permute-start(bf16[16,3,48,128]{3,2,1,0:T(8,128)(2,1)S(1)} %pack_half_of_shells.1.given_ref), channel_id=1, source_target_pairs={{0,16},{240,224},{1,17},{241,225},{2,18},{242,226},{3,19},{243,227... | collective-permute-start | bytes 1769480 | tf_op jit(solution)/shard_map/ppermute | solution.py:407
  6.5 7.5 %collective-permute-start.2 = (bf16[1024,128]{1,0:T(8,128)(2,1)S(1)}, bf16[1024,128]{1,0:T(8,128)(2,1)S(1)}, u32[]{:S(2)}, u32[]{:S(2)}) collective-permute-start(bf16[1024,128]{1,0:T(8,128)(2,1)S(1)} %get-tuple-element.16.far_ref), channel_id=1, source_target_pairs={{0,15},{1,2},{2,1},{3,4},{4,3},{5,6},{6,5},{7,8},{8,7},{9,10},{10,... | collective-permute-start | bytes 786440 | tf_op jit(solution)/shard_map/ppermute | solution.py:408
  14.0 0.0 collective-permute-start.1
  14.0 1.9 %pack_other_half_of_shells.1 = bf16[16,3,48,128]{3,2,1,0:T(8,128)(2,1)S(1)} custom-call(s32[2]{0:T(128)S(1)} %pad_add_fusion.place_ref, s32[96]{0:T(128)S(1)} %copy-done.2, bf16[32,64,384]{2,1,0:T(8,128)(2,1)S(1)} %copy-done, bf16[16,3,48,128]{3,2,1,0:T(8,128)(2,1)S(1)} %pack_half_of_shells.1.given_ref), custom_call_target="tpu_custom_call" | custom-call | bytes 4194304 | tf_op jit(solution)/shard_map/pack_other_half_of_shells/pallas_call | solution.py:277
  15.9 0.0 copy-start.1
  15.9 0.0 copy-start.3
  15.9 0.0 copy-start.4
  16.0 0.0 copy-done.9
  16.0 0.1 copy.7.reach_ref
  16.1 0.0 collective-permute-done
  16.1 2.0 %broadcast_select_fusion = bf16[16,3,48,128]{3,2,1,0:T(8,128)(2,1)} fusion(bf16[16,3,48,128]{3,2,1,0:T(8,128)(2,1)} %collective-permute-done, bf16[16,3,48,128]{3,2,1,0:T(8,128)(2,1)S(1)} %pack_other_half_of_shells.1, pred[]{:T(512)S(6)} %or.3), kind=kLoop, calls=%fused_computation | loop fusion | flops 294912 | bytes 1769473 | tf_op jit(solution)/shard_map/jit(_where)/select_n | solution.py:411
  18.1 4.2 %all-to-all-start = ((bf16[16,3,48,128]{3,2,1,0:T(8,128)(2,1)}), bf16[16,3,48,128]{3,2,1,0:T(8,128)(2,1)S(1)}, u32[]{:S(2)}, u32[]{:S(2)}) async-start(bf16[16,3,48,128]{3,2,1,0:T(8,128)(2,1)} %broadcast_select_fusion), calls=%async_computation | async-start | bytes 1179648 | tf_op jit(solution)/shard_map/all_to_all | solution.py:412
  22.3 0.0 copy-start.5
  22.3 0.0 collective-permute-done.2.far_ref
  22.3 4.2 %collective-permute-done.1.near_ref = bf16[1024,128]{1,0:T(8,128)(2,1)} collective-permute-done((bf16[1024,128]{1,0:T(8,128)(2,1)}, bf16[1024,128]{1,0:T(8,128)(2,1)}, u32[]{:S(2)}, u32[]{:S(2)}) %collective-permute-start.1) | collective-permute-done | bytes 262176 | tf_op jit(solution)/shard_map/ppermute | solution.py:409
  26.5 0.0 copy-done.1
  26.5 0.0 copy-done.3
  26.5 0.0 copy-done.4
  26.5 9.1 %smooth_along_longitude.1 = (bf16[32,64,384]{2,1,0:T(8,128)(2,1)S(1)}, bf16[32,32,384]{2,1,0:T(8,128)(2,1)}, bf16[32,32,384]{2,1,0:T(8,128)(2,1)S(1)}, bf16[64,128]{1,0:T(8,128)(2,1)S(1)}, bf16[256,256]{1,0:T(8,128)(2,1)S(1)}) custom-call(s32[2]{0:T(128)S(1)} %pad_add_fusion.place_ref, s32[1024]{0:T(1024)S(1)} %copy-done.4, ...), custom_call_target="tpu_custom_call" | custom-call | flops 68719476736 | bytes 16777216 | tf_op jit(solution)/shard_map/smooth_along_longitude/pallas_call | solution.py:277
  35.6 0.0 copy-start.7
  35.6 1.1 %copy-done.7 = bf16[32,64,384]{2,1,0:T(8,128)(2,1)} copy-done((bf16[32,64,384]{2,1,0:T(8,128)(2,1)}, bf16[32,64,384]{2,1,0:T(8,128)(2,1)S(1)}, u32[]{:S(2)}) %copy-start.7) | copy-done | bytes 1572888
  36.8 0.6 collective-permute-start.3
  37.3 3.1 %collective-permute-start.4 = (bf16[32,32,384]{2,1,0:T(8,128)(2,1)S(1)}, bf16[32,32,384]{2,1,0:T(8,128)(2,1)}, u32[]{:S(2)}, u32[]{:S(2)}) collective-permute-start(bf16[32,32,384]{2,1,0:T(8,128)(2,1)S(1)} %get-tuple-element.21), channel_id=1, source_target_pairs={{16,32},{32,16},{48,64},{64,48},{80,96},{96,80},{112,128},{128,112... | collective-permute-start | bytes 2359304 | tf_op jit(solution)/shard_map/ppermute | solution.py:416
  40.4 0.0 all-to-all-done.x_ref
  40.5 0.0 copy-done.5
  40.5 2.3 %smooth_and_turn_polar_circles.1 = bf16[16,3,48,128]{3,2,1,0:T(8,128)(2,1)} custom-call(s32[2]{0:T(128)S(1)} %pad_add_fusion.place_ref, s32[96]{0:T(128)S(1)} %copy-done.2, s32[96]{0:T(128)S(1)} %copy-done.5, s32[1024]{0:T(1024)S(1)} %copy-done.4, bf16[16,3,48,128]{3,2,1,0:T(8,128)(2,1)S(1)} %all-to-all-done.x_ref, ...), custom_call_target="tpu_custom_call" | custom-call | flops 1073741824 | bytes 4194304 | tf_op jit(solution)/shard_map/smooth_and_turn_polar_circles/pallas_call | solution.py:277
  42.8 5.1 %all-to-all-start.1 = ((bf16[16,3,48,128]{3,2,1,0:T(8,128)(2,1)}), bf16[16,3,48,128]{3,2,1,0:T(8,128)(2,1)S(1)}, u32[]{:S(2)}, u32[]{:S(2)}) async-start(bf16[16,3,48,128]{3,2,1,0:T(8,128)(2,1)} %smooth_and_turn_polar_circles.1), calls=%async_computation.1 | async-start | bytes 1179648 | tf_op jit(solution)/shard_map/all_to_all | solution.py:421
  47.8 0.0 collective-permute-done.3.near_ref
  47.8 3.1 %collective-permute-done.4.far_ref = bf16[32,32,384]{2,1,0:T(8,128)(2,1)} collective-permute-done((bf16[32,32,384]{2,1,0:T(8,128)(2,1)S(1)}, bf16[32,32,384]{2,1,0:T(8,128)(2,1)}, u32[]{:S(2)}, u32[]{:S(2)}) %collective-permute-start.4) | collective-permute-done | bytes 786464 | tf_op jit(solution)/shard_map/ppermute | solution.py:416
  50.9 0.0 copy-start.8
  50.9 1.4 %copy-done.8 = bf16[32,64,384]{2,1,0:T(8,128)(2,1)S(1)} copy-done((bf16[32,64,384]{2,1,0:T(8,128)(2,1)S(1)}, bf16[32,64,384]{2,1,0:T(8,128)(2,1)}, u32[]{:S(2)}) %copy-start.8) | copy-done | bytes 1572888
  52.3 3.0 %smooth_along_latitude.1 = (f32[32,64,384]{2,1,0:T(8,128)S(1)}, bf16[64,48]{1,0:T(8,128)(2,1)S(1)}) custom-call(s32[2]{0:T(128)S(1)} %pad_add_fusion.place_ref, s32[96]{0:T(128)S(1)} %copy-done.2, bf16[32,32,384]{2,1,0:T(8,128)(2,1)S(1)} %collective-permute-done.3.near_ref, bf16[32,64,384]{2,1,0:T(8,128)(2,1)S(1)} %copy-done.8, ...), custom_call_target="tpu_custom_call" | custom-call | flops 68719476736 | bytes 8388608 | tf_op jit(solution)/shard_map/smooth_along_latitude/pallas_call | solution.py:277
  55.4 0.0 copy-start.6
  55.4 1.6 %copy-done.6 = f32[32,64,384]{2,1,0:T(8,128)} copy-done((f32[32,64,384]{2,1,0:T(8,128)}, f32[32,64,384]{2,1,0:T(8,128)S(1)}, u32[]{:S(2)}) %copy-start.6) | copy-done | bytes 3145752
  57.0 8.9 %all-to-all-done.1.mine_ref = bf16[16,3,48,128]{3,2,1,0:T(8,128)(2,1)S(1)} async-done(((bf16[16,3,48,128]{3,2,1,0:T(8,128)(2,1)}), bf16[16,3,48,128]{3,2,1,0:T(8,128)(2,1)S(1)}, u32[]{:S(2)}, u32[]{:S(2)}) %all-to-all-start.1) | async-done | bytes 589856 | tf_op jit(solution)/shard_map/all_to_all | solution.py:421
  65.9 3.9 %collective-permute-start.5 = (bf16[16,3,48,128]{3,2,1,0:T(8,128)(2,1)S(1)}, bf16[16,3,48,128]{3,2,1,0:T(8,128)(2,1)S(1)}, u32[]{:S(2)}, u32[]{:S(2)}) collective-permute-start(bf16[16,3,48,128]{3,2,1,0:T(8,128)(2,1)S(1)} %all-to-all-done.1.mine_ref), channel_id=1, source_target_pairs={{0,16},{16,0},{240,224},{224,240},{1,17},{17,1},{241,225},{225,241... | collective-permute-start | bytes 1769480 | tf_op jit(solution)/shard_map/ppermute | solution.py:424
  69.8 1.6 %collective-permute-done.5.other_ref = bf16[16,3,48,128]{3,2,1,0:T(8,128)(2,1)S(1)} collective-permute-done((bf16[16,3,48,128]{3,2,1,0:T(8,128)(2,1)S(1)}, bf16[16,3,48,128]{3,2,1,0:T(8,128)(2,1)S(1)}, u32[]{:S(2)}, u32[]{:S(2)}) %collective-permute-start.5) | collective-permute-done | bytes 589856 | tf_op jit(solution)/shard_map/ppermute | solution.py:424
  71.4 5.4 %add_polar_rows_and_blend.1 = bf16[32,64,384]{2,1,0:T(8,128)(2,1)} custom-call(s32[2]{0:T(128)S(1)} %pad_add_fusion.place_ref, bf16[16,3,48,128]{3,2,1,0:T(8,128)(2,1)S(1)} %all-to-all-done.1.mine_ref, bf16[16,3,48,128]{3,2,1,0:T(8,128)(2,1)S(1)} %collective-permute-done.5.other_ref, bf16[64,48]{1,0:T(8,128)(2,1)S(1)} %get-tuple-element.24.polar_weight_ref, ...), custom_call_target="tpu_custom_call" | custom-call | flops 2147483648 | bytes 8388608 | tf_op jit(solution)/shard_map/add_polar_rows_and_blend/pallas_call | solution.py:277
Async XLA Ops:
  0.0 3.3 %copy-start.2 = (s32[96]{0:T(128)S(1)}, s32[96]{0:T(128)}, u32[]{:S(2)}) copy-start(s32[96]{0:T(128)} %rows_ref.7) | copy-start | bytes 1156
  0.1 1.4 %copy-start = (bf16[32,64,384]{2,1,0:T(8,128)(2,1)S(1)}, bf16[32,64,384]{2,1,0:T(8,128)(2,1)}, u32[]{:S(2)}) copy-start(bf16[32,64,384]{2,1,0:T(8,128)(2,1)} %x_ref.7) | copy-start | bytes 4718596
  5.2 10.7 %copy-start.9 = (s32[64]{0:T(128)S(1)}, s32[64]{0:T(128)}, u32[]{:S(2)}) copy-start(s32[64]{0:T(128)} %param.8) | copy-start | bytes 772
  5.2 10.8 %collective-permute-start = (bf16[16,3,48,128]{3,2,1,0:T(8,128)(2,1)S(1)}, bf16[16,3,48,128]{3,2,1,0:T(8,128)(2,1)}, u32[]{:S(2)}, u32[]{:S(2)}) collective-permute-start(bf16[16,3,48,128]{3,2,1,0:T(8,128)(2,1)S(1)} %pack_half_of_shells.1.given_ref), channel_id=1, source_target_pairs={{0,16},{240,224},{1,17},{241,225},{2,18},{242,226},{3,19},{243,227... | collective-permute-start | bytes 1769480 | tf_op jit(solution)/shard_map/ppermute | solution.py:407
  6.5 15.8 %collective-permute-start.2 = (bf16[1024,128]{1,0:T(8,128)(2,1)S(1)}, bf16[1024,128]{1,0:T(8,128)(2,1)S(1)}, u32[]{:S(2)}, u32[]{:S(2)}) collective-permute-start(bf16[1024,128]{1,0:T(8,128)(2,1)S(1)} %get-tuple-element.16.far_ref), channel_id=1, source_target_pairs={{0,15},{1,2},{2,1},{3,4},{4,3},{5,6},{6,5},{7,8},{8,7},{9,10},{10,... | collective-permute-start | bytes 786440 | tf_op jit(solution)/shard_map/ppermute | solution.py:408
  14.0 12.5 %collective-permute-start.1 = (bf16[1024,128]{1,0:T(8,128)(2,1)}, bf16[1024,128]{1,0:T(8,128)(2,1)}, u32[]{:S(2)}, u32[]{:S(2)}) collective-permute-start(bf16[1024,128]{1,0:T(8,128)(2,1)} %get-tuple-element.17), channel_id=1, source_target_pairs={{0,1},{1,0},{2,3},{3,2},{4,5},{5,4},{6,7},{7,6},{8,9},{9,8},{10,11... | collective-permute-start | bytes 786440 | tf_op jit(solution)/shard_map/ppermute | solution.py:409
  15.9 10.6 %copy-start.1 = (bf16[32,64,384]{2,1,0:T(8,128)(2,1)S(1)}, bf16[32,64,384]{2,1,0:T(8,128)(2,1)}, u32[]{:S(2)}) copy-start(bf16[32,64,384]{2,1,0:T(8,128)(2,1)} %x_ref.7) | copy-start | bytes 4718596
  15.9 10.6 %copy-start.3 = (bf16[32,32]{1,0:T(8,128)(2,1)S(1)}, bf16[32,32]{1,0:T(8,128)(2,1)}, u32[]{:S(2)}) copy-start(bf16[32,32]{1,0:T(8,128)(2,1)} %blend_ref.1) | copy-start | bytes 6148
  15.9 10.6 %copy-start.4 = (s32[1024]{0:T(1024)S(1)}, s32[1024]{0:T(1024)}, u32[]{:S(2)}) copy-start(s32[1024]{0:T(1024)} %halo_ref.3) | copy-start | bytes 12292
  18.1 22.3 %all-to-all-start = ((bf16[16,3,48,128]{3,2,1,0:T(8,128)(2,1)}), bf16[16,3,48,128]{3,2,1,0:T(8,128)(2,1)S(1)}, u32[]{:S(2)}, u32[]{:S(2)}) async-start(bf16[16,3,48,128]{3,2,1,0:T(8,128)(2,1)} %broadcast_select_fusion), calls=%async_computation | async-start | bytes 1179648 | tf_op jit(solution)/shard_map/all_to_all | solution.py:412
  22.3 18.2 %copy-start.5 = (s32[96]{0:T(128)S(1)}, s32[96]{0:T(128)}, u32[]{:S(2)}) copy-start(s32[96]{0:T(128)} %shift_ref.1) | copy-start | bytes 1156
  35.6 1.1 %copy-start.7 = (bf16[32,64,384]{2,1,0:T(8,128)(2,1)}, bf16[32,64,384]{2,1,0:T(8,128)(2,1)S(1)}, u32[]{:S(2)}) copy-start(bf16[32,64,384]{2,1,0:T(8,128)(2,1)S(1)} %get-tuple-element.20.own_ref) | copy-start | bytes 4718596
  36.8 11.1 %collective-permute-start.3 = (bf16[32,32,384]{2,1,0:T(8,128)(2,1)}, bf16[32,32,384]{2,1,0:T(8,128)(2,1)S(1)}, u32[]{:S(2)}, u32[]{:S(2)}) collective-permute-start(bf16[32,32,384]{2,1,0:T(8,128)(2,1)} %get-tuple-element.19), channel_id=1, source_target_pairs={{0,16},{16,0},{32,48},{48,32},{64,80},{80,64},{96,112},{112,96},{1... | collective-permute-start | bytes 2359304 | tf_op jit(solution)/shard_map/ppermute | solution.py:419
  37.3 13.6 %collective-permute-start.4 = (bf16[32,32,384]{2,1,0:T(8,128)(2,1)S(1)}, bf16[32,32,384]{2,1,0:T(8,128)(2,1)}, u32[]{:S(2)}, u32[]{:S(2)}) collective-permute-start(bf16[32,32,384]{2,1,0:T(8,128)(2,1)S(1)} %get-tuple-element.21), channel_id=1, source_target_pairs={{16,32},{32,16},{48,64},{64,48},{80,96},{96,80},{112,128},{128,112... | collective-permute-start | bytes 2359304 | tf_op jit(solution)/shard_map/ppermute | solution.py:416
  42.8 23.2 %all-to-all-start.1 = ((bf16[16,3,48,128]{3,2,1,0:T(8,128)(2,1)}), bf16[16,3,48,128]{3,2,1,0:T(8,128)(2,1)S(1)}, u32[]{:S(2)}, u32[]{:S(2)}) async-start(bf16[16,3,48,128]{3,2,1,0:T(8,128)(2,1)} %smooth_and_turn_polar_circles.1), calls=%async_computation.1 | async-start | bytes 1179648 | tf_op jit(solution)/shard_map/all_to_all | solution.py:421
  50.9 1.4 %copy-start.8 = (bf16[32,64,384]{2,1,0:T(8,128)(2,1)S(1)}, bf16[32,64,384]{2,1,0:T(8,128)(2,1)}, u32[]{:S(2)}) copy-start(bf16[32,64,384]{2,1,0:T(8,128)(2,1)} %copy-done.7) | copy-start | bytes 4718596
  55.4 1.6 %copy-start.6 = (f32[32,64,384]{2,1,0:T(8,128)}, f32[32,64,384]{2,1,0:T(8,128)S(1)}, u32[]{:S(2)}) copy-start(f32[32,64,384]{2,1,0:T(8,128)S(1)} %get-tuple-element.26.lat_ref) | copy-start | bytes 9437188
  65.9 5.5 %collective-permute-start.5 = (bf16[16,3,48,128]{3,2,1,0:T(8,128)(2,1)S(1)}, bf16[16,3,48,128]{3,2,1,0:T(8,128)(2,1)S(1)}, u32[]{:S(2)}, u32[]{:S(2)}) collective-permute-start(bf16[16,3,48,128]{3,2,1,0:T(8,128)(2,1)S(1)} %all-to-all-done.1.mine_ref), channel_id=1, source_target_pairs={{0,16},{16,0},{240,224},{224,240},{1,17},{17,1},{241,225},{225,241... | collective-permute-start | bytes 1769480 | tf_op jit(solution)/shard_map/ppermute | solution.py:424

commit v6 on v5

--- a/solution.py
+++ b/solution.py
@@ -18,7 +18,7 @@
     return lax.broadcasted_iota(jnp.int32, (rows, LANES), 1)
 
 
-def edge_kernel(place_ref, x_ref, near_ref, far_ref, tile_ref, sems):
+def edge_kernel(x_ref, near_ref, far_ref, tile_ref, sems):
     shells, row_count, col_count = x_ref.shape
     half = shells // 2
     size = half * row_count
@@ -33,7 +33,7 @@
     def part(e, shell):
         return tile_ref[e, shell : shell + half].reshape(size, LANES).astype(F32)
 
-    even = lax.rem(place_ref[1], 2) == 0
+    even = lax.rem(lax.axis_index("sector"), 2) == 0
     copies[0].wait()
     low = jnp.where(lane < HMAX, part(0, 0), pltpu.roll(part(0, half), HMAX, 1))
     copies[1].wait()
@@ -42,10 +42,10 @@
     far_ref[...] = jnp.where(even, low, high).astype(BF16)
 
 
-def write_polar(half, place_ref, rows_ref, x_ref, send_ref, wide_ref):
+def write_polar(half, rows_ref, x_ref, send_ref, wide_ref):
     _, row_count, col_count = x_ref.shape
     tiles = col_count // LANES
-    zone = place_ref[0]
+    zone = lax.axis_index("zone")
     for t in range(tiles):
         wide_ref[t] = (
             x_ref[half * PART : (half + 1) * PART, :, t * LANES : (t + 1) * LANES]
@@ -62,12 +62,12 @@
                 send_ref[k, r, t * PART : (t + 1) * PART, :] = values.astype(BF16)
 
 
-def first_kernel(place_ref, rows_ref, x_ref, far_ref, send_ref, wide_ref):
-    write_polar(1, place_ref, rows_ref, x_ref, send_ref, wide_ref)
-
-
-def second_kernel(place_ref, rows_ref, x_ref, given_ref, send_ref, wide_ref):
-    write_polar(0, place_ref, rows_ref, x_ref, send_ref, wide_ref)
+def first_kernel(rows_ref, x_ref, far_ref, send_ref, wide_ref):
+    write_polar(1, rows_ref, x_ref, send_ref, wide_ref)
+
+
+def second_kernel(rows_ref, x_ref, given_ref, send_ref, wide_ref):
+    write_polar(0, rows_ref, x_ref, send_ref, wide_ref)
 
 
 def band_terms(half_f):
@@ -77,18 +77,18 @@
     return rate, jnp.broadcast_to(1.0 / jnp.sum(terms, axis=1, keepdims=True), half_f.shape)
 
 
-def lon_kernel(place_ref, halo_ref, x_ref, near_ref, far_ref, reach_ref, blend_ref,
-               out_ref, near_rows_ref, far_rows_ref, weight_ref, mix_ref, wide_ref, done_ref, half_ref, rate_ref, scale_ref):
+def lon_kernel(halo_ref, x_ref, near_ref, far_ref,
+               out_ref, near_rows_ref, far_rows_ref, wide_ref, done_ref, half_ref, rate_ref, scale_ref):
     shells, row_count, col_count = x_ref.shape
     total = shells * row_count
     size = total // 2
     tiles = col_count // LANES
-    zone = place_ref[0]
+    zone = lax.axis_index("zone")
     for i in range(row_count):
         half_ref[i : i + 1, :] = jnp.full((1, LANES), halo_ref[zone * row_count + i], jnp.int32).astype(F32)
     rate_ref[...], scale_ref[...] = band_terms(half_ref[...])
     lane = lanes_of(size)
-    even = lax.rem(place_ref[1], 2) == 0
+    even = lax.rem(lax.axis_index("sector"), 2) == 0
     near = near_ref[...].astype(F32)
     far = far_ref[...].astype(F32)
     before = jnp.where(even, far, near)
@@ -132,16 +132,59 @@
     last = row_count - LMAX
     near_rows_ref[...] = out_ref[:, pl.ds(pl.multiple_of((1 - odd) * last, LMAX), LMAX), :]
     far_rows_ref[...] = out_ref[:, pl.ds(pl.multiple_of(odd * last, LMAX), LMAX), :]
-    frame_rows = weight_ref.shape[1]
+
+
+def hold_kernel(table_ref, x_ref, after_ref, out_ref, circle_ref):
+    sectors, held, block, _ = x_ref.shape
+    zone, sector = lax.axis_index("zone"), lax.axis_index("sector")
+    polar = 2 * sectors * held
+    cap = jnp.where(zone < 8, 0, sectors * held)
+    length = sectors * block
+    full_lon = length // PART * LANES
+    depth = 3 * LANES
+    for r in range(held):
+        for copy in range(2):
+            circle_ref[r, copy * length : (copy + 1) * length, :] = x_ref[:, r].reshape(length, LANES)
+        circle_ref[r, 2 * length : 2 * length + 2 * PART, :] = circle_ref[r, 0 : 2 * PART, :]
+    for r in range(held):
+        entry = cap + sector * held + r
+        half_f = jnp.full((1, LANES), table_ref[2 * polar + table_ref[entry]], jnp.int32).astype(F32)
+        rate, scale = band_terms(half_f)
+        start = lax.rem(2 * full_lon - table_ref[polar + entry] - HMAX, full_lon)
+        first = start // LANES
+        rest = start - first * LANES
+        offset = (
+            lanes_of(depth) - lax.broadcasted_iota(jnp.int32, (depth, LANES), 0) + (rest + HMAX)
+        ).astype(F32)
+        band = jnp.where(jnp.abs(offset) <= half_f, jnp.exp(-rate * (offset * offset)), 0.0) * scale
+        values = jnp.concatenate(
+            [circle_ref[r, pl.ds(pl.multiple_of((first + u) * PART, PART), length), :] for u in range(3)], axis=1
+        )
+        result = jnp.dot(values, band.astype(BF16), preferred_element_type=F32)
+        out_ref[:, r] = result.astype(BF16).reshape(sectors, block, LANES)
+
+
+def lat_kernel(rows_ref, near_ref, own_ref, far_ref, reach_ref, blend_ref,
+               out_ref, polar_weight_ref, mix_ref, pick_ref):
+    shells, row_count, col_count = own_ref.shape
+    frame_rows = row_count + 2 * LMAX
+    polar = pick_ref.shape[0]
+    zone = lax.axis_index("zone")
+    cap = jnp.where(zone < 8, 0, polar)
+    lane = lanes_of(1)
+    for p in range(polar):
+        pick_ref[p : p + 1, :] = (lane == rows_ref[cap + p] - zone * row_count + LMAX).astype(F32)
+    pick = pick_ref[...]
+    zones = lax.axis_size("zone")
     reach = reach_ref[...]
     column = lax.broadcasted_iota(jnp.int32, (row_count, frame_rows), 1)
     away = column - LMAX - lax.broadcasted_iota(jnp.int32, (row_count, frame_rows), 0)
     source = zone * row_count - LMAX + column
-    valid = (jnp.abs(away) <= reach) & (source >= 0) & (source < halo_ref.shape[0])
+    valid = (jnp.abs(away) <= reach) & (source >= 0) & (source < zones * row_count)
     reach_f = reach.astype(F32)
     away_f = away.astype(F32)
     weights = jnp.where(valid, jnp.exp(-(4.5 / (reach_f * reach_f)) * (away_f * away_f)), 0.0)
-    weight_ref[...] = (weights / jnp.sum(weights, axis=1, keepdims=True)).astype(BF16)
+    weight = (weights / jnp.sum(weights, axis=1, keepdims=True)).astype(BF16)
     length = mix_ref.shape[0]
     group = length // shells
     spread = (
@@ -155,49 +198,6 @@
         == lax.broadcasted_iota(jnp.int32, (length, length), 1) % group
     )
     mix_ref[...] = jnp.where(same, full, 0.0).astype(BF16)
-
-
-def hold_kernel(place_ref, rows_ref, shift_ref, halo_ref, x_ref, after_ref, out_ref, circle_ref):
-    sectors, held, block, _ = x_ref.shape
-    zone, sector = place_ref[0], place_ref[1]
-    cap = jnp.where(zone < 8, 0, sectors * held)
-    length = sectors * block
-    full_lon = length // PART * LANES
-    depth = 3 * LANES
-    for r in range(held):
-        for copy in range(2):
-            circle_ref[r, copy * length : (copy + 1) * length, :] = x_ref[:, r].reshape(length, LANES)
-        circle_ref[r, 2 * length : 2 * length + 2 * PART, :] = circle_ref[r, 0 : 2 * PART, :]
-    for r in range(held):
-        entry = cap + sector * held + r
-        half_f = jnp.full((1, LANES), halo_ref[rows_ref[entry]], jnp.int32).astype(F32)
-        rate, scale = band_terms(half_f)
-        start = lax.rem(2 * full_lon - shift_ref[entry] - HMAX, full_lon)
-        first = start // LANES
-        rest = start - first * LANES
-        offset = (
-            lanes_of(depth) - lax.broadcasted_iota(jnp.int32, (depth, LANES), 0) + (rest + HMAX)
-        ).astype(F32)
-        band = jnp.where(jnp.abs(offset) <= half_f, jnp.exp(-rate * (offset * offset)), 0.0) * scale
-        values = jnp.concatenate(
-            [circle_ref[r, pl.ds(pl.multiple_of((first + u) * PART, PART), length), :] for u in range(3)], axis=1
-        )
-        result = jnp.dot(values, band.astype(BF16), preferred_element_type=F32)
-        out_ref[:, r] = result.astype(BF16).reshape(sectors, block, LANES)
-
-
-def lat_kernel(place_ref, rows_ref, near_ref, own_ref, far_ref, weight_ref,
-               out_ref, polar_weight_ref, pick_ref):
-    shells, row_count, col_count = own_ref.shape
-    frame_rows = weight_ref.shape[1]
-    polar = pick_ref.shape[0]
-    zone = place_ref[0]
-    cap = jnp.where(zone < 8, 0, polar)
-    lane = lanes_of(1)
-    for p in range(polar):
-        pick_ref[p : p + 1, :] = (lane == rows_ref[cap + p] - zone * row_count + LMAX).astype(F32)
-    pick = pick_ref[...]
-    weight = weight_ref[...]
     polar_weight_ref[...] = lax.dot_general(
         weight, pick.astype(BF16), (((1,), (1,)), ((), ())), preferred_element_type=F32
     ).astype(BF16)
@@ -220,7 +220,7 @@
     lax.fori_loop(0, shells // 4, some_shells, 0)
 
 
-def final_kernel(place_ref, mine_ref, other_ref, polar_weight_ref, mix_ref, lat_ref,
+def final_kernel(mine_ref, other_ref, polar_weight_ref, mix_ref, lat_ref,
                  out_ref, polar_ref, sum_ref, stage_ref, sem, sems):
     shells, row_count, col_count = lat_ref.shape
     holders, held = mine_ref.shape[:2]
@@ -228,7 +228,7 @@
     polar = holders * held
     fetch = pltpu.make_async_copy(lat_ref, sum_ref, sem)
     fetch.start()
-    zone = place_ref[0]
+    zone = lax.axis_index("zone")
     outer = (zone == 0) | (zone == 15)
     mine_first = jnp.where(outer, 0, PART * polar)
     for ref, first in ((mine_ref, mine_first), (other_ref, PART * polar - mine_first)):
@@ -289,7 +289,7 @@
 struct = jax.ShapeDtypeStruct
 
 
-def pack(place, polar_rows, kernel, sectors):
+def pack(polar_rows, kernel, sectors):
     shells, row_count, col_count = kernel.shape
     tiles = col_count // LANES
     held = polar_rows.shape[0] // 2 // sectors
@@ -298,21 +298,21 @@
     wide = pltpu.VMEM((tiles, PART * row_count, LANES), F32)
     tile = pltpu.VMEM((2, shells, row_count, LANES), BF16)
     near, far = call(
-        edge_kernel, "cut_edges", (edge, edge), [place], [], [tile, pltpu.SemaphoreType.DMA((2,))],
+        edge_kernel, "cut_edges", (edge, edge), [], [], [tile, pltpu.SemaphoreType.DMA((2,))],
         moved=4 << 20, direct=[kernel],
     )
     given = call(
-        first_kernel, "pack_half_of_shells", send, [place, polar_rows], [kernel], [wide],
+        first_kernel, "pack_half_of_shells", send, [polar_rows], [kernel], [wide],
         moved=4 << 20, direct=[far],
     )
     kept = call(
-        second_kernel, "pack_other_half_of_shells", send, [place, polar_rows], [kernel], [wide],
+        second_kernel, "pack_other_half_of_shells", send, [polar_rows], [kernel], [wide],
         moved=4 << 20, direct=[given],
     )
     return given, kept, near, far
 
 
-def smooth_lon(place, lon_halo, kernel, near, far, reach, blend):
+def smooth_lon(lon_halo, kernel, near, far):
     shells, row_count, col_count = kernel.shape
     tiles = col_count // LANES
     rows = pltpu.VMEM((row_count, LANES), F32)
@@ -323,11 +323,9 @@
             struct((shells, row_count, col_count), BF16),
             struct((shells, LMAX, col_count), BF16),
             struct((shells, LMAX, col_count), BF16),
-            struct((row_count, row_count + 2 * LMAX), BF16),
-            struct((shells * 8, shells * 8), BF16),
         ),
-        [place, lon_halo],
-        [kernel, near, far, reach, blend],
+        [lon_halo],
+        [kernel, near, far],
         [
             pltpu.VMEM((tiles + 1, shells * row_count, LANES), F32),
             pltpu.VMEM((tiles, shells * row_count, LANES), F32),
@@ -341,13 +339,13 @@
     )
 
 
-def hold(place, polar_rows, polar_shift, lon_halo, circles, after):
+def hold(table, circles, after):
     sectors, held, block, _ = circles.shape
     return call(
         hold_kernel,
         "smooth_and_turn_polar_circles",
         struct(circles.shape, BF16),
-        [place, polar_rows, polar_shift, lon_halo],
+        [table],
         [circles],
         [pltpu.VMEM((held, 2 * sectors * block + 2 * PART, LANES), BF16)],
         flops=1 << 30,
@@ -356,29 +354,34 @@
     )
 
 
-def smooth_lat(place, polar_rows, near, own, far, weight):
-    row_count, frame_rows = weight.shape
+def smooth_lat(polar_rows, near, own, far, reach, blend):
+    shells, row_count, _ = own.shape
+    frame_rows = row_count + 2 * LMAX
     polar = polar_rows.shape[0] // 2
     return call(
         lat_kernel,
         "smooth_along_latitude",
-        (struct(own.shape, F32), struct((row_count, polar), BF16)),
-        [place, polar_rows],
-        [near, own, far, weight],
+        (
+            struct(own.shape, F32),
+            struct((row_count, polar), BF16),
+            struct((shells * 8, shells * 8), BF16),
+        ),
+        [polar_rows],
+        [near, own, far, reach, blend],
         [pltpu.VMEM((polar, frame_rows), F32)],
         flops=1 << 36,
         moved=8 << 20,
     )
 
 
-def finish(place, lat, mine, other, polar_weight, mix):
+def finish(lat, mine, other, polar_weight, mix):
     shells, _, col_count = lat.shape
     polar = polar_weight.shape[1]
     return call(
         final_kernel,
         "add_polar_rows_and_blend",
         struct(lat.shape, BF16),
-        [place],
+        [],
         [mine, other, polar_weight, mix],
         [
             pltpu.VMEM((col_count // LANES, shells * polar, LANES), F32),
@@ -399,30 +402,28 @@
     shells, row_count, col_count = kernel.shape
     sectors = lax.axis_size("sector")
     zones = lax.axis_size("zone")
-    zone_id = lax.axis_index("zone").astype(jnp.int32)
-    sector_id = lax.axis_index("sector").astype(jnp.int32)
-    place = jnp.stack([zone_id, sector_id])
+    zone_id = lax.axis_index("zone")
     last = zones - 1
-    packed, kept, near, far = pack(place, polar_rows, kernel, sectors)
+    packed, kept, near, far = pack(polar_rows, kernel, sectors)
     given = lax.ppermute(packed, "zone", [(0, 1), (last, last - 1)])
     far = lax.ppermute(far, "sector", [(i, (i + 1 if i % 2 else i - 1) % sectors) for i in range(sectors)])
     near = lax.ppermute(near, "sector", [(i, i ^ 1) for i in range(sectors)])
     inner = (zone_id == 1) | (zone_id == last - 1)
     parts = jnp.where(inner, given, kept)
     circles = lax.all_to_all(parts, "sector", 0, 0, tiled=True)
-    lon_smooth, near_rows, far_rows, lat_weight, mix = smooth_lon(
-        place, lon_halo, kernel, near, far, lat_reach[:, None], blend
-    )
+    lon_smooth, near_rows, far_rows = smooth_lon(lon_halo, kernel, near, far)
+    turned = hold(jnp.concatenate([polar_rows, polar_shift, lon_halo]), circles, far_rows)
     far_rows = lax.ppermute(
         far_rows, "zone", [(i, i + 1 if i % 2 else i - 1) for i in range(1, zones - 1)]
     )
     near_rows = lax.ppermute(near_rows, "zone", [(i, i ^ 1) for i in range(zones)])
-    turned = hold(place, polar_rows, polar_shift, lon_halo, circles, lat_weight)
     mine = lax.all_to_all(turned, "sector", 0, 0, tiled=True)
-    lat, polar_weight = smooth_lat(place, polar_rows, near_rows, lon_smooth, far_rows, lat_weight)
+    lat, polar_weight, mix = smooth_lat(
+        polar_rows, near_rows, lon_smooth, far_rows, lat_reach[:, None], blend
+    )
     mine, lat = lax.optimization_barrier((mine, lat))
     other = lax.ppermute(mine, "zone", [(0, 1), (1, 0), (last, last - 1), (last - 1, last)])
-    return finish(place, lat, mine, other, polar_weight, mix)
+    return finish(lat, mine, other, polar_weight, mix)
 
 
 def solution(mesh):

time: 77.4 us -> 74.3 us (0.960)
  Pallas kernels: 25.4 us -> 23.2 us
  starting transfers between devices: 25.6 us -> 24.1 us
    pallas_call x7, Pallas kernels: 25.4 us -> 23.2 us  [call(): pl.pallas_call(kernel, out_shape=out_shape, in_specs=[smem] * len(scalars...]
    ppermute x1, starting transfers between devices: 3.89 us -> 2.37 us  [per_device(): lax.ppermute(mine, 'zone', [(0, 1), (1, 0), (last, last - 1), (last - 1,...]
  transfers between devices with their start and end apart: 8 -> 8, of which waited for: 4 -> 4; matrix products, arithmetic and copies ran while one was open for 3% -> 3% of each run, Pallas kernels for 21% -> 22%
where the time goes in v6:
time: 74.3 us; the launch traced here: 73.8 us
  starting transfers between devices  24.1 us (32%)
  Pallas kernels  23.2 us (31%)
  waiting for transfers between devices  18.3 us (25%)
  local copies, waits for them, and re-layouts  5.85 us (8%)
  other arithmetic  2.11 us (3%)
    pallas_call x7, Pallas kernels, call(): pl.pallas_call(kernel, out_shape=out_shape, in_specs=[smem] * len(scalars...  23.2 us
    all_to_all x1, waiting for transfers between devices, per_device(): mine = lax.all_to_all(turned, 'sector', 0, 0, tiled=True)  9.39 us
    ppermute x1, starting transfers between devices, per_device(): lax.ppermute(far, 'sector', [(i, (i + 1 if i % 2 else i - 1) % sectors) f...  7.5 us
    unnamed x20, local copies, waits for them, and re-layouts  5.68 us
    all_to_all x1, starting transfers between devices, per_device(): mine = lax.all_to_all(turned, 'sector', 0, 0, tiled=True)  5.1 us
    ppermute x1, waiting for transfers between devices, per_device(): near = lax.ppermute(near, 'sector', [(i, i ^ 1) for i in range(sectors)])  4.24 us
    all_to_all x1, starting transfers between devices, per_device(): circles = lax.all_to_all(parts, 'sector', 0, 0, tiled=True)  4.18 us
    ppermute x1, waiting for transfers between devices, per_device(): lax.ppermute(far_rows, 'zone', [(i, i + 1 if i % 2 else i - 1) for i in r...  3.1 us
  transfers between devices with their start and end apart: 8, of which 4 were waited for; matrix products, arithmetic and copies ran while one was open for 3% of the time, Pallas kernels for 22%

profile of v6, /device:TPU:1, one launch (start us, length us, event | category | flops | bytes accessed | tf_op | source)
XLA Modules:
  0.0 73.8 jit_solution(2151850807732967949)
XLA Ops:
  0.0 0.0 copy-start
  0.0 1.4 %copy-done = bf16[32,64,384]{2,1,0:T(8,128)(2,1)S(1)} copy-done((bf16[32,64,384]{2,1,0:T(8,128)(2,1)S(1)}, bf16[32,64,384]{2,1,0:T(8,128)(2,1)}, u32[]{:S(2)}) %copy-start) | copy-done | bytes 1572888
  1.4 0.0 copy-start.2
  1.4 0.6 cut_edges.1
  2.0 0.1 copy-done.2
  2.1 1.9 %pack_half_of_shells.1.given_ref = bf16[16,3,48,128]{3,2,1,0:T(8,128)(2,1)S(1)} custom-call(s32[96]{0:T(128)S(1)} %copy-done.2, bf16[32,64,384]{2,1,0:T(8,128)(2,1)S(1)} %copy-done, bf16[1024,128]{1,0:T(8,128)(2,1)S(1)} %get-tuple-element.15.far_ref), custom_call_target="tpu_custom_call" | custom-call | bytes 4194304 | tf_op jit(solution)/shard_map/pack_half_of_shells/pallas_call | solution.py:277
  3.9 1.3 %collective-permute-start = (bf16[16,3,48,128]{3,2,1,0:T(8,128)(2,1)S(1)}, bf16[16,3,48,128]{3,2,1,0:T(8,128)(2,1)}, u32[]{:S(2)}, u32[]{:S(2)}) collective-permute-start(bf16[16,3,48,128]{3,2,1,0:T(8,128)(2,1)S(1)} %pack_half_of_shells.1.given_ref), channel_id=1, source_target_pairs={{0,16},{240,224},{1,17},{241,225},{2,18},{242,226},{3,19},{243,227... | collective-permute-start | bytes 1769480 | tf_op jit(solution)/shard_map/ppermute | solution.py:408
  5.2 7.5 %collective-permute-start.2 = (bf16[1024,128]{1,0:T(8,128)(2,1)S(1)}, bf16[1024,128]{1,0:T(8,128)(2,1)S(1)}, u32[]{:S(2)}, u32[]{:S(2)}) collective-permute-start(bf16[1024,128]{1,0:T(8,128)(2,1)S(1)} %get-tuple-element.15.far_ref), channel_id=1, source_target_pairs={{0,15},{1,2},{2,1},{3,4},{4,3},{5,6},{6,5},{7,8},{8,7},{9,10},{10,... | collective-permute-start | bytes 786440 | tf_op jit(solution)/shard_map/ppermute | solution.py:409
  12.7 0.0 collective-permute-start.1
  12.7 1.9 %pack_other_half_of_shells.1 = bf16[16,3,48,128]{3,2,1,0:T(8,128)(2,1)S(1)} custom-call(s32[96]{0:T(128)S(1)} %copy-done.2, bf16[32,64,384]{2,1,0:T(8,128)(2,1)S(1)} %copy-done, bf16[16,3,48,128]{3,2,1,0:T(8,128)(2,1)S(1)} %pack_half_of_shells.1.given_ref), custom_call_target="tpu_custom_call" | custom-call | bytes 4194304 | tf_op jit(solution)/shard_map/pack_other_half_of_shells/pallas_call | solution.py:277
  14.6 0.0 copy-start.1
  14.6 0.0 copy-start.3
  14.7 0.0 collective-permute-done
  14.7 2.1 %broadcast_select_fusion = bf16[16,3,48,128]{3,2,1,0:T(8,128)(2,1)} fusion(bf16[16,3,48,128]{3,2,1,0:T(8,128)(2,1)} %collective-permute-done, bf16[16,3,48,128]{3,2,1,0:T(8,128)(2,1)S(1)} %pack_other_half_of_shells.1, pred[]{:T(512)S(6)} %or.3), kind=kLoop, calls=%fused_computation | loop fusion | flops 294912 | bytes 1769473 | tf_op jit(solution)/shard_map/jit(_where)/select_n | solution.py:412
  16.8 4.2 %all-to-all-start = ((bf16[16,3,48,128]{3,2,1,0:T(8,128)(2,1)}), bf16[16,3,48,128]{3,2,1,0:T(8,128)(2,1)S(1)}, u32[]{:S(2)}, u32[]{:S(2)}) async-start(bf16[16,3,48,128]{3,2,1,0:T(8,128)(2,1)} %broadcast_select_fusion), calls=%async_computation | async-start | bytes 1179648 | tf_op jit(solution)/shard_map/all_to_all | solution.py:413
  21.0 0.0 copy-start.9
  21.0 0.0 copy-start.8
  21.0 4.2 %collective-permute-done.1.near_ref = bf16[1024,128]{1,0:T(8,128)(2,1)} collective-permute-done((bf16[1024,128]{1,0:T(8,128)(2,1)S(1)}, bf16[1024,128]{1,0:T(8,128)(2,1)}, u32[]{:S(2)}, u32[]{:S(2)}) %collective-permute-start.1) | collective-permute-done | bytes 262176 | tf_op jit(solution)/shard_map/ppermute | solution.py:410
  25.2 0.0 collective-permute-done.2.far_ref
  25.2 0.0 copy-done.1
  25.2 0.0 copy-done.3
  25.2 9.1 %smooth_along_longitude.1 = (bf16[32,64,384]{2,1,0:T(8,128)(2,1)S(1)}, bf16[32,32,384]{2,1,0:T(8,128)(2,1)}, bf16[32,32,384]{2,1,0:T(8,128)(2,1)}) custom-call(s32[1024]{0:T(1024)S(1)} %copy-done.3, bf16[32,64,384]{2,1,0:T(8,128)(2,1)S(1)} %copy-done.1, bf16[1024,128]{1,0:T(8,128)(2,1)} %collective-permute-done.1.near_ref, ...), custom_call_target="tpu_custom_call" | custom-call | flops 68719476736 | bytes 16777216 | tf_op jit(solution)/shard_map/smooth_along_longitude/pallas_call | solution.py:277
  34.4 0.0 copy-start.6
  34.4 1.1 %copy-done.6 = bf16[32,64,384]{2,1,0:T(8,128)(2,1)} copy-done((bf16[32,64,384]{2,1,0:T(8,128)(2,1)}, bf16[32,64,384]{2,1,0:T(8,128)(2,1)S(1)}, u32[]{:S(2)}) %copy-start.6) | copy-done | bytes 1572888
  35.5 0.6 collective-permute-start.3
  36.1 3.1 %collective-permute-start.4 = (bf16[32,32,384]{2,1,0:T(8,128)(2,1)}, bf16[32,32,384]{2,1,0:T(8,128)(2,1)S(1)}, u32[]{:S(2)}, u32[]{:S(2)}) collective-permute-start(bf16[32,32,384]{2,1,0:T(8,128)(2,1)} %get-tuple-element.17.after_ref), channel_id=1, source_target_pairs={{16,32},{32,16},{48,64},{64,48},{80,96},{96,80},{112,128},{128,112... | collective-permute-start | bytes 2359304 | tf_op jit(solution)/shard_map/ppermute | solution.py:416
  39.2 0.0 copy-done.9
  39.2 0.1 concatenate.3.table_ref
  39.3 0.0 copy-done.8
  39.3 0.1 copy.7.reach_ref
  39.4 0.0 copy-start.4
  39.4 0.0 all-to-all-done.x_ref
  39.4 2.3 %smooth_and_turn_polar_circles.1 = bf16[16,3,48,128]{3,2,1,0:T(8,128)(2,1)} custom-call(s32[1216]{0:T(1024)S(1)} %concatenate.3.table_ref, bf16[16,3,48,128]{3,2,1,0:T(8,128)(2,1)S(1)} %all-to-all-done.x_ref, bf16[32,32,384]{2,1,0:T(8,128)(2,1)} %get-tuple-element.17.after_ref), custom_call_target="tpu_custom_call" | custom-call | flops 1073741824 | bytes 4194304 | tf_op jit(solution)/shard_map/smooth_and_turn_polar_circles/pallas_call | solution.py:277
  41.7 5.1 %all-to-all-start.1 = ((bf16[16,3,48,128]{3,2,1,0:T(8,128)(2,1)}), bf16[16,3,48,128]{3,2,1,0:T(8,128)(2,1)S(1)}, u32[]{:S(2)}, u32[]{:S(2)}) async-start(bf16[16,3,48,128]{3,2,1,0:T(8,128)(2,1)} %smooth_and_turn_polar_circles.1), calls=%async_computation.1 | async-start | bytes 1179648 | tf_op jit(solution)/shard_map/all_to_all | solution.py:420
  46.8 0.0 collective-permute-done.3.near_ref
  46.8 3.1 %collective-permute-done.4.far_ref = bf16[32,32,384]{2,1,0:T(8,128)(2,1)S(1)} collective-permute-done((bf16[32,32,384]{2,1,0:T(8,128)(2,1)}, bf16[32,32,384]{2,1,0:T(8,128)(2,1)S(1)}, u32[]{:S(2)}, u32[]{:S(2)}) %collective-permute-start.4) | collective-permute-done | bytes 786464 | tf_op jit(solution)/shard_map/ppermute | solution.py:416
  49.9 0.0 copy-done.4
  49.9 0.0 copy-start.7
  49.9 1.4 %copy-done.7 = bf16[32,64,384]{2,1,0:T(8,128)(2,1)S(1)} copy-done((bf16[32,64,384]{2,1,0:T(8,128)(2,1)S(1)}, bf16[32,64,384]{2,1,0:T(8,128)(2,1)}, u32[]{:S(2)}) %copy-start.7) | copy-done | bytes 1572888
  51.3 2.6 %smooth_along_latitude.1 = (f32[32,64,384]{2,1,0:T(8,128)S(1)}, bf16[64,48]{1,0:T(8,128)(2,1)S(1)}, bf16[256,256]{1,0:T(8,128)(2,1)S(1)}) custom-call(s32[96]{0:T(128)S(1)} %copy-done.2, bf16[32,32,384]{2,1,0:T(8,128)(2,1)S(1)} %collective-permute-done.3.near_ref, bf16[32,64,384]{2,1,0:T(8,128)(2,1)S(1)} %copy-done.7, ...), custom_call_target="tpu_custom_call" | custom-call | flops 68719476736 | bytes 8388608 | tf_op jit(solution)/shard_map/smooth_along_latitude/pallas_call | solution.py:277
  53.9 0.0 copy-start.5
  53.9 1.6 %copy-done.5 = f32[32,64,384]{2,1,0:T(8,128)} copy-done((f32[32,64,384]{2,1,0:T(8,128)}, f32[32,64,384]{2,1,0:T(8,128)S(1)}, u32[]{:S(2)}) %copy-start.5) | copy-done | bytes 3145752
  55.5 9.4 %all-to-all-done.1.mine_ref = bf16[16,3,48,128]{3,2,1,0:T(8,128)(2,1)S(1)} async-done(((bf16[16,3,48,128]{3,2,1,0:T(8,128)(2,1)}), bf16[16,3,48,128]{3,2,1,0:T(8,128)(2,1)S(1)}, u32[]{:S(2)}, u32[]{:S(2)}) %all-to-all-start.1) | async-done | bytes 589856 | tf_op jit(solution)/shard_map/all_to_all | solution.py:420
  64.9 2.4 %collective-permute-start.5 = (bf16[16,3,48,128]{3,2,1,0:T(8,128)(2,1)S(1)}, bf16[16,3,48,128]{3,2,1,0:T(8,128)(2,1)S(1)}, u32[]{:S(2)}, u32[]{:S(2)}) collective-permute-start(bf16[16,3,48,128]{3,2,1,0:T(8,128)(2,1)S(1)} %all-to-all-done.1.mine_ref), channel_id=1, source_target_pairs={{0,16},{16,0},{240,224},{224,240},{1,17},{17,1},{241,225},{225,241... | collective-permute-start | bytes 1769480 | tf_op jit(solution)/shard_map/ppermute | solution.py:425
  67.3 1.6 %collective-permute-done.5.other_ref = bf16[16,3,48,128]{3,2,1,0:T(8,128)(2,1)S(1)} collective-permute-done((bf16[16,3,48,128]{3,2,1,0:T(8,128)(2,1)S(1)}, bf16[16,3,48,128]{3,2,1,0:T(8,128)(2,1)S(1)}, u32[]{:S(2)}, u32[]{:S(2)}) %collective-permute-start.5) | collective-permute-done | bytes 589856 | tf_op jit(solution)/shard_map/ppermute | solution.py:425
  68.9 4.9 %add_polar_rows_and_blend.1 = bf16[32,64,384]{2,1,0:T(8,128)(2,1)} custom-call(bf16[16,3,48,128]{3,2,1,0:T(8,128)(2,1)S(1)} %all-to-all-done.1.mine_ref, bf16[16,3,48,128]{3,2,1,0:T(8,128)(2,1)S(1)} %collective-permute-done.5.other_ref, bf16[64,48]{1,0:T(8,128)(2,1)S(1)} %get-tuple-element.22.polar_weight_ref, ...), custom_call_target="tpu_custom_call" | custom-call | flops 2147483648 | bytes 8388608 | tf_op jit(solution)/shard_map/add_polar_rows_and_blend/pallas_call | solution.py:277
Async XLA Ops:
  0.0 1.4 %copy-start = (bf16[32,64,384]{2,1,0:T(8,128)(2,1)S(1)}, bf16[32,64,384]{2,1,0:T(8,128)(2,1)}, u32[]{:S(2)}) copy-start(bf16[32,64,384]{2,1,0:T(8,128)(2,1)} %x_ref.7) | copy-start | bytes 4718596
  1.4 0.7 copy-start.2
  3.9 10.7 %collective-permute-start = (bf16[16,3,48,128]{3,2,1,0:T(8,128)(2,1)S(1)}, bf16[16,3,48,128]{3,2,1,0:T(8,128)(2,1)}, u32[]{:S(2)}, u32[]{:S(2)}) collective-permute-start(bf16[16,3,48,128]{3,2,1,0:T(8,128)(2,1)S(1)} %pack_half_of_shells.1.given_ref), channel_id=1, source_target_pairs={{0,16},{240,224},{1,17},{241,225},{2,18},{242,226},{3,19},{243,227... | collective-permute-start | bytes 1769480 | tf_op jit(solution)/shard_map/ppermute | solution.py:408
  5.2 20.0 %collective-permute-start.2 = (bf16[1024,128]{1,0:T(8,128)(2,1)S(1)}, bf16[1024,128]{1,0:T(8,128)(2,1)S(1)}, u32[]{:S(2)}, u32[]{:S(2)}) collective-permute-start(bf16[1024,128]{1,0:T(8,128)(2,1)S(1)} %get-tuple-element.15.far_ref), channel_id=1, source_target_pairs={{0,15},{1,2},{2,1},{3,4},{4,3},{5,6},{6,5},{7,8},{8,7},{9,10},{10,... | collective-permute-start | bytes 786440 | tf_op jit(solution)/shard_map/ppermute | solution.py:409
  12.7 12.5 %collective-permute-start.1 = (bf16[1024,128]{1,0:T(8,128)(2,1)S(1)}, bf16[1024,128]{1,0:T(8,128)(2,1)}, u32[]{:S(2)}, u32[]{:S(2)}) collective-permute-start(bf16[1024,128]{1,0:T(8,128)(2,1)S(1)} %get-tuple-element.16), channel_id=1, source_target_pairs={{0,1},{1,0},{2,3},{3,2},{4,5},{5,4},{6,7},{7,6},{8,9},{9,8},{10,11... | collective-permute-start | bytes 786440 | tf_op jit(solution)/shard_map/ppermute | solution.py:410
  14.6 10.6 %copy-start.1 = (bf16[32,64,384]{2,1,0:T(8,128)(2,1)S(1)}, bf16[32,64,384]{2,1,0:T(8,128)(2,1)}, u32[]{:S(2)}) copy-start(bf16[32,64,384]{2,1,0:T(8,128)(2,1)} %x_ref.7) | copy-start | bytes 4718596
  14.6 10.6 %copy-start.3 = (s32[1024]{0:T(1024)S(1)}, s32[1024]{0:T(1024)}, u32[]{:S(2)}) copy-start(s32[1024]{0:T(1024)} %halo_ref.1) | copy-start | bytes 12292
  16.8 22.6 %all-to-all-start = ((bf16[16,3,48,128]{3,2,1,0:T(8,128)(2,1)}), bf16[16,3,48,128]{3,2,1,0:T(8,128)(2,1)S(1)}, u32[]{:S(2)}, u32[]{:S(2)}) async-start(bf16[16,3,48,128]{3,2,1,0:T(8,128)(2,1)} %broadcast_select_fusion), calls=%async_computation | async-start | bytes 1179648 | tf_op jit(solution)/shard_map/all_to_all | solution.py:413
  21.0 18.3 %copy-start.9 = (s32[96]{0:T(128)S(1)}, s32[96]{0:T(128)}, u32[]{:S(2)}) copy-start(s32[96]{0:T(128)} %param.10) | copy-start | bytes 1156
  21.0 18.3 %copy-start.8 = (s32[64]{0:T(128)S(1)}, s32[64]{0:T(128)}, u32[]{:S(2)}) copy-start(s32[64]{0:T(128)} %param.8) | copy-start | bytes 772
  34.4 1.1 %copy-start.6 = (bf16[32,64,384]{2,1,0:T(8,128)(2,1)}, bf16[32,64,384]{2,1,0:T(8,128)(2,1)S(1)}, u32[]{:S(2)}) copy-start(bf16[32,64,384]{2,1,0:T(8,128)(2,1)S(1)} %get-tuple-element.19.own_ref) | copy-start | bytes 4718596
  35.5 11.3 %collective-permute-start.3 = (bf16[32,32,384]{2,1,0:T(8,128)(2,1)}, bf16[32,32,384]{2,1,0:T(8,128)(2,1)S(1)}, u32[]{:S(2)}, u32[]{:S(2)}) collective-permute-start(bf16[32,32,384]{2,1,0:T(8,128)(2,1)} %get-tuple-element.18), channel_id=1, source_target_pairs={{0,16},{16,0},{32,48},{48,32},{64,80},{80,64},{96,112},{112,96},{1... | collective-permute-start | bytes 2359304 | tf_op jit(solution)/shard_map/ppermute | solution.py:419
  36.1 13.8 %collective-permute-start.4 = (bf16[32,32,384]{2,1,0:T(8,128)(2,1)}, bf16[32,32,384]{2,1,0:T(8,128)(2,1)S(1)}, u32[]{:S(2)}, u32[]{:S(2)}) collective-permute-start(bf16[32,32,384]{2,1,0:T(8,128)(2,1)} %get-tuple-element.17.after_ref), channel_id=1, source_target_pairs={{16,32},{32,16},{48,64},{64,48},{80,96},{96,80},{112,128},{128,112... | collective-permute-start | bytes 2359304 | tf_op jit(solution)/shard_map/ppermute | solution.py:416
  39.4 10.5 %copy-start.4 = (bf16[32,32]{1,0:T(8,128)(2,1)S(1)}, bf16[32,32]{1,0:T(8,128)(2,1)}, u32[]{:S(2)}) copy-start(bf16[32,32]{1,0:T(8,128)(2,1)} %blend_ref.1) | copy-start | bytes 6148
  41.7 23.2 %all-to-all-start.1 = ((bf16[16,3,48,128]{3,2,1,0:T(8,128)(2,1)}), bf16[16,3,48,128]{3,2,1,0:T(8,128)(2,1)S(1)}, u32[]{:S(2)}, u32[]{:S(2)}) async-start(bf16[16,3,48,128]{3,2,1,0:T(8,128)(2,1)} %smooth_and_turn_polar_circles.1), calls=%async_computation.1 | async-start | bytes 1179648 | tf_op jit(solution)/shard_map/all_to_all | solution.py:420
  49.9 1.4 %copy-start.7 = (bf16[32,64,384]{2,1,0:T(8,128)(2,1)S(1)}, bf16[32,64,384]{2,1,0:T(8,128)(2,1)}, u32[]{:S(2)}) copy-start(bf16[32,64,384]{2,1,0:T(8,128)(2,1)} %copy-done.6) | copy-start | bytes 4718596
  53.9 1.6 %copy-start.5 = (f32[32,64,384]{2,1,0:T(8,128)}, f32[32,64,384]{2,1,0:T(8,128)S(1)}, u32[]{:S(2)}) copy-start(f32[32,64,384]{2,1,0:T(8,128)S(1)} %get-tuple-element.24.lat_ref) | copy-start | bytes 9437188
  64.9 4.0 %collective-permute-start.5 = (bf16[16,3,48,128]{3,2,1,0:T(8,128)(2,1)S(1)}, bf16[16,3,48,128]{3,2,1,0:T(8,128)(2,1)S(1)}, u32[]{:S(2)}, u32[]{:S(2)}) collective-permute-start(bf16[16,3,48,128]{3,2,1,0:T(8,128)(2,1)S(1)} %all-to-all-done.1.mine_ref), channel_id=1, source_target_pairs={{0,16},{16,0},{240,224},{224,240},{1,17},{17,1},{241,225},{225,241... | collective-permute-start | bytes 1769480 | tf_op jit(solution)/shard_map/ppermute | solution.py:425

commit v7 on v6

--- a/solution.py
+++ b/solution.py
@@ -10,6 +10,7 @@
 LANES = 128
 PART = 16
 UNROLL = 8
+PITCH = 65
 F32 = jnp.float32
 BF16 = jnp.bfloat16
 
@@ -47,18 +48,17 @@
     tiles = col_count // LANES
     zone = lax.axis_index("zone")
     for t in range(tiles):
-        wide_ref[t] = (
-            x_ref[half * PART : (half + 1) * PART, :, t * LANES : (t + 1) * LANES]
-            .reshape(PART * row_count, LANES)
-            .astype(F32)
-        )
+        for s in range(PART):
+            wide_ref[t, s * PITCH : s * PITCH + row_count, :] = x_ref[
+                half * PART + s, :, t * LANES : (t + 1) * LANES
+            ].astype(F32)
     holders, held = send_ref.shape[0], send_ref.shape[1]
     cap = jnp.where(zone < 8, 0, holders * held)
     for k in range(holders):
         for r in range(held):
             row = jnp.clip(rows_ref[cap + k * held + r] - zone * row_count, 0, row_count - 1)
             for t in range(tiles):
-                values = wide_ref[t, pl.ds(row, PART, stride=row_count), :]
+                values = wide_ref[t, pl.ds(row, PART, stride=PITCH), :]
                 send_ref[k, r, t * PART : (t + 1) * PART, :] = values.astype(BF16)
 
 
@@ -93,18 +93,23 @@
     far = far_ref[...].astype(F32)
     before = jnp.where(even, far, near)
     after = jnp.where(even, near, far)
+
+    def keep(t, part, values):
+        for s in range(shells // 2):
+            first = (part * (shells // 2) + s) * PITCH
+            wide_ref[t, first : first + row_count, :] = values[s * row_count : (s + 1) * row_count]
+
     for part in range(2):
-        rows = pl.ds(part * size, size)
         shell = slice(part * (shells // 2), (part + 1) * (shells // 2))
         previous = before if part == 0 else pltpu.roll(before, LANES - HMAX, 1)
         for t in range(tiles):
             turned = pltpu.roll(
                 x_ref[shell, :, t * LANES : (t + 1) * LANES].reshape(size, LANES).astype(F32), HMAX, 1
             )
-            wide_ref[t, rows, :] = jnp.where(lane < HMAX, previous, turned)
+            keep(t, part, jnp.where(lane < HMAX, previous, turned))
             previous = turned
         edge = pltpu.roll(after, HMAX, 1) if part == 0 else after
-        wide_ref[tiles, rows, :] = jnp.where(lane < HMAX, previous, jnp.where(lane < 2 * HMAX, edge, 0.0))
+        keep(tiles, part, jnp.where(lane < HMAX, previous, jnp.where(lane < 2 * HMAX, edge, 0.0)))
     depth = 2 * LANES
     offset = (lanes_of(depth) - lax.broadcasted_iota(jnp.int32, (depth, LANES), 0) + HMAX).astype(F32)
     square = offset * offset
@@ -116,18 +121,19 @@
             line = pl.ds(i, 1)
             band = jnp.where(distance <= half_ref[line, :], jnp.exp(-rate_ref[line, :] * square), 0.0)
             band = (band * scale_ref[line, :]).astype(BF16)
-            values = [wide_ref[t, pl.ds(i, shells, stride=row_count), :].astype(BF16) for t in range(tiles + 1)]
+            values = [wide_ref[t, pl.ds(i, shells, stride=PITCH), :].astype(BF16) for t in range(tiles + 1)]
             stacked = jnp.concatenate(
                 [jnp.concatenate(values[:tiles], axis=0), jnp.concatenate(values[1:], axis=0)], axis=1
             )
             result = jnp.dot(stacked, band, preferred_element_type=F32)
             for t in range(tiles):
-                done_ref[t, pl.ds(i, shells, stride=row_count), :] = result[t * shells : (t + 1) * shells]
+                done_ref[t, pl.ds(i, shells, stride=PITCH), :] = result[t * shells : (t + 1) * shells]
         return carry
 
     lax.fori_loop(0, row_count // UNROLL, some_rows, 0)
     for t in range(tiles):
-        out_ref[:, :, t * LANES : (t + 1) * LANES] = done_ref[t].astype(BF16).reshape(shells, row_count, LANES)
+        for s in range(shells):
+            out_ref[s, :, t * LANES : (t + 1) * LANES] = done_ref[t, s * PITCH : s * PITCH + row_count, :].astype(BF16)
     odd = lax.rem(zone, 2)
     last = row_count - LMAX
     near_rows_ref[...] = out_ref[:, pl.ds(pl.multiple_of((1 - odd) * last, LMAX), LMAX), :]
@@ -230,12 +236,12 @@
     fetch.start()
     zone = lax.axis_index("zone")
     outer = (zone == 0) | (zone == 15)
-    mine_first = jnp.where(outer, 0, PART * polar)
-    for ref, first in ((mine_ref, mine_first), (other_ref, PART * polar - mine_first)):
+    mine_first = jnp.where(outer, 0, PART * (polar + 1))
+    for ref, first in ((mine_ref, mine_first), (other_ref, PART * (polar + 1) - mine_first)):
         for k in range(holders):
             for r in range(held):
                 for t in range(tiles):
-                    polar_ref[t, pl.ds(first + k * held + r, PART, stride=polar), :] = ref[
+                    polar_ref[t, pl.ds(first + k * held + r, PART, stride=polar + 1), :] = ref[
                         k, r, t * PART : (t + 1) * PART, :
                     ].astype(F32)
     weight = polar_weight_ref[...]
@@ -244,7 +250,7 @@
     def some_shells(index, carry):
         for u in range(4):
             s = index * 4 + u
-            base = pl.multiple_of(s * polar, PART)
+            base = s * (polar + 1)
             values = jnp.concatenate(
                 [polar_ref[t, pl.ds(base, polar), :].astype(BF16) for t in range(tiles)], axis=1
             )
@@ -295,7 +301,7 @@
     held = polar_rows.shape[0] // 2 // sectors
     send = struct((sectors, held, tiles * PART, LANES), BF16)
     edge = struct((shells * row_count // 2, LANES), BF16)
-    wide = pltpu.VMEM((tiles, PART * row_count, LANES), F32)
+    wide = pltpu.VMEM((tiles, PART * PITCH, LANES), F32)
     tile = pltpu.VMEM((2, shells, row_count, LANES), BF16)
     near, far = call(
         edge_kernel, "cut_edges", (edge, edge), [], [], [tile, pltpu.SemaphoreType.DMA((2,))],
@@ -327,8 +333,8 @@
         [lon_halo],
         [kernel, near, far],
         [
-            pltpu.VMEM((tiles + 1, shells * row_count, LANES), F32),
-            pltpu.VMEM((tiles, shells * row_count, LANES), F32),
+            pltpu.VMEM((tiles + 1, shells * PITCH, LANES), F32),
+            pltpu.VMEM((tiles, shells * PITCH, LANES), F32),
             rows,
             rows,
             rows,
@@ -384,7 +390,7 @@
         [],
         [mine, other, polar_weight, mix],
         [
-            pltpu.VMEM((col_count // LANES, shells * polar, LANES), F32),
+            pltpu.VMEM((col_count // LANES, shells * (polar + 1), LANES), F32),
             pltpu.VMEM(lat.shape, F32),
             pltpu.VMEM(lat.shape, BF16),
             pltpu.SemaphoreType.DMA,

time: 74.3 us -> 71.9 us (0.968)
  Pallas kernels: 23.2 us -> 18.4 us
  starting transfers between devices: 24.1 us -> 26.9 us
    pallas_call x7, Pallas kernels: 23.2 us -> 18.4 us  [call(): pl.pallas_call(kernel, out_shape=out_shape, in_specs=[smem] * len(scalars...]
    ppermute x1, starting transfers between devices: 2.37 us -> 4.71 us  [per_device(): lax.ppermute(mine, 'zone', [(0, 1), (1, 0), (last, last - 1), (last - 1,...]
    ppermute x1, waiting for transfers between devices: 4.24 us -> 5.11 us  [per_device(): near = lax.ppermute(near, 'sector', [(i, i ^ 1) for i in range(sectors)])]
    all_to_all x1, waiting for transfers between devices: 9.39 us -> 8.62 us  [per_device(): mine = lax.all_to_all(turned, 'sector', 0, 0, tiled=True)]
  transfers between devices with their start and end apart: 8 -> 8, of which waited for: 4 -> 4; matrix products, arithmetic and copies ran while one was open for 3% -> 3% of each run, Pallas kernels for 22% -> 17%
where the time goes in v7:
time: 71.9 us; the launch traced here: 71.4 us
  starting transfers between devices  26.9 us (37%)
  Pallas kernels  18.4 us (26%)
  waiting for transfers between devices  18 us (25%)
  local copies, waits for them, and re-layouts  5.85 us (8%)
  other arithmetic  2.11 us (3%)
    pallas_call x7, Pallas kernels, call(): pl.pallas_call(kernel, out_shape=out_shape, in_specs=[smem] * len(scalars...  18.4 us
    all_to_all x1, waiting for transfers between devices, per_device(): mine = lax.all_to_all(turned, 'sector', 0, 0, tiled=True)  8.62 us
    ppermute x1, starting transfers between devices, per_device(): lax.ppermute(far, 'sector', [(i, (i + 1 if i % 2 else i - 1) % sectors) f...  7.5 us
    unnamed x20, local copies, waits for them, and re-layouts  5.68 us
    ppermute x1, waiting for transfers between devices, per_device(): near = lax.ppermute(near, 'sector', [(i, i ^ 1) for i in range(sectors)])  5.11 us
    all_to_all x1, starting transfers between devices, per_device(): mine = lax.all_to_all(turned, 'sector', 0, 0, tiled=True)  5.08 us
    ppermute x1, starting transfers between devices, per_device(): lax.ppermute(mine, 'zone', [(0, 1), (1, 0), (last, last - 1), (last - 1,...  4.71 us
    all_to_all x1, starting transfers between devices, per_device(): circles = lax.all_to_all(parts, 'sector', 0, 0, tiled=True)  4.41 us
  transfers between devices with their start and end apart: 8, of which 4 were waited for; matrix products, arithmetic and copies ran while one was open for 3% of the time, Pallas kernels for 17%

profile of v7, /device:TPU:1, one launch (start us, length us, event | category | flops | bytes accessed | tf_op | source)
XLA Modules:
  0.0 71.4 jit_solution(6902919445417058626)
XLA Ops:
  0.0 0.0 copy-start
  0.0 1.4 %copy-done = bf16[32,64,384]{2,1,0:T(8,128)(2,1)S(1)} copy-done((bf16[32,64,384]{2,1,0:T(8,128)(2,1)S(1)}, bf16[32,64,384]{2,1,0:T(8,128)(2,1)}, u32[]{:S(2)}) %copy-start) | copy-done | bytes 1572888
  1.4 0.0 copy-start.2
  1.4 0.6 cut_edges.1
  2.0 0.1 copy-done.2
  2.1 0.8 %pack_half_of_shells.1.given_ref = bf16[16,3,48,128]{3,2,1,0:T(8,128)(2,1)S(1)} custom-call(s32[96]{0:T(128)S(1)} %copy-done.2, bf16[32,64,384]{2,1,0:T(8,128)(2,1)S(1)} %copy-done, bf16[1024,128]{1,0:T(8,128)(2,1)S(1)} %get-tuple-element.15.far_ref), custom_call_target="tpu_custom_call" | custom-call | bytes 4194304 | tf_op jit(solution)/shard_map/pack_half_of_shells/pallas_call | solution.py:283
  2.8 1.3 %collective-permute-start = (bf16[16,3,48,128]{3,2,1,0:T(8,128)(2,1)S(1)}, bf16[16,3,48,128]{3,2,1,0:T(8,128)(2,1)}, u32[]{:S(2)}, u32[]{:S(2)}) collective-permute-start(bf16[16,3,48,128]{3,2,1,0:T(8,128)(2,1)S(1)} %pack_half_of_shells.1.given_ref), channel_id=1, source_target_pairs={{0,16},{240,224},{1,17},{241,225},{2,18},{242,226},{3,19},{243,227... | collective-permute-start | bytes 1769480 | tf_op jit(solution)/shard_map/ppermute | solution.py:414
  4.1 7.5 %collective-permute-start.2 = (bf16[1024,128]{1,0:T(8,128)(2,1)S(1)}, bf16[1024,128]{1,0:T(8,128)(2,1)S(1)}, u32[]{:S(2)}, u32[]{:S(2)}) collective-permute-start(bf16[1024,128]{1,0:T(8,128)(2,1)S(1)} %get-tuple-element.15.far_ref), channel_id=1, source_target_pairs={{0,15},{1,2},{2,1},{3,4},{4,3},{5,6},{6,5},{7,8},{8,7},{9,10},{10,... | collective-permute-start | bytes 786440 | tf_op jit(solution)/shard_map/ppermute | solution.py:415
  11.7 0.0 collective-permute-start.1
  11.7 0.8 %pack_other_half_of_shells.1 = bf16[16,3,48,128]{3,2,1,0:T(8,128)(2,1)S(1)} custom-call(s32[96]{0:T(128)S(1)} %copy-done.2, bf16[32,64,384]{2,1,0:T(8,128)(2,1)S(1)} %copy-done, bf16[16,3,48,128]{3,2,1,0:T(8,128)(2,1)S(1)} %pack_half_of_shells.1.given_ref), custom_call_target="tpu_custom_call" | custom-call | bytes 4194304 | tf_op jit(solution)/shard_map/pack_other_half_of_shells/pallas_call | solution.py:283
  12.4 0.0 copy-start.1
  12.4 0.0 copy-start.3
  12.5 0.0 collective-permute-done
  12.5 2.1 %broadcast_select_fusion = bf16[16,3,48,128]{3,2,1,0:T(8,128)(2,1)} fusion(bf16[16,3,48,128]{3,2,1,0:T(8,128)(2,1)} %collective-permute-done, bf16[16,3,48,128]{3,2,1,0:T(8,128)(2,1)S(1)} %pack_other_half_of_shells.1, pred[]{:T(512)S(6)} %or.3), kind=kLoop, calls=%fused_computation | loop fusion | flops 294912 | bytes 1769473 | tf_op jit(solution)/shard_map/jit(_where)/select_n | solution.py:418
  14.6 4.4 %all-to-all-start = ((bf16[16,3,48,128]{3,2,1,0:T(8,128)(2,1)}), bf16[16,3,48,128]{3,2,1,0:T(8,128)(2,1)S(1)}, u32[]{:S(2)}, u32[]{:S(2)}) async-start(bf16[16,3,48,128]{3,2,1,0:T(8,128)(2,1)} %broadcast_select_fusion), calls=%async_computation | async-start | bytes 1179648 | tf_op jit(solution)/shard_map/all_to_all | solution.py:419
  19.0 0.0 copy-start.9
  19.0 0.0 copy-start.8
  19.0 5.1 %collective-permute-done.1.near_ref = bf16[1024,128]{1,0:T(8,128)(2,1)} collective-permute-done((bf16[1024,128]{1,0:T(8,128)(2,1)S(1)}, bf16[1024,128]{1,0:T(8,128)(2,1)}, u32[]{:S(2)}, u32[]{:S(2)}) %collective-permute-start.1) | collective-permute-done | bytes 262176 | tf_op jit(solution)/shard_map/ppermute | solution.py:416
  24.1 0.0 collective-permute-done.2.far_ref
  24.1 0.0 copy-done.1
  24.1 0.0 copy-done.3
  24.2 6.6 %smooth_along_longitude.1 = (bf16[32,64,384]{2,1,0:T(8,128)(2,1)S(1)}, bf16[32,32,384]{2,1,0:T(8,128)(2,1)}, bf16[32,32,384]{2,1,0:T(8,128)(2,1)}) custom-call(s32[1024]{0:T(1024)S(1)} %copy-done.3, bf16[32,64,384]{2,1,0:T(8,128)(2,1)S(1)} %copy-done.1, bf16[1024,128]{1,0:T(8,128)(2,1)} %collective-permute-done.1.near_ref, ...), custom_call_target="tpu_custom_call" | custom-call | flops 68719476736 | bytes 16777216 | tf_op jit(solution)/shard_map/smooth_along_longitude/pallas_call | solution.py:283
  30.7 0.0 copy-start.6
  30.7 1.1 %copy-done.6 = bf16[32,64,384]{2,1,0:T(8,128)(2,1)} copy-done((bf16[32,64,384]{2,1,0:T(8,128)(2,1)}, bf16[32,64,384]{2,1,0:T(8,128)(2,1)S(1)}, u32[]{:S(2)}) %copy-start.6) | copy-done | bytes 1572888
  31.9 0.6 collective-permute-start.3
  32.5 3.3 %collective-permute-start.4 = (bf16[32,32,384]{2,1,0:T(8,128)(2,1)}, bf16[32,32,384]{2,1,0:T(8,128)(2,1)S(1)}, u32[]{:S(2)}, u32[]{:S(2)}) collective-permute-start(bf16[32,32,384]{2,1,0:T(8,128)(2,1)} %get-tuple-element.17.after_ref), channel_id=1, source_target_pairs={{16,32},{32,16},{48,64},{64,48},{80,96},{96,80},{112,128},{128,112... | collective-permute-start | bytes 2359304 | tf_op jit(solution)/shard_map/ppermute | solution.py:422
  35.8 0.0 copy-done.9
  35.8 0.1 concatenate.3.table_ref
  35.9 0.0 copy-done.8
  35.9 0.1 copy.7.reach_ref
  36.0 0.0 copy-start.4
  36.0 0.0 all-to-all-done.x_ref
  36.0 2.3 %smooth_and_turn_polar_circles.1 = bf16[16,3,48,128]{3,2,1,0:T(8,128)(2,1)} custom-call(s32[1216]{0:T(1024)S(1)} %concatenate.3.table_ref, bf16[16,3,48,128]{3,2,1,0:T(8,128)(2,1)S(1)} %all-to-all-done.x_ref, bf16[32,32,384]{2,1,0:T(8,128)(2,1)} %get-tuple-element.17.after_ref), custom_call_target="tpu_custom_call" | custom-call | flops 1073741824 | bytes 4194304 | tf_op jit(solution)/shard_map/smooth_and_turn_polar_circles/pallas_call | solution.py:283
  38.3 5.1 %all-to-all-start.1 = ((bf16[16,3,48,128]{3,2,1,0:T(8,128)(2,1)}), bf16[16,3,48,128]{3,2,1,0:T(8,128)(2,1)S(1)}, u32[]{:S(2)}, u32[]{:S(2)}) async-start(bf16[16,3,48,128]{3,2,1,0:T(8,128)(2,1)} %smooth_and_turn_polar_circles.1), calls=%async_computation.1 | async-start | bytes 1179648 | tf_op jit(solution)/shard_map/all_to_all | solution.py:426
  43.3 0.0 collective-permute-done.3.near_ref
  43.4 2.6 %collective-permute-done.4.far_ref = bf16[32,32,384]{2,1,0:T(8,128)(2,1)S(1)} collective-permute-done((bf16[32,32,384]{2,1,0:T(8,128)(2,1)}, bf16[32,32,384]{2,1,0:T(8,128)(2,1)S(1)}, u32[]{:S(2)}, u32[]{:S(2)}) %collective-permute-start.4) | collective-permute-done | bytes 786464 | tf_op jit(solution)/shard_map/ppermute | solution.py:422
  46.0 0.0 copy-done.4
  46.0 0.0 copy-start.7
  46.0 1.4 %copy-done.7 = bf16[32,64,384]{2,1,0:T(8,128)(2,1)S(1)} copy-done((bf16[32,64,384]{2,1,0:T(8,128)(2,1)S(1)}, bf16[32,64,384]{2,1,0:T(8,128)(2,1)}, u32[]{:S(2)}) %copy-start.7) | copy-done | bytes 1572888
  47.4 2.6 %smooth_along_latitude.1 = (f32[32,64,384]{2,1,0:T(8,128)S(1)}, bf16[64,48]{1,0:T(8,128)(2,1)S(1)}, bf16[256,256]{1,0:T(8,128)(2,1)S(1)}) custom-call(s32[96]{0:T(128)S(1)} %copy-done.2, bf16[32,32,384]{2,1,0:T(8,128)(2,1)S(1)} %collective-permute-done.3.near_ref, bf16[32,64,384]{2,1,0:T(8,128)(2,1)S(1)} %copy-done.7, ...), custom_call_target="tpu_custom_call" | custom-call | flops 68719476736 | bytes 8388608 | tf_op jit(solution)/shard_map/smooth_along_latitude/pallas_call | solution.py:283
  50.0 0.0 copy-start.5
  50.0 1.6 %copy-done.5 = f32[32,64,384]{2,1,0:T(8,128)} copy-done((f32[32,64,384]{2,1,0:T(8,128)}, f32[32,64,384]{2,1,0:T(8,128)S(1)}, u32[]{:S(2)}) %copy-start.5) | copy-done | bytes 3145752
  51.6 8.6 %all-to-all-done.1.mine_ref = bf16[16,3,48,128]{3,2,1,0:T(8,128)(2,1)S(1)} async-done(((bf16[16,3,48,128]{3,2,1,0:T(8,128)(2,1)}), bf16[16,3,48,128]{3,2,1,0:T(8,128)(2,1)S(1)}, u32[]{:S(2)}, u32[]{:S(2)}) %all-to-all-start.1) | async-done | bytes 589856 | tf_op jit(solution)/shard_map/all_to_all | solution.py:426
  60.2 4.7 %collective-permute-start.5 = (bf16[16,3,48,128]{3,2,1,0:T(8,128)(2,1)S(1)}, bf16[16,3,48,128]{3,2,1,0:T(8,128)(2,1)S(1)}, u32[]{:S(2)}, u32[]{:S(2)}) collective-permute-start(bf16[16,3,48,128]{3,2,1,0:T(8,128)(2,1)S(1)} %all-to-all-done.1.mine_ref), channel_id=1, source_target_pairs={{0,16},{16,0},{240,224},{224,240},{1,17},{17,1},{241,225},{225,241... | collective-permute-start | bytes 1769480 | tf_op jit(solution)/shard_map/ppermute | solution.py:431
  64.9 1.6 %collective-permute-done.5.other_ref = bf16[16,3,48,128]{3,2,1,0:T(8,128)(2,1)S(1)} collective-permute-done((bf16[16,3,48,128]{3,2,1,0:T(8,128)(2,1)S(1)}, bf16[16,3,48,128]{3,2,1,0:T(8,128)(2,1)S(1)}, u32[]{:S(2)}, u32[]{:S(2)}) %collective-permute-start.5) | collective-permute-done | bytes 589856 | tf_op jit(solution)/shard_map/ppermute | solution.py:431
  66.5 4.9 %add_polar_rows_and_blend.1 = bf16[32,64,384]{2,1,0:T(8,128)(2,1)} custom-call(bf16[16,3,48,128]{3,2,1,0:T(8,128)(2,1)S(1)} %all-to-all-done.1.mine_ref, bf16[16,3,48,128]{3,2,1,0:T(8,128)(2,1)S(1)} %collective-permute-done.5.other_ref, bf16[64,48]{1,0:T(8,128)(2,1)S(1)} %get-tuple-element.22.polar_weight_ref, ...), custom_call_target="tpu_custom_call" | custom-call | flops 2147483648 | bytes 8388608 | tf_op jit(solution)/shard_map/add_polar_rows_and_blend/pallas_call | solution.py:283
Async XLA Ops:
  0.0 1.4 %copy-start = (bf16[32,64,384]{2,1,0:T(8,128)(2,1)S(1)}, bf16[32,64,384]{2,1,0:T(8,128)(2,1)}, u32[]{:S(2)}) copy-start(bf16[32,64,384]{2,1,0:T(8,128)(2,1)} %x_ref.7) | copy-start | bytes 4718596
  1.4 0.7 copy-start.2
  2.8 9.6 %collective-permute-start = (bf16[16,3,48,128]{3,2,1,0:T(8,128)(2,1)S(1)}, bf16[16,3,48,128]{3,2,1,0:T(8,128)(2,1)}, u32[]{:S(2)}, u32[]{:S(2)}) collective-permute-start(bf16[16,3,48,128]{3,2,1,0:T(8,128)(2,1)S(1)} %pack_half_of_shells.1.given_ref), channel_id=1, source_target_pairs={{0,16},{240,224},{1,17},{241,225},{2,18},{242,226},{3,19},{243,227... | collective-permute-start | bytes 1769480 | tf_op jit(solution)/shard_map/ppermute | solution.py:414
  4.1 20.0 %collective-permute-start.2 = (bf16[1024,128]{1,0:T(8,128)(2,1)S(1)}, bf16[1024,128]{1,0:T(8,128)(2,1)S(1)}, u32[]{:S(2)}, u32[]{:S(2)}) collective-permute-start(bf16[1024,128]{1,0:T(8,128)(2,1)S(1)} %get-tuple-element.15.far_ref), channel_id=1, source_target_pairs={{0,15},{1,2},{2,1},{3,4},{4,3},{5,6},{6,5},{7,8},{8,7},{9,10},{10,... | collective-permute-start | bytes 786440 | tf_op jit(solution)/shard_map/ppermute | solution.py:415
  11.7 12.5 %collective-permute-start.1 = (bf16[1024,128]{1,0:T(8,128)(2,1)S(1)}, bf16[1024,128]{1,0:T(8,128)(2,1)}, u32[]{:S(2)}, u32[]{:S(2)}) collective-permute-start(bf16[1024,128]{1,0:T(8,128)(2,1)S(1)} %get-tuple-element.16), channel_id=1, source_target_pairs={{0,1},{1,0},{2,3},{3,2},{4,5},{5,4},{6,7},{7,6},{8,9},{9,8},{10,11... | collective-permute-start | bytes 786440 | tf_op jit(solution)/shard_map/ppermute | solution.py:416
  12.4 11.7 %copy-start.1 = (bf16[32,64,384]{2,1,0:T(8,128)(2,1)S(1)}, bf16[32,64,384]{2,1,0:T(8,128)(2,1)}, u32[]{:S(2)}) copy-start(bf16[32,64,384]{2,1,0:T(8,128)(2,1)} %x_ref.7) | copy-start | bytes 4718596
  12.4 11.7 %copy-start.3 = (s32[1024]{0:T(1024)S(1)}, s32[1024]{0:T(1024)}, u32[]{:S(2)}) copy-start(s32[1024]{0:T(1024)} %halo_ref.1) | copy-start | bytes 12292
  14.6 21.4 %all-to-all-start = ((bf16[16,3,48,128]{3,2,1,0:T(8,128)(2,1)}), bf16[16,3,48,128]{3,2,1,0:T(8,128)(2,1)S(1)}, u32[]{:S(2)}, u32[]{:S(2)}) async-start(bf16[16,3,48,128]{3,2,1,0:T(8,128)(2,1)} %broadcast_select_fusion), calls=%async_computation | async-start | bytes 1179648 | tf_op jit(solution)/shard_map/all_to_all | solution.py:419
  19.0 16.8 %copy-start.9 = (s32[96]{0:T(128)S(1)}, s32[96]{0:T(128)}, u32[]{:S(2)}) copy-start(s32[96]{0:T(128)} %param.10) | copy-start | bytes 1156
  19.0 16.8 %copy-start.8 = (s32[64]{0:T(128)S(1)}, s32[64]{0:T(128)}, u32[]{:S(2)}) copy-start(s32[64]{0:T(128)} %param.8) | copy-start | bytes 772
  30.7 1.1 %copy-start.6 = (bf16[32,64,384]{2,1,0:T(8,128)(2,1)}, bf16[32,64,384]{2,1,0:T(8,128)(2,1)S(1)}, u32[]{:S(2)}) copy-start(bf16[32,64,384]{2,1,0:T(8,128)(2,1)S(1)} %get-tuple-element.19.own_ref) | copy-start | bytes 4718596
  31.9 11.5 %collective-permute-start.3 = (bf16[32,32,384]{2,1,0:T(8,128)(2,1)}, bf16[32,32,384]{2,1,0:T(8,128)(2,1)S(1)}, u32[]{:S(2)}, u32[]{:S(2)}) collective-permute-start(bf16[32,32,384]{2,1,0:T(8,128)(2,1)} %get-tuple-element.18), channel_id=1, source_target_pairs={{0,16},{16,0},{32,48},{48,32},{64,80},{80,64},{96,112},{112,96},{1... | collective-permute-start | bytes 2359304 | tf_op jit(solution)/shard_map/ppermute | solution.py:425
  32.5 13.5 %collective-permute-start.4 = (bf16[32,32,384]{2,1,0:T(8,128)(2,1)}, bf16[32,32,384]{2,1,0:T(8,128)(2,1)S(1)}, u32[]{:S(2)}, u32[]{:S(2)}) collective-permute-start(bf16[32,32,384]{2,1,0:T(8,128)(2,1)} %get-tuple-element.17.after_ref), channel_id=1, source_target_pairs={{16,32},{32,16},{48,64},{64,48},{80,96},{96,80},{112,128},{128,112... | collective-permute-start | bytes 2359304 | tf_op jit(solution)/shard_map/ppermute | solution.py:422
  36.0 10.0 %copy-start.4 = (bf16[32,32]{1,0:T(8,128)(2,1)S(1)}, bf16[32,32]{1,0:T(8,128)(2,1)}, u32[]{:S(2)}) copy-start(bf16[32,32]{1,0:T(8,128)(2,1)} %blend_ref.1) | copy-start | bytes 6148
  38.3 22.0 %all-to-all-start.1 = ((bf16[16,3,48,128]{3,2,1,0:T(8,128)(2,1)}), bf16[16,3,48,128]{3,2,1,0:T(8,128)(2,1)S(1)}, u32[]{:S(2)}, u32[]{:S(2)}) async-start(bf16[16,3,48,128]{3,2,1,0:T(8,128)(2,1)} %smooth_and_turn_polar_circles.1), calls=%async_computation.1 | async-start | bytes 1179648 | tf_op jit(solution)/shard_map/all_to_all | solution.py:426
  46.0 1.4 %copy-start.7 = (bf16[32,64,384]{2,1,0:T(8,128)(2,1)S(1)}, bf16[32,64,384]{2,1,0:T(8,128)(2,1)}, u32[]{:S(2)}) copy-start(bf16[32,64,384]{2,1,0:T(8,128)(2,1)} %copy-done.6) | copy-start | bytes 4718596
  50.0 1.6 %copy-start.5 = (f32[32,64,384]{2,1,0:T(8,128)}, f32[32,64,384]{2,1,0:T(8,128)S(1)}, u32[]{:S(2)}) copy-start(f32[32,64,384]{2,1,0:T(8,128)S(1)} %get-tuple-element.24.lat_ref) | copy-start | bytes 9437188
  60.2 6.3 %collective-permute-start.5 = (bf16[16,3,48,128]{3,2,1,0:T(8,128)(2,1)S(1)}, bf16[16,3,48,128]{3,2,1,0:T(8,128)(2,1)S(1)}, u32[]{:S(2)}, u32[]{:S(2)}) collective-permute-start(bf16[16,3,48,128]{3,2,1,0:T(8,128)(2,1)S(1)} %all-to-all-done.1.mine_ref), channel_id=1, source_target_pairs={{0,16},{16,0},{240,224},{224,240},{1,17},{17,1},{241,225},{225,241... | collective-permute-start | bytes 1769480 | tf_op jit(solution)/shard_map/ppermute | solution.py:431

commit v8 on v7

--- a/solution.py
+++ b/solution.py
@@ -19,26 +19,19 @@
     return lax.broadcasted_iota(jnp.int32, (rows, LANES), 1)
 
 
-def edge_kernel(x_ref, near_ref, far_ref, tile_ref, sems):
+def write_edges(x_ref, near_ref, far_ref):
     shells, row_count, col_count = x_ref.shape
     half = shells // 2
     size = half * row_count
     lane = lanes_of(size)
-    first = (0, col_count - LANES)
-    copies = [
-        pltpu.make_async_copy(x_ref.at[:, :, pl.ds(first[e], LANES)], tile_ref.at[e], sems.at[e]) for e in range(2)
-    ]
-    for copy in copies:
-        copy.start()
-
-    def part(e, shell):
-        return tile_ref[e, shell : shell + half].reshape(size, LANES).astype(F32)
-
+
+    def part(column, shell):
+        return x_ref[shell : shell + half, :, column : column + LANES].reshape(size, LANES).astype(F32)
+
+    last = col_count - LANES
     even = lax.rem(lax.axis_index("sector"), 2) == 0
-    copies[0].wait()
     low = jnp.where(lane < HMAX, part(0, 0), pltpu.roll(part(0, half), HMAX, 1))
-    copies[1].wait()
-    high = jnp.where(lane < HMAX, pltpu.roll(part(1, 0), HMAX, 1), pltpu.roll(part(1, half), 2 * HMAX, 1))
+    high = jnp.where(lane < HMAX, pltpu.roll(part(last, 0), HMAX, 1), pltpu.roll(part(last, half), 2 * HMAX, 1))
     near_ref[...] = jnp.where(even, high, low).astype(BF16)
     far_ref[...] = jnp.where(even, low, high).astype(BF16)
 
@@ -62,12 +55,34 @@
                 send_ref[k, r, t * PART : (t + 1) * PART, :] = values.astype(BF16)
 
 
-def first_kernel(rows_ref, x_ref, far_ref, send_ref, wide_ref):
-    write_polar(1, rows_ref, x_ref, send_ref, wide_ref)
-
-
-def second_kernel(rows_ref, x_ref, given_ref, send_ref, wide_ref):
-    write_polar(0, rows_ref, x_ref, send_ref, wide_ref)
+def first_kernel(x_ref, far_rows_ref, send_ref, near_ref, far_ref, wide_ref, held_ref, rows_ref, sems):
+    fetch = pltpu.make_async_copy(far_rows_ref, rows_ref, sems.at[2])
+    fetch.start()
+    copies = []
+    for half in (1, 0):
+        shells = pl.ds(half * PART, PART)
+        copies.append(pltpu.make_async_copy(x_ref.at[shells], held_ref.at[shells], sems.at[half]))
+        copies[-1].start()
+    fetch.wait()
+    copies[0].wait()
+    write_polar(1, rows_ref, held_ref, send_ref, wide_ref)
+    copies[1].wait()
+    write_edges(held_ref, near_ref, far_ref)
+
+
+def second_kernel(rows_ref, x_ref, given_ref, send_ref, wide_ref, sem):
+    zone = lax.axis_index("zone")
+    inner = (zone == 1) | (zone == lax.axis_size("zone") - 2)
+
+    @pl.when(inner)
+    def _():
+        copy = pltpu.make_async_copy(given_ref, send_ref, sem)
+        copy.start()
+        copy.wait()
+
+    @pl.when(jnp.logical_not(inner))
+    def _():
+        write_polar(0, rows_ref, x_ref, send_ref, wide_ref)
 
 
 def band_terms(half_f):
@@ -226,38 +241,57 @@
     lax.fori_loop(0, shells // 4, some_shells, 0)
 
 
-def final_kernel(mine_ref, other_ref, polar_weight_ref, mix_ref, lat_ref,
-                 out_ref, polar_ref, sum_ref, stage_ref, sem, sems):
-    shells, row_count, col_count = lat_ref.shape
-    holders, held = mine_ref.shape[:2]
-    tiles = col_count // LANES
+def own_part():
+    zone = lax.axis_index("zone")
+    return jnp.where((zone == 0) | (zone == lax.axis_size("zone") - 1), 0, 1)
+
+
+def add_polar(part, source_ref, weight_ref, lat_ref, polar_ref, sum_ref, sem, put):
+    holders, held = source_ref.shape[:2]
+    tiles = polar_ref.shape[0]
     polar = holders * held
-    fetch = pltpu.make_async_copy(lat_ref, sum_ref, sem)
+    pitch = polar + 1
+    fetch = pltpu.make_async_copy(lat_ref.at[pl.ds(part * PART, PART)], sum_ref, sem)
     fetch.start()
-    zone = lax.axis_index("zone")
-    outer = (zone == 0) | (zone == 15)
-    mine_first = jnp.where(outer, 0, PART * (polar + 1))
-    for ref, first in ((mine_ref, mine_first), (other_ref, PART * (polar + 1) - mine_first)):
-        for k in range(holders):
-            for r in range(held):
-                for t in range(tiles):
-                    polar_ref[t, pl.ds(first + k * held + r, PART, stride=polar + 1), :] = ref[
-                        k, r, t * PART : (t + 1) * PART, :
-                    ].astype(F32)
-    weight = polar_weight_ref[...]
+    for k in range(holders):
+        for r in range(held):
+            for t in range(tiles):
+                polar_ref[t, pl.ds(k * held + r, PART, stride=pitch), :] = source_ref[
+                    k, r, t * PART : (t + 1) * PART, :
+                ].astype(F32)
+    weight = weight_ref[...]
     fetch.wait()
 
     def some_shells(index, carry):
         for u in range(4):
             s = index * 4 + u
-            base = s * (polar + 1)
             values = jnp.concatenate(
-                [polar_ref[t, pl.ds(base, polar), :].astype(BF16) for t in range(tiles)], axis=1
+                [polar_ref[t, pl.ds(s * pitch, polar), :].astype(BF16) for t in range(tiles)], axis=1
             )
-            sum_ref[s] += jnp.dot(weight, values, preferred_element_type=F32)
+            put(s, sum_ref[s] + jnp.dot(weight, values, preferred_element_type=F32))
         return carry
 
-    lax.fori_loop(0, shells // 4, some_shells, 0)
+    lax.fori_loop(0, PART // 4, some_shells, 0)
+
+
+def own_kernel(mine_ref, weight_ref, lat_ref, out_ref, polar_ref, sum_ref, sem):
+    def put(s, values):
+        out_ref[s] = values.astype(BF16)
+
+    add_polar(own_part(), mine_ref, weight_ref, lat_ref, polar_ref, sum_ref, sem, put)
+
+
+def final_kernel(other_ref, own_ref, weight_ref, mix_ref, lat_ref, out_ref,
+                 polar_ref, sum_ref, full_ref, stage_ref, sem, sems):
+    shells, row_count, col_count = lat_ref.shape
+    part = own_part()
+
+    def put(s, values):
+        full_ref[(1 - part) * PART + s] = values
+
+    add_polar(1 - part, other_ref, weight_ref, lat_ref, polar_ref, sum_ref, sem, put)
+    for s in range(PART):
+        full_ref[part * PART + s] = own_ref[s].astype(F32)
     group = mix_ref.shape[0] // shells
     mix = mix_ref[...]
     stores = []
@@ -265,7 +299,7 @@
         mixed = []
         for e in range(2):
             first = (2 * g + e) * group
-            values = sum_ref[:, first : first + group, :].reshape(shells * group, col_count).astype(BF16)
+            values = full_ref[:, first : first + group, :].reshape(shells * group, col_count).astype(BF16)
             mixed.append(jnp.dot(mix, values, preferred_element_type=F32).reshape(shells, group, col_count))
         rows = pl.ds(2 * g * group, 2 * group)
         stage_ref[:, rows, :] = jnp.concatenate(mixed, axis=1).astype(BF16)
@@ -295,27 +329,41 @@
 struct = jax.ShapeDtypeStruct
 
 
-def pack(polar_rows, kernel, sectors):
+def pack_first(polar_rows, kernel, sectors):
     shells, row_count, col_count = kernel.shape
     tiles = col_count // LANES
     held = polar_rows.shape[0] // 2 // sectors
-    send = struct((sectors, held, tiles * PART, LANES), BF16)
     edge = struct((shells * row_count // 2, LANES), BF16)
-    wide = pltpu.VMEM((tiles, PART * PITCH, LANES), F32)
-    tile = pltpu.VMEM((2, shells, row_count, LANES), BF16)
-    near, far = call(
-        edge_kernel, "cut_edges", (edge, edge), [], [], [tile, pltpu.SemaphoreType.DMA((2,))],
-        moved=4 << 20, direct=[kernel],
-    )
-    given = call(
-        first_kernel, "pack_half_of_shells", send, [polar_rows], [kernel], [wide],
-        moved=4 << 20, direct=[far],
-    )
-    kept = call(
-        second_kernel, "pack_other_half_of_shells", send, [polar_rows], [kernel], [wide],
-        moved=4 << 20, direct=[given],
-    )
-    return given, kept, near, far
+    return call(
+        first_kernel,
+        "pack_half_of_shells_and_edges",
+        (struct((sectors, held, tiles * PART, LANES), BF16), edge, edge),
+        [],
+        [],
+        [
+            pltpu.VMEM((tiles, PART * PITCH, LANES), F32),
+            pltpu.VMEM(kernel.shape, BF16),
+            pltpu.SMEM(polar_rows.shape, jnp.int32),
+            pltpu.SemaphoreType.DMA((3,)),
+        ],
+        moved=4 << 20,
+        direct=[kernel, polar_rows],
+        mib=52,
+    )
+
+
+def pack_second(polar_rows, kernel, given):
+    _, row_count, col_count = kernel.shape
+    return call(
+        second_kernel,
+        "pack_other_half_or_take_given",
+        struct(given.shape, BF16),
+        [polar_rows],
+        [kernel],
+        [pltpu.VMEM((col_count // LANES, PART * PITCH, LANES), F32), pltpu.SemaphoreType.DMA],
+        moved=4 << 20,
+        direct=[given],
+    )
 
 
 def smooth_lon(lon_halo, kernel, near, far):
@@ -380,17 +428,38 @@
     )
 
 
-def finish(lat, mine, other, polar_weight, mix):
-    shells, _, col_count = lat.shape
-    polar = polar_weight.shape[1]
+def add_own(lat, mine, polar_weight):
+    shells, row_count, col_count = lat.shape
+    half = (PART, row_count, col_count)
+    return call(
+        own_kernel,
+        "add_polar_rows_of_own_shells",
+        struct(half, BF16),
+        [],
+        [mine, polar_weight],
+        [
+            pltpu.VMEM((col_count // LANES, PART * (polar_weight.shape[1] + 1), LANES), F32),
+            pltpu.VMEM(half, F32),
+            pltpu.SemaphoreType.DMA,
+        ],
+        flops=1 << 30,
+        moved=4 << 20,
+        direct=[lat],
+        mib=50,
+    )
+
+
+def finish(lat, other, own, polar_weight, mix):
+    shells, row_count, col_count = lat.shape
     return call(
         final_kernel,
         "add_polar_rows_and_blend",
         struct(lat.shape, BF16),
         [],
-        [mine, other, polar_weight, mix],
+        [other, own, polar_weight, mix],
         [
-            pltpu.VMEM((col_count // LANES, shells * (polar + 1), LANES), F32),
+            pltpu.VMEM((col_count // LANES, PART * (polar_weight.shape[1] + 1), LANES), F32),
+            pltpu.VMEM((PART, row_count, col_count), F32),
             pltpu.VMEM(lat.shape, F32),
             pltpu.VMEM(lat.shape, BF16),
             pltpu.SemaphoreType.DMA,
@@ -408,14 +477,12 @@
     shells, row_count, col_count = kernel.shape
     sectors = lax.axis_size("sector")
     zones = lax.axis_size("zone")
-    zone_id = lax.axis_index("zone")
     last = zones - 1
-    packed, kept, near, far = pack(polar_rows, kernel, sectors)
+    packed, near, far = pack_first(polar_rows, kernel, sectors)
     given = lax.ppermute(packed, "zone", [(0, 1), (last, last - 1)])
     far = lax.ppermute(far, "sector", [(i, (i + 1 if i % 2 else i - 1) % sectors) for i in range(sectors)])
     near = lax.ppermute(near, "sector", [(i, i ^ 1) for i in range(sectors)])
-    inner = (zone_id == 1) | (zone_id == last - 1)
-    parts = jnp.where(inner, given, kept)
+    parts = pack_second(polar_rows, kernel, given)
     circles = lax.all_to_all(parts, "sector", 0, 0, tiled=True)
     lon_smooth, near_rows, far_rows = smooth_lon(lon_halo, kernel, near, far)
     turned = hold(jnp.concatenate([polar_rows, polar_shift, lon_halo]), circles, far_rows)
@@ -429,7 +496,8 @@
     )
     mine, lat = lax.optimization_barrier((mine, lat))
     other = lax.ppermute(mine, "zone", [(0, 1), (1, 0), (last, last - 1), (last - 1, last)])
-    return finish(lat, mine, other, polar_weight, mix)
+    own = add_own(lat, mine, polar_weight)
+    return finish(lat, other, own, polar_weight, mix)
 
 
 def solution(mesh):

time: 71.9 us -> 71.1 us (0.989)
  the two profiles are of different devices: /device:TPU:1 before, /device:TPU:23 now
where the time goes in v8:
time: 71.1 us; the launch traced here: 70.6 us
  starting transfers between devices  24.3 us (34%)
  Pallas kernels  20.8 us (29%)
  waiting for transfers between devices  20.2 us (28%)
  local copies, waits for them, and re-layouts  5.16 us (7%)
    pallas_call x7, Pallas kernels, call(): pl.pallas_call(kernel, out_shape=out_shape, in_specs=[smem] * len(scalars...  20.8 us
    all_to_all x1, waiting for transfers between devices, per_device(): mine = lax.all_to_all(turned, 'sector', 0, 0, tiled=True)  10.5 us
    all_to_all x1, waiting for transfers between devices, per_device(): circles = lax.all_to_all(parts, 'sector', 0, 0, tiled=True)  8.72 us
    ppermute x1, starting transfers between devices, per_device(): lax.ppermute(far, 'sector', [(i, (i + 1 if i % 2 else i - 1) % sectors) f...  5.76 us
    unnamed x20, local copies, waits for them, and re-layouts  4.99 us
    ppermute x1, starting transfers between devices, per_device(): lax.ppermute(mine, 'zone', [(0, 1), (1, 0), (last, last - 1), (last - 1,...  4.64 us
    all_to_all x1, starting transfers between devices, per_device(): circles = lax.all_to_all(parts, 'sector', 0, 0, tiled=True)  4.18 us
    all_to_all x1, starting transfers between devices, per_device(): mine = lax.all_to_all(turned, 'sector', 0, 0, tiled=True)  4.03 us
  transfers between devices with their start and end apart: 8, of which 3 were waited for; matrix products, arithmetic and copies ran while one was open for 0% of the time, Pallas kernels for 22%

profile of v8, /device:TPU:23, one launch (start us, length us, event | category | flops | bytes accessed | tf_op | source)
XLA Modules:
  0.0 70.6 jit_solution(15675656629502728797)
XLA Ops:
  0.0 0.0 copy-start
  0.0 0.0 copy-start.2
  0.0 0.8 %copy-done.2 = s32[96]{0:T(128)S(1)} copy-done((s32[96]{0:T(128)S(1)}, s32[96]{0:T(128)}, u32[]{:S(2)}) %copy-start.2) | copy-done | bytes 408
  0.8 1.7 %pack_half_of_shells_and_edges.1 = (bf16[16,3,48,128]{3,2,1,0:T(8,128)(2,1)S(1)}, bf16[1024,128]{1,0:T(8,128)(2,1)S(1)}, bf16[1024,128]{1,0:T(8,128)(2,1)S(1)}) custom-call(bf16[32,64,384]{2,1,0:T(8,128)(2,1)} %x_ref.5, s32[96]{0:T(128)S(1)} %copy-done.2), custom_call_target="tpu_custom_call" | custom-call | bytes 4194304 | tf_op jit(solution)/shard_map/pack_half_of_shells_and_edges/pallas_call | solution.py:317
  2.5 2.6 %collective-permute-start = (bf16[16,3,48,128]{3,2,1,0:T(8,128)(2,1)S(1)}, bf16[16,3,48,128]{3,2,1,0:T(8,128)(2,1)S(1)}, u32[]{:S(2)}, u32[]{:S(2)}) collective-permute-start(bf16[16,3,48,128]{3,2,1,0:T(8,128)(2,1)S(1)} %get-tuple-element.16), channel_id=1, source_target_pairs={{0,16},{240,224},{1,17},{241,225},{2,18},{242,226},{3,19},{243,227... | collective-permute-start | bytes 1769480 | tf_op jit(solution)/shard_map/ppermute | solution.py:482
  5.1 1.1 %collective-permute-start.1 = (bf16[1024,128]{1,0:T(8,128)(2,1)S(1)}, bf16[1024,128]{1,0:T(8,128)(2,1)S(1)}, u32[]{:S(2)}, u32[]{:S(2)}) collective-permute-start(bf16[1024,128]{1,0:T(8,128)(2,1)S(1)} %get-tuple-element.17), channel_id=1, source_target_pairs={{0,1},{1,0},{2,3},{3,2},{4,5},{5,4},{6,7},{7,6},{8,9},{9,8},{10,11... | collective-permute-start | bytes 786440 | tf_op jit(solution)/shard_map/ppermute | solution.py:484
  6.2 0.0 copy-start.4
  6.2 5.8 %collective-permute-start.2 = (bf16[1024,128]{1,0:T(8,128)(2,1)S(1)}, bf16[1024,128]{1,0:T(8,128)(2,1)S(1)}, u32[]{:S(2)}, u32[]{:S(2)}) collective-permute-start(bf16[1024,128]{1,0:T(8,128)(2,1)S(1)} %get-tuple-element.18), channel_id=1, source_target_pairs={{0,15},{1,2},{2,1},{3,4},{4,3},{5,6},{6,5},{7,8},{8,7},{9,10},{10,... | collective-permute-start | bytes 786440 | tf_op jit(solution)/shard_map/ppermute | solution.py:483
  12.0 0.0 collective-permute-done.given_ref
  12.0 0.0 copy-done
  12.0 1.6 %pack_other_half_or_take_given.1 = bf16[16,3,48,128]{3,2,1,0:T(8,128)(2,1)} custom-call(s32[96]{0:T(128)S(1)} %copy-done.2, bf16[32,64,384]{2,1,0:T(8,128)(2,1)S(1)} %copy-done, bf16[16,3,48,128]{3,2,1,0:T(8,128)(2,1)S(1)} %collective-permute-done.given_ref), custom_call_target="tpu_custom_call" | custom-call | bytes 4194304 | tf_op jit(solution)/shard_map/pack_other_half_or_take_given/pallas_call | solution.py:317
  13.6 4.2 %all-to-all-start = ((bf16[16,3,48,128]{3,2,1,0:T(8,128)(2,1)}), bf16[16,3,48,128]{3,2,1,0:T(8,128)(2,1)S(1)}, u32[]{:S(2)}, u32[]{:S(2)}) async-start(bf16[16,3,48,128]{3,2,1,0:T(8,128)(2,1)} %pack_other_half_or_take_given.1), calls=%async_computation | async-start | bytes 1179648 | tf_op jit(solution)/shard_map/all_to_all | solution.py:486
  17.8 0.0 copy-start.3
  17.8 0.0 copy-start.9
  17.8 0.0 copy-start.8
  17.8 1.0 %collective-permute-done.1.near_ref = bf16[1024,128]{1,0:T(8,128)(2,1)S(1)} collective-permute-done((bf16[1024,128]{1,0:T(8,128)(2,1)S(1)}, bf16[1024,128]{1,0:T(8,128)(2,1)S(1)}, u32[]{:S(2)}, u32[]{:S(2)}) %collective-permute-start.1) | collective-permute-done | bytes 262176 | tf_op jit(solution)/shard_map/ppermute | solution.py:484
  18.8 0.0 collective-permute-done.2.far_ref
  18.8 0.0 copy-done.4
  18.8 5.9 %smooth_along_longitude.1 = (bf16[32,64,384]{2,1,0:T(8,128)(2,1)S(1)}, bf16[32,32,384]{2,1,0:T(8,128)(2,1)}, bf16[32,32,384]{2,1,0:T(8,128)(2,1)S(1)}) custom-call(s32[1024]{0:T(1024)S(1)} %copy-done.4, bf16[32,64,384]{2,1,0:T(8,128)(2,1)S(1)} %copy-done, bf16[1024,128]{1,0:T(8,128)(2,1)S(1)} %collective-permute-done.1.near_ref, ...), custom_call_target="tpu_custom_call" | custom-call | flops 68719476736 | bytes 16777216 | tf_op jit(solution)/shard_map/smooth_along_longitude/pallas_call | solution.py:317
  24.7 0.0 copy-start.6
  24.7 1.1 %copy-done.6 = bf16[32,64,384]{2,1,0:T(8,128)(2,1)} copy-done((bf16[32,64,384]{2,1,0:T(8,128)(2,1)}, bf16[32,64,384]{2,1,0:T(8,128)(2,1)S(1)}, u32[]{:S(2)}) %copy-start.6) | copy-done | bytes 1572888
  25.9 0.4 collective-permute-start.3
  26.3 1.6 %collective-permute-start.4 = (bf16[32,32,384]{2,1,0:T(8,128)(2,1)S(1)}, bf16[32,32,384]{2,1,0:T(8,128)(2,1)}, u32[]{:S(2)}, u32[]{:S(2)}) collective-permute-start(bf16[32,32,384]{2,1,0:T(8,128)(2,1)S(1)} %get-tuple-element.19.after_ref), channel_id=1, source_target_pairs={{16,32},{32,16},{48,64},{64,48},{80,96},{96,80},{112,128},{128,112... | collective-permute-start | bytes 2359304 | tf_op jit(solution)/shard_map/ppermute | solution.py:489
  27.8 0.0 copy-done.3
  27.8 0.0 copy-done.9
  27.8 0.1 concatenate.3.table_ref
  27.9 0.0 copy-done.8
  27.9 0.1 copy.7.reach_ref
  28.0 0.0 copy-start.5
  28.0 8.7 %all-to-all-done.x_ref = bf16[16,3,48,128]{3,2,1,0:T(8,128)(2,1)S(1)} async-done(((bf16[16,3,48,128]{3,2,1,0:T(8,128)(2,1)}), bf16[16,3,48,128]{3,2,1,0:T(8,128)(2,1)S(1)}, u32[]{:S(2)}, u32[]{:S(2)}) %all-to-all-start) | async-done | bytes 589856 | tf_op jit(solution)/shard_map/all_to_all | solution.py:486
  36.7 2.3 %smooth_and_turn_polar_circles.1 = bf16[16,3,48,128]{3,2,1,0:T(8,128)(2,1)} custom-call(s32[1216]{0:T(1024)S(1)} %concatenate.3.table_ref, bf16[16,3,48,128]{3,2,1,0:T(8,128)(2,1)S(1)} %all-to-all-done.x_ref, bf16[32,32,384]{2,1,0:T(8,128)(2,1)S(1)} %get-tuple-element.19.after_ref), custom_call_target="tpu_custom_call" | custom-call | flops 1073741824 | bytes 4194304 | tf_op jit(solution)/shard_map/smooth_and_turn_polar_circles/pallas_call | solution.py:317
  39.0 4.0 %all-to-all-start.1 = ((bf16[16,3,48,128]{3,2,1,0:T(8,128)(2,1)}), bf16[16,3,48,128]{3,2,1,0:T(8,128)(2,1)S(1)}, u32[]{:S(2)}, u32[]{:S(2)}) async-start(bf16[16,3,48,128]{3,2,1,0:T(8,128)(2,1)} %smooth_and_turn_polar_circles.1), calls=%async_computation.1 | async-start | bytes 1179648 | tf_op jit(solution)/shard_map/all_to_all | solution.py:493
  43.1 0.0 collective-permute-done.3.near_ref
  43.1 0.0 collective-permute-done.4.far_ref
  43.1 0.0 copy-done.5
  43.1 0.0 copy-start.7
  43.1 1.4 %copy-done.7 = bf16[32,64,384]{2,1,0:T(8,128)(2,1)S(1)} copy-done((bf16[32,64,384]{2,1,0:T(8,128)(2,1)S(1)}, bf16[32,64,384]{2,1,0:T(8,128)(2,1)}, u32[]{:S(2)}) %copy-start.7) | copy-done | bytes 1572888
  44.5 3.2 %smooth_along_latitude.1 = (f32[32,64,384]{2,1,0:T(8,128)S(1)}, bf16[64,48]{1,0:T(8,128)(2,1)S(1)}, bf16[256,256]{1,0:T(8,128)(2,1)S(1)}) custom-call(s32[96]{0:T(128)S(1)} %copy-done.3, bf16[32,32,384]{2,1,0:T(8,128)(2,1)S(1)} %collective-permute-done.3.near_ref, bf16[32,64,384]{2,1,0:T(8,128)(2,1)S(1)} %copy-done.7, ...), custom_call_target="tpu_custom_call" | custom-call | flops 68719476736 | bytes 8388608 | tf_op jit(solution)/shard_map/smooth_along_latitude/pallas_call | solution.py:317
  47.7 0.0 copy-start.1
  47.7 1.6 %copy-done.1 = f32[32,64,384]{2,1,0:T(8,128)} copy-done((f32[32,64,384]{2,1,0:T(8,128)}, f32[32,64,384]{2,1,0:T(8,128)S(1)}, u32[]{:S(2)}) %copy-start.1) | copy-done | bytes 3145752
  49.3 10.5 %all-to-all-done.1.mine_ref = bf16[16,3,48,128]{3,2,1,0:T(8,128)(2,1)S(1)} async-done(((bf16[16,3,48,128]{3,2,1,0:T(8,128)(2,1)}), bf16[16,3,48,128]{3,2,1,0:T(8,128)(2,1)S(1)}, u32[]{:S(2)}, u32[]{:S(2)}) %all-to-all-start.1) | async-done | bytes 589856 | tf_op jit(solution)/shard_map/all_to_all | solution.py:493
  59.8 4.6 %collective-permute-start.5 = (bf16[16,3,48,128]{3,2,1,0:T(8,128)(2,1)S(1)}, bf16[16,3,48,128]{3,2,1,0:T(8,128)(2,1)S(1)}, u32[]{:S(2)}, u32[]{:S(2)}) collective-permute-start(bf16[16,3,48,128]{3,2,1,0:T(8,128)(2,1)S(1)} %all-to-all-done.1.mine_ref), channel_id=1, source_target_pairs={{0,16},{16,0},{240,224},{224,240},{1,17},{17,1},{241,225},{225,241... | collective-permute-start | bytes 1769480 | tf_op jit(solution)/shard_map/ppermute | solution.py:498
  64.5 2.2 %add_polar_rows_of_own_shells.1.own_ref = bf16[16,64,384]{2,1,0:T(8,128)(2,1)S(1)} custom-call(bf16[16,3,48,128]{3,2,1,0:T(8,128)(2,1)S(1)} %all-to-all-done.1.mine_ref, bf16[64,48]{1,0:T(8,128)(2,1)S(1)} %get-tuple-element.24.weight_ref, f32[32,64,384]{2,1,0:T(8,128)} %copy-done.1), custom_call_target="tpu_custom_call" | custom-call | flops 1073741824 | bytes 4194304 | tf_op jit(solution)/shard_map/add_polar_rows_of_own_shells/pallas_call | solution.py:317
  66.7 0.0 collective-permute-done.5.other_ref
  66.7 3.9 %add_polar_rows_and_blend.1 = bf16[32,64,384]{2,1,0:T(8,128)(2,1)} custom-call(bf16[16,3,48,128]{3,2,1,0:T(8,128)(2,1)S(1)} %collective-permute-done.5.other_ref, bf16[16,64,384]{2,1,0:T(8,128)(2,1)S(1)} %add_polar_rows_of_own_shells.1.own_ref, bf16[64,48]{1,0:T(8,128)(2,1)S(1)} %get-tuple-element.24.weight_ref, ...), custom_call_target="tpu_custom_call" | custom-call | flops 2147483648 | bytes 8388608 | tf_op jit(solution)/shard_map/add_polar_rows_and_blend/pallas_call | solution.py:317
Async XLA Ops:
  0.0 12.0 %copy-start = (bf16[32,64,384]{2,1,0:T(8,128)(2,1)S(1)}, bf16[32,64,384]{2,1,0:T(8,128)(2,1)}, u32[]{:S(2)}) copy-start(bf16[32,64,384]{2,1,0:T(8,128)(2,1)} %x_ref.5) | copy-start | bytes 4718596
  0.0 0.8 %copy-start.2 = (s32[96]{0:T(128)S(1)}, s32[96]{0:T(128)}, u32[]{:S(2)}) copy-start(s32[96]{0:T(128)} %rows_ref.3) | copy-start | bytes 1156
  2.5 9.5 %collective-permute-start = (bf16[16,3,48,128]{3,2,1,0:T(8,128)(2,1)S(1)}, bf16[16,3,48,128]{3,2,1,0:T(8,128)(2,1)S(1)}, u32[]{:S(2)}, u32[]{:S(2)}) collective-permute-start(bf16[16,3,48,128]{3,2,1,0:T(8,128)(2,1)S(1)} %get-tuple-element.16), channel_id=1, source_target_pairs={{0,16},{240,224},{1,17},{241,225},{2,18},{242,226},{3,19},{243,227... | collective-permute-start | bytes 1769480 | tf_op jit(solution)/shard_map/ppermute | solution.py:482
  5.1 13.7 %collective-permute-start.1 = (bf16[1024,128]{1,0:T(8,128)(2,1)S(1)}, bf16[1024,128]{1,0:T(8,128)(2,1)S(1)}, u32[]{:S(2)}, u32[]{:S(2)}) collective-permute-start(bf16[1024,128]{1,0:T(8,128)(2,1)S(1)} %get-tuple-element.17), channel_id=1, source_target_pairs={{0,1},{1,0},{2,3},{3,2},{4,5},{5,4},{6,7},{7,6},{8,9},{9,8},{10,11... | collective-permute-start | bytes 786440 | tf_op jit(solution)/shard_map/ppermute | solution.py:484
  6.2 12.6 %copy-start.4 = (s32[1024]{0:T(1024)S(1)}, s32[1024]{0:T(1024)}, u32[]{:S(2)}) copy-start(s32[1024]{0:T(1024)} %halo_ref.1) | copy-start | bytes 12292
  6.2 12.6 %collective-permute-start.2 = (bf16[1024,128]{1,0:T(8,128)(2,1)S(1)}, bf16[1024,128]{1,0:T(8,128)(2,1)S(1)}, u32[]{:S(2)}, u32[]{:S(2)}) collective-permute-start(bf16[1024,128]{1,0:T(8,128)(2,1)S(1)} %get-tuple-element.18), channel_id=1, source_target_pairs={{0,15},{1,2},{2,1},{3,4},{4,3},{5,6},{6,5},{7,8},{8,7},{9,10},{10,... | collective-permute-start | bytes 786440 | tf_op jit(solution)/shard_map/ppermute | solution.py:483
  13.6 23.1 %all-to-all-start = ((bf16[16,3,48,128]{3,2,1,0:T(8,128)(2,1)}), bf16[16,3,48,128]{3,2,1,0:T(8,128)(2,1)S(1)}, u32[]{:S(2)}, u32[]{:S(2)}) async-start(bf16[16,3,48,128]{3,2,1,0:T(8,128)(2,1)} %pack_other_half_or_take_given.1), calls=%async_computation | async-start | bytes 1179648 | tf_op jit(solution)/shard_map/all_to_all | solution.py:486
  17.8 10.1 %copy-start.3 = (s32[96]{0:T(128)S(1)}, s32[96]{0:T(128)}, u32[]{:S(2)}) copy-start(s32[96]{0:T(128)} %rows_ref.3) | copy-start | bytes 1156
  17.8 10.0 %copy-start.9 = (s32[96]{0:T(128)S(1)}, s32[96]{0:T(128)}, u32[]{:S(2)}) copy-start(s32[96]{0:T(128)} %param.10) | copy-start | bytes 1156
  17.8 10.1 %copy-start.8 = (s32[64]{0:T(128)S(1)}, s32[64]{0:T(128)}, u32[]{:S(2)}) copy-start(s32[64]{0:T(128)} %param.8) | copy-start | bytes 772
  24.7 1.1 %copy-start.6 = (bf16[32,64,384]{2,1,0:T(8,128)(2,1)}, bf16[32,64,384]{2,1,0:T(8,128)(2,1)S(1)}, u32[]{:S(2)}) copy-start(bf16[32,64,384]{2,1,0:T(8,128)(2,1)S(1)} %get-tuple-element.21.own_ref) | copy-start | bytes 4718596
  25.9 17.2 %collective-permute-start.3 = (bf16[32,32,384]{2,1,0:T(8,128)(2,1)}, bf16[32,32,384]{2,1,0:T(8,128)(2,1)S(1)}, u32[]{:S(2)}, u32[]{:S(2)}) collective-permute-start(bf16[32,32,384]{2,1,0:T(8,128)(2,1)} %get-tuple-element.20), channel_id=1, source_target_pairs={{0,16},{16,0},{32,48},{48,32},{64,80},{80,64},{96,112},{112,96},{1... | collective-permute-start | bytes 2359304 | tf_op jit(solution)/shard_map/ppermute | solution.py:492
  26.3 16.8 %collective-permute-start.4 = (bf16[32,32,384]{2,1,0:T(8,128)(2,1)S(1)}, bf16[32,32,384]{2,1,0:T(8,128)(2,1)}, u32[]{:S(2)}, u32[]{:S(2)}) collective-permute-start(bf16[32,32,384]{2,1,0:T(8,128)(2,1)S(1)} %get-tuple-element.19.after_ref), channel_id=1, source_target_pairs={{16,32},{32,16},{48,64},{64,48},{80,96},{96,80},{112,128},{128,112... | collective-permute-start | bytes 2359304 | tf_op jit(solution)/shard_map/ppermute | solution.py:489
  28.0 15.1 %copy-start.5 = (bf16[32,32]{1,0:T(8,128)(2,1)S(1)}, bf16[32,32]{1,0:T(8,128)(2,1)}, u32[]{:S(2)}) copy-start(bf16[32,32]{1,0:T(8,128)(2,1)} %blend_ref.1) | copy-start | bytes 6148
  39.0 20.8 %all-to-all-start.1 = ((bf16[16,3,48,128]{3,2,1,0:T(8,128)(2,1)}), bf16[16,3,48,128]{3,2,1,0:T(8,128)(2,1)S(1)}, u32[]{:S(2)}, u32[]{:S(2)}) async-start(bf16[16,3,48,128]{3,2,1,0:T(8,128)(2,1)} %smooth_and_turn_polar_circles.1), calls=%async_computation.1 | async-start | bytes 1179648 | tf_op jit(solution)/shard_map/all_to_all | solution.py:493
  43.1 1.4 %copy-start.7 = (bf16[32,64,384]{2,1,0:T(8,128)(2,1)S(1)}, bf16[32,64,384]{2,1,0:T(8,128)(2,1)}, u32[]{:S(2)}) copy-start(bf16[32,64,384]{2,1,0:T(8,128)(2,1)} %copy-done.6) | copy-start | bytes 4718596
  47.7 1.6 %copy-start.1 = (f32[32,64,384]{2,1,0:T(8,128)}, f32[32,64,384]{2,1,0:T(8,128)S(1)}, u32[]{:S(2)}) copy-start(f32[32,64,384]{2,1,0:T(8,128)S(1)} %get-tuple-element.25.lat_ref) | copy-start | bytes 9437188
  59.8 6.9 %collective-permute-start.5 = (bf16[16,3,48,128]{3,2,1,0:T(8,128)(2,1)S(1)}, bf16[16,3,48,128]{3,2,1,0:T(8,128)(2,1)S(1)}, u32[]{:S(2)}, u32[]{:S(2)}) collective-permute-start(bf16[16,3,48,128]{3,2,1,0:T(8,128)(2,1)S(1)} %all-to-all-done.1.mine_ref), channel_id=1, source_target_pairs={{0,16},{16,0},{240,224},{224,240},{1,17},{17,1},{241,225},{225,241... | collective-permute-start | bytes 1769480 | tf_op jit(solution)/shard_map/ppermute | solution.py:498

commit v9 on v8

--- a/solution.py
+++ b/solution.py
@@ -11,6 +11,7 @@
 PART = 16
 UNROLL = 8
 PITCH = 65
+SETS = 3
 F32 = jnp.float32
 BF16 = jnp.bfloat16
 
@@ -36,7 +37,11 @@
     far_ref[...] = jnp.where(even, low, high).astype(BF16)
 
 
-def write_polar(half, rows_ref, x_ref, send_ref, wide_ref):
+def from_pole(zone):
+    return jnp.minimum(zone, lax.axis_size("zone") - 1 - zone)
+
+
+def write_polar(half, holders, rows_ref, x_ref, wide_ref, store):
     _, row_count, col_count = x_ref.shape
     tiles = col_count // LANES
     zone = lax.axis_index("zone")
@@ -45,14 +50,12 @@
             wide_ref[t, s * PITCH : s * PITCH + row_count, :] = x_ref[
                 half * PART + s, :, t * LANES : (t + 1) * LANES
             ].astype(F32)
-    holders, held = send_ref.shape[0], send_ref.shape[1]
-    cap = jnp.where(zone < 8, 0, holders * held)
-    for k in range(holders):
-        for r in range(held):
-            row = jnp.clip(rows_ref[cap + k * held + r] - zone * row_count, 0, row_count - 1)
+    cap = jnp.where(zone < 8, 0, SETS * holders)
+    for r in range(SETS):
+        for k in range(holders):
+            row = jnp.clip(rows_ref[cap + r * holders + k] - zone * row_count, 0, row_count - 1)
             for t in range(tiles):
-                values = wide_ref[t, pl.ds(row, PART, stride=PITCH), :]
-                send_ref[k, r, t * PART : (t + 1) * PART, :] = values.astype(BF16)
+                store(r, k, t, wide_ref[t, pl.ds(row, PART, stride=PITCH), :].astype(BF16))
 
 
 def first_kernel(x_ref, far_rows_ref, send_ref, near_ref, far_ref, wide_ref, held_ref, rows_ref, sems):
@@ -65,24 +68,33 @@
         copies[-1].start()
     fetch.wait()
     copies[0].wait()
-    write_polar(1, rows_ref, held_ref, send_ref, wide_ref)
+
+    def store(r, k, t, values):
+        send_ref[r, k, t * PART : (t + 1) * PART, :] = values
+
+    write_polar(1, send_ref.shape[1], rows_ref, held_ref, wide_ref, store)
     copies[1].wait()
     write_edges(held_ref, near_ref, far_ref)
 
 
-def second_kernel(rows_ref, x_ref, given_ref, send_ref, wide_ref, sem):
-    zone = lax.axis_index("zone")
-    inner = (zone == 1) | (zone == lax.axis_size("zone") - 2)
+def second_kernel(rows_ref, x_ref, given_ref, stay_ref, right_ref, left_ref, wide_ref, sems):
+    outs = (stay_ref, right_ref, left_ref)
+    inner = from_pole(lax.axis_index("zone")) == 1
 
     @pl.when(inner)
     def _():
-        copy = pltpu.make_async_copy(given_ref, send_ref, sem)
-        copy.start()
-        copy.wait()
+        copies = [pltpu.make_async_copy(given_ref.at[r], outs[r], sems.at[r]) for r in range(SETS)]
+        for copy in copies:
+            copy.start()
+        for copy in copies:
+            copy.wait()
 
     @pl.when(jnp.logical_not(inner))
     def _():
-        write_polar(0, rows_ref, x_ref, send_ref, wide_ref)
+        def store(r, k, t, values):
+            outs[r][k, t * PART : (t + 1) * PART, :] = values
+
+        write_polar(0, stay_ref.shape[0], rows_ref, x_ref, wide_ref, store)
 
 
 def band_terms(half_f):
@@ -92,7 +104,7 @@
     return rate, jnp.broadcast_to(1.0 / jnp.sum(terms, axis=1, keepdims=True), half_f.shape)
 
 
-def lon_kernel(halo_ref, x_ref, near_ref, far_ref,
+def lon_kernel(halo_ref, x_ref, near_ref, far_ref, after_ref, table_ref, reach_ref,
                out_ref, near_rows_ref, far_rows_ref, wide_ref, done_ref, half_ref, rate_ref, scale_ref):
     shells, row_count, col_count = x_ref.shape
     total = shells * row_count
@@ -156,33 +168,30 @@
 
 
 def hold_kernel(table_ref, x_ref, after_ref, out_ref, circle_ref):
-    sectors, held, block, _ = x_ref.shape
+    sectors, block, _ = x_ref.shape
     zone, sector = lax.axis_index("zone"), lax.axis_index("sector")
-    polar = 2 * sectors * held
-    cap = jnp.where(zone < 8, 0, sectors * held)
+    polar = 2 * sectors * SETS
     length = sectors * block
     full_lon = length // PART * LANES
     depth = 3 * LANES
-    for r in range(held):
-        for copy in range(2):
-            circle_ref[r, copy * length : (copy + 1) * length, :] = x_ref[:, r].reshape(length, LANES)
-        circle_ref[r, 2 * length : 2 * length + 2 * PART, :] = circle_ref[r, 0 : 2 * PART, :]
-    for r in range(held):
-        entry = cap + sector * held + r
-        half_f = jnp.full((1, LANES), table_ref[2 * polar + table_ref[entry]], jnp.int32).astype(F32)
-        rate, scale = band_terms(half_f)
-        start = lax.rem(2 * full_lon - table_ref[polar + entry] - HMAX, full_lon)
-        first = start // LANES
-        rest = start - first * LANES
-        offset = (
-            lanes_of(depth) - lax.broadcasted_iota(jnp.int32, (depth, LANES), 0) + (rest + HMAX)
-        ).astype(F32)
-        band = jnp.where(jnp.abs(offset) <= half_f, jnp.exp(-rate * (offset * offset)), 0.0) * scale
-        values = jnp.concatenate(
-            [circle_ref[r, pl.ds(pl.multiple_of((first + u) * PART, PART), length), :] for u in range(3)], axis=1
-        )
-        result = jnp.dot(values, band.astype(BF16), preferred_element_type=F32)
-        out_ref[:, r] = result.astype(BF16).reshape(sectors, block, LANES)
+    for copy in range(2):
+        circle_ref[copy * length : (copy + 1) * length, :] = x_ref[...].reshape(length, LANES)
+    circle_ref[2 * length : 2 * length + 2 * PART, :] = circle_ref[0 : 2 * PART, :]
+    chip = from_pole(zone) // 2
+    kept = jnp.where(chip == 1, 1, jnp.where(chip == 3, 2, 0))
+    entry = jnp.where(zone < 8, 0, sectors * SETS) + kept * sectors + sector
+    half_f = jnp.full((1, LANES), table_ref[2 * polar + table_ref[entry]], jnp.int32).astype(F32)
+    rate, scale = band_terms(half_f)
+    start = lax.rem(2 * full_lon - table_ref[polar + entry] - HMAX, full_lon)
+    first = start // LANES
+    rest = start - first * LANES
+    offset = (lanes_of(depth) - lax.broadcasted_iota(jnp.int32, (depth, LANES), 0) + (rest + HMAX)).astype(F32)
+    band = jnp.where(jnp.abs(offset) <= half_f, jnp.exp(-rate * (offset * offset)), 0.0) * scale
+    values = jnp.concatenate(
+        [circle_ref[pl.ds(pl.multiple_of((first + u) * PART, PART), length), :] for u in range(3)], axis=1
+    )
+    result = jnp.dot(values, band.astype(BF16), preferred_element_type=F32)
+    out_ref[...] = result.astype(BF16).reshape(sectors, block, LANES)
 
 
 def lat_kernel(rows_ref, near_ref, own_ref, far_ref, reach_ref, blend_ref,
@@ -242,22 +251,21 @@
 
 
 def own_part():
-    zone = lax.axis_index("zone")
-    return jnp.where((zone == 0) | (zone == lax.axis_size("zone") - 1), 0, 1)
-
-
-def add_polar(part, source_ref, weight_ref, lat_ref, polar_ref, sum_ref, sem, put):
-    holders, held = source_ref.shape[:2]
+    return jnp.where(from_pole(lax.axis_index("zone")) == 0, 0, 1)
+
+
+def add_polar(part, source_refs, weight_ref, lat_ref, polar_ref, sum_ref, sem, put):
+    holders = source_refs[0].shape[0]
     tiles = polar_ref.shape[0]
-    polar = holders * held
+    polar = holders * SETS
     pitch = polar + 1
     fetch = pltpu.make_async_copy(lat_ref.at[pl.ds(part * PART, PART)], sum_ref, sem)
     fetch.start()
-    for k in range(holders):
-        for r in range(held):
+    for r in range(SETS):
+        for k in range(holders):
             for t in range(tiles):
-                polar_ref[t, pl.ds(k * held + r, PART, stride=pitch), :] = source_ref[
-                    k, r, t * PART : (t + 1) * PART, :
+                polar_ref[t, pl.ds(r * holders + k, PART, stride=pitch), :] = source_refs[r][
+                    k, t * PART : (t + 1) * PART, :
                 ].astype(F32)
     weight = weight_ref[...]
     fetch.wait()
@@ -274,14 +282,14 @@
     lax.fori_loop(0, PART // 4, some_shells, 0)
 
 
-def own_kernel(mine_ref, weight_ref, lat_ref, out_ref, polar_ref, sum_ref, sem):
+def own_kernel(stay_ref, right_ref, left_ref, weight_ref, lat_ref, out_ref, polar_ref, sum_ref, sem):
     def put(s, values):
         out_ref[s] = values.astype(BF16)
 
-    add_polar(own_part(), mine_ref, weight_ref, lat_ref, polar_ref, sum_ref, sem, put)
-
-
-def final_kernel(other_ref, own_ref, weight_ref, mix_ref, lat_ref, out_ref,
+    add_polar(own_part(), (stay_ref, right_ref, left_ref), weight_ref, lat_ref, polar_ref, sum_ref, sem, put)
+
+
+def final_kernel(stay_ref, right_ref, left_ref, own_ref, weight_ref, mix_ref, lat_ref, out_ref,
                  polar_ref, sum_ref, full_ref, stage_ref, sem, sems):
     shells, row_count, col_count = lat_ref.shape
     part = own_part()
@@ -289,7 +297,7 @@
     def put(s, values):
         full_ref[(1 - part) * PART + s] = values
 
-    add_polar(1 - part, other_ref, weight_ref, lat_ref, polar_ref, sum_ref, sem, put)
+    add_polar(1 - part, (stay_ref, right_ref, left_ref), weight_ref, lat_ref, polar_ref, sum_ref, sem, put)
     for s in range(PART):
         full_ref[part * PART + s] = own_ref[s].astype(F32)
     group = mix_ref.shape[0] // shells
@@ -332,12 +340,11 @@
 def pack_first(polar_rows, kernel, sectors):
     shells, row_count, col_count = kernel.shape
     tiles = col_count // LANES
-    held = polar_rows.shape[0] // 2 // sectors
     edge = struct((shells * row_count // 2, LANES), BF16)
     return call(
         first_kernel,
         "pack_half_of_shells_and_edges",
-        (struct((sectors, held, tiles * PART, LANES), BF16), edge, edge),
+        (struct((SETS, sectors, tiles * PART, LANES), BF16), edge, edge),
         [],
         [],
         [
@@ -357,16 +364,16 @@
     return call(
         second_kernel,
         "pack_other_half_or_take_given",
-        struct(given.shape, BF16),
+        (struct(given.shape[1:], BF16),) * SETS,
         [polar_rows],
         [kernel],
-        [pltpu.VMEM((col_count // LANES, PART * PITCH, LANES), F32), pltpu.SemaphoreType.DMA],
+        [pltpu.VMEM((col_count // LANES, PART * PITCH, LANES), F32), pltpu.SemaphoreType.DMA((SETS,))],
         moved=4 << 20,
         direct=[given],
     )
 
 
-def smooth_lon(lon_halo, kernel, near, far):
+def smooth_lon(lon_halo, kernel, near, far, *after):
     shells, row_count, col_count = kernel.shape
     tiles = col_count // LANES
     rows = pltpu.VMEM((row_count, LANES), F32)
@@ -389,20 +396,21 @@
         ],
         flops=1 << 36,
         moved=16 << 20,
+        direct=after,
         mib=20,
     )
 
 
 def hold(table, circles, after):
-    sectors, held, block, _ = circles.shape
+    sectors, block, _ = circles.shape
     return call(
         hold_kernel,
         "smooth_and_turn_polar_circles",
         struct(circles.shape, BF16),
         [table],
         [circles],
-        [pltpu.VMEM((held, 2 * sectors * block + 2 * PART, LANES), BF16)],
-        flops=1 << 30,
+        [pltpu.VMEM((2 * sectors * block + 2 * PART, LANES), BF16)],
+        flops=1 << 36,
         moved=4 << 20,
         direct=[after],
     )
@@ -436,7 +444,7 @@
         "add_polar_rows_of_own_shells",
         struct(half, BF16),
         [],
-        [mine, polar_weight],
+        [*mine, polar_weight],
         [
             pltpu.VMEM((col_count // LANES, PART * (polar_weight.shape[1] + 1), LANES), F32),
             pltpu.VMEM(half, F32),
@@ -456,7 +464,7 @@
         "add_polar_rows_and_blend",
         struct(lat.shape, BF16),
         [],
-        [other, own, polar_weight, mix],
+        [*other, own, polar_weight, mix],
         [
             pltpu.VMEM((col_count // LANES, PART * (polar_weight.shape[1] + 1), LANES), F32),
             pltpu.VMEM((PART, row_count, col_count), F32),
@@ -482,20 +490,32 @@
     given = lax.ppermute(packed, "zone", [(0, 1), (last, last - 1)])
     far = lax.ppermute(far, "sector", [(i, (i + 1 if i % 2 else i - 1) % sectors) for i in range(sectors)])
     near = lax.ppermute(near, "sector", [(i, i ^ 1) for i in range(sectors)])
-    parts = pack_second(polar_rows, kernel, given)
+    stay, right, left = pack_second(polar_rows, kernel, given)
+    to_right = [(0, 2), (1, 3), (last, last - 2), (last - 1, last - 3)]
+    to_left = [(0, 6), (1, 7), (last, last - 6), (last - 1, last - 7)]
+    right = lax.ppermute(right, "zone", to_right)
+    left = lax.ppermute(left, "zone", to_left)
+    away = from_pole(lax.axis_index("zone"))
+    parts = jnp.where((away == 2) | (away == 3), right, jnp.where((away == 6) | (away == 7), left, stay))
     circles = lax.all_to_all(parts, "sector", 0, 0, tiled=True)
-    lon_smooth, near_rows, far_rows = smooth_lon(lon_halo, kernel, near, far)
-    turned = hold(jnp.concatenate([polar_rows, polar_shift, lon_halo]), circles, far_rows)
+    table = jnp.concatenate([polar_rows, polar_shift, lon_halo])
+    reach = lat_reach[:, None]
+    lon_smooth, near_rows, far_rows = smooth_lon(lon_halo, kernel, near, far, parts, table, reach)
+    turned = hold(table, circles, far_rows)
     far_rows = lax.ppermute(
         far_rows, "zone", [(i, i + 1 if i % 2 else i - 1) for i in range(1, zones - 1)]
     )
     near_rows = lax.ppermute(near_rows, "zone", [(i, i ^ 1) for i in range(zones)])
     mine = lax.all_to_all(turned, "sector", 0, 0, tiled=True)
     lat, polar_weight, mix = smooth_lat(
-        polar_rows, near_rows, lon_smooth, far_rows, lat_reach[:, None], blend
+        polar_rows, near_rows, lon_smooth, far_rows, reach, blend
     )
     mine, lat = lax.optimization_barrier((mine, lat))
-    other = lax.ppermute(mine, "zone", [(0, 1), (1, 0), (last, last - 1), (last - 1, last)])
+    right = lax.ppermute(mine, "zone", [(j, i) for i, j in to_right])
+    left = lax.ppermute(mine, "zone", [(j, i) for i, j in to_left])
+    mine = (mine, right, left)
+    swap = [(0, 1), (1, 0), (last, last - 1), (last - 1, last)]
+    other = tuple(lax.ppermute(part, "zone", swap) for part in mine)
     own = add_own(lat, mine, polar_weight)
     return finish(lat, other, own, polar_weight, mix)
 

time: 71.1 us -> 78.7 us (1.11)
  the two profiles are of different devices: /device:TPU:23 before, /device:TPU:1 now
where the time goes in v9:
time: 78.7 us; the launch traced here: 78.1 us
  starting transfers between devices  35.9 us (46%)
  Pallas kernels  19.5 us (25%)
  waiting for transfers between devices  16.7 us (21%)
  local copies, waits for them, and re-layouts  5.14 us (7%)
    pallas_call x7, Pallas kernels, call(): pl.pallas_call(kernel, out_shape=out_shape, in_specs=[smem] * len(scalars...  19.5 us
    all_to_all x1, starting transfers between devices, per_device(): mine = lax.all_to_all(turned, 'sector', 0, 0, tiled=True)  8.01 us
    ppermute x3, starting transfers between devices, per_device(): other = tuple((lax.ppermute(part, 'zone', swap) for part in mine))  6.42 us
    all_to_all x1, starting transfers between devices, per_device(): circles = lax.all_to_all(parts, 'sector', 0, 0, tiled=True)  6.32 us
    ppermute x1, waiting for transfers between devices, per_device(): left = lax.ppermute(mine, 'zone', [(j, i) for i, j in to_left])  5.68 us
    ppermute x1, starting transfers between devices, per_device(): lax.ppermute(far, 'sector', [(i, (i + 1 if i % 2 else i - 1) % sectors) f...  5.46 us
    unnamed x20, local copies, waits for them, and re-layouts  4.97 us
    ppermute x1, waiting for transfers between devices, per_device(): given = lax.ppermute(packed, 'zone', [(0, 1), (last, last - 1)])  4.71 us
  transfers between devices with their start and end apart: 14, of which 5 were waited for; matrix products, arithmetic and copies ran while one was open for 1% of the time, Pallas kernels for 16%

profile of v9, /device:TPU:1, one launch (start us, length us, event | category | flops | bytes accessed | tf_op | source)
XLA Modules:
  0.0 78.1 jit_solution(15195999057812391429)
XLA Ops:
  0.0 0.8 copy-done.2
  0.8 1.8 %pack_half_of_shells_and_edges.1 = (bf16[3,16,48,128]{3,2,1,0:T(8,128)(2,1)S(1)}, bf16[1024,128]{1,0:T(8,128)(2,1)S(1)}, bf16[1024,128]{1,0:T(8,128)(2,1)S(1)}) custom-call(bf16[32,64,384]{2,1,0:T(8,128)(2,1)} %x_ref.5, s32[96]{0:T(128)S(1)} %copy-done.2), custom_call_target="tpu_custom_call" | custom-call | bytes 4194304 | tf_op jit(solution)/shard_map/pack_half_of_shells_and_edges/pallas_call | solution.py:325
  2.6 1.3 %collective-permute-start = (bf16[3,16,48,128]{3,2,1,0:T(8,128)(2,1)S(1)}, bf16[3,16,48,128]{3,2,1,0:T(8,128)(2,1)S(1)}, u32[]{:S(2)}, u32[]{:S(2)}) collective-permute-start(bf16[3,16,48,128]{3,2,1,0:T(8,128)(2,1)S(1)} %get-tuple-element.19), channel_id=1, source_target_pairs={{0,16},{240,224},{1,17},{241,225},{2,18},{242,226},{3,19},{243,227... | collective-permute-start | bytes 1769480 | tf_op jit(solution)/shard_map/ppermute | solution.py:490
  3.9 4.7 %collective-permute-done.given_ref = bf16[3,16,48,128]{3,2,1,0:T(8,128)(2,1)S(1)} collective-permute-done((bf16[3,16,48,128]{3,2,1,0:T(8,128)(2,1)S(1)}, bf16[3,16,48,128]{3,2,1,0:T(8,128)(2,1)S(1)}, u32[]{:S(2)}, u32[]{:S(2)}) %collective-permute-start) | collective-permute-done | bytes 589856 | tf_op jit(solution)/shard_map/ppermute | solution.py:490
  8.6 0.0 copy-done
  8.6 1.3 %pack_other_half_or_take_given.1 = (bf16[16,48,128]{2,1,0:T(8,128)(2,1)S(1)}, bf16[16,48,128]{2,1,0:T(8,128)(2,1)S(1)}, bf16[16,48,128]{2,1,0:T(8,128)(2,1)S(1)}) custom-call(s32[96]{0:T(128)S(1)} %copy-done.2, bf16[32,64,384]{2,1,0:T(8,128)(2,1)S(1)} %copy-done, bf16[3,16,48,128]{3,2,1,0:T(8,128)(2,1)S(1)} %collective-permute-done.given_ref), custom_call_target="tpu_custom_call" | custom-call | bytes 4194304 | tf_op jit(solution)/shard_map/pack_other_half_or_take_given/pallas_call | solution.py:325
  9.9 1.3 %collective-permute-start.1 = (bf16[16,48,128]{2,1,0:T(8,128)(2,1)S(1)}, bf16[16,48,128]{2,1,0:T(8,128)(2,1)S(1)}, u32[]{:S(2)}, u32[]{:S(2)}) collective-permute-start(bf16[16,48,128]{2,1,0:T(8,128)(2,1)S(1)} %get-tuple-element.20), channel_id=1, source_target_pairs={{0,32},{16,48},{240,208},{224,192},{1,33},{17,49},{241,209},{225,1... | collective-permute-start | bytes 589832 | tf_op jit(solution)/shard_map/ppermute | solution.py:496
  11.2 2.0 %collective-permute-start.2 = (bf16[16,48,128]{2,1,0:T(8,128)(2,1)S(1)}, bf16[16,48,128]{2,1,0:T(8,128)(2,1)}, u32[]{:S(2)}, u32[]{:S(2)}) collective-permute-start(bf16[16,48,128]{2,1,0:T(8,128)(2,1)S(1)} %get-tuple-element.21), channel_id=1, source_target_pairs={{0,96},{16,112},{240,144},{224,128},{1,97},{17,113},{241,145},{225... | collective-permute-start | bytes 589832 | tf_op jit(solution)/shard_map/ppermute | solution.py:497
  13.2 0.0 collective-permute-start.3
  13.2 5.5 %collective-permute-start.4 = (bf16[1024,128]{1,0:T(8,128)(2,1)S(1)}, bf16[1024,128]{1,0:T(8,128)(2,1)S(1)}, u32[]{:S(2)}, u32[]{:S(2)}) collective-permute-start(bf16[1024,128]{1,0:T(8,128)(2,1)S(1)} %get-tuple-element.24), channel_id=1, source_target_pairs={{0,15},{1,2},{2,1},{3,4},{4,3},{5,6},{6,5},{7,8},{8,7},{9,10},{10,... | collective-permute-start | bytes 786440 | tf_op jit(solution)/shard_map/ppermute | solution.py:491
  18.7 0.0 copy-done.8
  18.7 0.1 copy.7.reach_ref
  18.8 0.0 copy-done.3
  18.8 0.0 copy-done.4
  18.8 0.0 copy-done.9
  18.8 0.1 concatenate.3.table_ref
  18.9 0.0 collective-permute-done.1
  18.9 0.0 collective-permute-done.2
  18.9 0.7 select_select_fusion.after_ref
  19.6 6.3 %all-to-all-start = ((bf16[16,48,128]{2,1,0:T(8,128)(2,1)}), bf16[16,48,128]{2,1,0:T(8,128)(2,1)S(1)}, u32[]{:S(2)}, u32[]{:S(2)}) async-start(bf16[16,48,128]{2,1,0:T(8,128)(2,1)} %select_select_fusion.after_ref), calls=%async_computation | async-start | bytes 393216 | tf_op jit(solution)/shard_map/all_to_all | solution.py:500
  26.0 1.2 %collective-permute-done.3.near_ref = bf16[1024,128]{1,0:T(8,128)(2,1)S(1)} collective-permute-done((bf16[1024,128]{1,0:T(8,128)(2,1)S(1)}, bf16[1024,128]{1,0:T(8,128)(2,1)S(1)}, u32[]{:S(2)}, u32[]{:S(2)}) %collective-permute-start.3) | collective-permute-done | bytes 262176 | tf_op jit(solution)/shard_map/ppermute | solution.py:492
  27.1 0.0 collective-permute-done.4.far_ref
  27.1 5.9 %smooth_along_longitude.1 = (bf16[32,64,384]{2,1,0:T(8,128)(2,1)S(1)}, bf16[32,32,384]{2,1,0:T(8,128)(2,1)}, bf16[32,32,384]{2,1,0:T(8,128)(2,1)S(1)}) custom-call(s32[1024]{0:T(1024)S(1)} %copy-done.4, bf16[32,64,384]{2,1,0:T(8,128)(2,1)S(1)} %copy-done, bf16[1024,128]{1,0:T(8,128)(2,1)S(1)} %collective-permute-done.3.near_ref, ...), custom_call_target="tpu_custom_call" | custom-call | flops 68719476736 | bytes 16777216 | tf_op jit(solution)/shard_map/smooth_along_longitude/pallas_call | solution.py:325
  33.0 1.1 %copy-done.6 = bf16[32,64,384]{2,1,0:T(8,128)(2,1)} copy-done((bf16[32,64,384]{2,1,0:T(8,128)(2,1)}, bf16[32,64,384]{2,1,0:T(8,128)(2,1)S(1)}, u32[]{:S(2)}) %copy-start.6) | copy-done | bytes 1572888
  34.2 0.5 collective-permute-start.5
  34.7 2.0 %collective-permute-start.6 = (bf16[32,32,384]{2,1,0:T(8,128)(2,1)S(1)}, bf16[32,32,384]{2,1,0:T(8,128)(2,1)S(1)}, u32[]{:S(2)}, u32[]{:S(2)}) collective-permute-start(bf16[32,32,384]{2,1,0:T(8,128)(2,1)S(1)} %get-tuple-element.25.after_ref), channel_id=1, source_target_pairs={{16,32},{32,16},{48,64},{64,48},{80,96},{96,80},{112,128},{128,112... | collective-permute-start | bytes 2359304 | tf_op jit(solution)/shard_map/ppermute | solution.py:505
  36.7 0.0 all-to-all-done.x_ref
  36.7 1.7 %smooth_and_turn_polar_circles.1 = bf16[16,48,128]{2,1,0:T(8,128)(2,1)} custom-call(s32[1216]{0:T(1024)S(1)} %concatenate.3.table_ref, bf16[16,48,128]{2,1,0:T(8,128)(2,1)S(1)} %all-to-all-done.x_ref, bf16[32,32,384]{2,1,0:T(8,128)(2,1)S(1)} %get-tuple-element.25.after_ref), custom_call_target="tpu_custom_call" | custom-call | flops 68719476736 | bytes 4194304 | tf_op jit(solution)/shard_map/smooth_and_turn_polar_circles/pallas_call | solution.py:325
  38.4 8.0 %all-to-all-start.1 = ((bf16[16,48,128]{2,1,0:T(8,128)(2,1)}), bf16[16,48,128]{2,1,0:T(8,128)(2,1)S(1)}, u32[]{:S(2)}, u32[]{:S(2)}) async-start(bf16[16,48,128]{2,1,0:T(8,128)(2,1)} %smooth_and_turn_polar_circles.1), calls=%async_computation.1 | async-start | bytes 393216 | tf_op jit(solution)/shard_map/all_to_all | solution.py:509
  46.5 0.0 collective-permute-done.5.near_ref
  46.5 1.6 %collective-permute-done.6.far_ref = bf16[32,32,384]{2,1,0:T(8,128)(2,1)S(1)} collective-permute-done((bf16[32,32,384]{2,1,0:T(8,128)(2,1)S(1)}, bf16[32,32,384]{2,1,0:T(8,128)(2,1)S(1)}, u32[]{:S(2)}, u32[]{:S(2)}) %collective-permute-start.6) | collective-permute-done | bytes 786464 | tf_op jit(solution)/shard_map/ppermute | solution.py:505
  48.1 0.0 copy-done.5
  48.1 1.4 %copy-done.7 = bf16[32,64,384]{2,1,0:T(8,128)(2,1)S(1)} copy-done((bf16[32,64,384]{2,1,0:T(8,128)(2,1)S(1)}, bf16[32,64,384]{2,1,0:T(8,128)(2,1)}, u32[]{:S(2)}) %copy-start.7) | copy-done | bytes 1572888
  49.5 2.6 %smooth_along_latitude.1 = (f32[32,64,384]{2,1,0:T(8,128)S(1)}, bf16[64,48]{1,0:T(8,128)(2,1)S(1)}, bf16[256,256]{1,0:T(8,128)(2,1)S(1)}) custom-call(s32[96]{0:T(128)S(1)} %copy-done.3, bf16[32,32,384]{2,1,0:T(8,128)(2,1)S(1)} %collective-permute-done.5.near_ref, bf16[32,64,384]{2,1,0:T(8,128)(2,1)S(1)} %copy-done.7, ...), custom_call_target="tpu_custom_call" | custom-call | flops 68719476736 | bytes 8388608 | tf_op jit(solution)/shard_map/smooth_along_latitude/pallas_call | solution.py:325
  52.1 1.6 %copy-done.1 = f32[32,64,384]{2,1,0:T(8,128)} copy-done((f32[32,64,384]{2,1,0:T(8,128)}, f32[32,64,384]{2,1,0:T(8,128)S(1)}, u32[]{:S(2)}) %copy-start.1) | copy-done | bytes 3145752
  53.7 3.6 %all-to-all-done.1.stay_ref = bf16[16,48,128]{2,1,0:T(8,128)(2,1)S(1)} async-done(((bf16[16,48,128]{2,1,0:T(8,128)(2,1)}), bf16[16,48,128]{2,1,0:T(8,128)(2,1)S(1)}, u32[]{:S(2)}, u32[]{:S(2)}) %all-to-all-start.1) | async-done | bytes 196640 | tf_op jit(solution)/shard_map/all_to_all | solution.py:509
  57.2 1.3 %collective-permute-start.10 = (bf16[16,48,128]{2,1,0:T(8,128)(2,1)S(1)}, bf16[16,48,128]{2,1,0:T(8,128)(2,1)S(1)}, u32[]{:S(2)}, u32[]{:S(2)}) collective-permute-start(bf16[16,48,128]{2,1,0:T(8,128)(2,1)S(1)} %all-to-all-done.1.stay_ref), channel_id=1, source_target_pairs={{96,0},{112,16},{144,240},{128,224},{97,1},{113,17},{145,241},{129... | collective-permute-start | bytes 589832 | tf_op jit(solution)/shard_map/ppermute | solution.py:515
  58.5 1.3 %collective-permute-start.8 = (bf16[16,48,128]{2,1,0:T(8,128)(2,1)S(1)}, bf16[16,48,128]{2,1,0:T(8,128)(2,1)S(1)}, u32[]{:S(2)}, u32[]{:S(2)}) collective-permute-start(bf16[16,48,128]{2,1,0:T(8,128)(2,1)S(1)} %all-to-all-done.1.stay_ref), channel_id=1, source_target_pairs={{32,0},{48,16},{208,240},{192,224},{33,1},{49,17},{209,241},{193,2... | collective-permute-start | bytes 589832 | tf_op jit(solution)/shard_map/ppermute | solution.py:514
  59.8 2.1 %collective-permute-start.7 = (bf16[16,48,128]{2,1,0:T(8,128)(2,1)S(1)}, bf16[16,48,128]{2,1,0:T(8,128)(2,1)S(1)}, u32[]{:S(2)}, u32[]{:S(2)}) collective-permute-start(bf16[16,48,128]{2,1,0:T(8,128)(2,1)S(1)} %all-to-all-done.1.stay_ref), channel_id=1, source_target_pairs={{0,16},{16,0},{240,224},{224,240},{1,17},{17,1},{241,225},{225,241... | collective-permute-start | bytes 589832 | tf_op jit(solution)/shard_map/ppermute | solution.py:518
  61.9 5.7 %collective-permute-done.10.left_ref = bf16[16,48,128]{2,1,0:T(8,128)(2,1)S(1)} collective-permute-done((bf16[16,48,128]{2,1,0:T(8,128)(2,1)S(1)}, bf16[16,48,128]{2,1,0:T(8,128)(2,1)S(1)}, u32[]{:S(2)}, u32[]{:S(2)}) %collective-permute-start.10) | collective-permute-done | bytes 196640 | tf_op jit(solution)/shard_map/ppermute | solution.py:515
  67.6 1.9 %collective-permute-start.11 = (bf16[16,48,128]{2,1,0:T(8,128)(2,1)S(1)}, bf16[16,48,128]{2,1,0:T(8,128)(2,1)S(1)}, u32[]{:S(2)}, u32[]{:S(2)}) collective-permute-start(bf16[16,48,128]{2,1,0:T(8,128)(2,1)S(1)} %collective-permute-done.10.left_ref), channel_id=1, source_target_pairs={{0,16},{16,0},{240,224},{224,240},{1,17},{17,1},{241,225},{225,241... | collective-permute-start | bytes 589832 | tf_op jit(solution)/shard_map/ppermute | solution.py:518
  69.5 0.0 collective-permute-done.8.right_ref
  69.6 2.4 %collective-permute-start.9 = (bf16[16,48,128]{2,1,0:T(8,128)(2,1)S(1)}, bf16[16,48,128]{2,1,0:T(8,128)(2,1)S(1)}, u32[]{:S(2)}, u32[]{:S(2)}) collective-permute-start(bf16[16,48,128]{2,1,0:T(8,128)(2,1)S(1)} %collective-permute-done.8.right_ref), channel_id=1, source_target_pairs={{0,16},{16,0},{240,224},{224,240},{1,17},{17,1},{241,225},{225,241... | collective-permute-start | bytes 589832 | tf_op jit(solution)/shard_map/ppermute | solution.py:518
  72.0 2.2 %add_polar_rows_of_own_shells.1.own_ref = bf16[16,64,384]{2,1,0:T(8,128)(2,1)S(1)} custom-call(bf16[16,48,128]{2,1,0:T(8,128)(2,1)S(1)} %all-to-all-done.1.stay_ref, bf16[16,48,128]{2,1,0:T(8,128)(2,1)S(1)} %collective-permute-done.8.right_ref, bf16[16,48,128]{2,1,0:T(8,128)(2,1)S(1)} %collective-permute-done.10.left_ref, ...), custom_call_target="tpu_custom_call" | custom-call | flops 1073741824 | bytes 4194304 | tf_op jit(solution)/shard_map/add_polar_rows_of_own_shells/pallas_call | solution.py:325
  74.2 0.0 collective-permute-done.7.stay_ref
  74.2 0.0 collective-permute-done.11.left_ref
  74.2 0.0 collective-permute-done.9.right_ref
  74.2 3.9 %add_polar_rows_and_blend.1 = bf16[32,64,384]{2,1,0:T(8,128)(2,1)} custom-call(bf16[16,48,128]{2,1,0:T(8,128)(2,1)S(1)} %collective-permute-done.7.stay_ref, bf16[16,48,128]{2,1,0:T(8,128)(2,1)S(1)} %collective-permute-done.9.right_ref, bf16[16,48,128]{2,1,0:T(8,128)(2,1)S(1)} %collective-permute-done.11.left_ref, ...), custom_call_target="tpu_custom_call" | custom-call | flops 2147483648 | bytes 8388608 | tf_op jit(solution)/shard_map/add_polar_rows_and_blend/pallas_call | solution.py:325
  (10 shorter events, 0.0 us)
Async XLA Ops:
  0.0 8.6 %copy-start = (bf16[32,64,384]{2,1,0:T(8,128)(2,1)S(1)}, bf16[32,64,384]{2,1,0:T(8,128)(2,1)}, u32[]{:S(2)}) copy-start(bf16[32,64,384]{2,1,0:T(8,128)(2,1)} %x_ref.5) | copy-start | bytes 4718596
  0.0 0.8 copy-start.2
  0.8 17.9 %copy-start.8 = (s32[64]{0:T(128)S(1)}, s32[64]{0:T(128)}, u32[]{:S(2)}) copy-start(s32[64]{0:T(128)} %param.8) | copy-start | bytes 772
  0.8 18.0 %copy-start.3 = (s32[96]{0:T(128)S(1)}, s32[96]{0:T(128)}, u32[]{:S(2)}) copy-start(s32[96]{0:T(128)} %rows_ref.3) | copy-start | bytes 1156
  0.8 18.0 %copy-start.4 = (s32[1024]{0:T(1024)S(1)}, s32[1024]{0:T(1024)}, u32[]{:S(2)}) copy-start(s32[1024]{0:T(1024)} %halo_ref.1) | copy-start | bytes 12292
  0.8 18.0 %copy-start.9 = (s32[96]{0:T(128)S(1)}, s32[96]{0:T(128)}, u32[]{:S(2)}) copy-start(s32[96]{0:T(128)} %param.10) | copy-start | bytes 1156
  2.6 6.0 %collective-permute-start = (bf16[3,16,48,128]{3,2,1,0:T(8,128)(2,1)S(1)}, bf16[3,16,48,128]{3,2,1,0:T(8,128)(2,1)S(1)}, u32[]{:S(2)}, u32[]{:S(2)}) collective-permute-start(bf16[3,16,48,128]{3,2,1,0:T(8,128)(2,1)S(1)} %get-tuple-element.19), channel_id=1, source_target_pairs={{0,16},{240,224},{1,17},{241,225},{2,18},{242,226},{3,19},{243,227... | collective-permute-start | bytes 1769480 | tf_op jit(solution)/shard_map/ppermute | solution.py:490
  9.9 9.0 %collective-permute-start.1 = (bf16[16,48,128]{2,1,0:T(8,128)(2,1)S(1)}, bf16[16,48,128]{2,1,0:T(8,128)(2,1)S(1)}, u32[]{:S(2)}, u32[]{:S(2)}) collective-permute-start(bf16[16,48,128]{2,1,0:T(8,128)(2,1)S(1)} %get-tuple-element.20), channel_id=1, source_target_pairs={{0,32},{16,48},{240,208},{224,192},{1,33},{17,49},{241,209},{225,1... | collective-permute-start | bytes 589832 | tf_op jit(solution)/shard_map/ppermute | solution.py:496
  11.2 7.7 %collective-permute-start.2 = (bf16[16,48,128]{2,1,0:T(8,128)(2,1)S(1)}, bf16[16,48,128]{2,1,0:T(8,128)(2,1)}, u32[]{:S(2)}, u32[]{:S(2)}) collective-permute-start(bf16[16,48,128]{2,1,0:T(8,128)(2,1)S(1)} %get-tuple-element.21), channel_id=1, source_target_pairs={{0,96},{16,112},{240,144},{224,128},{1,97},{17,113},{241,145},{225... | collective-permute-start | bytes 589832 | tf_op jit(solution)/shard_map/ppermute | solution.py:497
  13.2 13.9 %collective-permute-start.3 = (bf16[1024,128]{1,0:T(8,128)(2,1)S(1)}, bf16[1024,128]{1,0:T(8,128)(2,1)S(1)}, u32[]{:S(2)}, u32[]{:S(2)}) collective-permute-start(bf16[1024,128]{1,0:T(8,128)(2,1)S(1)} %get-tuple-element.23), channel_id=1, source_target_pairs={{0,1},{1,0},{2,3},{3,2},{4,5},{5,4},{6,7},{7,6},{8,9},{9,8},{10,11... | collective-permute-start | bytes 786440 | tf_op jit(solution)/shard_map/ppermute | solution.py:492
  13.2 13.9 %collective-permute-start.4 = (bf16[1024,128]{1,0:T(8,128)(2,1)S(1)}, bf16[1024,128]{1,0:T(8,128)(2,1)S(1)}, u32[]{:S(2)}, u32[]{:S(2)}) collective-permute-start(bf16[1024,128]{1,0:T(8,128)(2,1)S(1)} %get-tuple-element.24), channel_id=1, source_target_pairs={{0,15},{1,2},{2,1},{3,4},{4,3},{5,6},{6,5},{7,8},{8,7},{9,10},{10,... | collective-permute-start | bytes 786440 | tf_op jit(solution)/shard_map/ppermute | solution.py:491
  19.6 17.1 %all-to-all-start = ((bf16[16,48,128]{2,1,0:T(8,128)(2,1)}), bf16[16,48,128]{2,1,0:T(8,128)(2,1)S(1)}, u32[]{:S(2)}, u32[]{:S(2)}) async-start(bf16[16,48,128]{2,1,0:T(8,128)(2,1)} %select_select_fusion.after_ref), calls=%async_computation | async-start | bytes 393216 | tf_op jit(solution)/shard_map/all_to_all | solution.py:500
  33.0 1.1 %copy-start.6 = (bf16[32,64,384]{2,1,0:T(8,128)(2,1)}, bf16[32,64,384]{2,1,0:T(8,128)(2,1)S(1)}, u32[]{:S(2)}) copy-start(bf16[32,64,384]{2,1,0:T(8,128)(2,1)S(1)} %get-tuple-element.27.own_ref) | copy-start | bytes 4718596
  34.2 12.3 %collective-permute-start.5 = (bf16[32,32,384]{2,1,0:T(8,128)(2,1)}, bf16[32,32,384]{2,1,0:T(8,128)(2,1)S(1)}, u32[]{:S(2)}, u32[]{:S(2)}) collective-permute-start(bf16[32,32,384]{2,1,0:T(8,128)(2,1)} %get-tuple-element.26), channel_id=1, source_target_pairs={{0,16},{16,0},{32,48},{48,32},{64,80},{80,64},{96,112},{112,96},{1... | collective-permute-start | bytes 2359304 | tf_op jit(solution)/shard_map/ppermute | solution.py:508
  34.7 13.4 %copy-start.5 = (bf16[32,32]{1,0:T(8,128)(2,1)S(1)}, bf16[32,32]{1,0:T(8,128)(2,1)}, u32[]{:S(2)}) copy-start(bf16[32,32]{1,0:T(8,128)(2,1)} %blend_ref.1) | copy-start | bytes 6148
  34.7 13.4 %collective-permute-start.6 = (bf16[32,32,384]{2,1,0:T(8,128)(2,1)S(1)}, bf16[32,32,384]{2,1,0:T(8,128)(2,1)S(1)}, u32[]{:S(2)}, u32[]{:S(2)}) collective-permute-start(bf16[32,32,384]{2,1,0:T(8,128)(2,1)S(1)} %get-tuple-element.25.after_ref), channel_id=1, source_target_pairs={{16,32},{32,16},{48,64},{64,48},{80,96},{96,80},{112,128},{128,112... | collective-permute-start | bytes 2359304 | tf_op jit(solution)/shard_map/ppermute | solution.py:505
  38.4 18.8 %all-to-all-start.1 = ((bf16[16,48,128]{2,1,0:T(8,128)(2,1)}), bf16[16,48,128]{2,1,0:T(8,128)(2,1)S(1)}, u32[]{:S(2)}, u32[]{:S(2)}) async-start(bf16[16,48,128]{2,1,0:T(8,128)(2,1)} %smooth_and_turn_polar_circles.1), calls=%async_computation.1 | async-start | bytes 393216 | tf_op jit(solution)/shard_map/all_to_all | solution.py:509
  48.1 1.4 %copy-start.7 = (bf16[32,64,384]{2,1,0:T(8,128)(2,1)S(1)}, bf16[32,64,384]{2,1,0:T(8,128)(2,1)}, u32[]{:S(2)}) copy-start(bf16[32,64,384]{2,1,0:T(8,128)(2,1)} %copy-done.6) | copy-start | bytes 4718596
  52.1 1.6 %copy-start.1 = (f32[32,64,384]{2,1,0:T(8,128)}, f32[32,64,384]{2,1,0:T(8,128)S(1)}, u32[]{:S(2)}) copy-start(f32[32,64,384]{2,1,0:T(8,128)S(1)} %get-tuple-element.31.lat_ref) | copy-start | bytes 9437188
  57.2 10.4 %collective-permute-start.10 = (bf16[16,48,128]{2,1,0:T(8,128)(2,1)S(1)}, bf16[16,48,128]{2,1,0:T(8,128)(2,1)S(1)}, u32[]{:S(2)}, u32[]{:S(2)}) collective-permute-start(bf16[16,48,128]{2,1,0:T(8,128)(2,1)S(1)} %all-to-all-done.1.stay_ref), channel_id=1, source_target_pairs={{96,0},{112,16},{144,240},{128,224},{97,1},{113,17},{145,241},{129... | collective-permute-start | bytes 589832 | tf_op jit(solution)/shard_map/ppermute | solution.py:515
  58.5 11.0 %collective-permute-start.8 = (bf16[16,48,128]{2,1,0:T(8,128)(2,1)S(1)}, bf16[16,48,128]{2,1,0:T(8,128)(2,1)S(1)}, u32[]{:S(2)}, u32[]{:S(2)}) collective-permute-start(bf16[16,48,128]{2,1,0:T(8,128)(2,1)S(1)} %all-to-all-done.1.stay_ref), channel_id=1, source_target_pairs={{32,0},{48,16},{208,240},{192,224},{33,1},{49,17},{209,241},{193,2... | collective-permute-start | bytes 589832 | tf_op jit(solution)/shard_map/ppermute | solution.py:514
  59.8 14.3 %collective-permute-start.7 = (bf16[16,48,128]{2,1,0:T(8,128)(2,1)S(1)}, bf16[16,48,128]{2,1,0:T(8,128)(2,1)S(1)}, u32[]{:S(2)}, u32[]{:S(2)}) collective-permute-start(bf16[16,48,128]{2,1,0:T(8,128)(2,1)S(1)} %all-to-all-done.1.stay_ref), channel_id=1, source_target_pairs={{0,16},{16,0},{240,224},{224,240},{1,17},{17,1},{241,225},{225,241... | collective-permute-start | bytes 589832 | tf_op jit(solution)/shard_map/ppermute | solution.py:518
  67.6 6.6 %collective-permute-start.11 = (bf16[16,48,128]{2,1,0:T(8,128)(2,1)S(1)}, bf16[16,48,128]{2,1,0:T(8,128)(2,1)S(1)}, u32[]{:S(2)}, u32[]{:S(2)}) collective-permute-start(bf16[16,48,128]{2,1,0:T(8,128)(2,1)S(1)} %collective-permute-done.10.left_ref), channel_id=1, source_target_pairs={{0,16},{16,0},{240,224},{224,240},{1,17},{17,1},{241,225},{225,241... | collective-permute-start | bytes 589832 | tf_op jit(solution)/shard_map/ppermute | solution.py:518
  69.6 4.6 %collective-permute-start.9 = (bf16[16,48,128]{2,1,0:T(8,128)(2,1)S(1)}, bf16[16,48,128]{2,1,0:T(8,128)(2,1)S(1)}, u32[]{:S(2)}, u32[]{:S(2)}) collective-permute-start(bf16[16,48,128]{2,1,0:T(8,128)(2,1)S(1)} %collective-permute-done.8.right_ref), channel_id=1, source_target_pairs={{0,16},{16,0},{240,224},{224,240},{1,17},{17,1},{241,225},{225,241... | collective-permute-start | bytes 589832 | tf_op jit(solution)/shard_map/ppermute | solution.py:518

commit v10 on v8

--- a/solution.py
+++ b/solution.py
@@ -55,7 +55,8 @@
                 send_ref[k, r, t * PART : (t + 1) * PART, :] = values.astype(BF16)
 
 
-def first_kernel(x_ref, far_rows_ref, send_ref, near_ref, far_ref, wide_ref, held_ref, rows_ref, sems):
+def first_kernel(x_ref, far_rows_ref, send_ref, near_ref, far_ref, kept_ref,
+                 wide_ref, held_ref, stage_ref, rows_ref, sems):
     fetch = pltpu.make_async_copy(far_rows_ref, rows_ref, sems.at[2])
     fetch.start()
     copies = []
@@ -67,22 +68,21 @@
     copies[0].wait()
     write_polar(1, rows_ref, held_ref, send_ref, wide_ref)
     copies[1].wait()
+    write_polar(0, rows_ref, held_ref, stage_ref, wide_ref)
+    store = pltpu.make_async_copy(stage_ref, kept_ref, sems.at[3])
+    store.start()
     write_edges(held_ref, near_ref, far_ref)
-
-
-def second_kernel(rows_ref, x_ref, given_ref, send_ref, wide_ref, sem):
+    store.wait()
+
+
+def second_kernel(given_ref, kept_ref, out_ref, sem):
     zone = lax.axis_index("zone")
-    inner = (zone == 1) | (zone == lax.axis_size("zone") - 2)
-
-    @pl.when(inner)
+
+    @pl.when((zone == 1) | (zone == lax.axis_size("zone") - 2))
     def _():
-        copy = pltpu.make_async_copy(given_ref, send_ref, sem)
+        copy = pltpu.make_async_copy(given_ref, out_ref, sem)
         copy.start()
         copy.wait()
-
-    @pl.when(jnp.logical_not(inner))
-    def _():
-        write_polar(0, rows_ref, x_ref, send_ref, wide_ref)
 
 
 def band_terms(half_f):
@@ -329,41 +329,44 @@
 struct = jax.ShapeDtypeStruct
 
 
-def pack_first(polar_rows, kernel, sectors):
+def pack(polar_rows, kernel, sectors):
     shells, row_count, col_count = kernel.shape
     tiles = col_count // LANES
     held = polar_rows.shape[0] // 2 // sectors
     edge = struct((shells * row_count // 2, LANES), BF16)
-    return call(
+    parts = struct((sectors, held, tiles * PART, LANES), BF16)
+    vmem = pl.BlockSpec(memory_space=pltpu.VMEM)
+    anywhere = pl.BlockSpec(memory_space=pl.ANY)
+    return pl.pallas_call(
         first_kernel,
-        "pack_half_of_shells_and_edges",
-        (struct((sectors, held, tiles * PART, LANES), BF16), edge, edge),
-        [],
-        [],
-        [
+        out_shape=(parts, edge, edge, parts),
+        in_specs=[anywhere, anywhere],
+        out_specs=(vmem, vmem, vmem, anywhere),
+        scratch_shapes=[
             pltpu.VMEM((tiles, PART * PITCH, LANES), F32),
             pltpu.VMEM(kernel.shape, BF16),
+            pltpu.VMEM(parts.shape, BF16),
             pltpu.SMEM(polar_rows.shape, jnp.int32),
-            pltpu.SemaphoreType.DMA((3,)),
+            pltpu.SemaphoreType.DMA((4,)),
         ],
-        moved=4 << 20,
-        direct=[kernel, polar_rows],
-        mib=52,
-    )
-
-
-def pack_second(polar_rows, kernel, given):
-    _, row_count, col_count = kernel.shape
-    return call(
+        compiler_params=pltpu.CompilerParams(vmem_limit_bytes=52 << 20),
+        cost_estimate=pl.CostEstimate(flops=0, bytes_accessed=4 << 20, transcendentals=0),
+        name="pack_polar_rows_and_edges",
+    )(kernel, polar_rows)
+
+
+def take_given(given, kept):
+    anywhere = pl.BlockSpec(memory_space=pl.ANY)
+    return pl.pallas_call(
         second_kernel,
-        "pack_other_half_or_take_given",
-        struct(given.shape, BF16),
-        [polar_rows],
-        [kernel],
-        [pltpu.VMEM((col_count // LANES, PART * PITCH, LANES), F32), pltpu.SemaphoreType.DMA],
-        moved=4 << 20,
-        direct=[given],
-    )
+        out_shape=struct(kept.shape, BF16),
+        in_specs=[anywhere, anywhere],
+        out_specs=anywhere,
+        scratch_shapes=[pltpu.SemaphoreType.DMA],
+        input_output_aliases={1: 0},
+        compiler_params=pltpu.CompilerParams(vmem_limit_bytes=4 << 20),
+        name="take_given",
+    )(given, kept)
 
 
 def smooth_lon(lon_halo, kernel, near, far):
@@ -478,11 +481,11 @@
     sectors = lax.axis_size("sector")
     zones = lax.axis_size("zone")
     last = zones - 1
-    packed, near, far = pack_first(polar_rows, kernel, sectors)
+    packed, near, far, kept = pack(polar_rows, kernel, sectors)
     given = lax.ppermute(packed, "zone", [(0, 1), (last, last - 1)])
     far = lax.ppermute(far, "sector", [(i, (i + 1 if i % 2 else i - 1) % sectors) for i in range(sectors)])
     near = lax.ppermute(near, "sector", [(i, i ^ 1) for i in range(sectors)])
-    parts = pack_second(polar_rows, kernel, given)
+    parts = take_given(given, kept)
     circles = lax.all_to_all(parts, "sector", 0, 0, tiled=True)
     lon_smooth, near_rows, far_rows = smooth_lon(lon_halo, kernel, near, far)
     turned = hold(jnp.concatenate([polar_rows, polar_shift, lon_halo]), circles, far_rows)

time: 71.1 us -> 71 us (level)
  the two profiles are of different devices: /device:TPU:23 before, /device:TPU:1 now
where the time goes in v10:
time: 71 us; the launch traced here: 70.5 us
  starting transfers between devices  30.2 us (43%)
  Pallas kernels  21.1 us (30%)
  waiting for transfers between devices  14 us (20%)
  local copies, waits for them, and re-layouts  5.05 us (7%)
    pallas_call x5, Pallas kernels, call(): pl.pallas_call(kernel, out_shape=out_shape, in_specs=[smem] * len(scalars...  17.5 us
    all_to_all x1, waiting for transfers between devices, per_device(): mine = lax.all_to_all(turned, 'sector', 0, 0, tiled=True)  9.46 us
    ppermute x1, starting transfers between devices, per_device(): lax.ppermute(mine, 'zone', [(0, 1), (1, 0), (last, last - 1), (last - 1,...  6.09 us
    ppermute x1, starting transfers between devices, per_device(): lax.ppermute(far, 'sector', [(i, (i + 1 if i % 2 else i - 1) % sectors) f...  5.46 us
    all_to_all x1, starting transfers between devices, per_device(): circles = lax.all_to_all(parts, 'sector', 0, 0, tiled=True)  5.06 us
    unnamed x20, local copies, waits for them, and re-layouts  4.87 us
    all_to_all x1, waiting for transfers between devices, per_device(): circles = lax.all_to_all(parts, 'sector', 0, 0, tiled=True)  4.49 us
    all_to_all x1, starting transfers between devices, per_device(): mine = lax.all_to_all(turned, 'sector', 0, 0, tiled=True)  4.28 us
  transfers between devices with their start and end apart: 8, of which 2 were waited for; matrix products, arithmetic and copies ran while one was open for 0% of the time, Pallas kernels for 20%

profile of v10, /device:TPU:1, one launch (start us, length us, event | category | flops | bytes accessed | tf_op | source)
XLA Modules:
  0.0 70.5 jit_solution(12115265650026005128)
XLA Ops:
  0.0 0.0 copy-start.3
  0.0 0.7 copy-done.3
  0.7 2.7 %pack_polar_rows_and_edges.1 = (bf16[16,3,48,128]{3,2,1,0:T(8,128)(2,1)S(1)}, bf16[1024,128]{1,0:T(8,128)(2,1)S(1)}, bf16[1024,128]{1,0:T(8,128)(2,1)S(1)}, bf16[16,3,48,128]{3,2,1,0:T(8,128)(2,1)}) custom-call(bf16[32,64,384]{2,1,0:T(8,128)(2,1)} %x_ref.3, s32[96]{0:T(128)S(1)} %copy-done.3), custom_call_target="tpu_custom_call" | custom-call | bytes 4194304 | tf_op jit(solution)/shard_map/pack_polar_rows_and_edges/pallas_call | solution.py:340
  3.4 0.0 copy-start.1
  3.4 0.0 copy-start.2
  3.4 1.4 %collective-permute-start = (bf16[16,3,48,128]{3,2,1,0:T(8,128)(2,1)S(1)}, bf16[16,3,48,128]{3,2,1,0:T(8,128)(2,1)S(1)}, u32[]{:S(2)}, u32[]{:S(2)}) collective-permute-start(bf16[16,3,48,128]{3,2,1,0:T(8,128)(2,1)S(1)} %get-tuple-element.17), channel_id=1, source_target_pairs={{0,16},{240,224},{1,17},{241,225},{2,18},{242,226},{3,19},{243,227... | collective-permute-start | bytes 1769480 | tf_op jit(solution)/shard_map/ppermute | solution.py:485
  4.8 2.2 %collective-permute-start.1 = (bf16[1024,128]{1,0:T(8,128)(2,1)S(1)}, bf16[1024,128]{1,0:T(8,128)(2,1)S(1)}, u32[]{:S(2)}, u32[]{:S(2)}) collective-permute-start(bf16[1024,128]{1,0:T(8,128)(2,1)S(1)} %get-tuple-element.19), channel_id=1, source_target_pairs={{0,1},{1,0},{2,3},{3,2},{4,5},{5,4},{6,7},{7,6},{8,9},{9,8},{10,11... | collective-permute-start | bytes 786440 | tf_op jit(solution)/shard_map/ppermute | solution.py:487
  7.1 5.5 %collective-permute-start.2 = (bf16[1024,128]{1,0:T(8,128)(2,1)S(1)}, bf16[1024,128]{1,0:T(8,128)(2,1)S(1)}, u32[]{:S(2)}, u32[]{:S(2)}) collective-permute-start(bf16[1024,128]{1,0:T(8,128)(2,1)S(1)} %get-tuple-element.20), channel_id=1, source_target_pairs={{0,15},{1,2},{2,1},{3,4},{4,3},{5,6},{6,5},{7,8},{8,7},{9,10},{10,... | collective-permute-start | bytes 786440 | tf_op jit(solution)/shard_map/ppermute | solution.py:486
  12.5 0.0 collective-permute-done.given_ref
  12.5 0.8 %take_given.1 = bf16[16,3,48,128]{3,2,1,0:T(8,128)(2,1)} custom-call(bf16[16,3,48,128]{3,2,1,0:T(8,128)(2,1)S(1)} %collective-permute-done.given_ref, bf16[16,3,48,128]{3,2,1,0:T(8,128)(2,1)} %get-tuple-element.18.kept_ref), custom_call_target="tpu_custom_call", output_to_operand_aliasing={{}: (1, {})} | custom-call | tf_op jit(solution)/shard_map/take_given/pallas_call | solution.py:360
  13.4 5.1 %all-to-all-start = ((bf16[16,3,48,128]{3,2,1,0:T(8,128)(2,1)}), bf16[16,3,48,128]{3,2,1,0:T(8,128)(2,1)S(1)}, u32[]{:S(2)}, u32[]{:S(2)}) async-start(bf16[16,3,48,128]{3,2,1,0:T(8,128)(2,1)} %take_given.1), calls=%async_computation | async-start | bytes 1179648 | tf_op jit(solution)/shard_map/all_to_all | solution.py:489
  18.4 0.0 copy-start.4
  18.4 0.0 copy-start.9
  18.5 0.0 copy-start.8
  18.5 0.0 collective-permute-done.1.near_ref
  18.5 0.0 collective-permute-done.2.far_ref
  18.5 0.0 copy-done.1
  18.5 0.0 copy-done.2
  18.5 5.9 %smooth_along_longitude.1 = (bf16[32,64,384]{2,1,0:T(8,128)(2,1)S(1)}, bf16[32,32,384]{2,1,0:T(8,128)(2,1)}, bf16[32,32,384]{2,1,0:T(8,128)(2,1)S(1)}) custom-call(s32[1024]{0:T(1024)S(1)} %copy-done.2, bf16[32,64,384]{2,1,0:T(8,128)(2,1)S(1)} %copy-done.1, bf16[1024,128]{1,0:T(8,128)(2,1)S(1)} %collective-permute-done.1.near_ref, ...), custom_call_target="tpu_custom_call" | custom-call | flops 68719476736 | bytes 16777216 | tf_op jit(solution)/shard_map/smooth_along_longitude/pallas_call | solution.py:317
  24.5 0.0 copy-start.6
  24.5 1.1 %copy-done.6 = bf16[32,64,384]{2,1,0:T(8,128)(2,1)} copy-done((bf16[32,64,384]{2,1,0:T(8,128)(2,1)}, bf16[32,64,384]{2,1,0:T(8,128)(2,1)S(1)}, u32[]{:S(2)}) %copy-start.6) | copy-done | bytes 1572888
  25.6 1.7 %collective-permute-start.3 = (bf16[32,32,384]{2,1,0:T(8,128)(2,1)}, bf16[32,32,384]{2,1,0:T(8,128)(2,1)S(1)}, u32[]{:S(2)}, u32[]{:S(2)}) collective-permute-start(bf16[32,32,384]{2,1,0:T(8,128)(2,1)} %get-tuple-element.22), channel_id=1, source_target_pairs={{0,16},{16,0},{32,48},{48,32},{64,80},{80,64},{96,112},{112,96},{1... | collective-permute-start | bytes 2359304 | tf_op jit(solution)/shard_map/ppermute | solution.py:495
  27.3 4.0 %collective-permute-start.4 = (bf16[32,32,384]{2,1,0:T(8,128)(2,1)S(1)}, bf16[32,32,384]{2,1,0:T(8,128)(2,1)}, u32[]{:S(2)}, u32[]{:S(2)}) collective-permute-start(bf16[32,32,384]{2,1,0:T(8,128)(2,1)S(1)} %get-tuple-element.21.after_ref), channel_id=1, source_target_pairs={{16,32},{32,16},{48,64},{64,48},{80,96},{96,80},{112,128},{128,112... | collective-permute-start | bytes 2359304 | tf_op jit(solution)/shard_map/ppermute | solution.py:492
  31.3 0.0 copy-done.4
  31.3 0.0 copy-done.9
  31.3 0.1 concatenate.3.table_ref
  31.4 0.0 copy-done.8
  31.4 0.1 copy.8.reach_ref
  31.5 0.0 copy-start.5
  31.5 4.5 %all-to-all-done.x_ref = bf16[16,3,48,128]{3,2,1,0:T(8,128)(2,1)S(1)} async-done(((bf16[16,3,48,128]{3,2,1,0:T(8,128)(2,1)}), bf16[16,3,48,128]{3,2,1,0:T(8,128)(2,1)S(1)}, u32[]{:S(2)}, u32[]{:S(2)}) %all-to-all-start) | async-done | bytes 589856 | tf_op jit(solution)/shard_map/all_to_all | solution.py:489
  36.0 2.3 %smooth_and_turn_polar_circles.1 = bf16[16,3,48,128]{3,2,1,0:T(8,128)(2,1)} custom-call(s32[1216]{0:T(1024)S(1)} %concatenate.3.table_ref, bf16[16,3,48,128]{3,2,1,0:T(8,128)(2,1)S(1)} %all-to-all-done.x_ref, bf16[32,32,384]{2,1,0:T(8,128)(2,1)S(1)} %get-tuple-element.21.after_ref), custom_call_target="tpu_custom_call" | custom-call | flops 1073741824 | bytes 4194304 | tf_op jit(solution)/shard_map/smooth_and_turn_polar_circles/pallas_call | solution.py:317
  38.3 4.3 %all-to-all-start.1 = ((bf16[16,3,48,128]{3,2,1,0:T(8,128)(2,1)}), bf16[16,3,48,128]{3,2,1,0:T(8,128)(2,1)S(1)}, u32[]{:S(2)}, u32[]{:S(2)}) async-start(bf16[16,3,48,128]{3,2,1,0:T(8,128)(2,1)} %smooth_and_turn_polar_circles.1), calls=%async_computation.1 | async-start | bytes 1179648 | tf_op jit(solution)/shard_map/all_to_all | solution.py:496
  42.5 0.0 collective-permute-done.3.near_ref
  42.6 0.0 collective-permute-done.4.far_ref
  42.6 0.0 copy-done.5
  42.6 0.0 copy-start.7
  42.6 1.4 %copy-done.7 = bf16[32,64,384]{2,1,0:T(8,128)(2,1)S(1)} copy-done((bf16[32,64,384]{2,1,0:T(8,128)(2,1)S(1)}, bf16[32,64,384]{2,1,0:T(8,128)(2,1)}, u32[]{:S(2)}) %copy-start.7) | copy-done | bytes 1572888
  44.0 3.2 %smooth_along_latitude.1 = (f32[32,64,384]{2,1,0:T(8,128)S(1)}, bf16[64,48]{1,0:T(8,128)(2,1)S(1)}, bf16[256,256]{1,0:T(8,128)(2,1)S(1)}) custom-call(s32[96]{0:T(128)S(1)} %copy-done.4, bf16[32,32,384]{2,1,0:T(8,128)(2,1)S(1)} %collective-permute-done.3.near_ref, bf16[32,64,384]{2,1,0:T(8,128)(2,1)S(1)} %copy-done.7, ...), custom_call_target="tpu_custom_call" | custom-call | flops 68719476736 | bytes 8388608 | tf_op jit(solution)/shard_map/smooth_along_latitude/pallas_call | solution.py:317
  47.2 0.0 copy-start
  47.2 1.6 %copy-done = f32[32,64,384]{2,1,0:T(8,128)} copy-done((f32[32,64,384]{2,1,0:T(8,128)}, f32[32,64,384]{2,1,0:T(8,128)S(1)}, u32[]{:S(2)}) %copy-start) | copy-done | bytes 3145752
  48.8 9.5 %all-to-all-done.1.mine_ref = bf16[16,3,48,128]{3,2,1,0:T(8,128)(2,1)S(1)} async-done(((bf16[16,3,48,128]{3,2,1,0:T(8,128)(2,1)}), bf16[16,3,48,128]{3,2,1,0:T(8,128)(2,1)S(1)}, u32[]{:S(2)}, u32[]{:S(2)}) %all-to-all-start.1) | async-done | bytes 589856 | tf_op jit(solution)/shard_map/all_to_all | solution.py:496
  58.3 6.1 %collective-permute-start.5 = (bf16[16,3,48,128]{3,2,1,0:T(8,128)(2,1)S(1)}, bf16[16,3,48,128]{3,2,1,0:T(8,128)(2,1)S(1)}, u32[]{:S(2)}, u32[]{:S(2)}) collective-permute-start(bf16[16,3,48,128]{3,2,1,0:T(8,128)(2,1)S(1)} %all-to-all-done.1.mine_ref), channel_id=1, source_target_pairs={{0,16},{16,0},{240,224},{224,240},{1,17},{17,1},{241,225},{225,241... | collective-permute-start | bytes 1769480 | tf_op jit(solution)/shard_map/ppermute | solution.py:501
  64.4 2.2 %add_polar_rows_of_own_shells.1.own_ref = bf16[16,64,384]{2,1,0:T(8,128)(2,1)S(1)} custom-call(bf16[16,3,48,128]{3,2,1,0:T(8,128)(2,1)S(1)} %all-to-all-done.1.mine_ref, bf16[64,48]{1,0:T(8,128)(2,1)S(1)} %get-tuple-element.26.weight_ref, f32[32,64,384]{2,1,0:T(8,128)} %copy-done), custom_call_target="tpu_custom_call" | custom-call | flops 1073741824 | bytes 4194304 | tf_op jit(solution)/shard_map/add_polar_rows_of_own_shells/pallas_call | solution.py:317
  66.6 0.0 collective-permute-done.5.other_ref
  66.6 3.9 %add_polar_rows_and_blend.1 = bf16[32,64,384]{2,1,0:T(8,128)(2,1)} custom-call(bf16[16,3,48,128]{3,2,1,0:T(8,128)(2,1)S(1)} %collective-permute-done.5.other_ref, bf16[16,64,384]{2,1,0:T(8,128)(2,1)S(1)} %add_polar_rows_of_own_shells.1.own_ref, bf16[64,48]{1,0:T(8,128)(2,1)S(1)} %get-tuple-element.26.weight_ref, ...), custom_call_target="tpu_custom_call" | custom-call | flops 2147483648 | bytes 8388608 | tf_op jit(solution)/shard_map/add_polar_rows_and_blend/pallas_call | solution.py:317
Async XLA Ops:
  0.0 0.7 copy-start.3
  3.4 15.1 %copy-start.1 = (bf16[32,64,384]{2,1,0:T(8,128)(2,1)S(1)}, bf16[32,64,384]{2,1,0:T(8,128)(2,1)}, u32[]{:S(2)}) copy-start(bf16[32,64,384]{2,1,0:T(8,128)(2,1)} %x_ref.3) | copy-start | bytes 4718596
  3.4 15.1 %copy-start.2 = (s32[1024]{0:T(1024)S(1)}, s32[1024]{0:T(1024)}, u32[]{:S(2)}) copy-start(s32[1024]{0:T(1024)} %halo_ref.1) | copy-start | bytes 12292
  3.4 9.1 %collective-permute-start = (bf16[16,3,48,128]{3,2,1,0:T(8,128)(2,1)S(1)}, bf16[16,3,48,128]{3,2,1,0:T(8,128)(2,1)S(1)}, u32[]{:S(2)}, u32[]{:S(2)}) collective-permute-start(bf16[16,3,48,128]{3,2,1,0:T(8,128)(2,1)S(1)} %get-tuple-element.17), channel_id=1, source_target_pairs={{0,16},{240,224},{1,17},{241,225},{2,18},{242,226},{3,19},{243,227... | collective-permute-start | bytes 1769480 | tf_op jit(solution)/shard_map/ppermute | solution.py:485
  4.8 13.6 %collective-permute-start.1 = (bf16[1024,128]{1,0:T(8,128)(2,1)S(1)}, bf16[1024,128]{1,0:T(8,128)(2,1)S(1)}, u32[]{:S(2)}, u32[]{:S(2)}) collective-permute-start(bf16[1024,128]{1,0:T(8,128)(2,1)S(1)} %get-tuple-element.19), channel_id=1, source_target_pairs={{0,1},{1,0},{2,3},{3,2},{4,5},{5,4},{6,7},{7,6},{8,9},{9,8},{10,11... | collective-permute-start | bytes 786440 | tf_op jit(solution)/shard_map/ppermute | solution.py:487
  7.1 11.4 %collective-permute-start.2 = (bf16[1024,128]{1,0:T(8,128)(2,1)S(1)}, bf16[1024,128]{1,0:T(8,128)(2,1)S(1)}, u32[]{:S(2)}, u32[]{:S(2)}) collective-permute-start(bf16[1024,128]{1,0:T(8,128)(2,1)S(1)} %get-tuple-element.20), channel_id=1, source_target_pairs={{0,15},{1,2},{2,1},{3,4},{4,3},{5,6},{6,5},{7,8},{8,7},{9,10},{10,... | collective-permute-start | bytes 786440 | tf_op jit(solution)/shard_map/ppermute | solution.py:486
  13.4 22.6 %all-to-all-start = ((bf16[16,3,48,128]{3,2,1,0:T(8,128)(2,1)}), bf16[16,3,48,128]{3,2,1,0:T(8,128)(2,1)S(1)}, u32[]{:S(2)}, u32[]{:S(2)}) async-start(bf16[16,3,48,128]{3,2,1,0:T(8,128)(2,1)} %take_given.1), calls=%async_computation | async-start | bytes 1179648 | tf_op jit(solution)/shard_map/all_to_all | solution.py:489
  18.4 12.9 %copy-start.4 = (s32[96]{0:T(128)S(1)}, s32[96]{0:T(128)}, u32[]{:S(2)}) copy-start(s32[96]{0:T(128)} %rows_ref.1) | copy-start | bytes 1156
  18.4 12.9 %copy-start.9 = (s32[96]{0:T(128)S(1)}, s32[96]{0:T(128)}, u32[]{:S(2)}) copy-start(s32[96]{0:T(128)} %param.10) | copy-start | bytes 1156
  18.5 12.9 %copy-start.8 = (s32[64]{0:T(128)S(1)}, s32[64]{0:T(128)}, u32[]{:S(2)}) copy-start(s32[64]{0:T(128)} %param.8) | copy-start | bytes 772
  24.5 1.1 %copy-start.6 = (bf16[32,64,384]{2,1,0:T(8,128)(2,1)}, bf16[32,64,384]{2,1,0:T(8,128)(2,1)S(1)}, u32[]{:S(2)}) copy-start(bf16[32,64,384]{2,1,0:T(8,128)(2,1)S(1)} %get-tuple-element.23.own_ref) | copy-start | bytes 4718596
  25.6 17.0 %collective-permute-start.3 = (bf16[32,32,384]{2,1,0:T(8,128)(2,1)}, bf16[32,32,384]{2,1,0:T(8,128)(2,1)S(1)}, u32[]{:S(2)}, u32[]{:S(2)}) collective-permute-start(bf16[32,32,384]{2,1,0:T(8,128)(2,1)} %get-tuple-element.22), channel_id=1, source_target_pairs={{0,16},{16,0},{32,48},{48,32},{64,80},{80,64},{96,112},{112,96},{1... | collective-permute-start | bytes 2359304 | tf_op jit(solution)/shard_map/ppermute | solution.py:495
  27.3 15.3 %collective-permute-start.4 = (bf16[32,32,384]{2,1,0:T(8,128)(2,1)S(1)}, bf16[32,32,384]{2,1,0:T(8,128)(2,1)}, u32[]{:S(2)}, u32[]{:S(2)}) collective-permute-start(bf16[32,32,384]{2,1,0:T(8,128)(2,1)S(1)} %get-tuple-element.21.after_ref), channel_id=1, source_target_pairs={{16,32},{32,16},{48,64},{64,48},{80,96},{96,80},{112,128},{128,112... | collective-permute-start | bytes 2359304 | tf_op jit(solution)/shard_map/ppermute | solution.py:492
  31.5 11.1 %copy-start.5 = (bf16[32,32]{1,0:T(8,128)(2,1)S(1)}, bf16[32,32]{1,0:T(8,128)(2,1)}, u32[]{:S(2)}) copy-start(bf16[32,32]{1,0:T(8,128)(2,1)} %blend_ref.1) | copy-start | bytes 6148
  38.3 20.0 %all-to-all-start.1 = ((bf16[16,3,48,128]{3,2,1,0:T(8,128)(2,1)}), bf16[16,3,48,128]{3,2,1,0:T(8,128)(2,1)S(1)}, u32[]{:S(2)}, u32[]{:S(2)}) async-start(bf16[16,3,48,128]{3,2,1,0:T(8,128)(2,1)} %smooth_and_turn_polar_circles.1), calls=%async_computation.1 | async-start | bytes 1179648 | tf_op jit(solution)/shard_map/all_to_all | solution.py:496
  42.6 1.4 %copy-start.7 = (bf16[32,64,384]{2,1,0:T(8,128)(2,1)S(1)}, bf16[32,64,384]{2,1,0:T(8,128)(2,1)}, u32[]{:S(2)}) copy-start(bf16[32,64,384]{2,1,0:T(8,128)(2,1)} %copy-done.6) | copy-start | bytes 4718596
  47.2 1.6 %copy-start = (f32[32,64,384]{2,1,0:T(8,128)}, f32[32,64,384]{2,1,0:T(8,128)S(1)}, u32[]{:S(2)}) copy-start(f32[32,64,384]{2,1,0:T(8,128)S(1)} %get-tuple-element.27.lat_ref) | copy-start | bytes 9437188
  58.3 8.3 %collective-permute-start.5 = (bf16[16,3,48,128]{3,2,1,0:T(8,128)(2,1)S(1)}, bf16[16,3,48,128]{3,2,1,0:T(8,128)(2,1)S(1)}, u32[]{:S(2)}, u32[]{:S(2)}) collective-permute-start(bf16[16,3,48,128]{3,2,1,0:T(8,128)(2,1)S(1)} %all-to-all-done.1.mine_ref), channel_id=1, source_target_pairs={{0,16},{16,0},{240,224},{224,240},{1,17},{17,1},{241,225},{225,241... | collective-permute-start | bytes 1769480 | tf_op jit(solution)/shard_map/ppermute | solution.py:501

commit v11 on v10

--- a/solution.py
+++ b/solution.py
@@ -9,6 +9,7 @@
 LMAX = 32
 LANES = 128
 PART = 16
+PIECES = 8
 UNROLL = 8
 PITCH = 65
 F32 = jnp.float32
@@ -19,21 +20,36 @@
     return lax.broadcasted_iota(jnp.int32, (rows, LANES), 1)
 
 
+def places(tile):
+    first = tile * LANES // HMAX
+    last = ((tile + 1) * LANES - 1) // HMAX
+    return [(piece, piece * HMAX - tile * LANES) for piece in range(first, last + 1)]
+
+
 def write_edges(x_ref, near_ref, far_ref):
     shells, row_count, col_count = x_ref.shape
-    half = shells // 2
-    size = half * row_count
+    some = shells // PIECES
+    size = some * row_count
     lane = lanes_of(size)
-
-    def part(column, shell):
-        return x_ref[shell : shell + half, :, column : column + LANES].reshape(size, LANES).astype(F32)
-
     last = col_count - LANES
     even = lax.rem(lax.axis_index("sector"), 2) == 0
-    low = jnp.where(lane < HMAX, part(0, 0), pltpu.roll(part(0, half), HMAX, 1))
-    high = jnp.where(lane < HMAX, pltpu.roll(part(last, 0), HMAX, 1), pltpu.roll(part(last, half), 2 * HMAX, 1))
-    near_ref[...] = jnp.where(even, high, low).astype(BF16)
-    far_ref[...] = jnp.where(even, low, high).astype(BF16)
+
+    def packed(column, turn, tile):
+        result = None
+        for piece, place in places(tile):
+            values = x_ref[piece * some : (piece + 1) * some, :, column : column + LANES].reshape(size, LANES)
+            shift = (place + turn) % LANES
+            values = values.astype(F32)
+            values = pltpu.roll(values, shift, 1) if shift else values
+            result = values if result is None else jnp.where(lane < place, result, values)
+        return result
+
+    for tile in range(PIECES * HMAX // LANES):
+        low = packed(0, 0, tile)
+        high = packed(last, HMAX, tile)
+        rows = slice(tile * size, (tile + 1) * size)
+        near_ref[rows, :] = jnp.where(even, high, low).astype(BF16)
+        far_ref[rows, :] = jnp.where(even, low, high).astype(BF16)
 
 
 def write_polar(half, rows_ref, x_ref, send_ref, wide_ref):
@@ -95,8 +111,8 @@
 def lon_kernel(halo_ref, x_ref, near_ref, far_ref,
                out_ref, near_rows_ref, far_rows_ref, wide_ref, done_ref, half_ref, rate_ref, scale_ref):
     shells, row_count, col_count = x_ref.shape
-    total = shells * row_count
-    size = total // 2
+    some = shells // PIECES
+    size = some * row_count
     tiles = col_count // LANES
     zone = lax.axis_index("zone")
     for i in range(row_count):
@@ -104,27 +120,35 @@
     rate_ref[...], scale_ref[...] = band_terms(half_ref[...])
     lane = lanes_of(size)
     even = lax.rem(lax.axis_index("sector"), 2) == 0
-    near = near_ref[...].astype(F32)
-    far = far_ref[...].astype(F32)
-    before = jnp.where(even, far, near)
-    after = jnp.where(even, near, far)
-
-    def keep(t, part, values):
-        for s in range(shells // 2):
-            first = (part * (shells // 2) + s) * PITCH
-            wide_ref[t, first : first + row_count, :] = values[s * row_count : (s + 1) * row_count]
-
-    for part in range(2):
-        shell = slice(part * (shells // 2), (part + 1) * (shells // 2))
-        previous = before if part == 0 else pltpu.roll(before, LANES - HMAX, 1)
+
+    def unpacked(piece, turn, first, second):
+        result = None
+        for tile in range(piece * HMAX // LANES, ((piece + 1) * HMAX - 1) // LANES + 1):
+            rows = slice(tile * size, (tile + 1) * size)
+            place = piece * HMAX - tile * LANES
+            values = jnp.where(even, first[rows, :].astype(F32), second[rows, :].astype(F32))
+            shift = (turn - place) % LANES
+            values = pltpu.roll(values, shift, 1) if shift else values
+            result = values if result is None else jnp.where(lane < turn - place, result, values)
+        return result
+
+    for piece in range(PIECES):
+        shell = slice(piece * some, (piece + 1) * some)
+
+        def keep(t, values):
+            for s in range(some):
+                first = (piece * some + s) * PITCH
+                wide_ref[t, first : first + row_count, :] = values[s * row_count : (s + 1) * row_count]
+
+        previous = unpacked(piece, 0, far_ref, near_ref)
         for t in range(tiles):
             turned = pltpu.roll(
                 x_ref[shell, :, t * LANES : (t + 1) * LANES].reshape(size, LANES).astype(F32), HMAX, 1
             )
-            keep(t, part, jnp.where(lane < HMAX, previous, turned))
+            keep(t, jnp.where(lane < HMAX, previous, turned))
             previous = turned
-        edge = pltpu.roll(after, HMAX, 1) if part == 0 else after
-        keep(tiles, part, jnp.where(lane < HMAX, previous, jnp.where(lane < 2 * HMAX, edge, 0.0)))
+        after = unpacked(piece, HMAX, near_ref, far_ref)
+        keep(tiles, jnp.where(lane < HMAX, previous, jnp.where(lane < 2 * HMAX, after, 0.0)))
     depth = 2 * LANES
     offset = (lanes_of(depth) - lax.broadcasted_iota(jnp.int32, (depth, LANES), 0) + HMAX).astype(F32)
     square = offset * offset
@@ -333,7 +357,7 @@
     shells, row_count, col_count = kernel.shape
     tiles = col_count // LANES
     held = polar_rows.shape[0] // 2 // sectors
-    edge = struct((shells * row_count // 2, LANES), BF16)
+    edge = struct((shells * row_count * HMAX // LANES, LANES), BF16)
     parts = struct((sectors, held, tiles * PART, LANES), BF16)
     vmem = pl.BlockSpec(memory_space=pltpu.VMEM)
     anywhere = pl.BlockSpec(memory_space=pl.ANY)

time: 71 us -> 71.6 us (level)
  waiting for transfers between devices: 14 us -> 19.2 us
  starting transfers between devices: 30.2 us -> 25.3 us
    all_to_all x1, waiting for transfers between devices: 4.49 us -> 8.64 us  [per_device(): circles = lax.all_to_all(parts, 'sector', 0, 0, tiled=True)]
    ppermute x1, starting transfers between devices: 3.96 us -> 1.92 us  [per_device(): lax.ppermute(far_rows, 'zone', [(i, i + 1 if i % 2 else i - 1) for i in r...]
    ppermute x1, starting transfers between devices: 6.09 us -> 4.63 us  [per_device(): lax.ppermute(mine, 'zone', [(0, 1), (1, 0), (last, last - 1), (last - 1,...]
    ppermute x1, starting transfers between devices: 1.71 us -> 0.6 us  [per_device(): lax.ppermute(near_rows, 'zone', [(i, i ^ 1) for i in range(zones)])]
    all_to_all x1, waiting for transfers between devices: 9.46 us -> 10.5 us  [per_device(): mine = lax.all_to_all(turned, 'sector', 0, 0, tiled=True)]
  transfers between devices with their start and end apart: 8 -> 8, of which waited for: 2 -> 2; matrix products, arithmetic and copies ran while one was open for 0% -> 0% of each run, Pallas kernels for 20% -> 21%
where the time goes in v11:
time: 71.6 us; the launch traced here: 71.1 us
  starting transfers between devices  25.3 us (35%)
  Pallas kernels  21.3 us (30%)
  waiting for transfers between devices  19.2 us (27%)
  local copies, waits for them, and re-layouts  5.05 us (7%)
    pallas_call x5, Pallas kernels, call(): pl.pallas_call(kernel, out_shape=out_shape, in_specs=[smem] * len(scalars...  17.7 us
    all_to_all x1, waiting for transfers between devices, per_device(): mine = lax.all_to_all(turned, 'sector', 0, 0, tiled=True)  10.5 us
    all_to_all x1, waiting for transfers between devices, per_device(): circles = lax.all_to_all(parts, 'sector', 0, 0, tiled=True)  8.64 us
    ppermute x1, starting transfers between devices, per_device(): lax.ppermute(far, 'sector', [(i, (i + 1 if i % 2 else i - 1) % sectors) f...  5.46 us
    all_to_all x1, starting transfers between devices, per_device(): circles = lax.all_to_all(parts, 'sector', 0, 0, tiled=True)  5.06 us
    unnamed x20, local copies, waits for them, and re-layouts  4.87 us
    ppermute x1, starting transfers between devices, per_device(): lax.ppermute(mine, 'zone', [(0, 1), (1, 0), (last, last - 1), (last - 1,...  4.63 us
    all_to_all x1, starting transfers between devices, per_device(): mine = lax.all_to_all(turned, 'sector', 0, 0, tiled=True)  3.98 us
  transfers between devices with their start and end apart: 8, of which 2 were waited for; matrix products, arithmetic and copies ran while one was open for 0% of the time, Pallas kernels for 21%

profile of v11, /device:TPU:1, one launch (start us, length us, event | category | flops | bytes accessed | tf_op | source)
XLA Modules:
  0.0 71.1 jit_solution(16180189957613247329)
XLA Ops:
  0.0 0.0 copy-start.3
  0.0 0.7 copy-done.3
  0.7 2.8 %pack_polar_rows_and_edges.1 = (bf16[16,3,48,128]{3,2,1,0:T(8,128)(2,1)S(1)}, bf16[768,128]{1,0:T(8,128)(2,1)S(1)}, bf16[768,128]{1,0:T(8,128)(2,1)S(1)}, bf16[16,3,48,128]{3,2,1,0:T(8,128)(2,1)}) custom-call(bf16[32,64,384]{2,1,0:T(8,128)(2,1)} %x_ref.3, s32[96]{0:T(128)S(1)} %copy-done.3), custom_call_target="tpu_custom_call" | custom-call | bytes 4194304 | tf_op jit(solution)/shard_map/pack_polar_rows_and_edges/pallas_call | solution.py:364
  3.5 0.0 copy-start.1
  3.5 0.0 copy-start.2
  3.5 1.4 %collective-permute-start = (bf16[16,3,48,128]{3,2,1,0:T(8,128)(2,1)S(1)}, bf16[16,3,48,128]{3,2,1,0:T(8,128)(2,1)S(1)}, u32[]{:S(2)}, u32[]{:S(2)}) collective-permute-start(bf16[16,3,48,128]{3,2,1,0:T(8,128)(2,1)S(1)} %get-tuple-element.17), channel_id=1, source_target_pairs={{0,16},{240,224},{1,17},{241,225},{2,18},{242,226},{3,19},{243,227... | collective-permute-start | bytes 1769480 | tf_op jit(solution)/shard_map/ppermute | solution.py:509
  4.9 2.2 %collective-permute-start.1 = (bf16[768,128]{1,0:T(8,128)(2,1)S(1)}, bf16[768,128]{1,0:T(8,128)(2,1)S(1)}, u32[]{:S(2)}, u32[]{:S(2)}) collective-permute-start(bf16[768,128]{1,0:T(8,128)(2,1)S(1)} %get-tuple-element.19), channel_id=1, source_target_pairs={{0,1},{1,0},{2,3},{3,2},{4,5},{5,4},{6,7},{7,6},{8,9},{9,8},{10,11... | collective-permute-start | bytes 589832 | tf_op jit(solution)/shard_map/ppermute | solution.py:511
  7.1 5.5 %collective-permute-start.2 = (bf16[768,128]{1,0:T(8,128)(2,1)S(1)}, bf16[768,128]{1,0:T(8,128)(2,1)S(1)}, u32[]{:S(2)}, u32[]{:S(2)}) collective-permute-start(bf16[768,128]{1,0:T(8,128)(2,1)S(1)} %get-tuple-element.20), channel_id=1, source_target_pairs={{0,15},{1,2},{2,1},{3,4},{4,3},{5,6},{6,5},{7,8},{8,7},{9,10},{10,... | collective-permute-start | bytes 589832 | tf_op jit(solution)/shard_map/ppermute | solution.py:510
  12.6 0.0 collective-permute-done.given_ref
  12.6 0.8 %take_given.1 = bf16[16,3,48,128]{3,2,1,0:T(8,128)(2,1)} custom-call(bf16[16,3,48,128]{3,2,1,0:T(8,128)(2,1)S(1)} %collective-permute-done.given_ref, bf16[16,3,48,128]{3,2,1,0:T(8,128)(2,1)} %get-tuple-element.18.kept_ref), custom_call_target="tpu_custom_call", output_to_operand_aliasing={{}: (1, {})} | custom-call | tf_op jit(solution)/shard_map/take_given/pallas_call | solution.py:384
  13.4 5.1 %all-to-all-start = ((bf16[16,3,48,128]{3,2,1,0:T(8,128)(2,1)}), bf16[16,3,48,128]{3,2,1,0:T(8,128)(2,1)S(1)}, u32[]{:S(2)}, u32[]{:S(2)}) async-start(bf16[16,3,48,128]{3,2,1,0:T(8,128)(2,1)} %take_given.1), calls=%async_computation | async-start | bytes 1179648 | tf_op jit(solution)/shard_map/all_to_all | solution.py:513
  18.5 0.0 copy-start.4
  18.5 0.0 copy-start.9
  18.5 0.0 copy-start.8
  18.5 0.0 collective-permute-done.1.near_ref
  18.5 0.0 collective-permute-done.2.far_ref
  18.5 0.0 copy-done.1
  18.6 0.0 copy-done.2
  18.6 6.2 %smooth_along_longitude.1 = (bf16[32,64,384]{2,1,0:T(8,128)(2,1)S(1)}, bf16[32,32,384]{2,1,0:T(8,128)(2,1)}, bf16[32,32,384]{2,1,0:T(8,128)(2,1)S(1)}) custom-call(s32[1024]{0:T(1024)S(1)} %copy-done.2, bf16[32,64,384]{2,1,0:T(8,128)(2,1)S(1)} %copy-done.1, bf16[768,128]{1,0:T(8,128)(2,1)S(1)} %collective-permute-done.1.near_ref, ...), custom_call_target="tpu_custom_call" | custom-call | flops 68719476736 | bytes 16777216 | tf_op jit(solution)/shard_map/smooth_along_longitude/pallas_call | solution.py:341
  24.7 0.0 copy-start.6
  24.7 1.1 %copy-done.6 = bf16[32,64,384]{2,1,0:T(8,128)(2,1)} copy-done((bf16[32,64,384]{2,1,0:T(8,128)(2,1)}, bf16[32,64,384]{2,1,0:T(8,128)(2,1)S(1)}, u32[]{:S(2)}) %copy-start.6) | copy-done | bytes 1572888
  25.9 0.6 collective-permute-start.3
  26.5 1.9 %collective-permute-start.4 = (bf16[32,32,384]{2,1,0:T(8,128)(2,1)S(1)}, bf16[32,32,384]{2,1,0:T(8,128)(2,1)}, u32[]{:S(2)}, u32[]{:S(2)}) collective-permute-start(bf16[32,32,384]{2,1,0:T(8,128)(2,1)S(1)} %get-tuple-element.21.after_ref), channel_id=1, source_target_pairs={{16,32},{32,16},{48,64},{64,48},{80,96},{96,80},{112,128},{128,112... | collective-permute-start | bytes 2359304 | tf_op jit(solution)/shard_map/ppermute | solution.py:516
  28.4 0.0 copy-done.4
  28.4 0.0 copy-done.9
  28.4 0.1 concatenate.3.table_ref
  28.5 0.0 copy-done.8
  28.5 0.1 copy.8.reach_ref
  28.6 0.0 copy-start.5
  28.6 8.6 %all-to-all-done.x_ref = bf16[16,3,48,128]{3,2,1,0:T(8,128)(2,1)S(1)} async-done(((bf16[16,3,48,128]{3,2,1,0:T(8,128)(2,1)}), bf16[16,3,48,128]{3,2,1,0:T(8,128)(2,1)S(1)}, u32[]{:S(2)}, u32[]{:S(2)}) %all-to-all-start) | async-done | bytes 589856 | tf_op jit(solution)/shard_map/all_to_all | solution.py:513
  37.2 2.3 %smooth_and_turn_polar_circles.1 = bf16[16,3,48,128]{3,2,1,0:T(8,128)(2,1)} custom-call(s32[1216]{0:T(1024)S(1)} %concatenate.3.table_ref, bf16[16,3,48,128]{3,2,1,0:T(8,128)(2,1)S(1)} %all-to-all-done.x_ref, bf16[32,32,384]{2,1,0:T(8,128)(2,1)S(1)} %get-tuple-element.21.after_ref), custom_call_target="tpu_custom_call" | custom-call | flops 1073741824 | bytes 4194304 | tf_op jit(solution)/shard_map/smooth_and_turn_polar_circles/pallas_call | solution.py:341
  39.5 4.0 %all-to-all-start.1 = ((bf16[16,3,48,128]{3,2,1,0:T(8,128)(2,1)}), bf16[16,3,48,128]{3,2,1,0:T(8,128)(2,1)S(1)}, u32[]{:S(2)}, u32[]{:S(2)}) async-start(bf16[16,3,48,128]{3,2,1,0:T(8,128)(2,1)} %smooth_and_turn_polar_circles.1), calls=%async_computation.1 | async-start | bytes 1179648 | tf_op jit(solution)/shard_map/all_to_all | solution.py:520
  43.5 0.0 collective-permute-done.3.near_ref
  43.5 0.0 collective-permute-done.4.far_ref
  43.5 0.0 copy-done.5
  43.5 0.0 copy-start.7
  43.5 1.4 %copy-done.7 = bf16[32,64,384]{2,1,0:T(8,128)(2,1)S(1)} copy-done((bf16[32,64,384]{2,1,0:T(8,128)(2,1)S(1)}, bf16[32,64,384]{2,1,0:T(8,128)(2,1)}, u32[]{:S(2)}) %copy-start.7) | copy-done | bytes 1572888
  44.9 3.2 %smooth_along_latitude.1 = (f32[32,64,384]{2,1,0:T(8,128)S(1)}, bf16[64,48]{1,0:T(8,128)(2,1)S(1)}, bf16[256,256]{1,0:T(8,128)(2,1)S(1)}) custom-call(s32[96]{0:T(128)S(1)} %copy-done.4, bf16[32,32,384]{2,1,0:T(8,128)(2,1)S(1)} %collective-permute-done.3.near_ref, bf16[32,64,384]{2,1,0:T(8,128)(2,1)S(1)} %copy-done.7, ...), custom_call_target="tpu_custom_call" | custom-call | flops 68719476736 | bytes 8388608 | tf_op jit(solution)/shard_map/smooth_along_latitude/pallas_call | solution.py:341
  48.1 0.0 copy-start
  48.1 1.6 %copy-done = f32[32,64,384]{2,1,0:T(8,128)} copy-done((f32[32,64,384]{2,1,0:T(8,128)}, f32[32,64,384]{2,1,0:T(8,128)S(1)}, u32[]{:S(2)}) %copy-start) | copy-done | bytes 3145752
  49.8 10.5 %all-to-all-done.1.mine_ref = bf16[16,3,48,128]{3,2,1,0:T(8,128)(2,1)S(1)} async-done(((bf16[16,3,48,128]{3,2,1,0:T(8,128)(2,1)}), bf16[16,3,48,128]{3,2,1,0:T(8,128)(2,1)S(1)}, u32[]{:S(2)}, u32[]{:S(2)}) %all-to-all-start.1) | async-done | bytes 589856 | tf_op jit(solution)/shard_map/all_to_all | solution.py:520
  60.3 4.6 %collective-permute-start.5 = (bf16[16,3,48,128]{3,2,1,0:T(8,128)(2,1)S(1)}, bf16[16,3,48,128]{3,2,1,0:T(8,128)(2,1)S(1)}, u32[]{:S(2)}, u32[]{:S(2)}) collective-permute-start(bf16[16,3,48,128]{3,2,1,0:T(8,128)(2,1)S(1)} %all-to-all-done.1.mine_ref), channel_id=1, source_target_pairs={{0,16},{16,0},{240,224},{224,240},{1,17},{17,1},{241,225},{225,241... | collective-permute-start | bytes 1769480 | tf_op jit(solution)/shard_map/ppermute | solution.py:525
  64.9 2.2 %add_polar_rows_of_own_shells.1.own_ref = bf16[16,64,384]{2,1,0:T(8,128)(2,1)S(1)} custom-call(bf16[16,3,48,128]{3,2,1,0:T(8,128)(2,1)S(1)} %all-to-all-done.1.mine_ref, bf16[64,48]{1,0:T(8,128)(2,1)S(1)} %get-tuple-element.26.weight_ref, f32[32,64,384]{2,1,0:T(8,128)} %copy-done), custom_call_target="tpu_custom_call" | custom-call | flops 1073741824 | bytes 4194304 | tf_op jit(solution)/shard_map/add_polar_rows_of_own_shells/pallas_call | solution.py:341
  67.1 0.0 collective-permute-done.5.other_ref
  67.1 3.9 %add_polar_rows_and_blend.1 = bf16[32,64,384]{2,1,0:T(8,128)(2,1)} custom-call(bf16[16,3,48,128]{3,2,1,0:T(8,128)(2,1)S(1)} %collective-permute-done.5.other_ref, bf16[16,64,384]{2,1,0:T(8,128)(2,1)S(1)} %add_polar_rows_of_own_shells.1.own_ref, bf16[64,48]{1,0:T(8,128)(2,1)S(1)} %get-tuple-element.26.weight_ref, ...), custom_call_target="tpu_custom_call" | custom-call | flops 2147483648 | bytes 8388608 | tf_op jit(solution)/shard_map/add_polar_rows_and_blend/pallas_call | solution.py:341
Async XLA Ops:
  0.0 0.7 copy-start.3
  3.5 15.1 %copy-start.1 = (bf16[32,64,384]{2,1,0:T(8,128)(2,1)S(1)}, bf16[32,64,384]{2,1,0:T(8,128)(2,1)}, u32[]{:S(2)}) copy-start(bf16[32,64,384]{2,1,0:T(8,128)(2,1)} %x_ref.3) | copy-start | bytes 4718596
  3.5 15.1 %copy-start.2 = (s32[1024]{0:T(1024)S(1)}, s32[1024]{0:T(1024)}, u32[]{:S(2)}) copy-start(s32[1024]{0:T(1024)} %halo_ref.1) | copy-start | bytes 12292
  3.5 9.1 %collective-permute-start = (bf16[16,3,48,128]{3,2,1,0:T(8,128)(2,1)S(1)}, bf16[16,3,48,128]{3,2,1,0:T(8,128)(2,1)S(1)}, u32[]{:S(2)}, u32[]{:S(2)}) collective-permute-start(bf16[16,3,48,128]{3,2,1,0:T(8,128)(2,1)S(1)} %get-tuple-element.17), channel_id=1, source_target_pairs={{0,16},{240,224},{1,17},{241,225},{2,18},{242,226},{3,19},{243,227... | collective-permute-start | bytes 1769480 | tf_op jit(solution)/shard_map/ppermute | solution.py:509
  4.9 13.6 %collective-permute-start.1 = (bf16[768,128]{1,0:T(8,128)(2,1)S(1)}, bf16[768,128]{1,0:T(8,128)(2,1)S(1)}, u32[]{:S(2)}, u32[]{:S(2)}) collective-permute-start(bf16[768,128]{1,0:T(8,128)(2,1)S(1)} %get-tuple-element.19), channel_id=1, source_target_pairs={{0,1},{1,0},{2,3},{3,2},{4,5},{5,4},{6,7},{7,6},{8,9},{9,8},{10,11... | collective-permute-start | bytes 589832 | tf_op jit(solution)/shard_map/ppermute | solution.py:511
  7.1 11.4 %collective-permute-start.2 = (bf16[768,128]{1,0:T(8,128)(2,1)S(1)}, bf16[768,128]{1,0:T(8,128)(2,1)S(1)}, u32[]{:S(2)}, u32[]{:S(2)}) collective-permute-start(bf16[768,128]{1,0:T(8,128)(2,1)S(1)} %get-tuple-element.20), channel_id=1, source_target_pairs={{0,15},{1,2},{2,1},{3,4},{4,3},{5,6},{6,5},{7,8},{8,7},{9,10},{10,... | collective-permute-start | bytes 589832 | tf_op jit(solution)/shard_map/ppermute | solution.py:510
  13.4 23.8 %all-to-all-start = ((bf16[16,3,48,128]{3,2,1,0:T(8,128)(2,1)}), bf16[16,3,48,128]{3,2,1,0:T(8,128)(2,1)S(1)}, u32[]{:S(2)}, u32[]{:S(2)}) async-start(bf16[16,3,48,128]{3,2,1,0:T(8,128)(2,1)} %take_given.1), calls=%async_computation | async-start | bytes 1179648 | tf_op jit(solution)/shard_map/all_to_all | solution.py:513
  18.5 9.9 %copy-start.4 = (s32[96]{0:T(128)S(1)}, s32[96]{0:T(128)}, u32[]{:S(2)}) copy-start(s32[96]{0:T(128)} %rows_ref.1) | copy-start | bytes 1156
  18.5 9.9 %copy-start.9 = (s32[96]{0:T(128)S(1)}, s32[96]{0:T(128)}, u32[]{:S(2)}) copy-start(s32[96]{0:T(128)} %param.10) | copy-start | bytes 1156
  18.5 10.0 %copy-start.8 = (s32[64]{0:T(128)S(1)}, s32[64]{0:T(128)}, u32[]{:S(2)}) copy-start(s32[64]{0:T(128)} %param.8) | copy-start | bytes 772
  24.7 1.1 %copy-start.6 = (bf16[32,64,384]{2,1,0:T(8,128)(2,1)}, bf16[32,64,384]{2,1,0:T(8,128)(2,1)S(1)}, u32[]{:S(2)}) copy-start(bf16[32,64,384]{2,1,0:T(8,128)(2,1)S(1)} %get-tuple-element.23.own_ref) | copy-start | bytes 4718596
  25.9 17.6 %collective-permute-start.3 = (bf16[32,32,384]{2,1,0:T(8,128)(2,1)}, bf16[32,32,384]{2,1,0:T(8,128)(2,1)S(1)}, u32[]{:S(2)}, u32[]{:S(2)}) collective-permute-start(bf16[32,32,384]{2,1,0:T(8,128)(2,1)} %get-tuple-element.22), channel_id=1, source_target_pairs={{0,16},{16,0},{32,48},{48,32},{64,80},{80,64},{96,112},{112,96},{1... | collective-permute-start | bytes 2359304 | tf_op jit(solution)/shard_map/ppermute | solution.py:519
  26.5 17.1 %collective-permute-start.4 = (bf16[32,32,384]{2,1,0:T(8,128)(2,1)S(1)}, bf16[32,32,384]{2,1,0:T(8,128)(2,1)}, u32[]{:S(2)}, u32[]{:S(2)}) collective-permute-start(bf16[32,32,384]{2,1,0:T(8,128)(2,1)S(1)} %get-tuple-element.21.after_ref), channel_id=1, source_target_pairs={{16,32},{32,16},{48,64},{64,48},{80,96},{96,80},{112,128},{128,112... | collective-permute-start | bytes 2359304 | tf_op jit(solution)/shard_map/ppermute | solution.py:516
  28.6 14.9 %copy-start.5 = (bf16[32,32]{1,0:T(8,128)(2,1)S(1)}, bf16[32,32]{1,0:T(8,128)(2,1)}, u32[]{:S(2)}) copy-start(bf16[32,32]{1,0:T(8,128)(2,1)} %blend_ref.1) | copy-start | bytes 6148
  39.5 20.8 %all-to-all-start.1 = ((bf16[16,3,48,128]{3,2,1,0:T(8,128)(2,1)}), bf16[16,3,48,128]{3,2,1,0:T(8,128)(2,1)S(1)}, u32[]{:S(2)}, u32[]{:S(2)}) async-start(bf16[16,3,48,128]{3,2,1,0:T(8,128)(2,1)} %smooth_and_turn_polar_circles.1), calls=%async_computation.1 | async-start | bytes 1179648 | tf_op jit(solution)/shard_map/all_to_all | solution.py:520
  43.5 1.4 %copy-start.7 = (bf16[32,64,384]{2,1,0:T(8,128)(2,1)S(1)}, bf16[32,64,384]{2,1,0:T(8,128)(2,1)}, u32[]{:S(2)}) copy-start(bf16[32,64,384]{2,1,0:T(8,128)(2,1)} %copy-done.6) | copy-start | bytes 4718596
  48.1 1.6 %copy-start = (f32[32,64,384]{2,1,0:T(8,128)}, f32[32,64,384]{2,1,0:T(8,128)S(1)}, u32[]{:S(2)}) copy-start(f32[32,64,384]{2,1,0:T(8,128)S(1)} %get-tuple-element.27.lat_ref) | copy-start | bytes 9437188
  60.3 6.8 %collective-permute-start.5 = (bf16[16,3,48,128]{3,2,1,0:T(8,128)(2,1)S(1)}, bf16[16,3,48,128]{3,2,1,0:T(8,128)(2,1)S(1)}, u32[]{:S(2)}, u32[]{:S(2)}) collective-permute-start(bf16[16,3,48,128]{3,2,1,0:T(8,128)(2,1)S(1)} %all-to-all-done.1.mine_ref), channel_id=1, source_target_pairs={{0,16},{16,0},{240,224},{224,240},{1,17},{17,1},{241,225},{225,241... | collective-permute-start | bytes 1769480 | tf_op jit(solution)/shard_map/ppermute | solution.py:525

commit v12 on v10

--- a/solution.py
+++ b/solution.py
@@ -262,16 +262,11 @@
     weight = weight_ref[...]
     fetch.wait()
 
-    def some_shells(index, carry):
-        for u in range(4):
-            s = index * 4 + u
-            values = jnp.concatenate(
-                [polar_ref[t, pl.ds(s * pitch, polar), :].astype(BF16) for t in range(tiles)], axis=1
-            )
-            put(s, sum_ref[s] + jnp.dot(weight, values, preferred_element_type=F32))
-        return carry
-
-    lax.fori_loop(0, PART // 4, some_shells, 0)
+    for s in range(PART):
+        values = jnp.concatenate(
+            [polar_ref[t, pl.ds(s * pitch, polar), :].astype(BF16) for t in range(tiles)], axis=1
+        )
+        put(s, sum_ref[s] + jnp.dot(weight, values, preferred_element_type=F32))
 
 
 def own_kernel(mine_ref, weight_ref, lat_ref, out_ref, polar_ref, sum_ref, sem):

time: 71 us -> 70.1 us (0.987)
  Pallas kernels: 21.1 us -> 20.1 us
    pallas_call x5, Pallas kernels: 17.5 us -> 16.6 us  [call(): pl.pallas_call(kernel, out_shape=out_shape, in_specs=[smem] * len(scalars...]
where the time goes in v12:
time: 70.1 us; the launch traced here: 69.6 us
  starting transfers between devices  30.2 us (43%)
  Pallas kernels  20.1 us (29%)
  waiting for transfers between devices  14 us (20%)
  local copies, waits for them, and re-layouts  5.05 us (7%)
    pallas_call x5, Pallas kernels, call(): pl.pallas_call(kernel, out_shape=out_shape, in_specs=[smem] * len(scalars...  16.6 us
    all_to_all x1, waiting for transfers between devices, per_device(): mine = lax.all_to_all(turned, 'sector', 0, 0, tiled=True)  9.46 us
    ppermute x1, starting transfers between devices, per_device(): lax.ppermute(mine, 'zone', [(0, 1), (1, 0), (last, last - 1), (last - 1,...  6.09 us
    ppermute x1, starting transfers between devices, per_device(): lax.ppermute(far, 'sector', [(i, (i + 1 if i % 2 else i - 1) % sectors) f...  5.46 us
    all_to_all x1, starting transfers between devices, per_device(): circles = lax.all_to_all(parts, 'sector', 0, 0, tiled=True)  5.06 us
    unnamed x20, local copies, waits for them, and re-layouts  4.87 us
    all_to_all x1, waiting for transfers between devices, per_device(): circles = lax.all_to_all(parts, 'sector', 0, 0, tiled=True)  4.49 us
    all_to_all x1, starting transfers between devices, per_device(): mine = lax.all_to_all(turned, 'sector', 0, 0, tiled=True)  4.29 us
  transfers between devices with their start and end apart: 8, of which 2 were waited for; matrix products, arithmetic and copies ran while one was open for 0% of the time, Pallas kernels for 20%

profile of v12, /device:TPU:1, one launch (start us, length us, event | category | flops | bytes accessed | tf_op | source)
XLA Modules:
  0.0 69.6 jit_solution(15600645979486498294)
XLA Ops:
  0.0 0.0 copy-start.3
  0.0 0.7 copy-done.3
  0.7 2.7 %pack_polar_rows_and_edges.1 = (bf16[16,3,48,128]{3,2,1,0:T(8,128)(2,1)S(1)}, bf16[1024,128]{1,0:T(8,128)(2,1)S(1)}, bf16[1024,128]{1,0:T(8,128)(2,1)S(1)}, bf16[16,3,48,128]{3,2,1,0:T(8,128)(2,1)}) custom-call(bf16[32,64,384]{2,1,0:T(8,128)(2,1)} %x_ref.3, s32[96]{0:T(128)S(1)} %copy-done.3), custom_call_target="tpu_custom_call" | custom-call | bytes 4194304 | tf_op jit(solution)/shard_map/pack_polar_rows_and_edges/pallas_call | solution.py:335
  3.4 0.0 copy-start.1
  3.4 0.0 copy-start.2
  3.4 1.4 %collective-permute-start = (bf16[16,3,48,128]{3,2,1,0:T(8,128)(2,1)S(1)}, bf16[16,3,48,128]{3,2,1,0:T(8,128)(2,1)S(1)}, u32[]{:S(2)}, u32[]{:S(2)}) collective-permute-start(bf16[16,3,48,128]{3,2,1,0:T(8,128)(2,1)S(1)} %get-tuple-element.17), channel_id=1, source_target_pairs={{0,16},{240,224},{1,17},{241,225},{2,18},{242,226},{3,19},{243,227... | collective-permute-start | bytes 1769480 | tf_op jit(solution)/shard_map/ppermute | solution.py:480
  4.8 2.2 %collective-permute-start.1 = (bf16[1024,128]{1,0:T(8,128)(2,1)S(1)}, bf16[1024,128]{1,0:T(8,128)(2,1)S(1)}, u32[]{:S(2)}, u32[]{:S(2)}) collective-permute-start(bf16[1024,128]{1,0:T(8,128)(2,1)S(1)} %get-tuple-element.19), channel_id=1, source_target_pairs={{0,1},{1,0},{2,3},{3,2},{4,5},{5,4},{6,7},{7,6},{8,9},{9,8},{10,11... | collective-permute-start | bytes 786440 | tf_op jit(solution)/shard_map/ppermute | solution.py:482
  7.1 5.5 %collective-permute-start.2 = (bf16[1024,128]{1,0:T(8,128)(2,1)S(1)}, bf16[1024,128]{1,0:T(8,128)(2,1)S(1)}, u32[]{:S(2)}, u32[]{:S(2)}) collective-permute-start(bf16[1024,128]{1,0:T(8,128)(2,1)S(1)} %get-tuple-element.20), channel_id=1, source_target_pairs={{0,15},{1,2},{2,1},{3,4},{4,3},{5,6},{6,5},{7,8},{8,7},{9,10},{10,... | collective-permute-start | bytes 786440 | tf_op jit(solution)/shard_map/ppermute | solution.py:481
  12.5 0.0 collective-permute-done.given_ref
  12.5 0.8 %take_given.1 = bf16[16,3,48,128]{3,2,1,0:T(8,128)(2,1)} custom-call(bf16[16,3,48,128]{3,2,1,0:T(8,128)(2,1)S(1)} %collective-permute-done.given_ref, bf16[16,3,48,128]{3,2,1,0:T(8,128)(2,1)} %get-tuple-element.18.kept_ref), custom_call_target="tpu_custom_call", output_to_operand_aliasing={{}: (1, {})} | custom-call | tf_op jit(solution)/shard_map/take_given/pallas_call | solution.py:355
  13.4 5.1 %all-to-all-start = ((bf16[16,3,48,128]{3,2,1,0:T(8,128)(2,1)}), bf16[16,3,48,128]{3,2,1,0:T(8,128)(2,1)S(1)}, u32[]{:S(2)}, u32[]{:S(2)}) async-start(bf16[16,3,48,128]{3,2,1,0:T(8,128)(2,1)} %take_given.1), calls=%async_computation | async-start | bytes 1179648 | tf_op jit(solution)/shard_map/all_to_all | solution.py:484
  18.4 0.0 copy-start.4
  18.4 0.0 copy-start.9
  18.5 0.0 copy-start.8
  18.5 0.0 collective-permute-done.1.near_ref
  18.5 0.0 collective-permute-done.2.far_ref
  18.5 0.0 copy-done.1
  18.5 0.0 copy-done.2
  18.5 5.9 %smooth_along_longitude.1 = (bf16[32,64,384]{2,1,0:T(8,128)(2,1)S(1)}, bf16[32,32,384]{2,1,0:T(8,128)(2,1)}, bf16[32,32,384]{2,1,0:T(8,128)(2,1)S(1)}) custom-call(s32[1024]{0:T(1024)S(1)} %copy-done.2, bf16[32,64,384]{2,1,0:T(8,128)(2,1)S(1)} %copy-done.1, bf16[1024,128]{1,0:T(8,128)(2,1)S(1)} %collective-permute-done.1.near_ref, ...), custom_call_target="tpu_custom_call" | custom-call | flops 68719476736 | bytes 16777216 | tf_op jit(solution)/shard_map/smooth_along_longitude/pallas_call | solution.py:312
  24.5 0.0 copy-start.6
  24.5 1.1 %copy-done.6 = bf16[32,64,384]{2,1,0:T(8,128)(2,1)} copy-done((bf16[32,64,384]{2,1,0:T(8,128)(2,1)}, bf16[32,64,384]{2,1,0:T(8,128)(2,1)S(1)}, u32[]{:S(2)}) %copy-start.6) | copy-done | bytes 1572888
  25.6 1.7 %collective-permute-start.3 = (bf16[32,32,384]{2,1,0:T(8,128)(2,1)}, bf16[32,32,384]{2,1,0:T(8,128)(2,1)S(1)}, u32[]{:S(2)}, u32[]{:S(2)}) collective-permute-start(bf16[32,32,384]{2,1,0:T(8,128)(2,1)} %get-tuple-element.22), channel_id=1, source_target_pairs={{0,16},{16,0},{32,48},{48,32},{64,80},{80,64},{96,112},{112,96},{1... | collective-permute-start | bytes 2359304 | tf_op jit(solution)/shard_map/ppermute | solution.py:490
  27.3 4.0 %collective-permute-start.4 = (bf16[32,32,384]{2,1,0:T(8,128)(2,1)S(1)}, bf16[32,32,384]{2,1,0:T(8,128)(2,1)}, u32[]{:S(2)}, u32[]{:S(2)}) collective-permute-start(bf16[32,32,384]{2,1,0:T(8,128)(2,1)S(1)} %get-tuple-element.21.after_ref), channel_id=1, source_target_pairs={{16,32},{32,16},{48,64},{64,48},{80,96},{96,80},{112,128},{128,112... | collective-permute-start | bytes 2359304 | tf_op jit(solution)/shard_map/ppermute | solution.py:487
  31.3 0.0 copy-done.4
  31.3 0.0 copy-done.9
  31.3 0.1 concatenate.3.table_ref
  31.4 0.0 copy-done.8
  31.4 0.1 copy.8.reach_ref
  31.5 0.0 copy-start.5
  31.5 4.5 %all-to-all-done.x_ref = bf16[16,3,48,128]{3,2,1,0:T(8,128)(2,1)S(1)} async-done(((bf16[16,3,48,128]{3,2,1,0:T(8,128)(2,1)}), bf16[16,3,48,128]{3,2,1,0:T(8,128)(2,1)S(1)}, u32[]{:S(2)}, u32[]{:S(2)}) %all-to-all-start) | async-done | bytes 589856 | tf_op jit(solution)/shard_map/all_to_all | solution.py:484
  36.0 2.3 %smooth_and_turn_polar_circles.1 = bf16[16,3,48,128]{3,2,1,0:T(8,128)(2,1)} custom-call(s32[1216]{0:T(1024)S(1)} %concatenate.3.table_ref, bf16[16,3,48,128]{3,2,1,0:T(8,128)(2,1)S(1)} %all-to-all-done.x_ref, bf16[32,32,384]{2,1,0:T(8,128)(2,1)S(1)} %get-tuple-element.21.after_ref), custom_call_target="tpu_custom_call" | custom-call | flops 1073741824 | bytes 4194304 | tf_op jit(solution)/shard_map/smooth_and_turn_polar_circles/pallas_call | solution.py:312
  38.3 4.3 %all-to-all-start.1 = ((bf16[16,3,48,128]{3,2,1,0:T(8,128)(2,1)}), bf16[16,3,48,128]{3,2,1,0:T(8,128)(2,1)S(1)}, u32[]{:S(2)}, u32[]{:S(2)}) async-start(bf16[16,3,48,128]{3,2,1,0:T(8,128)(2,1)} %smooth_and_turn_polar_circles.1), calls=%async_computation.1 | async-start | bytes 1179648 | tf_op jit(solution)/shard_map/all_to_all | solution.py:491
  42.5 0.0 collective-permute-done.3.near_ref
  42.6 0.0 collective-permute-done.4.far_ref
  42.6 0.0 copy-done.5
  42.6 0.0 copy-start.7
  42.6 1.4 %copy-done.7 = bf16[32,64,384]{2,1,0:T(8,128)(2,1)S(1)} copy-done((bf16[32,64,384]{2,1,0:T(8,128)(2,1)S(1)}, bf16[32,64,384]{2,1,0:T(8,128)(2,1)}, u32[]{:S(2)}) %copy-start.7) | copy-done | bytes 1572888
  44.0 3.2 %smooth_along_latitude.1 = (f32[32,64,384]{2,1,0:T(8,128)S(1)}, bf16[64,48]{1,0:T(8,128)(2,1)S(1)}, bf16[256,256]{1,0:T(8,128)(2,1)S(1)}) custom-call(s32[96]{0:T(128)S(1)} %copy-done.4, bf16[32,32,384]{2,1,0:T(8,128)(2,1)S(1)} %collective-permute-done.3.near_ref, bf16[32,64,384]{2,1,0:T(8,128)(2,1)S(1)} %copy-done.7, ...), custom_call_target="tpu_custom_call" | custom-call | flops 68719476736 | bytes 8388608 | tf_op jit(solution)/shard_map/smooth_along_latitude/pallas_call | solution.py:312
  47.2 0.0 copy-start
  47.2 1.6 %copy-done = f32[32,64,384]{2,1,0:T(8,128)} copy-done((f32[32,64,384]{2,1,0:T(8,128)}, f32[32,64,384]{2,1,0:T(8,128)S(1)}, u32[]{:S(2)}) %copy-start) | copy-done | bytes 3145752
  48.8 9.5 %all-to-all-done.1.mine_ref = bf16[16,3,48,128]{3,2,1,0:T(8,128)(2,1)S(1)} async-done(((bf16[16,3,48,128]{3,2,1,0:T(8,128)(2,1)}), bf16[16,3,48,128]{3,2,1,0:T(8,128)(2,1)S(1)}, u32[]{:S(2)}, u32[]{:S(2)}) %all-to-all-start.1) | async-done | bytes 589856 | tf_op jit(solution)/shard_map/all_to_all | solution.py:491
  58.3 6.1 %collective-permute-start.5 = (bf16[16,3,48,128]{3,2,1,0:T(8,128)(2,1)S(1)}, bf16[16,3,48,128]{3,2,1,0:T(8,128)(2,1)S(1)}, u32[]{:S(2)}, u32[]{:S(2)}) collective-permute-start(bf16[16,3,48,128]{3,2,1,0:T(8,128)(2,1)S(1)} %all-to-all-done.1.mine_ref), channel_id=1, source_target_pairs={{0,16},{16,0},{240,224},{224,240},{1,17},{17,1},{241,225},{225,241... | collective-permute-start | bytes 1769480 | tf_op jit(solution)/shard_map/ppermute | solution.py:496
  64.4 1.8 %add_polar_rows_of_own_shells.1.own_ref = bf16[16,64,384]{2,1,0:T(8,128)(2,1)S(1)} custom-call(bf16[16,3,48,128]{3,2,1,0:T(8,128)(2,1)S(1)} %all-to-all-done.1.mine_ref, bf16[64,48]{1,0:T(8,128)(2,1)S(1)} %get-tuple-element.26.weight_ref, f32[32,64,384]{2,1,0:T(8,128)} %copy-done), custom_call_target="tpu_custom_call" | custom-call | flops 1073741824 | bytes 4194304 | tf_op jit(solution)/shard_map/add_polar_rows_of_own_shells/pallas_call | solution.py:312
  66.2 0.0 collective-permute-done.5.other_ref
  66.2 3.4 %add_polar_rows_and_blend.1 = bf16[32,64,384]{2,1,0:T(8,128)(2,1)} custom-call(bf16[16,3,48,128]{3,2,1,0:T(8,128)(2,1)S(1)} %collective-permute-done.5.other_ref, bf16[16,64,384]{2,1,0:T(8,128)(2,1)S(1)} %add_polar_rows_of_own_shells.1.own_ref, bf16[64,48]{1,0:T(8,128)(2,1)S(1)} %get-tuple-element.26.weight_ref, ...), custom_call_target="tpu_custom_call" | custom-call | flops 2147483648 | bytes 8388608 | tf_op jit(solution)/shard_map/add_polar_rows_and_blend/pallas_call | solution.py:312
Async XLA Ops:
  0.0 0.7 copy-start.3
  3.4 15.1 %copy-start.1 = (bf16[32,64,384]{2,1,0:T(8,128)(2,1)S(1)}, bf16[32,64,384]{2,1,0:T(8,128)(2,1)}, u32[]{:S(2)}) copy-start(bf16[32,64,384]{2,1,0:T(8,128)(2,1)} %x_ref.3) | copy-start | bytes 4718596
  3.4 15.1 %copy-start.2 = (s32[1024]{0:T(1024)S(1)}, s32[1024]{0:T(1024)}, u32[]{:S(2)}) copy-start(s32[1024]{0:T(1024)} %halo_ref.1) | copy-start | bytes 12292
  3.4 9.1 %collective-permute-start = (bf16[16,3,48,128]{3,2,1,0:T(8,128)(2,1)S(1)}, bf16[16,3,48,128]{3,2,1,0:T(8,128)(2,1)S(1)}, u32[]{:S(2)}, u32[]{:S(2)}) collective-permute-start(bf16[16,3,48,128]{3,2,1,0:T(8,128)(2,1)S(1)} %get-tuple-element.17), channel_id=1, source_target_pairs={{0,16},{240,224},{1,17},{241,225},{2,18},{242,226},{3,19},{243,227... | collective-permute-start | bytes 1769480 | tf_op jit(solution)/shard_map/ppermute | solution.py:480
  4.8 13.6 %collective-permute-start.1 = (bf16[1024,128]{1,0:T(8,128)(2,1)S(1)}, bf16[1024,128]{1,0:T(8,128)(2,1)S(1)}, u32[]{:S(2)}, u32[]{:S(2)}) collective-permute-start(bf16[1024,128]{1,0:T(8,128)(2,1)S(1)} %get-tuple-element.19), channel_id=1, source_target_pairs={{0,1},{1,0},{2,3},{3,2},{4,5},{5,4},{6,7},{7,6},{8,9},{9,8},{10,11... | collective-permute-start | bytes 786440 | tf_op jit(solution)/shard_map/ppermute | solution.py:482
  7.1 11.4 %collective-permute-start.2 = (bf16[1024,128]{1,0:T(8,128)(2,1)S(1)}, bf16[1024,128]{1,0:T(8,128)(2,1)S(1)}, u32[]{:S(2)}, u32[]{:S(2)}) collective-permute-start(bf16[1024,128]{1,0:T(8,128)(2,1)S(1)} %get-tuple-element.20), channel_id=1, source_target_pairs={{0,15},{1,2},{2,1},{3,4},{4,3},{5,6},{6,5},{7,8},{8,7},{9,10},{10,... | collective-permute-start | bytes 786440 | tf_op jit(solution)/shard_map/ppermute | solution.py:481
  13.4 22.6 %all-to-all-start = ((bf16[16,3,48,128]{3,2,1,0:T(8,128)(2,1)}), bf16[16,3,48,128]{3,2,1,0:T(8,128)(2,1)S(1)}, u32[]{:S(2)}, u32[]{:S(2)}) async-start(bf16[16,3,48,128]{3,2,1,0:T(8,128)(2,1)} %take_given.1), calls=%async_computation | async-start | bytes 1179648 | tf_op jit(solution)/shard_map/all_to_all | solution.py:484
  18.4 12.9 %copy-start.4 = (s32[96]{0:T(128)S(1)}, s32[96]{0:T(128)}, u32[]{:S(2)}) copy-start(s32[96]{0:T(128)} %rows_ref.1) | copy-start | bytes 1156
  18.4 12.9 %copy-start.9 = (s32[96]{0:T(128)S(1)}, s32[96]{0:T(128)}, u32[]{:S(2)}) copy-start(s32[96]{0:T(128)} %param.10) | copy-start | bytes 1156
  18.5 12.9 %copy-start.8 = (s32[64]{0:T(128)S(1)}, s32[64]{0:T(128)}, u32[]{:S(2)}) copy-start(s32[64]{0:T(128)} %param.8) | copy-start | bytes 772
  24.5 1.1 %copy-start.6 = (bf16[32,64,384]{2,1,0:T(8,128)(2,1)}, bf16[32,64,384]{2,1,0:T(8,128)(2,1)S(1)}, u32[]{:S(2)}) copy-start(bf16[32,64,384]{2,1,0:T(8,128)(2,1)S(1)} %get-tuple-element.23.own_ref) | copy-start | bytes 4718596
  25.6 17.0 %collective-permute-start.3 = (bf16[32,32,384]{2,1,0:T(8,128)(2,1)}, bf16[32,32,384]{2,1,0:T(8,128)(2,1)S(1)}, u32[]{:S(2)}, u32[]{:S(2)}) collective-permute-start(bf16[32,32,384]{2,1,0:T(8,128)(2,1)} %get-tuple-element.22), channel_id=1, source_target_pairs={{0,16},{16,0},{32,48},{48,32},{64,80},{80,64},{96,112},{112,96},{1... | collective-permute-start | bytes 2359304 | tf_op jit(solution)/shard_map/ppermute | solution.py:490
  27.3 15.3 %collective-permute-start.4 = (bf16[32,32,384]{2,1,0:T(8,128)(2,1)S(1)}, bf16[32,32,384]{2,1,0:T(8,128)(2,1)}, u32[]{:S(2)}, u32[]{:S(2)}) collective-permute-start(bf16[32,32,384]{2,1,0:T(8,128)(2,1)S(1)} %get-tuple-element.21.after_ref), channel_id=1, source_target_pairs={{16,32},{32,16},{48,64},{64,48},{80,96},{96,80},{112,128},{128,112... | collective-permute-start | bytes 2359304 | tf_op jit(solution)/shard_map/ppermute | solution.py:487
  31.5 11.1 %copy-start.5 = (bf16[32,32]{1,0:T(8,128)(2,1)S(1)}, bf16[32,32]{1,0:T(8,128)(2,1)}, u32[]{:S(2)}) copy-start(bf16[32,32]{1,0:T(8,128)(2,1)} %blend_ref.1) | copy-start | bytes 6148
  38.3 20.0 %all-to-all-start.1 = ((bf16[16,3,48,128]{3,2,1,0:T(8,128)(2,1)}), bf16[16,3,48,128]{3,2,1,0:T(8,128)(2,1)S(1)}, u32[]{:S(2)}, u32[]{:S(2)}) async-start(bf16[16,3,48,128]{3,2,1,0:T(8,128)(2,1)} %smooth_and_turn_polar_circles.1), calls=%async_computation.1 | async-start | bytes 1179648 | tf_op jit(solution)/shard_map/all_to_all | solution.py:491
  42.6 1.4 %copy-start.7 = (bf16[32,64,384]{2,1,0:T(8,128)(2,1)S(1)}, bf16[32,64,384]{2,1,0:T(8,128)(2,1)}, u32[]{:S(2)}) copy-start(bf16[32,64,384]{2,1,0:T(8,128)(2,1)} %copy-done.6) | copy-start | bytes 4718596
  47.2 1.6 %copy-start = (f32[32,64,384]{2,1,0:T(8,128)}, f32[32,64,384]{2,1,0:T(8,128)S(1)}, u32[]{:S(2)}) copy-start(f32[32,64,384]{2,1,0:T(8,128)S(1)} %get-tuple-element.27.lat_ref) | copy-start | bytes 9437188
  58.3 7.9 %collective-permute-start.5 = (bf16[16,3,48,128]{3,2,1,0:T(8,128)(2,1)S(1)}, bf16[16,3,48,128]{3,2,1,0:T(8,128)(2,1)S(1)}, u32[]{:S(2)}, u32[]{:S(2)}) collective-permute-start(bf16[16,3,48,128]{3,2,1,0:T(8,128)(2,1)S(1)} %all-to-all-done.1.mine_ref), channel_id=1, source_target_pairs={{0,16},{16,0},{240,224},{224,240},{1,17},{17,1},{241,225},{225,241... | collective-permute-start | bytes 1769480 | tf_op jit(solution)/shard_map/ppermute | solution.py:496

commit v13 on v12

--- a/solution.py
+++ b/solution.py
@@ -9,7 +9,7 @@
 LMAX = 32
 LANES = 128
 PART = 16
-UNROLL = 8
+UNROLL = 16
 PITCH = 65
 F32 = jnp.float32
 BF16 = jnp.bfloat16
@@ -231,14 +231,9 @@
     )
     rest = jnp.where(lax.rem(zone, 2) == 0, turned, rest).astype(BF16)
 
-    def some_shells(block, carry):
-        for u in range(4):
-            s = block * 4 + u
-            values = jnp.concatenate([near_ref[s], own_ref[s], far_ref[s]], axis=0)
-            out_ref[s] = jnp.dot(rest, values, preferred_element_type=F32)
-        return carry
-
-    lax.fori_loop(0, shells // 4, some_shells, 0)
+    for s in range(shells):
+        values = jnp.concatenate([near_ref[s], own_ref[s], far_ref[s]], axis=0)
+        out_ref[s] = jnp.dot(rest, values, preferred_element_type=F32)
 
 
 def own_part():

time: 70.1 us -> 70.1 us (level)
  waiting for transfers between devices: 14 us -> 16.1 us
  Pallas kernels: 20.1 us -> 18.5 us
    pallas_call x5, Pallas kernels: 16.6 us -> 14.9 us  [call(): pl.pallas_call(kernel, out_shape=out_shape, in_specs=[smem] * len(scalars...]
    all_to_all x1, waiting for transfers between devices: 4.49 us -> 5.58 us  [per_device(): circles = lax.all_to_all(parts, 'sector', 0, 0, tiled=True)]
    all_to_all x1, waiting for transfers between devices: 9.46 us -> 10.5 us  [per_device(): mine = lax.all_to_all(turned, 'sector', 0, 0, tiled=True)]
  transfers between devices with their start and end apart: 8 -> 8, of which waited for: 2 -> 2; matrix products, arithmetic and copies ran while one was open for 0% -> 0% of each run, Pallas kernels for 20% -> 18%
where the time goes in v13:
time: 70.1 us; the launch traced here: 69.6 us
  starting transfers between devices  29.7 us (42%)
  Pallas kernels  18.5 us (26%)
  waiting for transfers between devices  16.1 us (23%)
  local copies, waits for them, and re-layouts  5.05 us (7%)
    pallas_call x5, Pallas kernels, call(): pl.pallas_call(kernel, out_shape=out_shape, in_specs=[smem] * len(scalars...  14.9 us
    all_to_all x1, waiting for transfers between devices, per_device(): mine = lax.all_to_all(turned, 'sector', 0, 0, tiled=True)  10.5 us
    ppermute x1, starting transfers between devices, per_device(): lax.ppermute(mine, 'zone', [(0, 1), (1, 0), (last, last - 1), (last - 1,...  6.1 us
    all_to_all x1, waiting for transfers between devices, per_device(): circles = lax.all_to_all(parts, 'sector', 0, 0, tiled=True)  5.58 us
    ppermute x1, starting transfers between devices, per_device(): lax.ppermute(far, 'sector', [(i, (i + 1 if i % 2 else i - 1) % sectors) f...  5.46 us
    all_to_all x1, starting transfers between devices, per_device(): circles = lax.all_to_all(parts, 'sector', 0, 0, tiled=True)  5.06 us
    unnamed x20, local copies, waits for them, and re-layouts  4.87 us
    ppermute x1, starting transfers between devices, per_device(): lax.ppermute(far_rows, 'zone', [(i, i + 1 if i % 2 else i - 1) for i in r...  3.96 us
  transfers between devices with their start and end apart: 8, of which 2 were waited for; matrix products, arithmetic and copies ran while one was open for 0% of the time, Pallas kernels for 18%

profile of v13, /device:TPU:1, one launch (start us, length us, event | category | flops | bytes accessed | tf_op | source)
XLA Modules:
  0.0 69.6 jit_solution(6116581693138487784)
XLA Ops:
  0.0 0.0 copy-start.3
  0.0 0.7 copy-done.3
  0.7 2.7 %pack_polar_rows_and_edges.1 = (bf16[16,3,48,128]{3,2,1,0:T(8,128)(2,1)S(1)}, bf16[1024,128]{1,0:T(8,128)(2,1)S(1)}, bf16[1024,128]{1,0:T(8,128)(2,1)S(1)}, bf16[16,3,48,128]{3,2,1,0:T(8,128)(2,1)}) custom-call(bf16[32,64,384]{2,1,0:T(8,128)(2,1)} %x_ref.3, s32[96]{0:T(128)S(1)} %copy-done.3), custom_call_target="tpu_custom_call" | custom-call | bytes 4194304 | tf_op jit(solution)/shard_map/pack_polar_rows_and_edges/pallas_call | solution.py:330
  3.4 0.0 copy-start.1
  3.4 0.0 copy-start.2
  3.4 1.4 %collective-permute-start = (bf16[16,3,48,128]{3,2,1,0:T(8,128)(2,1)S(1)}, bf16[16,3,48,128]{3,2,1,0:T(8,128)(2,1)S(1)}, u32[]{:S(2)}, u32[]{:S(2)}) collective-permute-start(bf16[16,3,48,128]{3,2,1,0:T(8,128)(2,1)S(1)} %get-tuple-element.17), channel_id=1, source_target_pairs={{0,16},{240,224},{1,17},{241,225},{2,18},{242,226},{3,19},{243,227... | collective-permute-start | bytes 1769480 | tf_op jit(solution)/shard_map/ppermute | solution.py:475
  4.8 2.2 %collective-permute-start.1 = (bf16[1024,128]{1,0:T(8,128)(2,1)S(1)}, bf16[1024,128]{1,0:T(8,128)(2,1)S(1)}, u32[]{:S(2)}, u32[]{:S(2)}) collective-permute-start(bf16[1024,128]{1,0:T(8,128)(2,1)S(1)} %get-tuple-element.19), channel_id=1, source_target_pairs={{0,1},{1,0},{2,3},{3,2},{4,5},{5,4},{6,7},{7,6},{8,9},{9,8},{10,11... | collective-permute-start | bytes 786440 | tf_op jit(solution)/shard_map/ppermute | solution.py:477
  7.1 5.5 %collective-permute-start.2 = (bf16[1024,128]{1,0:T(8,128)(2,1)S(1)}, bf16[1024,128]{1,0:T(8,128)(2,1)S(1)}, u32[]{:S(2)}, u32[]{:S(2)}) collective-permute-start(bf16[1024,128]{1,0:T(8,128)(2,1)S(1)} %get-tuple-element.20), channel_id=1, source_target_pairs={{0,15},{1,2},{2,1},{3,4},{4,3},{5,6},{6,5},{7,8},{8,7},{9,10},{10,... | collective-permute-start | bytes 786440 | tf_op jit(solution)/shard_map/ppermute | solution.py:476
  12.5 0.0 collective-permute-done.given_ref
  12.5 0.8 %take_given.1 = bf16[16,3,48,128]{3,2,1,0:T(8,128)(2,1)} custom-call(bf16[16,3,48,128]{3,2,1,0:T(8,128)(2,1)S(1)} %collective-permute-done.given_ref, bf16[16,3,48,128]{3,2,1,0:T(8,128)(2,1)} %get-tuple-element.18.kept_ref), custom_call_target="tpu_custom_call", output_to_operand_aliasing={{}: (1, {})} | custom-call | tf_op jit(solution)/shard_map/take_given/pallas_call | solution.py:350
  13.4 5.1 %all-to-all-start = ((bf16[16,3,48,128]{3,2,1,0:T(8,128)(2,1)}), bf16[16,3,48,128]{3,2,1,0:T(8,128)(2,1)S(1)}, u32[]{:S(2)}, u32[]{:S(2)}) async-start(bf16[16,3,48,128]{3,2,1,0:T(8,128)(2,1)} %take_given.1), calls=%async_computation | async-start | bytes 1179648 | tf_op jit(solution)/shard_map/all_to_all | solution.py:479
  18.4 0.0 copy-start.4
  18.4 0.0 copy-start.9
  18.5 0.0 copy-start.8
  18.5 0.0 collective-permute-done.1.near_ref
  18.5 0.0 collective-permute-done.2.far_ref
  18.5 0.0 copy-done.1
  18.5 0.0 copy-done.2
  18.5 5.3 %smooth_along_longitude.1 = (bf16[32,64,384]{2,1,0:T(8,128)(2,1)S(1)}, bf16[32,32,384]{2,1,0:T(8,128)(2,1)}, bf16[32,32,384]{2,1,0:T(8,128)(2,1)S(1)}) custom-call(s32[1024]{0:T(1024)S(1)} %copy-done.2, bf16[32,64,384]{2,1,0:T(8,128)(2,1)S(1)} %copy-done.1, bf16[1024,128]{1,0:T(8,128)(2,1)S(1)} %collective-permute-done.1.near_ref, ...), custom_call_target="tpu_custom_call" | custom-call | flops 68719476736 | bytes 16777216 | tf_op jit(solution)/shard_map/smooth_along_longitude/pallas_call | solution.py:307
  23.8 0.0 copy-start.6
  23.8 1.1 %copy-done.6 = bf16[32,64,384]{2,1,0:T(8,128)(2,1)} copy-done((bf16[32,64,384]{2,1,0:T(8,128)(2,1)}, bf16[32,64,384]{2,1,0:T(8,128)(2,1)S(1)}, u32[]{:S(2)}) %copy-start.6) | copy-done | bytes 1572888
  25.0 1.7 %collective-permute-start.3 = (bf16[32,32,384]{2,1,0:T(8,128)(2,1)}, bf16[32,32,384]{2,1,0:T(8,128)(2,1)S(1)}, u32[]{:S(2)}, u32[]{:S(2)}) collective-permute-start(bf16[32,32,384]{2,1,0:T(8,128)(2,1)} %get-tuple-element.22), channel_id=1, source_target_pairs={{0,16},{16,0},{32,48},{48,32},{64,80},{80,64},{96,112},{112,96},{1... | collective-permute-start | bytes 2359304 | tf_op jit(solution)/shard_map/ppermute | solution.py:485
  26.7 4.0 %collective-permute-start.4 = (bf16[32,32,384]{2,1,0:T(8,128)(2,1)S(1)}, bf16[32,32,384]{2,1,0:T(8,128)(2,1)}, u32[]{:S(2)}, u32[]{:S(2)}) collective-permute-start(bf16[32,32,384]{2,1,0:T(8,128)(2,1)S(1)} %get-tuple-element.21.after_ref), channel_id=1, source_target_pairs={{16,32},{32,16},{48,64},{64,48},{80,96},{96,80},{112,128},{128,112... | collective-permute-start | bytes 2359304 | tf_op jit(solution)/shard_map/ppermute | solution.py:482
  30.7 0.0 copy-done.4
  30.7 0.0 copy-done.9
  30.7 0.1 concatenate.3.table_ref
  30.8 0.0 copy-done.8
  30.8 0.1 copy.8.reach_ref
  30.9 0.0 copy-start.5
  30.9 5.6 %all-to-all-done.x_ref = bf16[16,3,48,128]{3,2,1,0:T(8,128)(2,1)S(1)} async-done(((bf16[16,3,48,128]{3,2,1,0:T(8,128)(2,1)}), bf16[16,3,48,128]{3,2,1,0:T(8,128)(2,1)S(1)}, u32[]{:S(2)}, u32[]{:S(2)}) %all-to-all-start) | async-done | bytes 589856 | tf_op jit(solution)/shard_map/all_to_all | solution.py:479
  36.5 2.3 %smooth_and_turn_polar_circles.1 = bf16[16,3,48,128]{3,2,1,0:T(8,128)(2,1)} custom-call(s32[1216]{0:T(1024)S(1)} %concatenate.3.table_ref, bf16[16,3,48,128]{3,2,1,0:T(8,128)(2,1)S(1)} %all-to-all-done.x_ref, bf16[32,32,384]{2,1,0:T(8,128)(2,1)S(1)} %get-tuple-element.21.after_ref), custom_call_target="tpu_custom_call" | custom-call | flops 1073741824 | bytes 4194304 | tf_op jit(solution)/shard_map/smooth_and_turn_polar_circles/pallas_call | solution.py:307
  38.7 3.8 %all-to-all-start.1 = ((bf16[16,3,48,128]{3,2,1,0:T(8,128)(2,1)}), bf16[16,3,48,128]{3,2,1,0:T(8,128)(2,1)S(1)}, u32[]{:S(2)}, u32[]{:S(2)}) async-start(bf16[16,3,48,128]{3,2,1,0:T(8,128)(2,1)} %smooth_and_turn_polar_circles.1), calls=%async_computation.1 | async-start | bytes 1179648 | tf_op jit(solution)/shard_map/all_to_all | solution.py:486
  42.5 0.0 collective-permute-done.3.near_ref
  42.6 0.0 collective-permute-done.4.far_ref
  42.6 0.0 copy-done.5
  42.6 0.0 copy-start.7
  42.6 1.4 %copy-done.7 = bf16[32,64,384]{2,1,0:T(8,128)(2,1)S(1)} copy-done((bf16[32,64,384]{2,1,0:T(8,128)(2,1)S(1)}, bf16[32,64,384]{2,1,0:T(8,128)(2,1)}, u32[]{:S(2)}) %copy-start.7) | copy-done | bytes 1572888
  44.0 2.1 %smooth_along_latitude.1 = (f32[32,64,384]{2,1,0:T(8,128)S(1)}, bf16[64,48]{1,0:T(8,128)(2,1)S(1)}, bf16[256,256]{1,0:T(8,128)(2,1)S(1)}) custom-call(s32[96]{0:T(128)S(1)} %copy-done.4, bf16[32,32,384]{2,1,0:T(8,128)(2,1)S(1)} %collective-permute-done.3.near_ref, bf16[32,64,384]{2,1,0:T(8,128)(2,1)S(1)} %copy-done.7, ...), custom_call_target="tpu_custom_call" | custom-call | flops 68719476736 | bytes 8388608 | tf_op jit(solution)/shard_map/smooth_along_latitude/pallas_call | solution.py:307
  46.1 0.0 copy-start
  46.1 1.6 %copy-done = f32[32,64,384]{2,1,0:T(8,128)} copy-done((f32[32,64,384]{2,1,0:T(8,128)}, f32[32,64,384]{2,1,0:T(8,128)S(1)}, u32[]{:S(2)}) %copy-start) | copy-done | bytes 3145752
  47.7 10.5 %all-to-all-done.1.mine_ref = bf16[16,3,48,128]{3,2,1,0:T(8,128)(2,1)S(1)} async-done(((bf16[16,3,48,128]{3,2,1,0:T(8,128)(2,1)}), bf16[16,3,48,128]{3,2,1,0:T(8,128)(2,1)S(1)}, u32[]{:S(2)}, u32[]{:S(2)}) %all-to-all-start.1) | async-done | bytes 589856 | tf_op jit(solution)/shard_map/all_to_all | solution.py:486
  58.3 6.1 %collective-permute-start.5 = (bf16[16,3,48,128]{3,2,1,0:T(8,128)(2,1)S(1)}, bf16[16,3,48,128]{3,2,1,0:T(8,128)(2,1)S(1)}, u32[]{:S(2)}, u32[]{:S(2)}) collective-permute-start(bf16[16,3,48,128]{3,2,1,0:T(8,128)(2,1)S(1)} %all-to-all-done.1.mine_ref), channel_id=1, source_target_pairs={{0,16},{16,0},{240,224},{224,240},{1,17},{17,1},{241,225},{225,241... | collective-permute-start | bytes 1769480 | tf_op jit(solution)/shard_map/ppermute | solution.py:491
  64.4 1.8 %add_polar_rows_of_own_shells.1.own_ref = bf16[16,64,384]{2,1,0:T(8,128)(2,1)S(1)} custom-call(bf16[16,3,48,128]{3,2,1,0:T(8,128)(2,1)S(1)} %all-to-all-done.1.mine_ref, bf16[64,48]{1,0:T(8,128)(2,1)S(1)} %get-tuple-element.26.weight_ref, f32[32,64,384]{2,1,0:T(8,128)} %copy-done), custom_call_target="tpu_custom_call" | custom-call | flops 1073741824 | bytes 4194304 | tf_op jit(solution)/shard_map/add_polar_rows_of_own_shells/pallas_call | solution.py:307
  66.2 0.0 collective-permute-done.5.other_ref
  66.2 3.4 %add_polar_rows_and_blend.1 = bf16[32,64,384]{2,1,0:T(8,128)(2,1)} custom-call(bf16[16,3,48,128]{3,2,1,0:T(8,128)(2,1)S(1)} %collective-permute-done.5.other_ref, bf16[16,64,384]{2,1,0:T(8,128)(2,1)S(1)} %add_polar_rows_of_own_shells.1.own_ref, bf16[64,48]{1,0:T(8,128)(2,1)S(1)} %get-tuple-element.26.weight_ref, ...), custom_call_target="tpu_custom_call" | custom-call | flops 2147483648 | bytes 8388608 | tf_op jit(solution)/shard_map/add_polar_rows_and_blend/pallas_call | solution.py:307
Async XLA Ops:
  0.0 0.7 copy-start.3
  3.4 15.1 %copy-start.1 = (bf16[32,64,384]{2,1,0:T(8,128)(2,1)S(1)}, bf16[32,64,384]{2,1,0:T(8,128)(2,1)}, u32[]{:S(2)}) copy-start(bf16[32,64,384]{2,1,0:T(8,128)(2,1)} %x_ref.3) | copy-start | bytes 4718596
  3.4 15.1 %copy-start.2 = (s32[1024]{0:T(1024)S(1)}, s32[1024]{0:T(1024)}, u32[]{:S(2)}) copy-start(s32[1024]{0:T(1024)} %halo_ref.1) | copy-start | bytes 12292
  3.4 9.1 %collective-permute-start = (bf16[16,3,48,128]{3,2,1,0:T(8,128)(2,1)S(1)}, bf16[16,3,48,128]{3,2,1,0:T(8,128)(2,1)S(1)}, u32[]{:S(2)}, u32[]{:S(2)}) collective-permute-start(bf16[16,3,48,128]{3,2,1,0:T(8,128)(2,1)S(1)} %get-tuple-element.17), channel_id=1, source_target_pairs={{0,16},{240,224},{1,17},{241,225},{2,18},{242,226},{3,19},{243,227... | collective-permute-start | bytes 1769480 | tf_op jit(solution)/shard_map/ppermute | solution.py:475
  4.8 13.6 %collective-permute-start.1 = (bf16[1024,128]{1,0:T(8,128)(2,1)S(1)}, bf16[1024,128]{1,0:T(8,128)(2,1)S(1)}, u32[]{:S(2)}, u32[]{:S(2)}) collective-permute-start(bf16[1024,128]{1,0:T(8,128)(2,1)S(1)} %get-tuple-element.19), channel_id=1, source_target_pairs={{0,1},{1,0},{2,3},{3,2},{4,5},{5,4},{6,7},{7,6},{8,9},{9,8},{10,11... | collective-permute-start | bytes 786440 | tf_op jit(solution)/shard_map/ppermute | solution.py:477
  7.1 11.4 %collective-permute-start.2 = (bf16[1024,128]{1,0:T(8,128)(2,1)S(1)}, bf16[1024,128]{1,0:T(8,128)(2,1)S(1)}, u32[]{:S(2)}, u32[]{:S(2)}) collective-permute-start(bf16[1024,128]{1,0:T(8,128)(2,1)S(1)} %get-tuple-element.20), channel_id=1, source_target_pairs={{0,15},{1,2},{2,1},{3,4},{4,3},{5,6},{6,5},{7,8},{8,7},{9,10},{10,... | collective-permute-start | bytes 786440 | tf_op jit(solution)/shard_map/ppermute | solution.py:476
  13.4 23.1 %all-to-all-start = ((bf16[16,3,48,128]{3,2,1,0:T(8,128)(2,1)}), bf16[16,3,48,128]{3,2,1,0:T(8,128)(2,1)S(1)}, u32[]{:S(2)}, u32[]{:S(2)}) async-start(bf16[16,3,48,128]{3,2,1,0:T(8,128)(2,1)} %take_given.1), calls=%async_computation | async-start | bytes 1179648 | tf_op jit(solution)/shard_map/all_to_all | solution.py:479
  18.4 12.2 %copy-start.4 = (s32[96]{0:T(128)S(1)}, s32[96]{0:T(128)}, u32[]{:S(2)}) copy-start(s32[96]{0:T(128)} %rows_ref.1) | copy-start | bytes 1156
  18.4 12.2 %copy-start.9 = (s32[96]{0:T(128)S(1)}, s32[96]{0:T(128)}, u32[]{:S(2)}) copy-start(s32[96]{0:T(128)} %param.10) | copy-start | bytes 1156
  18.5 12.3 %copy-start.8 = (s32[64]{0:T(128)S(1)}, s32[64]{0:T(128)}, u32[]{:S(2)}) copy-start(s32[64]{0:T(128)} %param.8) | copy-start | bytes 772
  23.8 1.1 %copy-start.6 = (bf16[32,64,384]{2,1,0:T(8,128)(2,1)}, bf16[32,64,384]{2,1,0:T(8,128)(2,1)S(1)}, u32[]{:S(2)}) copy-start(bf16[32,64,384]{2,1,0:T(8,128)(2,1)S(1)} %get-tuple-element.23.own_ref) | copy-start | bytes 4718596
  25.0 17.6 %collective-permute-start.3 = (bf16[32,32,384]{2,1,0:T(8,128)(2,1)}, bf16[32,32,384]{2,1,0:T(8,128)(2,1)S(1)}, u32[]{:S(2)}, u32[]{:S(2)}) collective-permute-start(bf16[32,32,384]{2,1,0:T(8,128)(2,1)} %get-tuple-element.22), channel_id=1, source_target_pairs={{0,16},{16,0},{32,48},{48,32},{64,80},{80,64},{96,112},{112,96},{1... | collective-permute-start | bytes 2359304 | tf_op jit(solution)/shard_map/ppermute | solution.py:485
  26.7 15.9 %collective-permute-start.4 = (bf16[32,32,384]{2,1,0:T(8,128)(2,1)S(1)}, bf16[32,32,384]{2,1,0:T(8,128)(2,1)}, u32[]{:S(2)}, u32[]{:S(2)}) collective-permute-start(bf16[32,32,384]{2,1,0:T(8,128)(2,1)S(1)} %get-tuple-element.21.after_ref), channel_id=1, source_target_pairs={{16,32},{32,16},{48,64},{64,48},{80,96},{96,80},{112,128},{128,112... | collective-permute-start | bytes 2359304 | tf_op jit(solution)/shard_map/ppermute | solution.py:482
  30.9 11.7 %copy-start.5 = (bf16[32,32]{1,0:T(8,128)(2,1)S(1)}, bf16[32,32]{1,0:T(8,128)(2,1)}, u32[]{:S(2)}) copy-start(bf16[32,32]{1,0:T(8,128)(2,1)} %blend_ref.1) | copy-start | bytes 6148
  38.7 19.5 %all-to-all-start.1 = ((bf16[16,3,48,128]{3,2,1,0:T(8,128)(2,1)}), bf16[16,3,48,128]{3,2,1,0:T(8,128)(2,1)S(1)}, u32[]{:S(2)}, u32[]{:S(2)}) async-start(bf16[16,3,48,128]{3,2,1,0:T(8,128)(2,1)} %smooth_and_turn_polar_circles.1), calls=%async_computation.1 | async-start | bytes 1179648 | tf_op jit(solution)/shard_map/all_to_all | solution.py:486
  42.6 1.4 %copy-start.7 = (bf16[32,64,384]{2,1,0:T(8,128)(2,1)S(1)}, bf16[32,64,384]{2,1,0:T(8,128)(2,1)}, u32[]{:S(2)}) copy-start(bf16[32,64,384]{2,1,0:T(8,128)(2,1)} %copy-done.6) | copy-start | bytes 4718596
  46.1 1.6 %copy-start = (f32[32,64,384]{2,1,0:T(8,128)}, f32[32,64,384]{2,1,0:T(8,128)S(1)}, u32[]{:S(2)}) copy-start(f32[32,64,384]{2,1,0:T(8,128)S(1)} %get-tuple-element.27.lat_ref) | copy-start | bytes 9437188
  58.3 7.9 %collective-permute-start.5 = (bf16[16,3,48,128]{3,2,1,0:T(8,128)(2,1)S(1)}, bf16[16,3,48,128]{3,2,1,0:T(8,128)(2,1)S(1)}, u32[]{:S(2)}, u32[]{:S(2)}) collective-permute-start(bf16[16,3,48,128]{3,2,1,0:T(8,128)(2,1)S(1)} %all-to-all-done.1.mine_ref), channel_id=1, source_target_pairs={{0,16},{16,0},{240,224},{224,240},{1,17},{17,1},{241,225},{225,241... | collective-permute-start | bytes 1769480 | tf_op jit(solution)/shard_map/ppermute | solution.py:491

commit v14 on v13

--- a/solution.py
+++ b/solution.py
@@ -60,17 +60,17 @@
     fetch = pltpu.make_async_copy(far_rows_ref, rows_ref, sems.at[2])
     fetch.start()
     copies = []
-    for half in (1, 0):
+    for half in (0, 1):
         shells = pl.ds(half * PART, PART)
         copies.append(pltpu.make_async_copy(x_ref.at[shells], held_ref.at[shells], sems.at[half]))
         copies[-1].start()
     fetch.wait()
     copies[0].wait()
-    write_polar(1, rows_ref, held_ref, send_ref, wide_ref)
-    copies[1].wait()
     write_polar(0, rows_ref, held_ref, stage_ref, wide_ref)
     store = pltpu.make_async_copy(stage_ref, kept_ref, sems.at[3])
     store.start()
+    copies[1].wait()
+    write_polar(1, rows_ref, held_ref, send_ref, wide_ref)
     write_edges(held_ref, near_ref, far_ref)
     store.wait()
 

time: 70.1 us -> 69.6 us (level)
  no operation moved by 1% of the time
where the time goes in v14:
time: 69.6 us; the launch traced here: 69.1 us
  starting transfers between devices  29.8 us (43%)
  Pallas kernels  18 us (26%)
  waiting for transfers between devices  16.1 us (23%)
  local copies, waits for them, and re-layouts  5.05 us (7%)
    pallas_call x5, Pallas kernels, call(): pl.pallas_call(kernel, out_shape=out_shape, in_specs=[smem] * len(scalars...  14.9 us
    all_to_all x1, waiting for transfers between devices, per_device(): mine = lax.all_to_all(turned, 'sector', 0, 0, tiled=True)  10.5 us
    ppermute x1, starting transfers between devices, per_device(): lax.ppermute(mine, 'zone', [(0, 1), (1, 0), (last, last - 1), (last - 1,...  6.12 us
    all_to_all x1, waiting for transfers between devices, per_device(): circles = lax.all_to_all(parts, 'sector', 0, 0, tiled=True)  5.58 us
    ppermute x1, starting transfers between devices, per_device(): lax.ppermute(far, 'sector', [(i, (i + 1 if i % 2 else i - 1) % sectors) f...  5.46 us
    all_to_all x1, starting transfers between devices, per_device(): circles = lax.all_to_all(parts, 'sector', 0, 0, tiled=True)  5.06 us
    unnamed x20, local copies, waits for them, and re-layouts  4.87 us
    ppermute x1, starting transfers between devices, per_device(): lax.ppermute(far_rows, 'zone', [(i, i + 1 if i % 2 else i - 1) for i in r...  3.97 us
  transfers between devices with their start and end apart: 8, of which 2 were waited for; matrix products, arithmetic and copies ran while one was open for 0% of the time, Pallas kernels for 18%

profile of v14, /device:TPU:1, one launch (start us, length us, event | category | flops | bytes accessed | tf_op | source)
XLA Modules:
  0.0 69.1 jit_solution(9463574713446144497)
XLA Ops:
  0.0 0.0 copy-start.3
  0.0 0.7 copy-done.3
  0.7 2.2 %pack_polar_rows_and_edges.1 = (bf16[16,3,48,128]{3,2,1,0:T(8,128)(2,1)S(1)}, bf16[1024,128]{1,0:T(8,128)(2,1)S(1)}, bf16[1024,128]{1,0:T(8,128)(2,1)S(1)}, bf16[16,3,48,128]{3,2,1,0:T(8,128)(2,1)}) custom-call(bf16[32,64,384]{2,1,0:T(8,128)(2,1)} %x_ref.3, s32[96]{0:T(128)S(1)} %copy-done.3), custom_call_target="tpu_custom_call" | custom-call | bytes 4194304 | tf_op jit(solution)/shard_map/pack_polar_rows_and_edges/pallas_call | solution.py:330
  2.9 0.0 copy-start.1
  2.9 0.0 copy-start.2
  2.9 1.4 %collective-permute-start = (bf16[16,3,48,128]{3,2,1,0:T(8,128)(2,1)S(1)}, bf16[16,3,48,128]{3,2,1,0:T(8,128)(2,1)S(1)}, u32[]{:S(2)}, u32[]{:S(2)}) collective-permute-start(bf16[16,3,48,128]{3,2,1,0:T(8,128)(2,1)S(1)} %get-tuple-element.17), channel_id=1, source_target_pairs={{0,16},{240,224},{1,17},{241,225},{2,18},{242,226},{3,19},{243,227... | collective-permute-start | bytes 1769480 | tf_op jit(solution)/shard_map/ppermute | solution.py:475
  4.3 2.2 %collective-permute-start.1 = (bf16[1024,128]{1,0:T(8,128)(2,1)S(1)}, bf16[1024,128]{1,0:T(8,128)(2,1)S(1)}, u32[]{:S(2)}, u32[]{:S(2)}) collective-permute-start(bf16[1024,128]{1,0:T(8,128)(2,1)S(1)} %get-tuple-element.19), channel_id=1, source_target_pairs={{0,1},{1,0},{2,3},{3,2},{4,5},{5,4},{6,7},{7,6},{8,9},{9,8},{10,11... | collective-permute-start | bytes 786440 | tf_op jit(solution)/shard_map/ppermute | solution.py:477
  6.6 5.5 %collective-permute-start.2 = (bf16[1024,128]{1,0:T(8,128)(2,1)S(1)}, bf16[1024,128]{1,0:T(8,128)(2,1)S(1)}, u32[]{:S(2)}, u32[]{:S(2)}) collective-permute-start(bf16[1024,128]{1,0:T(8,128)(2,1)S(1)} %get-tuple-element.20), channel_id=1, source_target_pairs={{0,15},{1,2},{2,1},{3,4},{4,3},{5,6},{6,5},{7,8},{8,7},{9,10},{10,... | collective-permute-start | bytes 786440 | tf_op jit(solution)/shard_map/ppermute | solution.py:476
  12.0 0.0 collective-permute-done.given_ref
  12.0 0.8 %take_given.1 = bf16[16,3,48,128]{3,2,1,0:T(8,128)(2,1)} custom-call(bf16[16,3,48,128]{3,2,1,0:T(8,128)(2,1)S(1)} %collective-permute-done.given_ref, bf16[16,3,48,128]{3,2,1,0:T(8,128)(2,1)} %get-tuple-element.18.kept_ref), custom_call_target="tpu_custom_call", output_to_operand_aliasing={{}: (1, {})} | custom-call | tf_op jit(solution)/shard_map/take_given/pallas_call | solution.py:350
  12.8 5.1 %all-to-all-start = ((bf16[16,3,48,128]{3,2,1,0:T(8,128)(2,1)}), bf16[16,3,48,128]{3,2,1,0:T(8,128)(2,1)S(1)}, u32[]{:S(2)}, u32[]{:S(2)}) async-start(bf16[16,3,48,128]{3,2,1,0:T(8,128)(2,1)} %take_given.1), calls=%async_computation | async-start | bytes 1179648 | tf_op jit(solution)/shard_map/all_to_all | solution.py:479
  17.9 0.0 copy-start.4
  17.9 0.0 copy-start.9
  17.9 0.0 copy-start.8
  18.0 0.0 collective-permute-done.1.near_ref
  18.0 0.0 collective-permute-done.2.far_ref
  18.0 0.0 copy-done.1
  18.0 0.0 copy-done.2
  18.0 5.3 %smooth_along_longitude.1 = (bf16[32,64,384]{2,1,0:T(8,128)(2,1)S(1)}, bf16[32,32,384]{2,1,0:T(8,128)(2,1)}, bf16[32,32,384]{2,1,0:T(8,128)(2,1)S(1)}) custom-call(s32[1024]{0:T(1024)S(1)} %copy-done.2, bf16[32,64,384]{2,1,0:T(8,128)(2,1)S(1)} %copy-done.1, bf16[1024,128]{1,0:T(8,128)(2,1)S(1)} %collective-permute-done.1.near_ref, ...), custom_call_target="tpu_custom_call" | custom-call | flops 68719476736 | bytes 16777216 | tf_op jit(solution)/shard_map/smooth_along_longitude/pallas_call | solution.py:307
  23.3 0.0 copy-start.6
  23.3 1.1 %copy-done.6 = bf16[32,64,384]{2,1,0:T(8,128)(2,1)} copy-done((bf16[32,64,384]{2,1,0:T(8,128)(2,1)}, bf16[32,64,384]{2,1,0:T(8,128)(2,1)S(1)}, u32[]{:S(2)}) %copy-start.6) | copy-done | bytes 1572888
  24.5 1.7 %collective-permute-start.3 = (bf16[32,32,384]{2,1,0:T(8,128)(2,1)}, bf16[32,32,384]{2,1,0:T(8,128)(2,1)S(1)}, u32[]{:S(2)}, u32[]{:S(2)}) collective-permute-start(bf16[32,32,384]{2,1,0:T(8,128)(2,1)} %get-tuple-element.22), channel_id=1, source_target_pairs={{0,16},{16,0},{32,48},{48,32},{64,80},{80,64},{96,112},{112,96},{1... | collective-permute-start | bytes 2359304 | tf_op jit(solution)/shard_map/ppermute | solution.py:485
  26.2 4.0 %collective-permute-start.4 = (bf16[32,32,384]{2,1,0:T(8,128)(2,1)S(1)}, bf16[32,32,384]{2,1,0:T(8,128)(2,1)}, u32[]{:S(2)}, u32[]{:S(2)}) collective-permute-start(bf16[32,32,384]{2,1,0:T(8,128)(2,1)S(1)} %get-tuple-element.21.after_ref), channel_id=1, source_target_pairs={{16,32},{32,16},{48,64},{64,48},{80,96},{96,80},{112,128},{128,112... | collective-permute-start | bytes 2359304 | tf_op jit(solution)/shard_map/ppermute | solution.py:482
  30.2 0.0 copy-done.4
  30.2 0.0 copy-done.9
  30.2 0.1 concatenate.3.table_ref
  30.3 0.0 copy-done.8
  30.3 0.1 copy.8.reach_ref
  30.4 0.0 copy-start.5
  30.4 5.6 %all-to-all-done.x_ref = bf16[16,3,48,128]{3,2,1,0:T(8,128)(2,1)S(1)} async-done(((bf16[16,3,48,128]{3,2,1,0:T(8,128)(2,1)}), bf16[16,3,48,128]{3,2,1,0:T(8,128)(2,1)S(1)}, u32[]{:S(2)}, u32[]{:S(2)}) %all-to-all-start) | async-done | bytes 589856 | tf_op jit(solution)/shard_map/all_to_all | solution.py:479
  35.9 2.3 %smooth_and_turn_polar_circles.1 = bf16[16,3,48,128]{3,2,1,0:T(8,128)(2,1)} custom-call(s32[1216]{0:T(1024)S(1)} %concatenate.3.table_ref, bf16[16,3,48,128]{3,2,1,0:T(8,128)(2,1)S(1)} %all-to-all-done.x_ref, bf16[32,32,384]{2,1,0:T(8,128)(2,1)S(1)} %get-tuple-element.21.after_ref), custom_call_target="tpu_custom_call" | custom-call | flops 1073741824 | bytes 4194304 | tf_op jit(solution)/shard_map/smooth_and_turn_polar_circles/pallas_call | solution.py:307
  38.2 3.8 %all-to-all-start.1 = ((bf16[16,3,48,128]{3,2,1,0:T(8,128)(2,1)}), bf16[16,3,48,128]{3,2,1,0:T(8,128)(2,1)S(1)}, u32[]{:S(2)}, u32[]{:S(2)}) async-start(bf16[16,3,48,128]{3,2,1,0:T(8,128)(2,1)} %smooth_and_turn_polar_circles.1), calls=%async_computation.1 | async-start | bytes 1179648 | tf_op jit(solution)/shard_map/all_to_all | solution.py:486
  42.0 0.0 collective-permute-done.3.near_ref
  42.1 0.0 collective-permute-done.4.far_ref
  42.1 0.0 copy-done.5
  42.1 0.0 copy-start.7
  42.1 1.4 %copy-done.7 = bf16[32,64,384]{2,1,0:T(8,128)(2,1)S(1)} copy-done((bf16[32,64,384]{2,1,0:T(8,128)(2,1)S(1)}, bf16[32,64,384]{2,1,0:T(8,128)(2,1)}, u32[]{:S(2)}) %copy-start.7) | copy-done | bytes 1572888
  43.5 2.1 %smooth_along_latitude.1 = (f32[32,64,384]{2,1,0:T(8,128)S(1)}, bf16[64,48]{1,0:T(8,128)(2,1)S(1)}, bf16[256,256]{1,0:T(8,128)(2,1)S(1)}) custom-call(s32[96]{0:T(128)S(1)} %copy-done.4, bf16[32,32,384]{2,1,0:T(8,128)(2,1)S(1)} %collective-permute-done.3.near_ref, bf16[32,64,384]{2,1,0:T(8,128)(2,1)S(1)} %copy-done.7, ...), custom_call_target="tpu_custom_call" | custom-call | flops 68719476736 | bytes 8388608 | tf_op jit(solution)/shard_map/smooth_along_latitude/pallas_call | solution.py:307
  45.6 0.0 copy-start
  45.6 1.6 %copy-done = f32[32,64,384]{2,1,0:T(8,128)} copy-done((f32[32,64,384]{2,1,0:T(8,128)}, f32[32,64,384]{2,1,0:T(8,128)S(1)}, u32[]{:S(2)}) %copy-start) | copy-done | bytes 3145752
  47.2 10.5 %all-to-all-done.1.mine_ref = bf16[16,3,48,128]{3,2,1,0:T(8,128)(2,1)S(1)} async-done(((bf16[16,3,48,128]{3,2,1,0:T(8,128)(2,1)}), bf16[16,3,48,128]{3,2,1,0:T(8,128)(2,1)S(1)}, u32[]{:S(2)}, u32[]{:S(2)}) %all-to-all-start.1) | async-done | bytes 589856 | tf_op jit(solution)/shard_map/all_to_all | solution.py:486
  57.7 6.1 %collective-permute-start.5 = (bf16[16,3,48,128]{3,2,1,0:T(8,128)(2,1)S(1)}, bf16[16,3,48,128]{3,2,1,0:T(8,128)(2,1)S(1)}, u32[]{:S(2)}, u32[]{:S(2)}) collective-permute-start(bf16[16,3,48,128]{3,2,1,0:T(8,128)(2,1)S(1)} %all-to-all-done.1.mine_ref), channel_id=1, source_target_pairs={{0,16},{16,0},{240,224},{224,240},{1,17},{17,1},{241,225},{225,241... | collective-permute-start | bytes 1769480 | tf_op jit(solution)/shard_map/ppermute | solution.py:491
  63.9 1.8 %add_polar_rows_of_own_shells.1.own_ref = bf16[16,64,384]{2,1,0:T(8,128)(2,1)S(1)} custom-call(bf16[16,3,48,128]{3,2,1,0:T(8,128)(2,1)S(1)} %all-to-all-done.1.mine_ref, bf16[64,48]{1,0:T(8,128)(2,1)S(1)} %get-tuple-element.26.weight_ref, f32[32,64,384]{2,1,0:T(8,128)} %copy-done), custom_call_target="tpu_custom_call" | custom-call | flops 1073741824 | bytes 4194304 | tf_op jit(solution)/shard_map/add_polar_rows_of_own_shells/pallas_call | solution.py:307
  65.6 0.0 collective-permute-done.5.other_ref
  65.7 3.4 %add_polar_rows_and_blend.1 = bf16[32,64,384]{2,1,0:T(8,128)(2,1)} custom-call(bf16[16,3,48,128]{3,2,1,0:T(8,128)(2,1)S(1)} %collective-permute-done.5.other_ref, bf16[16,64,384]{2,1,0:T(8,128)(2,1)S(1)} %add_polar_rows_of_own_shells.1.own_ref, bf16[64,48]{1,0:T(8,128)(2,1)S(1)} %get-tuple-element.26.weight_ref, ...), custom_call_target="tpu_custom_call" | custom-call | flops 2147483648 | bytes 8388608 | tf_op jit(solution)/shard_map/add_polar_rows_and_blend/pallas_call | solution.py:307
Async XLA Ops:
  0.0 0.7 copy-start.3
  2.9 15.1 %copy-start.1 = (bf16[32,64,384]{2,1,0:T(8,128)(2,1)S(1)}, bf16[32,64,384]{2,1,0:T(8,128)(2,1)}, u32[]{:S(2)}) copy-start(bf16[32,64,384]{2,1,0:T(8,128)(2,1)} %x_ref.3) | copy-start | bytes 4718596
  2.9 15.1 %copy-start.2 = (s32[1024]{0:T(1024)S(1)}, s32[1024]{0:T(1024)}, u32[]{:S(2)}) copy-start(s32[1024]{0:T(1024)} %halo_ref.1) | copy-start | bytes 12292
  2.9 9.1 %collective-permute-start = (bf16[16,3,48,128]{3,2,1,0:T(8,128)(2,1)S(1)}, bf16[16,3,48,128]{3,2,1,0:T(8,128)(2,1)S(1)}, u32[]{:S(2)}, u32[]{:S(2)}) collective-permute-start(bf16[16,3,48,128]{3,2,1,0:T(8,128)(2,1)S(1)} %get-tuple-element.17), channel_id=1, source_target_pairs={{0,16},{240,224},{1,17},{241,225},{2,18},{242,226},{3,19},{243,227... | collective-permute-start | bytes 1769480 | tf_op jit(solution)/shard_map/ppermute | solution.py:475
  4.3 13.6 %collective-permute-start.1 = (bf16[1024,128]{1,0:T(8,128)(2,1)S(1)}, bf16[1024,128]{1,0:T(8,128)(2,1)S(1)}, u32[]{:S(2)}, u32[]{:S(2)}) collective-permute-start(bf16[1024,128]{1,0:T(8,128)(2,1)S(1)} %get-tuple-element.19), channel_id=1, source_target_pairs={{0,1},{1,0},{2,3},{3,2},{4,5},{5,4},{6,7},{7,6},{8,9},{9,8},{10,11... | collective-permute-start | bytes 786440 | tf_op jit(solution)/shard_map/ppermute | solution.py:477
  6.6 11.4 %collective-permute-start.2 = (bf16[1024,128]{1,0:T(8,128)(2,1)S(1)}, bf16[1024,128]{1,0:T(8,128)(2,1)S(1)}, u32[]{:S(2)}, u32[]{:S(2)}) collective-permute-start(bf16[1024,128]{1,0:T(8,128)(2,1)S(1)} %get-tuple-element.20), channel_id=1, source_target_pairs={{0,15},{1,2},{2,1},{3,4},{4,3},{5,6},{6,5},{7,8},{8,7},{9,10},{10,... | collective-permute-start | bytes 786440 | tf_op jit(solution)/shard_map/ppermute | solution.py:476
  12.8 23.1 %all-to-all-start = ((bf16[16,3,48,128]{3,2,1,0:T(8,128)(2,1)}), bf16[16,3,48,128]{3,2,1,0:T(8,128)(2,1)S(1)}, u32[]{:S(2)}, u32[]{:S(2)}) async-start(bf16[16,3,48,128]{3,2,1,0:T(8,128)(2,1)} %take_given.1), calls=%async_computation | async-start | bytes 1179648 | tf_op jit(solution)/shard_map/all_to_all | solution.py:479
  17.9 12.2 %copy-start.4 = (s32[96]{0:T(128)S(1)}, s32[96]{0:T(128)}, u32[]{:S(2)}) copy-start(s32[96]{0:T(128)} %rows_ref.1) | copy-start | bytes 1156
  17.9 12.2 %copy-start.9 = (s32[96]{0:T(128)S(1)}, s32[96]{0:T(128)}, u32[]{:S(2)}) copy-start(s32[96]{0:T(128)} %param.10) | copy-start | bytes 1156
  17.9 12.3 %copy-start.8 = (s32[64]{0:T(128)S(1)}, s32[64]{0:T(128)}, u32[]{:S(2)}) copy-start(s32[64]{0:T(128)} %param.8) | copy-start | bytes 772
  23.3 1.1 %copy-start.6 = (bf16[32,64,384]{2,1,0:T(8,128)(2,1)}, bf16[32,64,384]{2,1,0:T(8,128)(2,1)S(1)}, u32[]{:S(2)}) copy-start(bf16[32,64,384]{2,1,0:T(8,128)(2,1)S(1)} %get-tuple-element.23.own_ref) | copy-start | bytes 4718596
  24.5 17.6 %collective-permute-start.3 = (bf16[32,32,384]{2,1,0:T(8,128)(2,1)}, bf16[32,32,384]{2,1,0:T(8,128)(2,1)S(1)}, u32[]{:S(2)}, u32[]{:S(2)}) collective-permute-start(bf16[32,32,384]{2,1,0:T(8,128)(2,1)} %get-tuple-element.22), channel_id=1, source_target_pairs={{0,16},{16,0},{32,48},{48,32},{64,80},{80,64},{96,112},{112,96},{1... | collective-permute-start | bytes 2359304 | tf_op jit(solution)/shard_map/ppermute | solution.py:485
  26.2 15.9 %collective-permute-start.4 = (bf16[32,32,384]{2,1,0:T(8,128)(2,1)S(1)}, bf16[32,32,384]{2,1,0:T(8,128)(2,1)}, u32[]{:S(2)}, u32[]{:S(2)}) collective-permute-start(bf16[32,32,384]{2,1,0:T(8,128)(2,1)S(1)} %get-tuple-element.21.after_ref), channel_id=1, source_target_pairs={{16,32},{32,16},{48,64},{64,48},{80,96},{96,80},{112,128},{128,112... | collective-permute-start | bytes 2359304 | tf_op jit(solution)/shard_map/ppermute | solution.py:482
  30.4 11.7 %copy-start.5 = (bf16[32,32]{1,0:T(8,128)(2,1)S(1)}, bf16[32,32]{1,0:T(8,128)(2,1)}, u32[]{:S(2)}) copy-start(bf16[32,32]{1,0:T(8,128)(2,1)} %blend_ref.1) | copy-start | bytes 6148
  38.2 19.5 %all-to-all-start.1 = ((bf16[16,3,48,128]{3,2,1,0:T(8,128)(2,1)}), bf16[16,3,48,128]{3,2,1,0:T(8,128)(2,1)S(1)}, u32[]{:S(2)}, u32[]{:S(2)}) async-start(bf16[16,3,48,128]{3,2,1,0:T(8,128)(2,1)} %smooth_and_turn_polar_circles.1), calls=%async_computation.1 | async-start | bytes 1179648 | tf_op jit(solution)/shard_map/all_to_all | solution.py:486
  42.1 1.4 %copy-start.7 = (bf16[32,64,384]{2,1,0:T(8,128)(2,1)S(1)}, bf16[32,64,384]{2,1,0:T(8,128)(2,1)}, u32[]{:S(2)}) copy-start(bf16[32,64,384]{2,1,0:T(8,128)(2,1)} %copy-done.6) | copy-start | bytes 4718596
  45.6 1.6 %copy-start = (f32[32,64,384]{2,1,0:T(8,128)}, f32[32,64,384]{2,1,0:T(8,128)S(1)}, u32[]{:S(2)}) copy-start(f32[32,64,384]{2,1,0:T(8,128)S(1)} %get-tuple-element.27.lat_ref) | copy-start | bytes 9437188
  57.7 7.9 %collective-permute-start.5 = (bf16[16,3,48,128]{3,2,1,0:T(8,128)(2,1)S(1)}, bf16[16,3,48,128]{3,2,1,0:T(8,128)(2,1)S(1)}, u32[]{:S(2)}, u32[]{:S(2)}) collective-permute-start(bf16[16,3,48,128]{3,2,1,0:T(8,128)(2,1)S(1)} %all-to-all-done.1.mine_ref), channel_id=1, source_target_pairs={{0,16},{16,0},{240,224},{224,240},{1,17},{17,1},{241,225},{225,241... | collective-permute-start | bytes 1769480 | tf_op jit(solution)/shard_map/ppermute | solution.py:491

commit v15 on v14

--- a/solution.py
+++ b/solution.py
@@ -155,7 +155,7 @@
     far_rows_ref[...] = out_ref[:, pl.ds(pl.multiple_of(odd * last, LMAX), LMAX), :]
 
 
-def hold_kernel(table_ref, x_ref, after_ref, out_ref, circle_ref):
+def hold_kernel(table_ref, x_ref, after_ref, out_ref, circle_ref, stage_ref, sems):
     sectors, held, block, _ = x_ref.shape
     zone, sector = lax.axis_index("zone"), lax.axis_index("sector")
     polar = 2 * sectors * held
@@ -167,6 +167,7 @@
         for copy in range(2):
             circle_ref[r, copy * length : (copy + 1) * length, :] = x_ref[:, r].reshape(length, LANES)
         circle_ref[r, 2 * length : 2 * length + 2 * PART, :] = circle_ref[r, 0 : 2 * PART, :]
+    stores = []
     for r in range(held):
         entry = cap + sector * held + r
         half_f = jnp.full((1, LANES), table_ref[2 * polar + table_ref[entry]], jnp.int32).astype(F32)
@@ -182,7 +183,11 @@
             [circle_ref[r, pl.ds(pl.multiple_of((first + u) * PART, PART), length), :] for u in range(3)], axis=1
         )
         result = jnp.dot(values, band.astype(BF16), preferred_element_type=F32)
-        out_ref[:, r] = result.astype(BF16).reshape(sectors, block, LANES)
+        stage_ref[r] = result.astype(BF16).reshape(sectors, block, LANES)
+        stores.append(pltpu.make_async_copy(stage_ref.at[r], out_ref.at[:, r], sems.at[r]))
+        stores[-1].start()
+    for store in stores:
+        store.wait()
 
 
 def lat_kernel(rows_ref, near_ref, own_ref, far_ref, reach_ref, blend_ref,
@@ -394,10 +399,15 @@
         struct(circles.shape, BF16),
         [table],
         [circles],
-        [pltpu.VMEM((held, 2 * sectors * block + 2 * PART, LANES), BF16)],
+        [
+            pltpu.VMEM((held, 2 * sectors * block + 2 * PART, LANES), BF16),
+            pltpu.VMEM((held, sectors, block, LANES), BF16),
+            pltpu.SemaphoreType.DMA((held,)),
+        ],
         flops=1 << 30,
         moved=4 << 20,
         direct=[after],
+        far=True,
     )
 
 

time: 69.6 us -> 69.5 us (level)
  no operation moved by 1% of the time
where the time goes in v15:
time: 69.5 us; the launch traced here: 69 us
  starting transfers between devices  29.8 us (43%)
  Pallas kernels  17.8 us (26%)
  waiting for transfers between devices  16.1 us (23%)
  local copies, waits for them, and re-layouts  5.05 us (7%)
    pallas_call x5, Pallas kernels, call(): pl.pallas_call(kernel, out_shape=out_shape, in_specs=[smem] * len(scalars...  14.8 us
    all_to_all x1, waiting for transfers between devices, per_device(): mine = lax.all_to_all(turned, 'sector', 0, 0, tiled=True)  10.5 us
    ppermute x1, starting transfers between devices, per_device(): lax.ppermute(mine, 'zone', [(0, 1), (1, 0), (last, last - 1), (last - 1,...  6.12 us
    all_to_all x1, waiting for transfers between devices, per_device(): circles = lax.all_to_all(parts, 'sector', 0, 0, tiled=True)  5.58 us
    ppermute x1, starting transfers between devices, per_device(): lax.ppermute(far, 'sector', [(i, (i + 1 if i % 2 else i - 1) % sectors) f...  5.46 us
    all_to_all x1, starting transfers between devices, per_device(): circles = lax.all_to_all(parts, 'sector', 0, 0, tiled=True)  5.06 us
    unnamed x20, local copies, waits for them, and re-layouts  4.87 us
    ppermute x1, starting transfers between devices, per_device(): lax.ppermute(far_rows, 'zone', [(i, i + 1 if i % 2 else i - 1) for i in r...  3.97 us
  transfers between devices with their start and end apart: 8, of which 2 were waited for; matrix products, arithmetic and copies ran while one was open for 0% of the time, Pallas kernels for 18%

profile of v15, /device:TPU:1, one launch (start us, length us, event | category | flops | bytes accessed | tf_op | source)
XLA Modules:
  0.0 69.0 jit_solution(3525495780493269695)
XLA Ops:
  0.0 0.0 copy-start.3
  0.0 0.7 copy-done.3
  0.7 2.2 %pack_polar_rows_and_edges.1 = (bf16[16,3,48,128]{3,2,1,0:T(8,128)(2,1)S(1)}, bf16[1024,128]{1,0:T(8,128)(2,1)S(1)}, bf16[1024,128]{1,0:T(8,128)(2,1)S(1)}, bf16[16,3,48,128]{3,2,1,0:T(8,128)(2,1)}) custom-call(bf16[32,64,384]{2,1,0:T(8,128)(2,1)} %x_ref.3, s32[96]{0:T(128)S(1)} %copy-done.3), custom_call_target="tpu_custom_call" | custom-call | bytes 4194304 | tf_op jit(solution)/shard_map/pack_polar_rows_and_edges/pallas_call | solution.py:335
  2.9 0.0 copy-start.1
  2.9 0.0 copy-start.2
  2.9 1.4 %collective-permute-start = (bf16[16,3,48,128]{3,2,1,0:T(8,128)(2,1)S(1)}, bf16[16,3,48,128]{3,2,1,0:T(8,128)(2,1)S(1)}, u32[]{:S(2)}, u32[]{:S(2)}) collective-permute-start(bf16[16,3,48,128]{3,2,1,0:T(8,128)(2,1)S(1)} %get-tuple-element.17), channel_id=1, source_target_pairs={{0,16},{240,224},{1,17},{241,225},{2,18},{242,226},{3,19},{243,227... | collective-permute-start | bytes 1769480 | tf_op jit(solution)/shard_map/ppermute | solution.py:485
  4.3 2.2 %collective-permute-start.1 = (bf16[1024,128]{1,0:T(8,128)(2,1)S(1)}, bf16[1024,128]{1,0:T(8,128)(2,1)S(1)}, u32[]{:S(2)}, u32[]{:S(2)}) collective-permute-start(bf16[1024,128]{1,0:T(8,128)(2,1)S(1)} %get-tuple-element.19), channel_id=1, source_target_pairs={{0,1},{1,0},{2,3},{3,2},{4,5},{5,4},{6,7},{7,6},{8,9},{9,8},{10,11... | collective-permute-start | bytes 786440 | tf_op jit(solution)/shard_map/ppermute | solution.py:487
  6.6 5.5 %collective-permute-start.2 = (bf16[1024,128]{1,0:T(8,128)(2,1)S(1)}, bf16[1024,128]{1,0:T(8,128)(2,1)S(1)}, u32[]{:S(2)}, u32[]{:S(2)}) collective-permute-start(bf16[1024,128]{1,0:T(8,128)(2,1)S(1)} %get-tuple-element.20), channel_id=1, source_target_pairs={{0,15},{1,2},{2,1},{3,4},{4,3},{5,6},{6,5},{7,8},{8,7},{9,10},{10,... | collective-permute-start | bytes 786440 | tf_op jit(solution)/shard_map/ppermute | solution.py:486
  12.0 0.0 collective-permute-done.given_ref
  12.0 0.8 %take_given.1 = bf16[16,3,48,128]{3,2,1,0:T(8,128)(2,1)} custom-call(bf16[16,3,48,128]{3,2,1,0:T(8,128)(2,1)S(1)} %collective-permute-done.given_ref, bf16[16,3,48,128]{3,2,1,0:T(8,128)(2,1)} %get-tuple-element.18.kept_ref), custom_call_target="tpu_custom_call", output_to_operand_aliasing={{}: (1, {})} | custom-call | tf_op jit(solution)/shard_map/take_given/pallas_call | solution.py:355
  12.8 5.1 %all-to-all-start = ((bf16[16,3,48,128]{3,2,1,0:T(8,128)(2,1)}), bf16[16,3,48,128]{3,2,1,0:T(8,128)(2,1)S(1)}, u32[]{:S(2)}, u32[]{:S(2)}) async-start(bf16[16,3,48,128]{3,2,1,0:T(8,128)(2,1)} %take_given.1), calls=%async_computation | async-start | bytes 1179648 | tf_op jit(solution)/shard_map/all_to_all | solution.py:489
  17.9 0.0 copy-start.4
  17.9 0.0 copy-start.9
  17.9 0.0 copy-start.8
  18.0 0.0 collective-permute-done.1.near_ref
  18.0 0.0 collective-permute-done.2.far_ref
  18.0 0.0 copy-done.1
  18.0 0.0 copy-done.2
  18.0 5.3 %smooth_along_longitude.1 = (bf16[32,64,384]{2,1,0:T(8,128)(2,1)S(1)}, bf16[32,32,384]{2,1,0:T(8,128)(2,1)}, bf16[32,32,384]{2,1,0:T(8,128)(2,1)S(1)}) custom-call(s32[1024]{0:T(1024)S(1)} %copy-done.2, bf16[32,64,384]{2,1,0:T(8,128)(2,1)S(1)} %copy-done.1, bf16[1024,128]{1,0:T(8,128)(2,1)S(1)} %collective-permute-done.1.near_ref, ...), custom_call_target="tpu_custom_call" | custom-call | flops 68719476736 | bytes 16777216 | tf_op jit(solution)/shard_map/smooth_along_longitude/pallas_call | solution.py:312
  23.3 0.0 copy-start.6
  23.3 1.1 %copy-done.6 = bf16[32,64,384]{2,1,0:T(8,128)(2,1)} copy-done((bf16[32,64,384]{2,1,0:T(8,128)(2,1)}, bf16[32,64,384]{2,1,0:T(8,128)(2,1)S(1)}, u32[]{:S(2)}) %copy-start.6) | copy-done | bytes 1572888
  24.5 1.7 %collective-permute-start.3 = (bf16[32,32,384]{2,1,0:T(8,128)(2,1)}, bf16[32,32,384]{2,1,0:T(8,128)(2,1)S(1)}, u32[]{:S(2)}, u32[]{:S(2)}) collective-permute-start(bf16[32,32,384]{2,1,0:T(8,128)(2,1)} %get-tuple-element.22), channel_id=1, source_target_pairs={{0,16},{16,0},{32,48},{48,32},{64,80},{80,64},{96,112},{112,96},{1... | collective-permute-start | bytes 2359304 | tf_op jit(solution)/shard_map/ppermute | solution.py:495
  26.2 4.0 %collective-permute-start.4 = (bf16[32,32,384]{2,1,0:T(8,128)(2,1)S(1)}, bf16[32,32,384]{2,1,0:T(8,128)(2,1)}, u32[]{:S(2)}, u32[]{:S(2)}) collective-permute-start(bf16[32,32,384]{2,1,0:T(8,128)(2,1)S(1)} %get-tuple-element.21.after_ref), channel_id=1, source_target_pairs={{16,32},{32,16},{48,64},{64,48},{80,96},{96,80},{112,128},{128,112... | collective-permute-start | bytes 2359304 | tf_op jit(solution)/shard_map/ppermute | solution.py:492
  30.2 0.0 copy-done.4
  30.2 0.0 copy-done.9
  30.2 0.1 concatenate.3.table_ref
  30.3 0.0 copy-done.8
  30.3 0.1 copy.8.reach_ref
  30.4 0.0 copy-start.5
  30.4 5.6 %all-to-all-done.x_ref = bf16[16,3,48,128]{3,2,1,0:T(8,128)(2,1)S(1)} async-done(((bf16[16,3,48,128]{3,2,1,0:T(8,128)(2,1)}), bf16[16,3,48,128]{3,2,1,0:T(8,128)(2,1)S(1)}, u32[]{:S(2)}, u32[]{:S(2)}) %all-to-all-start) | async-done | bytes 589856 | tf_op jit(solution)/shard_map/all_to_all | solution.py:489
  35.9 2.2 %smooth_and_turn_polar_circles.1 = bf16[16,3,48,128]{3,2,1,0:T(8,128)(2,1)} custom-call(s32[1216]{0:T(1024)S(1)} %concatenate.3.table_ref, bf16[16,3,48,128]{3,2,1,0:T(8,128)(2,1)S(1)} %all-to-all-done.x_ref, bf16[32,32,384]{2,1,0:T(8,128)(2,1)S(1)} %get-tuple-element.21.after_ref), custom_call_target="tpu_custom_call" | custom-call | flops 1073741824 | bytes 4194304 | tf_op jit(solution)/shard_map/smooth_and_turn_polar_circles/pallas_call | solution.py:312
  38.1 3.8 %all-to-all-start.1 = ((bf16[16,3,48,128]{3,2,1,0:T(8,128)(2,1)}), bf16[16,3,48,128]{3,2,1,0:T(8,128)(2,1)S(1)}, u32[]{:S(2)}, u32[]{:S(2)}) async-start(bf16[16,3,48,128]{3,2,1,0:T(8,128)(2,1)} %smooth_and_turn_polar_circles.1), calls=%async_computation.1 | async-start | bytes 1179648 | tf_op jit(solution)/shard_map/all_to_all | solution.py:496
  41.9 0.0 collective-permute-done.3.near_ref
  41.9 0.0 collective-permute-done.4.far_ref
  42.0 0.0 copy-done.5
  42.0 0.0 copy-start.7
  42.0 1.4 %copy-done.7 = bf16[32,64,384]{2,1,0:T(8,128)(2,1)S(1)} copy-done((bf16[32,64,384]{2,1,0:T(8,128)(2,1)S(1)}, bf16[32,64,384]{2,1,0:T(8,128)(2,1)}, u32[]{:S(2)}) %copy-start.7) | copy-done | bytes 1572888
  43.4 2.1 %smooth_along_latitude.1 = (f32[32,64,384]{2,1,0:T(8,128)S(1)}, bf16[64,48]{1,0:T(8,128)(2,1)S(1)}, bf16[256,256]{1,0:T(8,128)(2,1)S(1)}) custom-call(s32[96]{0:T(128)S(1)} %copy-done.4, bf16[32,32,384]{2,1,0:T(8,128)(2,1)S(1)} %collective-permute-done.3.near_ref, bf16[32,64,384]{2,1,0:T(8,128)(2,1)S(1)} %copy-done.7, ...), custom_call_target="tpu_custom_call" | custom-call | flops 68719476736 | bytes 8388608 | tf_op jit(solution)/shard_map/smooth_along_latitude/pallas_call | solution.py:312
  45.5 0.0 copy-start
  45.5 1.6 %copy-done = f32[32,64,384]{2,1,0:T(8,128)} copy-done((f32[32,64,384]{2,1,0:T(8,128)}, f32[32,64,384]{2,1,0:T(8,128)S(1)}, u32[]{:S(2)}) %copy-start) | copy-done | bytes 3145752
  47.1 10.5 %all-to-all-done.1.mine_ref = bf16[16,3,48,128]{3,2,1,0:T(8,128)(2,1)S(1)} async-done(((bf16[16,3,48,128]{3,2,1,0:T(8,128)(2,1)}), bf16[16,3,48,128]{3,2,1,0:T(8,128)(2,1)S(1)}, u32[]{:S(2)}, u32[]{:S(2)}) %all-to-all-start.1) | async-done | bytes 589856 | tf_op jit(solution)/shard_map/all_to_all | solution.py:496
  57.6 6.1 %collective-permute-start.5 = (bf16[16,3,48,128]{3,2,1,0:T(8,128)(2,1)S(1)}, bf16[16,3,48,128]{3,2,1,0:T(8,128)(2,1)S(1)}, u32[]{:S(2)}, u32[]{:S(2)}) collective-permute-start(bf16[16,3,48,128]{3,2,1,0:T(8,128)(2,1)S(1)} %all-to-all-done.1.mine_ref), channel_id=1, source_target_pairs={{0,16},{16,0},{240,224},{224,240},{1,17},{17,1},{241,225},{225,241... | collective-permute-start | bytes 1769480 | tf_op jit(solution)/shard_map/ppermute | solution.py:501
  63.8 1.8 %add_polar_rows_of_own_shells.1.own_ref = bf16[16,64,384]{2,1,0:T(8,128)(2,1)S(1)} custom-call(bf16[16,3,48,128]{3,2,1,0:T(8,128)(2,1)S(1)} %all-to-all-done.1.mine_ref, bf16[64,48]{1,0:T(8,128)(2,1)S(1)} %get-tuple-element.26.weight_ref, f32[32,64,384]{2,1,0:T(8,128)} %copy-done), custom_call_target="tpu_custom_call" | custom-call | flops 1073741824 | bytes 4194304 | tf_op jit(solution)/shard_map/add_polar_rows_of_own_shells/pallas_call | solution.py:312
  65.5 0.0 collective-permute-done.5.other_ref
  65.5 3.4 %add_polar_rows_and_blend.1 = bf16[32,64,384]{2,1,0:T(8,128)(2,1)} custom-call(bf16[16,3,48,128]{3,2,1,0:T(8,128)(2,1)S(1)} %collective-permute-done.5.other_ref, bf16[16,64,384]{2,1,0:T(8,128)(2,1)S(1)} %add_polar_rows_of_own_shells.1.own_ref, bf16[64,48]{1,0:T(8,128)(2,1)S(1)} %get-tuple-element.26.weight_ref, ...), custom_call_target="tpu_custom_call" | custom-call | flops 2147483648 | bytes 8388608 | tf_op jit(solution)/shard_map/add_polar_rows_and_blend/pallas_call | solution.py:312
Async XLA Ops:
  0.0 0.7 copy-start.3
  2.9 15.1 %copy-start.1 = (bf16[32,64,384]{2,1,0:T(8,128)(2,1)S(1)}, bf16[32,64,384]{2,1,0:T(8,128)(2,1)}, u32[]{:S(2)}) copy-start(bf16[32,64,384]{2,1,0:T(8,128)(2,1)} %x_ref.3) | copy-start | bytes 4718596
  2.9 15.1 %copy-start.2 = (s32[1024]{0:T(1024)S(1)}, s32[1024]{0:T(1024)}, u32[]{:S(2)}) copy-start(s32[1024]{0:T(1024)} %halo_ref.1) | copy-start | bytes 12292
  2.9 9.1 %collective-permute-start = (bf16[16,3,48,128]{3,2,1,0:T(8,128)(2,1)S(1)}, bf16[16,3,48,128]{3,2,1,0:T(8,128)(2,1)S(1)}, u32[]{:S(2)}, u32[]{:S(2)}) collective-permute-start(bf16[16,3,48,128]{3,2,1,0:T(8,128)(2,1)S(1)} %get-tuple-element.17), channel_id=1, source_target_pairs={{0,16},{240,224},{1,17},{241,225},{2,18},{242,226},{3,19},{243,227... | collective-permute-start | bytes 1769480 | tf_op jit(solution)/shard_map/ppermute | solution.py:485
  4.3 13.6 %collective-permute-start.1 = (bf16[1024,128]{1,0:T(8,128)(2,1)S(1)}, bf16[1024,128]{1,0:T(8,128)(2,1)S(1)}, u32[]{:S(2)}, u32[]{:S(2)}) collective-permute-start(bf16[1024,128]{1,0:T(8,128)(2,1)S(1)} %get-tuple-element.19), channel_id=1, source_target_pairs={{0,1},{1,0},{2,3},{3,2},{4,5},{5,4},{6,7},{7,6},{8,9},{9,8},{10,11... | collective-permute-start | bytes 786440 | tf_op jit(solution)/shard_map/ppermute | solution.py:487
  6.6 11.4 %collective-permute-start.2 = (bf16[1024,128]{1,0:T(8,128)(2,1)S(1)}, bf16[1024,128]{1,0:T(8,128)(2,1)S(1)}, u32[]{:S(2)}, u32[]{:S(2)}) collective-permute-start(bf16[1024,128]{1,0:T(8,128)(2,1)S(1)} %get-tuple-element.20), channel_id=1, source_target_pairs={{0,15},{1,2},{2,1},{3,4},{4,3},{5,6},{6,5},{7,8},{8,7},{9,10},{10,... | collective-permute-start | bytes 786440 | tf_op jit(solution)/shard_map/ppermute | solution.py:486
  12.8 23.1 %all-to-all-start = ((bf16[16,3,48,128]{3,2,1,0:T(8,128)(2,1)}), bf16[16,3,48,128]{3,2,1,0:T(8,128)(2,1)S(1)}, u32[]{:S(2)}, u32[]{:S(2)}) async-start(bf16[16,3,48,128]{3,2,1,0:T(8,128)(2,1)} %take_given.1), calls=%async_computation | async-start | bytes 1179648 | tf_op jit(solution)/shard_map/all_to_all | solution.py:489
  17.9 12.2 %copy-start.4 = (s32[96]{0:T(128)S(1)}, s32[96]{0:T(128)}, u32[]{:S(2)}) copy-start(s32[96]{0:T(128)} %rows_ref.1) | copy-start | bytes 1156
  17.9 12.2 %copy-start.9 = (s32[96]{0:T(128)S(1)}, s32[96]{0:T(128)}, u32[]{:S(2)}) copy-start(s32[96]{0:T(128)} %param.10) | copy-start | bytes 1156
  17.9 12.3 %copy-start.8 = (s32[64]{0:T(128)S(1)}, s32[64]{0:T(128)}, u32[]{:S(2)}) copy-start(s32[64]{0:T(128)} %param.8) | copy-start | bytes 772
  23.3 1.1 %copy-start.6 = (bf16[32,64,384]{2,1,0:T(8,128)(2,1)}, bf16[32,64,384]{2,1,0:T(8,128)(2,1)S(1)}, u32[]{:S(2)}) copy-start(bf16[32,64,384]{2,1,0:T(8,128)(2,1)S(1)} %get-tuple-element.23.own_ref) | copy-start | bytes 4718596
  24.5 17.5 %collective-permute-start.3 = (bf16[32,32,384]{2,1,0:T(8,128)(2,1)}, bf16[32,32,384]{2,1,0:T(8,128)(2,1)S(1)}, u32[]{:S(2)}, u32[]{:S(2)}) collective-permute-start(bf16[32,32,384]{2,1,0:T(8,128)(2,1)} %get-tuple-element.22), channel_id=1, source_target_pairs={{0,16},{16,0},{32,48},{48,32},{64,80},{80,64},{96,112},{112,96},{1... | collective-permute-start | bytes 2359304 | tf_op jit(solution)/shard_map/ppermute | solution.py:495
  26.2 15.8 %collective-permute-start.4 = (bf16[32,32,384]{2,1,0:T(8,128)(2,1)S(1)}, bf16[32,32,384]{2,1,0:T(8,128)(2,1)}, u32[]{:S(2)}, u32[]{:S(2)}) collective-permute-start(bf16[32,32,384]{2,1,0:T(8,128)(2,1)S(1)} %get-tuple-element.21.after_ref), channel_id=1, source_target_pairs={{16,32},{32,16},{48,64},{64,48},{80,96},{96,80},{112,128},{128,112... | collective-permute-start | bytes 2359304 | tf_op jit(solution)/shard_map/ppermute | solution.py:492
  30.4 11.6 %copy-start.5 = (bf16[32,32]{1,0:T(8,128)(2,1)S(1)}, bf16[32,32]{1,0:T(8,128)(2,1)}, u32[]{:S(2)}) copy-start(bf16[32,32]{1,0:T(8,128)(2,1)} %blend_ref.1) | copy-start | bytes 6148
  38.1 19.5 %all-to-all-start.1 = ((bf16[16,3,48,128]{3,2,1,0:T(8,128)(2,1)}), bf16[16,3,48,128]{3,2,1,0:T(8,128)(2,1)S(1)}, u32[]{:S(2)}, u32[]{:S(2)}) async-start(bf16[16,3,48,128]{3,2,1,0:T(8,128)(2,1)} %smooth_and_turn_polar_circles.1), calls=%async_computation.1 | async-start | bytes 1179648 | tf_op jit(solution)/shard_map/all_to_all | solution.py:496
  42.0 1.4 %copy-start.7 = (bf16[32,64,384]{2,1,0:T(8,128)(2,1)S(1)}, bf16[32,64,384]{2,1,0:T(8,128)(2,1)}, u32[]{:S(2)}) copy-start(bf16[32,64,384]{2,1,0:T(8,128)(2,1)} %copy-done.6) | copy-start | bytes 4718596
  45.5 1.6 %copy-start = (f32[32,64,384]{2,1,0:T(8,128)}, f32[32,64,384]{2,1,0:T(8,128)S(1)}, u32[]{:S(2)}) copy-start(f32[32,64,384]{2,1,0:T(8,128)S(1)} %get-tuple-element.27.lat_ref) | copy-start | bytes 9437188
  57.6 7.9 %collective-permute-start.5 = (bf16[16,3,48,128]{3,2,1,0:T(8,128)(2,1)S(1)}, bf16[16,3,48,128]{3,2,1,0:T(8,128)(2,1)S(1)}, u32[]{:S(2)}, u32[]{:S(2)}) collective-permute-start(bf16[16,3,48,128]{3,2,1,0:T(8,128)(2,1)S(1)} %all-to-all-done.1.mine_ref), channel_id=1, source_target_pairs={{0,16},{16,0},{240,224},{224,240},{1,17},{17,1},{241,225},{225,241... | collective-permute-start | bytes 1769480 | tf_op jit(solution)/shard_map/ppermute | solution.py:501
